TPU v7x, 256 devices: a whole 4x4x8 slice. The times are simulated.
256 devices in a mesh: row: 32 (over z, x), col: 8 (over y, core).
Axes of the slice: x: 4, y: 4, z: 8, core: 2. Of those that a mesh axis runs over, the one named last changes fastest.
Arguments:
- normed_input: bfloat16 [2048, 16384], P('col', 'row'), may hold values from -6 to 6
- attended: bfloat16 [2048, 16384], P('col', 'row'), may hold values from -6 to 6
- qkv_grad: bfloat16 [2048, 18432], P('row', 'col'), may hold values from -0.13183594 to 0.13183594
- proj_grad: bfloat16 [2048, 16384], P('row', 'col'), may hold values from -0.13183594 to 0.13183594
Outputs:
- qkv_weight_grad: bfloat16 [16384, 18432], P('row', 'col')
- out_weight_grad: bfloat16 [16384, 16384], P('row', 'col')
All inputs are finite; a program needn't handle non-finite values.
Results may differ from a plain program's by a relative error of at most 0.001.
Values may be sent and summed in bfloat16 or wider, within the bound.
No kernel may reach another device: no remote copies, remote signals or barrier semaphores. Data moves between devices by JAX's collectives and lax.ppermute only.
A program may use at most 128 MiB of HBM per device.

v0:
```python
import jax
import jax.numpy as jnp
from jax import lax
from jax.sharding import PartitionSpec as P


def contract(left, right):
    return lax.dot_general(
        left, right, (((0,), (0,)), ((), ())), preferred_element_type=jnp.float32
    )


def body(normed_input, attended, qkv_grad, proj_grad):
    inputs_all, attended_all = (
        lax.all_gather(normed_input, "col", axis=0, tiled=True),
        lax.all_gather(attended, "col", axis=0, tiled=True),
    )
    qkv_total = contract(inputs_all, lax.all_gather(qkv_grad, "row", axis=0, tiled=True))
    out_total = contract(attended_all, lax.all_gather(proj_grad, "row", axis=0, tiled=True))
    return (qkv_total.astype(jnp.bfloat16), out_total.astype(jnp.bfloat16))


def solution(mesh):
    placed = (P("col", "row"), P("col", "row"), P("row", "col"), P("row", "col"))
    return jax.shard_map(
        body,
        mesh=mesh,
        in_specs=placed,
        out_specs=(P("row", "col"), P("row", "col")),
        check_vma=False,
    )
```

profile of v0, /device:TPU:8, one launch (start us, length us, event | category | flops | bytes accessed | tf_op | source)
XLA Modules:
  0.0 291.6 jit_solution(18367470680000510965)
XLA Ops:
  7.2 0.0 all-gather.9.cloned.1.call-start
  7.2 0.7 all-gather.9.cloned.1.call-update
  7.9 0.0 all-gather.11.cloned.1.call-start
  7.9 0.7 all-gather.11.cloned.1.call-update
  8.6 0.0 all-gather.5.cloned.1.call-start
  8.7 0.7 all-gather.5.cloned.1.call-update
  9.4 0.0 all-gather.7.cloned.1.call-start
  9.4 0.5 all-gather.7.cloned.1.call-update
  10.0 29.6 %all-gather.9.cloned.1.call-done = bf16[2048,512]{1,0:T(8,128)(2,1)} async-done(((bf16[256,512]{1,0:T(8,128)(2,1)}), bf16[2048,512]{1,0:T(8,128)(2,1)}) %all-gather.9.cloned.1.call-update) | async-done | bytes 2097168 | tf_op jit(solution)/shard_map/all_gather | solution.py:16
  39.6 102.2 %all-gather.11.cloned.1.call-done = bf16[2048,2048]{1,0:T(8,128)(2,1)} async-done(((bf16[64,2048]{1,0:T(8,128)(2,1)}), bf16[2048,2048]{1,0:T(8,128)(2,1)}) %all-gather.11.cloned.1.call-update) | async-done | bytes 8388624 | tf_op jit(solution)/shard_map/all_gather | solution.py:19
  141.7 9.9 %convolution_convert_fusion.1 = bf16[512,2048]{1,0:T(8,128)(2,1)} fusion(bf16[2048,512]{1,0:T(8,128)(2,1)} %all-gather.9.cloned.1.call-done, bf16[2048,2048]{1,0:T(8,128)(2,1)} %all-gather.11.cloned.1.call-done), kind=kOutput, calls=%fused_computation.1 | convolution fusion | flops 4296015872 | bytes 12582912 | tf_op jit(solution)/shard_map/dot_general | solution.py:8
  151.6 15.9 %all-gather.5.cloned.1.call-done = bf16[2048,512]{1,0:T(8,128)(2,1)} async-done(((bf16[256,512]{1,0:T(8,128)(2,1)}), bf16[2048,512]{1,0:T(8,128)(2,1)}) %all-gather.5.cloned.1.call-update) | async-done | bytes 2097168 | tf_op jit(solution)/shard_map/all_gather | solution.py:15
  167.5 107.2 %all-gather.7.cloned.1.call-done = bf16[2048,2304]{1,0:T(8,128)(2,1)} async-done(((bf16[64,2304]{1,0:T(8,128)(2,1)}), bf16[2048,2304]{1,0:T(8,128)(2,1)}) %all-gather.7.cloned.1.call-update) | async-done | bytes 9437200 | tf_op jit(solution)/shard_map/all_gather | solution.py:18
  274.7 10.3 %convolution_convert_fusion = bf16[512,2304]{1,0:T(8,128)(2,1)} fusion(bf16[2048,512]{1,0:T(8,128)(2,1)} %all-gather.5.cloned.1.call-done, bf16[2048,2304]{1,0:T(8,128)(2,1)} %all-gather.7.cloned.1.call-done), kind=kOutput, calls=%fused_computation | convolution fusion | flops 4833017856 | bytes 13893632 | tf_op jit(solution)/shard_map/dot_general | solution.py:8
Async XLA Ops:
  7.2 32.4 %all-gather.9.cloned.1.call-start = ((), (), s32[]{:S(2)}) async-start(), calls=%async_computation.2 | async-start | bytes 2359296 | tf_op jit(solution)/shard_map/all_gather | solution.py:16
  7.9 133.8 %all-gather.11.cloned.1.call-start = ((), (), s32[]{:S(2)}) async-start(), calls=%async_computation.3 | async-start | bytes 8650752 | tf_op jit(solution)/shard_map/all_gather | solution.py:19
  8.6 158.9 %all-gather.5.cloned.1.call-start = ((), (), s32[]{:S(2)}) async-start(), calls=%async_computation | async-start | bytes 2359296 | tf_op jit(solution)/shard_map/all_gather | solution.py:15
  9.4 265.4 %all-gather.7.cloned.1.call-start = ((), (), s32[]{:S(2)}) async-start(), calls=%async_computation.1 | async-start | bytes 9732096 | tf_op jit(solution)/shard_map/all_gather | solution.py:18
Sparse Core Ops, SparseCore 0:
  9.9 29.6 all-gather.8
  42.1 99.5 all-gather.10
  143.6 23.8 all-gather.4
  170.0 104.7 all-gather.6
where the time goes:
time: 292 us
  waiting for transfers between devices  257 us (88%)
  matrix products  20.2 us (7%)
  between operations  13.8 us (5%)
    all_gather x1, waiting for transfers between devices, body(): lax.all_gather(qkv_grad, 'row', axis=0, tiled=True)  107 us
    all_gather x1, waiting for transfers between devices, body(): lax.all_gather(proj_grad, 'row', axis=0, tiled=True)  102 us
    all_gather x1, waiting for transfers between devices, body(): lax.all_gather(attended, 'col', axis=0, tiled=True)  29.6 us
    dot_general x2, matrix products, contract(): lax.dot_general(left, right, (((0,), (0,)), ((), ())), preferred_element_...  20.2 us
    all_gather x1, waiting for transfers between devices, body(): lax.all_gather(normed_input, 'col', axis=0, tiled=True)  15.9 us
  transfers between devices with their start and end apart: 4, of which 4 were waited for; matrix products, arithmetic and copies ran while one was open for 3% of the time, Pallas kernels for 0%

commit v1 on v0

v1 whole, which is shorter than its diff:
```python
import jax
import jax.numpy as jnp
from jax import lax
from jax.sharding import PartitionSpec as P

Z, X = 8, 4


def hop(value, dz, dx):
    pairs = [
        (z * X + x, ((z + dz) % Z) * X + (x + dx) % X) for z in range(Z) for x in range(X)
    ]
    return lax.ppermute(value, "row", pairs)


def ring(value, size, step):
    up = lambda v: hop(v, *step)
    down = lambda v: hop(v, -step[0], -step[1])
    blocks = {0: value}
    below = above = value
    for distance in range(1, size // 2):
        below, above = up(below), down(above)
        blocks[-distance], blocks[distance] = below, above
    half = value.shape[0] // 2
    blocks[size // 2] = jnp.concatenate([up(below[:half]), down(above[half:])])
    return blocks


Z_ORDER = (0, -1, 1, -2, 2, -3, 3, 4)
X_ORDER = (0, -1, 1, 2)


def contract(left, right):
    return lax.dot_general(
        left, right, (((0,), (0,)), ((), ())), preferred_element_type=jnp.float32
    )


def body(normed_input, attended, qkv_grad, proj_grad):
    place = lax.axis_index("row")
    z, x = place // X, place % X
    features = normed_input.shape[1]
    both = lax.all_gather(
        jnp.concatenate([normed_input, attended], axis=1), "col", axis=0, tiled=True
    )
    tokens = both.shape[0]
    both = both.reshape(Z, X, tokens // (Z * X), 2 * features)
    both = lax.dynamic_slice_in_dim(jnp.concatenate([both, both], 0), z, Z, 0)
    both = lax.dynamic_slice_in_dim(jnp.concatenate([both, both], 1), x, X, 1)

    def tokens_at(dz, dx, op):
        return both[dz % Z, dx % X, :, op * features : (op + 1) * features]

    near = ring(proj_grad, X, (0, 1))
    far = ring(jnp.concatenate([near[d] for d in X_ORDER]), Z, (1, 0))
    tall = ring(qkv_grad, Z, (1, 0))
    wide = ring(jnp.concatenate([tall[d] for d in Z_ORDER]), X, (0, 1))

    qkv = 0
    for dx in X_ORDER:
        left = jnp.concatenate([tokens_at(dz, dx, 0) for dz in Z_ORDER])
        qkv = qkv + contract(left, wide[dx])
    out = 0
    for dz in Z_ORDER:
        left = jnp.concatenate([tokens_at(dz, dx, 1) for dx in X_ORDER])
        out = out + contract(left, far[dz])
    return qkv.astype(jnp.bfloat16), out.astype(jnp.bfloat16)


def solution(mesh):
    placed = (P("col", "row"), P("col", "row"), P("row", "col"), P("row", "col"))
    return jax.shard_map(
        body,
        mesh=mesh,
        in_specs=placed,
        out_specs=(P("row", "col"), P("row", "col")),
        check_vma=False,
    )
```

time: 292 us -> 194 us (0.66)
  waiting for transfers between devices: 257 us -> 69.4 us
  starting transfers between devices: 0.15 us -> 38 us
  local copies, waits for them, and re-layouts: 0 us -> 25.9 us
  matrix products: 20.2 us -> 37.3 us
  other arithmetic: 0 us -> 6.78 us
    all_gather x4 -> x1, waiting for transfers between devices: 255 us -> 0.01 us  [body(): lax.all_gather(jnp.concatenate([normed_input, attended], axis=1), 'col',...]
    ppermute x0 -> x24, waiting for transfers between devices: none -> 69.3 us  [hop(): return lax.ppermute(value, 'row', pairs)]
    ppermute x0 -> x24, starting transfers between devices: none -> 38 us  [hop(): return lax.ppermute(value, 'row', pairs)]
    dot_general x2 -> x12, matrix products: 20.2 us -> 37.3 us  [contract(): lax.dot_general(left, right, (((0,), (0,)), ((), ())), preferred_element_...]
    unnamed x0 -> x69, local copies, waits for them, and re-layouts: none -> 15 us
    concatenate x0 -> x3, other arithmetic: none -> 6.78 us  [the longest x1 3.12 us: body(): both = lax.dynamic_slice_in_dim(jnp.concatenate([both, both], 0), z, Z, 0)]
    slice x0 -> x8, local copies, waits for them, and re-layouts: none -> 6.23 us  [ring(): blocks[size // 2] = jnp.concatenate([up(below[:half]), down(above[half:])])]
    squeeze x0 -> x2, local copies, waits for them, and re-layouts: none -> 3.05 us  [tokens_at(): return both[dz % Z, dx % X, :, op * features:(op + 1) * features]]
  transfers between devices with their start and end apart: 4 -> 25, of which waited for: 4 -> 7; matrix products, arithmetic and copies ran while one was open for 3% -> 28% of each run, Pallas kernels for 0% -> 0%
where the time goes in v1:
time: 194 us; the launch traced here: 192 us
  waiting for transfers between devices  69.4 us (36%)
  starting transfers between devices  38 us (20%)
  matrix products  37.3 us (19%)
  local copies, waits for them, and re-layouts  25.9 us (13%)
  between operations  14.6 us (8%)
  other arithmetic  6.78 us (3%)
    ppermute x24, waiting for transfers between devices, hop(): return lax.ppermute(value, 'row', pairs)  69.3 us
    ppermute x24, starting transfers between devices, hop(): return lax.ppermute(value, 'row', pairs)  38 us
    dot_general x12, matrix products, contract(): lax.dot_general(left, right, (((0,), (0,)), ((), ())), preferred_element_...  37.3 us
    unnamed x69, local copies, waits for them, and re-layouts  15 us
    slice x8, local copies, waits for them, and re-layouts, ring(): blocks[size // 2] = jnp.concatenate([up(below[:half]), down(above[half:])])  6.23 us
  transfers between devices with their start and end apart: 25, of which 7 were waited for; matrix products, arithmetic and copies ran while one was open for 28% of the time, Pallas kernels for 0%

profile of v1, /device:TPU:8, one launch (start us, length us, event | category | flops | bytes accessed | tf_op | source)
XLA Modules:
  0.0 192.0 jit_solution(3771187819546106378)
XLA Ops:
  7.2 1.9 pad_maximum_fusion
  10.7 1.7 collective-permute-start.13
  12.4 1.9 collective-permute-start
  14.3 3.9 %collective-permute-start.1 = (bf16[64,2304]{1,0:T(8,128)(2,1)}, bf16[64,2304]{1,0:T(8,128)(2,1)S(1)}, u32[]{:S(2)}, u32[]{:S(2)}) collective-permute-start(bf16[64,2304]{1,0:T(8,128)(2,1)} %param.6), channel_id=1, source_target_pairs={{0,224},{8,232},{16,240},{24,248},{32,0},{40,8},{48,16},{56,24},{6... | collective-permute-start | bytes 884744 | tf_op jit(solution)/shard_map/ppermute | solution.py:13
  18.3 1.7 constant_dynamic-update-slice_fusion.16
  21.4 3.0 %collective-permute-start.15 = (bf16[32,2048]{1,0:T(8,128)(2,1)S(1)}, bf16[32,2048]{1,0:T(8,128)(2,1)S(1)}, u32[]{:S(2)}, u32[]{:S(2)}) collective-permute-start(bf16[32,2048]{1,0:T(8,128)(2,1)S(1)} %slice.329), channel_id=1, source_target_pairs={{0,24},{8,0},{16,8},{24,16},{32,56},{40,32},{48,40},{56,48},{64,88... | collective-permute-start | bytes 393224 | tf_op jit(solution)/shard_map/ppermute | solution.py:13
  24.9 3.2 %collective-permute-start.3 = (bf16[64,2304]{1,0:T(8,128)(2,1)S(1)}, bf16[64,2304]{1,0:T(8,128)(2,1)S(1)}, u32[]{:S(2)}, u32[]{:S(2)}) collective-permute-start(bf16[64,2304]{1,0:T(8,128)(2,1)S(1)} %collective-permute-done.1), channel_id=1, source_target_pairs={{0,224},{8,232},{16,240},{24,248},{32,0},{40,8},{48,16},{56,24},{6... | collective-permute-start | bytes 884744 | tf_op jit(solution)/shard_map/ppermute | solution.py:13
  29.7 2.0 %collective-permute-start.17 = (bf16[256,2048]{1,0:T(8,128)(2,1)S(1)}, bf16[256,2048]{1,0:T(8,128)(2,1)S(1)}, u32[]{:S(2)}, u32[]{:S(2)}) collective-permute-start(bf16[256,2048]{1,0:T(8,128)(2,1)S(1)} %constant_dynamic-update-slice_fusion.41), channel_id=1, source_target_pairs={{0,224},{8,232},{16,240},{24,248},{32,0},{40,8},{48,16},{56,24},{6... | collective-permute-start | bytes 3145736 | tf_op jit(solution)/shard_map/ppermute | solution.py:13
  31.8 2.4 %collective-permute-done.2 = bf16[64,2304]{1,0:T(8,128)(2,1)S(1)} collective-permute-done((bf16[64,2304]{1,0:T(8,128)(2,1)S(1)}, bf16[64,2304]{1,0:T(8,128)(2,1)S(1)}, u32[]{:S(2)}, u32[]{:S(2)}) %collective-permute-start.2) | collective-permute-done | bytes 294944 | tf_op jit(solution)/shard_map/ppermute | solution.py:13
  35.6 3.7 %collective-permute-start.5 = (bf16[64,2304]{1,0:T(8,128)(2,1)S(1)}, bf16[64,2304]{1,0:T(8,128)(2,1)S(1)}, u32[]{:S(2)}, u32[]{:S(2)}) collective-permute-start(bf16[64,2304]{1,0:T(8,128)(2,1)S(1)} %collective-permute-done.3), channel_id=1, source_target_pairs={{0,224},{8,232},{16,240},{24,248},{32,0},{40,8},{48,16},{56,24},{6... | collective-permute-start | bytes 884744 | tf_op jit(solution)/shard_map/ppermute | solution.py:13
  40.8 21.7 %collective-permute-done.4 = bf16[64,2304]{1,0:T(8,128)(2,1)S(1)} collective-permute-done((bf16[64,2304]{1,0:T(8,128)(2,1)S(1)}, bf16[64,2304]{1,0:T(8,128)(2,1)S(1)}, u32[]{:S(2)}, u32[]{:S(2)}) %collective-permute-start.4) | collective-permute-done | bytes 294944 | tf_op jit(solution)/shard_map/ppermute | solution.py:13
  62.6 3.3 %collective-permute-start.7 = (bf16[32,2304]{1,0:T(8,128)(2,1)S(1)}, bf16[32,2304]{1,0:T(8,128)(2,1)S(1)}, u32[]{:S(2)}, u32[]{:S(2)}) collective-permute-start(bf16[32,2304]{1,0:T(8,128)(2,1)S(1)} %slice.297), channel_id=1, source_target_pairs={{0,224},{8,232},{16,240},{24,248},{32,0},{40,8},{48,16},{56,24},{6... | collective-permute-start | bytes 442376 | tf_op jit(solution)/shard_map/ppermute | solution.py:13
  72.3 2.7 %collective-permute-start.19 = (bf16[256,2048]{1,0:T(8,128)(2,1)S(1)}, bf16[256,2048]{1,0:T(8,128)(2,1)}, u32[]{:S(2)}, u32[]{:S(2)}) collective-permute-start(bf16[256,2048]{1,0:T(8,128)(2,1)S(1)} %collective-permute-done.17), channel_id=1, source_target_pairs={{0,224},{8,232},{16,240},{24,248},{32,0},{40,8},{48,16},{56,24},{6... | collective-permute-start | bytes 3145736 | tf_op jit(solution)/shard_map/ppermute | solution.py:13
  75.0 19.5 %collective-permute-done.19 = bf16[256,2048]{1,0:T(8,128)(2,1)} collective-permute-done((bf16[256,2048]{1,0:T(8,128)(2,1)S(1)}, bf16[256,2048]{1,0:T(8,128)(2,1)}, u32[]{:S(2)}, u32[]{:S(2)}) %collective-permute-start.19) | collective-permute-done | bytes 1048608 | tf_op jit(solution)/shard_map/ppermute | solution.py:13
  94.5 3.6 %collective-permute-start.21 = (bf16[256,2048]{1,0:T(8,128)(2,1)}, bf16[256,2048]{1,0:T(8,128)(2,1)S(1)}, u32[]{:S(2)}, u32[]{:S(2)}) collective-permute-start(bf16[256,2048]{1,0:T(8,128)(2,1)} %collective-permute-done.19), channel_id=1, source_target_pairs={{0,224},{8,232},{16,240},{24,248},{32,0},{40,8},{48,16},{56,24},{6... | collective-permute-start | bytes 3145736 | tf_op jit(solution)/shard_map/ppermute | solution.py:13
  98.1 22.4 %collective-permute-done.9 = bf16[512,2304]{1,0:T(8,128)(2,1)S(1)} collective-permute-done((bf16[512,2304]{1,0:T(8,128)(2,1)}, bf16[512,2304]{1,0:T(8,128)(2,1)S(1)}, u32[]{:S(2)}, u32[]{:S(2)}) %collective-permute-start.9) | collective-permute-done | bytes 2359328 | tf_op jit(solution)/shard_map/ppermute | solution.py:13
  122.8 2.4 %slice.322 = bf16[256,2304]{1,0:T(8,128)(2,1)} slice(bf16[512,2304]{1,0:T(8,128)(2,1)} %collective-permute-done.8), slice={[0:256], [0:2304]} | slice | bytes 2359296 | tf_op jit(solution)/shard_map/slice | solution.py:25
  126.8 2.7 %collective-permute-start.23 = (bf16[128,2048]{1,0:T(8,128)(2,1)}, bf16[128,2048]{1,0:T(8,128)(2,1)}, u32[]{:S(2)}, u32[]{:S(2)}) collective-permute-start(bf16[128,2048]{1,0:T(8,128)(2,1)} %slice.359), channel_id=1, source_target_pairs={{0,224},{8,232},{16,240},{24,248},{32,0},{40,8},{48,16},{56,24},{6... | collective-permute-start | bytes 1572872 | tf_op jit(solution)/shard_map/ppermute | solution.py:13
  129.5 1.9 slice.358
  131.4 3.1 %fusion.4 = bf16[8,4,64,1024]{3,2,1,0:T(8,128)(2,1)S(1)} fusion(s32[]{:T(128)S(6)} %select_n.18, bf16[8,4,64,1024]{3,2,1,0:T(8,128)(2,1)} %bitcast.207), kind=kLoop, calls=%fused_computation.9 | loop fusion | flops 2097152 | bytes 8388612 | tf_op jit(solution)/shard_map/concatenate | solution.py:48
  134.5 1.8 fusion.3
  145.2 2.2 %slice_bitcast_fusion.7 = (bf16[64,512]{1,0:T(8,128)(2,1)S(1)}, bf16[64,512]{1,0:T(8,128)(2,1)}, bf16[64,512]{1,0:T(8,128)(2,1)}, bf16[64,512]{1,0:T(8,128)(2,1)...) fusion(bf16[8,4,64,1024]{3,2,1,0:T(8,128)(2,1)} %copy-done), kind=kLoop, calls=%fused_computation.136 | loop fusion | bytes 2490368 | tf_op jit(solution)/shard_map/squeeze | solution.py:52
  148.8 3.1 %fusion.87 = f32[512,2304]{1,0:T(8,128)S(1)} fusion(bf16[512,512]{1,0:T(8,128)(2,1)S(1)} %get-tuple-element.37, bf16[512,2304]{1,0:T(8,128)(2,1)} %collective-permute-done.8), kind=kOutput, calls=%fused_computation.202 | convolution fusion | flops 1207959552 | bytes 7602176 | tf_op jit(solution)/shard_map/dot_general | solution.py:34
  152.0 3.1 %fusion.5 = f32[512,2304]{1,0:T(8,128)S(1)} fusion(bf16[512,512]{1,0:T(8,128)(2,1)S(1)} %get-tuple-element.35, bf16[256,2304]{1,0:T(8,128)(2,1)} %collective-permute-done.11, bf16[256,2304]{1,0:T(8,128)(2,1)} %collective-permute-done.10), kind=kOutput, calls=%fused_computation.11 | convolution fusion | flops 1212678144 | bytes 7602176 | tf_op jit(solution)/shard_map/dot_general | solution.py:34
  155.0 5.2 %fusion.2 = bf16[512,2304]{1,0:T(8,128)(2,1)} fusion(f32[512,2304]{1,0:T(8,128)S(1)} %fusion.5, f32[512,2304]{1,0:T(8,128)S(1)} %fusion.88, f32[512,2304]{1,0:T(8,128)S(1)} %fusion.87, bf16[512,512]{1,0:T(8,128)(2,1)S(1)} %get-tuple-element.34, bf16[512,2304]{1,0:T(8,128)(2,1)} %constant_dynamic-update-slice_fusion.8), kind=kOutput, calls=%fused_computation.7 | convolution fusion | flops 1212678144 | bytes 19398656 | tf_op jit(solution)/shard_map/dot_general | solution.py:34
  160.9 2.0 %fusion.53 = f32[512,2048]{1,0:T(8,128)S(1)} fusion(bf16[256,2048]{1,0:T(8,128)(2,1)} %collective-permute-done.20, bf16[64,512]{1,0:T(8,128)(2,1)S(1)} %get-tuple-element.9, bf16[64,512]{1,0:T(8,128)(2,1)S(1)} %get-tuple-element.10, bf16[64,512]{1,0:T(8,128)(2,1)S(1)} %get-tuple-element.11, bf16[64,512]{1,0:T(8,128)(2,1)S(1)} %get-tuple-element.12), kind=kOutput, calls=%fused_computation.60 | convolution fusion | flops 537919488 | bytes 5505024 | tf_op jit(solution)/shard_map/dot_general | solution.py:34
  162.9 2.0 %fusion.45 = f32[512,2048]{1,0:T(8,128)S(1)} fusion(bf16[256,2048]{1,0:T(8,128)(2,1)} %collective-permute-done.19, bf16[64,512]{1,0:T(8,128)(2,1)S(1)} %get-tuple-element.13, bf16[64,512]{1,0:T(8,128)(2,1)S(1)} %get-tuple-element.14, bf16[64,512]{1,0:T(8,128)(2,1)S(1)} %get-tuple-element.15, bf16[64,512]{1,0:T(8,128)(2,1)S(1)} %get-tuple-element.16), kind=kOutput, calls=%fused_computation.52 | convolution fusion | flops 537919488 | bytes 5505024 | tf_op jit(solution)/shard_map/dot_general | solution.py:34
  165.1 2.0 %fusion.37 = f32[512,2048]{1,0:T(8,128)S(1)} fusion(bf16[256,2048]{1,0:T(8,128)(2,1)} %collective-permute-done.18, bf16[64,512]{1,0:T(8,128)(2,1)S(1)} %copy-done.13, bf16[64,512]{1,0:T(8,128)(2,1)S(1)} %copy-done.14, bf16[64,512]{1,0:T(8,128)(2,1)S(1)} %copy-done.15, bf16[64,512]{1,0:T(8,128)(2,1)S(1)} %copy-done.16), kind=kOutput, calls=%fused_computation.44 | convolution fusion | flops 537919488 | bytes 5505024 | tf_op jit(solution)/shard_map/dot_general | solution.py:34
  167.2 2.7 %fusion.21 = f32[512,2048]{1,0:T(8,128)} fusion(bf16[256,2048]{1,0:T(8,128)(2,1)S(1)} %copy-done.6, bf16[64,512]{1,0:T(8,128)(2,1)S(1)} %copy-done.22, bf16[64,512]{1,0:T(8,128)(2,1)S(1)} %copy-done.23, bf16[64,512]{1,0:T(8,128)(2,1)S(1)} %copy-done.24, bf16[64,512]{1,0:T(8,128)(2,1)S(1)} %copy-done.21), kind=kOutput, calls=%fused_computation.28 | convolution fusion | flops 537919488 | bytes 5505024 | tf_op jit(solution)/shard_map/dot_general | solution.py:34
  170.0 2.7 %fusion.29 = f32[512,2048]{1,0:T(8,128)} fusion(bf16[256,2048]{1,0:T(8,128)(2,1)S(1)} %copy-done.4, bf16[64,512]{1,0:T(8,128)(2,1)S(1)} %copy-done.17, bf16[64,512]{1,0:T(8,128)(2,1)S(1)} %copy-done.18, bf16[64,512]{1,0:T(8,128)(2,1)S(1)} %copy-done.19, bf16[64,512]{1,0:T(8,128)(2,1)S(1)} %copy-done.20), kind=kOutput, calls=%fused_computation.36 | convolution fusion | flops 537919488 | bytes 5505024 | tf_op jit(solution)/shard_map/dot_general | solution.py:34
  172.8 4.0 %fusion.9 = f32[512,2048]{1,0:T(8,128)} fusion(bf16[128,2048]{1,0:T(8,128)(2,1)} %collective-permute-done.23, bf16[128,2048]{1,0:T(8,128)(2,1)} %collective-permute-done.22, bf16[64,512]{1,0:T(8,128)(2,1)S(1)} %copy-done.12, bf16[64,512]{1,0:T(8,128)(2,1)S(1)} %copy-done.9, bf16[64,512]{1,0:T(8,128)(2,1)S(1)} %copy-done.10, bf16[64,512]{1,0:T(8,128)(2,1)S(1)} %copy-done.11), kind=kOutput, calls=%fused_computation.15 | convolution fusion | flops 540016640 | bytes 5505024 | tf_op jit(solution)/shard_map/dot_general | solution.py:34
  176.8 8.3 %add_convert_fusion = bf16[512,2048]{1,0:T(8,128)(2,1)} fusion(f32[512,2048]{1,0:T(8,128)} %fusion.9, f32[512,2048]{1,0:T(8,128)S(1)} %fusion.53, f32[512,2048]{1,0:T(8,128)S(1)} %fusion.45, f32[512,2048]{1,0:T(8,128)S(1)} %fusion.37, f32[512,2048]{1,0:T(8,128)} %fusion.29, f32[512,2048]{1,0:T(8,128)S(1)} %fusion.13, f32[512,2048]{1,0:T(8,128)} %fusion.21, ...), kind=kOutput, calls=%fused_computation.10 | convolution fusion | flops 546308096 | bytes 32768000 | tf_op jit(solution)/shard_map/dot_general | solution.py:34
  (116 shorter events, 29.6 us)
Async XLA Ops:
  7.2 124.2 %all-gather.2.cloned.1.call-start = ((), (), s32[]{:S(2)}) async-start(), calls=%async_computation | async-start | bytes 4718592 | tf_op jit(solution)/shard_map/all_gather | solution.py:43
  9.1 11.9 %collective-permute-start.12 = (bf16[64,2048]{1,0:T(8,128)(2,1)}, bf16[64,2048]{1,0:T(8,128)(2,1)S(1)}, u32[]{:S(2)}, u32[]{:S(2)}) collective-permute-start(bf16[64,2048]{1,0:T(8,128)(2,1)} %param.7), channel_id=1, source_target_pairs={{0,8},{8,16},{16,24},{24,0},{32,40},{40,48},{48,56},{56,32},{64,72... | collective-permute-start | bytes 786440 | tf_op jit(solution)/shard_map/ppermute | solution.py:13
  10.7 10.7 %collective-permute-start.13 = (bf16[64,2048]{1,0:T(8,128)(2,1)}, bf16[64,2048]{1,0:T(8,128)(2,1)S(1)}, u32[]{:S(2)}, u32[]{:S(2)}) collective-permute-start(bf16[64,2048]{1,0:T(8,128)(2,1)} %param.7), channel_id=1, source_target_pairs={{0,24},{8,0},{16,8},{24,16},{32,56},{40,32},{48,40},{56,48},{64,88... | collective-permute-start | bytes 786440 | tf_op jit(solution)/shard_map/ppermute | solution.py:13
  12.4 12.5 %collective-permute-start = (bf16[64,2304]{1,0:T(8,128)(2,1)}, bf16[64,2304]{1,0:T(8,128)(2,1)S(1)}, u32[]{:S(2)}, u32[]{:S(2)}) collective-permute-start(bf16[64,2304]{1,0:T(8,128)(2,1)} %param.6), channel_id=1, source_target_pairs={{0,32},{8,40},{16,48},{24,56},{32,64},{40,72},{48,80},{56,88},{64,... | collective-permute-start | bytes 884744 | tf_op jit(solution)/shard_map/ppermute | solution.py:13
  14.3 10.6 %collective-permute-start.1 = (bf16[64,2304]{1,0:T(8,128)(2,1)}, bf16[64,2304]{1,0:T(8,128)(2,1)S(1)}, u32[]{:S(2)}, u32[]{:S(2)}) collective-permute-start(bf16[64,2304]{1,0:T(8,128)(2,1)} %param.6), channel_id=1, source_target_pairs={{0,224},{8,232},{16,240},{24,248},{32,0},{40,8},{48,16},{56,24},{6... | collective-permute-start | bytes 884744 | tf_op jit(solution)/shard_map/ppermute | solution.py:13
  21.0 8.7 %collective-permute-start.14 = (bf16[32,2048]{1,0:T(8,128)(2,1)S(1)}, bf16[32,2048]{1,0:T(8,128)(2,1)S(1)}, u32[]{:S(2)}, u32[]{:S(2)}) collective-permute-start(bf16[32,2048]{1,0:T(8,128)(2,1)S(1)} %slice.328), channel_id=1, source_target_pairs={{0,8},{8,16},{16,24},{24,0},{32,40},{40,48},{48,56},{56,32},{64,72... | collective-permute-start | bytes 393224 | tf_op jit(solution)/shard_map/ppermute | solution.py:13
  21.4 8.3 %collective-permute-start.15 = (bf16[32,2048]{1,0:T(8,128)(2,1)S(1)}, bf16[32,2048]{1,0:T(8,128)(2,1)S(1)}, u32[]{:S(2)}, u32[]{:S(2)}) collective-permute-start(bf16[32,2048]{1,0:T(8,128)(2,1)S(1)} %slice.329), channel_id=1, source_target_pairs={{0,24},{8,0},{16,8},{24,16},{32,56},{40,32},{48,40},{56,48},{64,88... | collective-permute-start | bytes 393224 | tf_op jit(solution)/shard_map/ppermute | solution.py:13
  24.9 9.3 %collective-permute-start.2 = (bf16[64,2304]{1,0:T(8,128)(2,1)S(1)}, bf16[64,2304]{1,0:T(8,128)(2,1)S(1)}, u32[]{:S(2)}, u32[]{:S(2)}) collective-permute-start(bf16[64,2304]{1,0:T(8,128)(2,1)S(1)} %collective-permute-done), channel_id=1, source_target_pairs={{0,32},{8,40},{16,48},{24,56},{32,64},{40,72},{48,80},{56,88},{64,... | collective-permute-start | bytes 884744 | tf_op jit(solution)/shard_map/ppermute | solution.py:13
  24.9 10.7 %collective-permute-start.3 = (bf16[64,2304]{1,0:T(8,128)(2,1)S(1)}, bf16[64,2304]{1,0:T(8,128)(2,1)S(1)}, u32[]{:S(2)}, u32[]{:S(2)}) collective-permute-start(bf16[64,2304]{1,0:T(8,128)(2,1)S(1)} %collective-permute-done.1), channel_id=1, source_target_pairs={{0,224},{8,232},{16,240},{24,248},{32,0},{40,8},{48,16},{56,24},{6... | collective-permute-start | bytes 884744 | tf_op jit(solution)/shard_map/ppermute | solution.py:13
  29.7 45.3 %copy-start.1 = (bf16[256,2048]{1,0:T(8,128)(2,1)}, bf16[256,2048]{1,0:T(8,128)(2,1)S(1)}, u32[]{:S(2)}) copy-start(bf16[256,2048]{1,0:T(8,128)(2,1)S(1)} %constant_dynamic-update-slice_fusion.41) | copy-start | bytes 3145732
  29.7 42.6 %collective-permute-start.17 = (bf16[256,2048]{1,0:T(8,128)(2,1)S(1)}, bf16[256,2048]{1,0:T(8,128)(2,1)S(1)}, u32[]{:S(2)}, u32[]{:S(2)}) collective-permute-start(bf16[256,2048]{1,0:T(8,128)(2,1)S(1)} %constant_dynamic-update-slice_fusion.41), channel_id=1, source_target_pairs={{0,224},{8,232},{16,240},{24,248},{32,0},{40,8},{48,16},{56,24},{6... | collective-permute-start | bytes 3145736 | tf_op jit(solution)/shard_map/ppermute | solution.py:13
  31.7 43.2 %collective-permute-start.16 = (bf16[256,2048]{1,0:T(8,128)(2,1)S(1)}, bf16[256,2048]{1,0:T(8,128)(2,1)S(1)}, u32[]{:S(2)}, u32[]{:S(2)}) collective-permute-start(bf16[256,2048]{1,0:T(8,128)(2,1)S(1)} %constant_dynamic-update-slice_fusion.41), channel_id=1, source_target_pairs={{0,32},{8,40},{16,48},{24,56},{32,64},{40,72},{48,80},{56,88},{64,... | collective-permute-start | bytes 3145736 | tf_op jit(solution)/shard_map/ppermute | solution.py:13
  34.2 28.3 %collective-permute-start.4 = (bf16[64,2304]{1,0:T(8,128)(2,1)S(1)}, bf16[64,2304]{1,0:T(8,128)(2,1)S(1)}, u32[]{:S(2)}, u32[]{:S(2)}) collective-permute-start(bf16[64,2304]{1,0:T(8,128)(2,1)S(1)} %collective-permute-done.2), channel_id=1, source_target_pairs={{0,32},{8,40},{16,48},{24,56},{32,64},{40,72},{48,80},{56,88},{64,... | collective-permute-start | bytes 884744 | tf_op jit(solution)/shard_map/ppermute | solution.py:13
  35.6 27.0 %collective-permute-start.5 = (bf16[64,2304]{1,0:T(8,128)(2,1)S(1)}, bf16[64,2304]{1,0:T(8,128)(2,1)S(1)}, u32[]{:S(2)}, u32[]{:S(2)}) collective-permute-start(bf16[64,2304]{1,0:T(8,128)(2,1)S(1)} %collective-permute-done.3), channel_id=1, source_target_pairs={{0,224},{8,232},{16,240},{24,248},{32,0},{40,8},{48,16},{56,24},{6... | collective-permute-start | bytes 884744 | tf_op jit(solution)/shard_map/ppermute | solution.py:13
  62.5 6.4 %collective-permute-start.6 = (bf16[32,2304]{1,0:T(8,128)(2,1)S(1)}, bf16[32,2304]{1,0:T(8,128)(2,1)S(1)}, u32[]{:S(2)}, u32[]{:S(2)}) collective-permute-start(bf16[32,2304]{1,0:T(8,128)(2,1)S(1)} %slice.296), channel_id=1, source_target_pairs={{0,32},{8,40},{16,48},{24,56},{32,64},{40,72},{48,80},{56,88},{64,... | collective-permute-start | bytes 442376 | tf_op jit(solution)/shard_map/ppermute | solution.py:13
  62.6 7.0 %collective-permute-start.7 = (bf16[32,2304]{1,0:T(8,128)(2,1)S(1)}, bf16[32,2304]{1,0:T(8,128)(2,1)S(1)}, u32[]{:S(2)}, u32[]{:S(2)}) collective-permute-start(bf16[32,2304]{1,0:T(8,128)(2,1)S(1)} %slice.297), channel_id=1, source_target_pairs={{0,224},{8,232},{16,240},{24,248},{32,0},{40,8},{48,16},{56,24},{6... | collective-permute-start | bytes 442376 | tf_op jit(solution)/shard_map/ppermute | solution.py:13
  70.3 50.2 %collective-permute-start.9 = (bf16[512,2304]{1,0:T(8,128)(2,1)}, bf16[512,2304]{1,0:T(8,128)(2,1)S(1)}, u32[]{:S(2)}, u32[]{:S(2)}) collective-permute-start(bf16[512,2304]{1,0:T(8,128)(2,1)} %constant_dynamic-update-slice_fusion.8), channel_id=1, source_target_pairs={{0,24},{8,0},{16,8},{24,16},{32,56},{40,32},{48,40},{56,48},{64,88... | collective-permute-start | bytes 7077896 | tf_op jit(solution)/shard_map/ppermute | solution.py:13
  71.8 51.0 %collective-permute-start.8 = (bf16[512,2304]{1,0:T(8,128)(2,1)}, bf16[512,2304]{1,0:T(8,128)(2,1)}, u32[]{:S(2)}, u32[]{:S(2)}) collective-permute-start(bf16[512,2304]{1,0:T(8,128)(2,1)} %constant_dynamic-update-slice_fusion.8), channel_id=1, source_target_pairs={{0,8},{8,16},{16,24},{24,0},{32,40},{40,48},{48,56},{56,32},{64,72... | collective-permute-start | bytes 7077896 | tf_op jit(solution)/shard_map/ppermute | solution.py:13
  72.3 22.2 %copy-start.3 = (bf16[256,2048]{1,0:T(8,128)(2,1)}, bf16[256,2048]{1,0:T(8,128)(2,1)S(1)}, u32[]{:S(2)}) copy-start(bf16[256,2048]{1,0:T(8,128)(2,1)S(1)} %collective-permute-done.17) | copy-start | bytes 3145732
  72.3 22.2 %collective-permute-start.19 = (bf16[256,2048]{1,0:T(8,128)(2,1)S(1)}, bf16[256,2048]{1,0:T(8,128)(2,1)}, u32[]{:S(2)}, u32[]{:S(2)}) collective-permute-start(bf16[256,2048]{1,0:T(8,128)(2,1)S(1)} %collective-permute-done.17), channel_id=1, source_target_pairs={{0,224},{8,232},{16,240},{24,248},{32,0},{40,8},{48,16},{56,24},{6... | collective-permute-start | bytes 3145736 | tf_op jit(solution)/shard_map/ppermute | solution.py:13
  75.0 23.1 %copy-start.5 = (bf16[256,2048]{1,0:T(8,128)(2,1)}, bf16[256,2048]{1,0:T(8,128)(2,1)S(1)}, u32[]{:S(2)}) copy-start(bf16[256,2048]{1,0:T(8,128)(2,1)S(1)} %collective-permute-done.16) | copy-start | bytes 3145732
  75.0 23.1 %collective-permute-start.18 = (bf16[256,2048]{1,0:T(8,128)(2,1)S(1)}, bf16[256,2048]{1,0:T(8,128)(2,1)}, u32[]{:S(2)}, u32[]{:S(2)}) collective-permute-start(bf16[256,2048]{1,0:T(8,128)(2,1)S(1)} %collective-permute-done.16), channel_id=1, source_target_pairs={{0,32},{8,40},{16,48},{24,56},{32,64},{40,72},{48,80},{56,88},{64,... | collective-permute-start | bytes 3145736 | tf_op jit(solution)/shard_map/ppermute | solution.py:13
  94.5 31.5 %collective-permute-start.21 = (bf16[256,2048]{1,0:T(8,128)(2,1)}, bf16[256,2048]{1,0:T(8,128)(2,1)S(1)}, u32[]{:S(2)}, u32[]{:S(2)}) collective-permute-start(bf16[256,2048]{1,0:T(8,128)(2,1)} %collective-permute-done.19), channel_id=1, source_target_pairs={{0,224},{8,232},{16,240},{24,248},{32,0},{40,8},{48,16},{56,24},{6... | collective-permute-start | bytes 3145736 | tf_op jit(solution)/shard_map/ppermute | solution.py:13
  98.1 31.4 %collective-permute-start.20 = (bf16[256,2048]{1,0:T(8,128)(2,1)}, bf16[256,2048]{1,0:T(8,128)(2,1)}, u32[]{:S(2)}, u32[]{:S(2)}) collective-permute-start(bf16[256,2048]{1,0:T(8,128)(2,1)} %collective-permute-done.18), channel_id=1, source_target_pairs={{0,32},{8,40},{16,48},{24,56},{32,64},{40,72},{48,80},{56,88},{64,... | collective-permute-start | bytes 3145736 | tf_op jit(solution)/shard_map/ppermute | solution.py:13
  121.6 30.4 %collective-permute-start.11 = (bf16[256,2304]{1,0:T(8,128)(2,1)}, bf16[256,2304]{1,0:T(8,128)(2,1)}, u32[]{:S(2)}, u32[]{:S(2)}) collective-permute-start(bf16[256,2304]{1,0:T(8,128)(2,1)} %slice.323), channel_id=1, source_target_pairs={{0,24},{8,0},{16,8},{24,16},{32,56},{40,32},{48,40},{56,48},{64,88... | collective-permute-start | bytes 3538952 | tf_op jit(solution)/shard_map/ppermute | solution.py:13
  125.2 26.8 %collective-permute-start.10 = (bf16[256,2304]{1,0:T(8,128)(2,1)}, bf16[256,2304]{1,0:T(8,128)(2,1)}, u32[]{:S(2)}, u32[]{:S(2)}) collective-permute-start(bf16[256,2304]{1,0:T(8,128)(2,1)} %slice.322), channel_id=1, source_target_pairs={{0,8},{8,16},{16,24},{24,0},{32,40},{40,48},{48,56},{56,32},{64,72... | collective-permute-start | bytes 3538952 | tf_op jit(solution)/shard_map/ppermute | solution.py:13
  126.8 45.9 %collective-permute-start.23 = (bf16[128,2048]{1,0:T(8,128)(2,1)}, bf16[128,2048]{1,0:T(8,128)(2,1)}, u32[]{:S(2)}, u32[]{:S(2)}) collective-permute-start(bf16[128,2048]{1,0:T(8,128)(2,1)} %slice.359), channel_id=1, source_target_pairs={{0,224},{8,232},{16,240},{24,248},{32,0},{40,8},{48,16},{56,24},{6... | collective-permute-start | bytes 1572872 | tf_op jit(solution)/shard_map/ppermute | solution.py:13
  131.4 41.4 %collective-permute-start.22 = (bf16[128,2048]{1,0:T(8,128)(2,1)}, bf16[128,2048]{1,0:T(8,128)(2,1)}, u32[]{:S(2)}, u32[]{:S(2)}) collective-permute-start(bf16[128,2048]{1,0:T(8,128)(2,1)} %slice.358), channel_id=1, source_target_pairs={{0,32},{8,40},{16,48},{24,56},{32,64},{40,72},{48,80},{56,88},{64,... | collective-permute-start | bytes 1572872 | tf_op jit(solution)/shard_map/ppermute | solution.py:13
  155.0 5.2 %copy-start.2 = (bf16[256,2048]{1,0:T(8,128)(2,1)S(1)}, bf16[256,2048]{1,0:T(8,128)(2,1)}, u32[]{:S(2)}) copy-start(bf16[256,2048]{1,0:T(8,128)(2,1)} %copy-done.1) | copy-start | bytes 3145732
  167.1 2.9 %copy-start.4 = (bf16[256,2048]{1,0:T(8,128)(2,1)S(1)}, bf16[256,2048]{1,0:T(8,128)(2,1)}, u32[]{:S(2)}) copy-start(bf16[256,2048]{1,0:T(8,128)(2,1)} %copy-done.3) | copy-start | bytes 3145732
  172.7 4.1 %copy-start.7 = (bf16[64,512]{1,0:T(8,128)(2,1)S(1)}, bf16[64,512]{1,0:T(8,128)(2,1)}, u32[]{:S(2)}) copy-start(bf16[64,512]{1,0:T(8,128)(2,1)} %get-tuple-element.7) | copy-start | bytes 196612
  172.7 4.1 %copy-start.8 = (bf16[64,512]{1,0:T(8,128)(2,1)S(1)}, bf16[64,512]{1,0:T(8,128)(2,1)}, u32[]{:S(2)}) copy-start(bf16[64,512]{1,0:T(8,128)(2,1)} %get-tuple-element.8) | copy-start | bytes 196612
  (18 other events, 44.3 us)
Sparse Core Ops, SparseCore 0:
  9.9 36.5 all-gather.1

commit v2 on v0

v2 whole, which is shorter than its diff:
```python
import functools

import jax
import jax.numpy as jnp
from jax import lax
from jax.experimental import pallas as pl
from jax.experimental.pallas import tpu as pltpu
from jax.sharding import PartitionSpec as P

Z, X, Y, C = 8, 4, 4, 2
BLOCK = 64
FEATURES = 512
TILE = 256
SPLIT = 256

X_ORDER = (0, -1, 1, 2)
NEAR, FAR = (0, -1, 1), (-2, 2, -3, 3, 4)


def hop(value, dz, dx):
    pairs = [
        (z * X + x, ((z + dz) % Z) * X + (x + dx) % X) for z in range(Z) for x in range(X)
    ]
    return lax.ppermute(value, "row", pairs)


def hop_y(value, dy, swap=0):
    pairs = [(y * C + c, ((y + dy) % Y) * C + (c ^ swap)) for y in range(Y) for c in range(C)]
    return lax.ppermute(value, "col", pairs)


def halves(value):
    half = value.shape[0] // 2
    return value[:half], value[half:]


def kernel(rows, sizes, added, ops, tiles, prefix, place_ref, mine_ref, other_ref, *refs):
    grads, refs = refs[: len(sizes)], refs[len(sizes) :]
    if added:
        total_ref, *refs = refs
    if prefix:
        prefix_ref, *refs = refs
    *outs, left, right, turned, sems = refs
    tile = pl.program_id(0)

    @pl.when(tile == 0)
    def _():
        z, x, y, core = (place_ref[i] for i in range(4))
        features = pl.ds(ops[0] * FEATURES, len(ops) * FEATURES)
        at = 0
        for i, (dz, dx, start, size) in enumerate(rows):
            group = lax.rem(z + (dz + Z), Z)
            away = lax.rem(group // C + Y - y, Y)
            slot = jnp.where(away == 0, 0, jnp.where(away == Y - 1, 1, jnp.where(away == 1, 2, 3)))
            row = slot * (X * BLOCK) + lax.rem(x + (dx + X), X) * BLOCK + start
            source = pl.ds(pl.multiple_of(row, 32), size)
            target = left.at[pl.ds(at, size)]
            swapped = lax.rem(group, C) != core

            @pl.when(swapped)
            def _():
                pltpu.make_async_copy(other_ref.at[source, features], target, sems.at[i]).start()

            @pl.when(jnp.logical_not(swapped))
            def _():
                pltpu.make_async_copy(mine_ref.at[source, features], target, sems.at[i]).start()

            at += size
        at = 0
        for i, (_, _, _, size) in enumerate(rows):
            span = left.at[pl.ds(at, size)]
            pltpu.make_async_copy(span, span, sems.at[i]).wait()
            at += size
        for i in range(len(ops)):
            turned[i] = left[:, i * FEATURES : (i + 1) * FEATURES].T

    def work(op, out_ref):
        at = 0
        for grad, size in zip(grads, sizes):
            right[pl.ds(at, size)] = grad[...]
            at += size
        part = jnp.dot(turned[op], right[...], preferred_element_type=jnp.float32)
        if added:
            part += total_ref[...]
        out_ref[...] = part.astype(out_ref.dtype)

    if prefix:
        pl.when(tile < prefix)(lambda: outs[0].__setitem__(..., prefix_ref[...]))
        pl.when(tile >= prefix)(lambda: work(0, outs[0]))
    elif len(ops) == 1:
        work(0, outs[0])
    else:
        pl.when(tile < tiles)(lambda: work(0, outs[0]))
        pl.when(tile >= tiles)(lambda: work(1, outs[-1]))


def contract(place, operand, ops, blocks, total=None, prefix=None, split=None, dtype=jnp.float32):
    grads = [array for array, _ in blocks]
    rows = [row for _, some in blocks for row in some]
    sizes = [array.shape[0] for array in grads]
    depth, width = sum(sizes), grads[0].shape[1]
    assert depth == sum(row[3] for row in rows)
    ahead = 0 if prefix is None else prefix.shape[1] // TILE
    tiles = ahead + width // TILE
    cut = tiles if split is None else split // TILE
    anywhere = pl.BlockSpec(memory_space=pl.ANY)
    here = lambda height: pl.BlockSpec((height, TILE), lambda t: (0, jnp.maximum(t - ahead, 0)))
    if dtype == jnp.float32 or len(ops) == 1:
        widths, specs = [tiles * TILE], [pl.BlockSpec((FEATURES, TILE), lambda t: (0, t))]
    else:
        widths = [cut * TILE, (tiles - cut) * TILE]
        specs = [
            pl.BlockSpec((FEATURES, TILE), lambda t: (0, jnp.minimum(t, cut - 1))),
            pl.BlockSpec((FEATURES, TILE), lambda t: (0, jnp.maximum(t - cut, 0))),
        ]
    extra, extra_specs = [], []
    if total is not None:
        extra, extra_specs = [total], [here(FEATURES)]
    if prefix is not None:
        extra.append(prefix)
        extra_specs.append(
            pl.BlockSpec((FEATURES, TILE), lambda t: (0, jnp.minimum(t, ahead - 1)))
        )
    results = pl.pallas_call(
        functools.partial(kernel, rows, sizes, total is not None, ops, cut, ahead),
        grid=(tiles,),
        out_shape=[jax.ShapeDtypeStruct((FEATURES, w), dtype) for w in widths],
        in_specs=[pl.BlockSpec(memory_space=pltpu.SMEM), anywhere, anywhere]
        + [here(size) for size in sizes]
        + extra_specs,
        out_specs=specs,
        scratch_shapes=[
            pltpu.VMEM((depth, len(ops) * FEATURES), jnp.bfloat16),
            pltpu.VMEM((depth, TILE), jnp.bfloat16),
            pltpu.VMEM((len(ops), FEATURES, depth), jnp.bfloat16),
            pltpu.SemaphoreType.DMA((len(rows),)),
        ],
        compiler_params=pltpu.CompilerParams(vmem_limit_bytes=24 << 20),
        cost_estimate=pl.CostEstimate(
            flops=2 * FEATURES * depth * width,
            bytes_accessed=2 * depth * (width + FEATURES) + 4 * FEATURES * width,
            transcendentals=0,
        ),
    )(place, *operand, *grads, *extra)
    return results if len(results) > 1 else results[0]


def whole(dzs, dx):
    return [(dz, dx, 0, BLOCK) for dz in dzs]


def parts(rows):
    half, first, second = sum(row[3] for row in rows) // 2, [], []
    for dz, dx, start, size in rows:
        here = min(size, half)
        if here:
            first.append((dz, dx, start, here))
        if here < size:
            second.append((dz, dx, start + here, size - here))
        half -= here
    return first, second


def body(normed_input, attended, qkv_grad, proj_grad):
    row, col = lax.axis_index("row"), lax.axis_index("col")
    place = jnp.stack([row // X, row % X, col // C, col % C])

    tall = jnp.concatenate([qkv_grad, proj_grad[:, :SPLIT]], axis=1)
    wide = proj_grad[:, SPLIT:]

    below, above = hop(tall, 1, 0), hop(tall, -1, 0)
    left, right = hop(wide, 0, 1), hop(wide, 0, -1)
    near = jnp.concatenate([tall, below, above])
    far = []
    for distance in (2, 3):
        below, above = hop(below, 1, 0), hop(above, -1, 0)
        far += [below, above]
    far += [hop(halves(below)[0], 1, 0), hop(halves(above)[1], -1, 0)]
    left_half, right_half = hop(halves(left)[0], 0, 1), hop(halves(right)[1], 0, -1)
    wide = jnp.concatenate([wide, left, right, left_half, right_half])

    mine = jnp.concatenate([normed_input, attended], axis=1)
    down, up = hop_y(mine, 1), hop_y(mine, -1)
    mine = jnp.concatenate(
        [mine, down, up, hop_y(halves(down)[0], 1), hop_y(halves(up)[1], -1)]
    )
    operand = (mine, hop_y(mine, 0, 1))

    near_left, near_right = hop(near, 0, 1), hop(near, 0, -1)
    near_rows = {dx: whole(NEAR, dx) for dx in X_ORDER}
    far, wide, below, above = lax.optimization_barrier((far, wide, below, above))
    far = jnp.concatenate(far)
    far_rows = {dx: whole(FAR, dx) for dx in X_ORDER}
    far_left, far_right = hop(far, 0, 1), hop(far, 0, -1)
    near_split, far_split = parts(near_rows[2]), parts(far_rows[2])
    tall_first = [
        (near, near_rows[0]),
        (near_left, near_rows[-1]),
        (near_right, near_rows[1]),
        (hop(halves(near_left)[0], 0, 1), near_split[0]),
        (hop(halves(near_right)[1], 0, -1), near_split[1]),
        (far, far_rows[0]),
    ]
    tall_second = [(far_left, far_rows[-1]), (far_right, far_rows[1])]
    width = qkv_grad.shape[1]
    tall_sum = contract(place, operand, (0, 1), tall_first, split=width)
    far_left, far_right, tall_sum = lax.optimization_barrier((far_left, far_right, tall_sum))
    tall_third = [
        (hop(halves(far_left)[0], 0, 1), far_split[0]),
        (hop(halves(far_right)[1], 0, -1), far_split[1]),
    ]

    wide_rows = {dz: [(dz, dx, 0, BLOCK) for dx in X_ORDER] for dz in range(-4, 5)}
    wide_first = [(wide, wide_rows[0])]
    below = above = wide
    for distance in (1, 2):
        below, above = hop(below, 1, 0), hop(above, -1, 0)
        wide_first += [(below, wide_rows[-distance]), (above, wide_rows[distance])]
    wide_sum = contract(place, operand, (1,), wide_first)
    below, above = hop(below, 1, 0), hop(above, -1, 0)
    below, above, wide_sum = lax.optimization_barrier((below, above, wide_sum))
    wide_second = [(below, wide_rows[-3]), (above, wide_rows[3])]
    wide_split = parts(wide_rows[4])
    wide_third = [
        (hop(halves(below)[0], 1, 0), wide_split[0]),
        (hop(halves(above)[1], -1, 0), wide_split[1]),
    ]

    tall_sum = contract(place, operand, (0, 1), tall_second, tall_sum, split=width)
    wide_sum = contract(place, operand, (1,), wide_second, wide_sum)
    qkv, low = contract(
        place, operand, (0, 1), tall_third, tall_sum, split=width, dtype=jnp.bfloat16
    )
    out = contract(place, operand, (1,), wide_third, wide_sum, low, dtype=jnp.bfloat16)
    return qkv, out


def solution(mesh):
    placed = (P("col", "row"), P("col", "row"), P("row", "col"), P("row", "col"))
    return jax.shard_map(
        body,
        mesh=mesh,
        in_specs=placed,
        out_specs=(P("row", "col"), P("row", "col")),
        check_vma=False,
    )
```

time: 292 us -> 169 us (0.58)
  waiting for transfers between devices: 257 us -> 35.6 us
  starting transfers between devices: 0.15 us -> 58.9 us
  Pallas kernels: 0 us -> 49.5 us
  local copies, waits for them, and re-layouts: 0 us -> 22.8 us
  matrix products: 20.2 us -> 0 us
  between operations: 13.8 us -> 1.22 us
    all_gather x4 -> x0, waiting for transfers between devices: 255 us -> none  [the longest x1 107 us: body(): lax.all_gather(qkv_grad, 'row', axis=0, tiled=True)]
    ppermute x0 -> x33, starting transfers between devices: none -> 58.9 us  [the longest x28 54.3 us: hop(): return lax.ppermute(value, 'row', pairs)]
    pallas_call x0 -> x6, Pallas kernels: none -> 49.5 us  [contract(): pl.pallas_call(functools.partial(kernel, rows, sizes, total is not None,...]
    ppermute x0 -> x33, waiting for transfers between devices: none -> 35.6 us  [the longest x28 35.6 us: hop(): return lax.ppermute(value, 'row', pairs)]
    dot_general x2 -> x0, matrix products: 20.2 us -> none  [contract(): lax.dot_general(left, right, (((0,), (0,)), ((), ())), preferred_element_...]
    unnamed x0 -> x42, local copies, waits for them, and re-layouts: none -> 14.5 us
    slice x0 -> x14, local copies, waits for them, and re-layouts: none -> 6.52 us  [the longest x12 4.79 us: halves(): return (value[:half], value[half:])]
  transfers between devices with their start and end apart: 4 -> 33, of which waited for: 4 -> 8; matrix products, arithmetic and copies ran while one was open for 3% -> 7% of each run, Pallas kernels for 0% -> 27%
where the time goes in v2:
time: 169 us; the launch traced here: 168 us
  starting transfers between devices  58.9 us (35%)
  Pallas kernels  49.5 us (29%)
  waiting for transfers between devices  35.6 us (21%)
  local copies, waits for them, and re-layouts  22.8 us (13%)
    ppermute x28, starting transfers between devices, hop(): return lax.ppermute(value, 'row', pairs)  54.3 us
    pallas_call x6, Pallas kernels, contract(): pl.pallas_call(functools.partial(kernel, rows, sizes, total is not None,...  49.5 us
    ppermute x28, waiting for transfers between devices, hop(): return lax.ppermute(value, 'row', pairs)  35.6 us
    unnamed x42, local copies, waits for them, and re-layouts  14.5 us
    slice x12, local copies, waits for them, and re-layouts, halves(): return (value[:half], value[half:])  4.79 us
    ppermute x5, starting transfers between devices, hop_y(): return lax.ppermute(value, 'col', pairs)  4.55 us
  transfers between devices with their start and end apart: 33, of which 8 were waited for; matrix products, arithmetic and copies ran while one was open for 7% of the time, Pallas kernels for 27%

profile of v2, /device:TPU:8, one launch (start us, length us, event | category | flops | bytes accessed | tf_op | source)
XLA Modules:
  0.0 168.1 jit_solution(11435166315289920144)
XLA Ops:
  2.7 1.7 collective-permute-start
  6.0 1.3 collective-permute-start.13
  8.1 2.0 %collective-permute-start.5 = (bf16[64,2560]{1,0:T(8,128)(2,1)S(1)}, bf16[64,2560]{1,0:T(8,128)(2,1)S(1)}, u32[]{:S(2)}, u32[]{:S(2)}) collective-permute-start(bf16[64,2560]{1,0:T(8,128)(2,1)S(1)} %pad_maximum_fusion.1), channel_id=1, source_target_pairs={{0,32},{8,40},{16,48},{24,56},{32,64},{40,72},{48,80},{56,88},{64,... | collective-permute-start | bytes 983048 | tf_op jit(solution)/shard_map/ppermute | solution.py:24
  10.1 4.0 %collective-permute-start.7 = (bf16[64,2560]{1,0:T(8,128)(2,1)S(1)}, bf16[64,2560]{1,0:T(8,128)(2,1)S(1)}, u32[]{:S(2)}, u32[]{:S(2)}) collective-permute-start(bf16[64,2560]{1,0:T(8,128)(2,1)S(1)} %pad_maximum_fusion.1), channel_id=1, source_target_pairs={{0,224},{8,232},{16,240},{24,248},{32,0},{40,8},{48,16},{56,24},{6... | collective-permute-start | bytes 983048 | tf_op jit(solution)/shard_map/ppermute | solution.py:24
  14.1 1.7 %collective-permute-start.14 = (bf16[64,1792]{1,0:T(8,128)(2,1)S(1)}, bf16[64,1792]{1,0:T(8,128)(2,1)S(1)}, u32[]{:S(2)}, u32[]{:S(2)}) collective-permute-start(bf16[64,1792]{1,0:T(8,128)(2,1)S(1)} %get-tuple-element.32), channel_id=1, source_target_pairs={{0,24},{8,0},{16,8},{24,16},{32,56},{40,32},{48,40},{56,48},{64,88... | collective-permute-start | bytes 688136 | tf_op jit(solution)/shard_map/ppermute | solution.py:24
  15.9 4.4 %collective-permute-done.14 = bf16[64,1792]{1,0:T(8,128)(2,1)S(1)} collective-permute-done((bf16[64,1792]{1,0:T(8,128)(2,1)S(1)}, bf16[64,1792]{1,0:T(8,128)(2,1)S(1)}, u32[]{:S(2)}, u32[]{:S(2)}) %collective-permute-start.14) | collective-permute-done | bytes 229408 | tf_op jit(solution)/shard_map/ppermute | solution.py:24
  20.4 1.5 collective-permute-start.15
  22.2 4.0 %collective-permute-start.8 = (bf16[64,2560]{1,0:T(8,128)(2,1)S(1)}, bf16[64,2560]{1,0:T(8,128)(2,1)S(1)}, u32[]{:S(2)}, u32[]{:S(2)}) collective-permute-start(bf16[64,2560]{1,0:T(8,128)(2,1)S(1)} %collective-permute-done.7), channel_id=1, source_target_pairs={{0,224},{8,232},{16,240},{24,248},{32,0},{40,8},{48,16},{56,24},{6... | collective-permute-start | bytes 983048 | tf_op jit(solution)/shard_map/ppermute | solution.py:24
  26.4 3.0 %collective-permute-start.16 = (bf16[32,1792]{1,0:T(8,128)(2,1)S(1)}, bf16[32,1792]{1,0:T(8,128)(2,1)S(1)}, u32[]{:S(2)}, u32[]{:S(2)}) collective-permute-start(bf16[32,1792]{1,0:T(8,128)(2,1)S(1)} %slice.61), channel_id=1, source_target_pairs={{0,24},{8,0},{16,8},{24,16},{32,56},{40,32},{48,40},{56,48},{64,88... | collective-permute-start | bytes 344072 | tf_op jit(solution)/shard_map/ppermute | solution.py:24
  29.4 2.2 %collective-permute-done.16 = bf16[32,1792]{1,0:T(8,128)(2,1)S(1)} collective-permute-done((bf16[32,1792]{1,0:T(8,128)(2,1)S(1)}, bf16[32,1792]{1,0:T(8,128)(2,1)S(1)}, u32[]{:S(2)}, u32[]{:S(2)}) %collective-permute-start.16) | collective-permute-done | bytes 114720 | tf_op jit(solution)/shard_map/ppermute | solution.py:24
  31.7 1.6 collective-permute-start.2
  34.5 3.9 %collective-permute-start.10 = (bf16[64,2560]{1,0:T(8,128)(2,1)S(1)}, bf16[64,2560]{1,0:T(8,128)(2,1)S(1)}, u32[]{:S(2)}, u32[]{:S(2)}) collective-permute-start(bf16[64,2560]{1,0:T(8,128)(2,1)S(1)} %collective-permute-done.8), channel_id=1, source_target_pairs={{0,224},{8,232},{16,240},{24,248},{32,0},{40,8},{48,16},{56,24},{6... | collective-permute-start | bytes 983048 | tf_op jit(solution)/shard_map/ppermute | solution.py:24
  39.0 4.3 %collective-permute-done.9 = bf16[64,2560]{1,0:T(8,128)(2,1)S(1)} collective-permute-done((bf16[64,2560]{1,0:T(8,128)(2,1)S(1)}, bf16[64,2560]{1,0:T(8,128)(2,1)S(1)}, u32[]{:S(2)}, u32[]{:S(2)}) %collective-permute-start.9) | collective-permute-done | bytes 327712 | tf_op jit(solution)/shard_map/ppermute | solution.py:24
  43.3 5.4 %collective-permute-start.20 = (bf16[192,2560]{1,0:T(8,128)(2,1)S(1)}, bf16[192,2560]{1,0:T(8,128)(2,1)S(1)}, u32[]{:S(2)}, u32[]{:S(2)}) collective-permute-start(bf16[192,2560]{1,0:T(8,128)(2,1)S(1)} %pad_maximum_fusion.refs_0_), channel_id=1, source_target_pairs={{0,24},{8,0},{16,8},{24,16},{32,56},{40,32},{48,40},{56,48},{64,88... | collective-permute-start | bytes 2949128 | tf_op jit(solution)/shard_map/ppermute | solution.py:24
  48.9 3.3 %collective-permute-start.12 = (bf16[32,2560]{1,0:T(8,128)(2,1)S(1)}, bf16[32,2560]{1,0:T(8,128)(2,1)S(1)}, u32[]{:S(2)}, u32[]{:S(2)}) collective-permute-start(bf16[32,2560]{1,0:T(8,128)(2,1)S(1)} %slice.59), channel_id=1, source_target_pairs={{0,224},{8,232},{16,240},{24,248},{32,0},{40,8},{48,16},{56,24},{6... | collective-permute-start | bytes 491528 | tf_op jit(solution)/shard_map/ppermute | solution.py:24
  52.3 3.0 %collective-permute-done.11 = bf16[32,2560]{1,0:T(8,128)(2,1)S(1)} collective-permute-done((bf16[32,2560]{1,0:T(8,128)(2,1)S(1)}, bf16[32,2560]{1,0:T(8,128)(2,1)S(1)}, u32[]{:S(2)}, u32[]{:S(2)}) %collective-permute-start.11) | collective-permute-done | bytes 163872 | tf_op jit(solution)/shard_map/ppermute | solution.py:24
  55.4 3.3 %collective-permute-start.28 = (bf16[256,1792]{1,0:T(8,128)(2,1)S(1)}, bf16[256,1792]{1,0:T(8,128)(2,1)S(1)}, u32[]{:S(2)}, u32[]{:S(2)}) collective-permute-start(bf16[256,1792]{1,0:T(8,128)(2,1)S(1)} %constant_dynamic-update-slice_fusion.8.refs_0_), channel_id=1, source_target_pairs={{0,224},{8,232},{16,240},{24,248},{32,0},{40,8},{48,16},{56,24},{6... | collective-permute-start | bytes 2752520 | tf_op jit(solution)/shard_map/ppermute | solution.py:24
  63.6 2.4 %collective-permute-start.22 = (bf16[96,2560]{1,0:T(8,128)(2,1)S(1)}, bf16[96,2560]{1,0:T(8,128)(2,1)S(1)}, u32[]{:S(2)}, u32[]{:S(2)}) collective-permute-start(bf16[96,2560]{1,0:T(8,128)(2,1)S(1)} %slice.63), channel_id=1, source_target_pairs={{0,24},{8,0},{16,8},{24,16},{32,56},{40,32},{48,40},{56,48},{64,88... | collective-permute-start | bytes 1474568 | tf_op jit(solution)/shard_map/ppermute | solution.py:24
  67.4 5.6 %collective-permute-done.21.refs_3_ = bf16[96,2560]{1,0:T(8,128)(2,1)S(1)} collective-permute-done((bf16[96,2560]{1,0:T(8,128)(2,1)S(1)}, bf16[96,2560]{1,0:T(8,128)(2,1)S(1)}, u32[]{:S(2)}, u32[]{:S(2)}) %collective-permute-start.21) | collective-permute-done | bytes 491552 | tf_op jit(solution)/shard_map/ppermute | solution.py:24
  74.5 3.2 %collective-permute-start.18 = (bf16[320,2560]{1,0:T(8,128)(2,1)}, bf16[320,2560]{1,0:T(8,128)(2,1)}, u32[]{:S(2)}, u32[]{:S(2)}) collective-permute-start(bf16[320,2560]{1,0:T(8,128)(2,1)} %constant_dynamic-update-slice_fusion.13.refs_5_), channel_id=1, source_target_pairs={{0,24},{8,0},{16,8},{24,16},{32,56},{40,32},{48,40},{56,48},{64,88... | collective-permute-start | bytes 4915208 | tf_op jit(solution)/shard_map/ppermute | solution.py:24
  78.7 3.2 %collective-permute-start.29 = (bf16[256,1792]{1,0:T(8,128)(2,1)S(1)}, bf16[256,1792]{1,0:T(8,128)(2,1)}, u32[]{:S(2)}, u32[]{:S(2)}) collective-permute-start(bf16[256,1792]{1,0:T(8,128)(2,1)S(1)} %collective-permute-done.28.refs_2_), channel_id=1, source_target_pairs={{0,224},{8,232},{16,240},{24,248},{32,0},{40,8},{48,16},{56,24},{6... | collective-permute-start | bytes 2752520 | tf_op jit(solution)/shard_map/ppermute | solution.py:24
  83.0 15.1 %collective-permute-done.26.refs_3_ = bf16[256,1792]{1,0:T(8,128)(2,1)} collective-permute-done((bf16[256,1792]{1,0:T(8,128)(2,1)S(1)}, bf16[256,1792]{1,0:T(8,128)(2,1)}, u32[]{:S(2)}, u32[]{:S(2)}) %collective-permute-start.26) | collective-permute-done | bytes 917536 | tf_op jit(solution)/shard_map/ppermute | solution.py:24
  98.8 3.5 %collective-permute-start.30 = (bf16[256,1792]{1,0:T(8,128)(2,1)}, bf16[256,1792]{1,0:T(8,128)(2,1)}, u32[]{:S(2)}, u32[]{:S(2)}) collective-permute-start(bf16[256,1792]{1,0:T(8,128)(2,1)} %collective-permute-done.29.refs_4_), channel_id=1, source_target_pairs={{0,224},{8,232},{16,240},{24,248},{32,0},{40,8},{48,16},{56,24},{6... | collective-permute-start | bytes 2752520 | tf_op jit(solution)/shard_map/ppermute | solution.py:24
  106.8 11.5 %shard_map.59.refs_2_ = f32[512,2560]{1,0:T(8,128)S(1)} custom-call(s32[4]{0:T(128)S(1)} %pad_add_fusion.place_ref, bf16[1024,1024]{1,0:T(8,128)(2,1)S(1)} %constant_dynamic-update-slice_fusion.2.mine_ref, bf16[1024,1024]{1,0:T(8,128)(2,1)} %collective-permute-done.4.other_ref, bf16[192,2560]{1,0:T(8,128)(2,1)S(1)} %pad_maximum_fusion.refs_0_, ...), custom_call_target="tpu_custom_call" | custom-call | flops 2852126720 | bytes 11927552 | tf_op jit(solution)/shard_map/pallas_call | solution.py:124
  118.4 1.3 slice.52
  121.0 3.3 %collective-permute-start.24 = (bf16[160,2560]{1,0:T(8,128)(2,1)S(1)}, bf16[160,2560]{1,0:T(8,128)(2,1)S(1)}, u32[]{:S(2)}, u32[]{:S(2)}) collective-permute-start(bf16[160,2560]{1,0:T(8,128)(2,1)S(1)} %slice.53), channel_id=1, source_target_pairs={{0,24},{8,0},{16,8},{24,16},{32,56},{40,32},{48,40},{56,48},{64,88... | collective-permute-start | bytes 2457608 | tf_op jit(solution)/shard_map/ppermute | solution.py:24
  124.3 8.1 %shard_map.62.refs_2_ = f32[512,1792]{1,0:T(8,128)S(1)} custom-call(s32[4]{0:T(128)S(1)} %pad_add_fusion.place_ref, bf16[1024,1024]{1,0:T(8,128)(2,1)S(1)} %constant_dynamic-update-slice_fusion.2.mine_ref, bf16[1024,1024]{1,0:T(8,128)(2,1)} %collective-permute-done.4.other_ref, bf16[256,1792]{1,0:T(8,128)(2,1)S(1)} %copy-done.5, ...), custom_call_target="tpu_custom_call" | custom-call | flops 2348810240 | bytes 9568256 | tf_op jit(solution)/shard_map/pallas_call | solution.py:124
  134.7 3.3 %collective-permute-start.32 = (bf16[128,1792]{1,0:T(8,128)(2,1)S(1)}, bf16[128,1792]{1,0:T(8,128)(2,1)S(1)}, u32[]{:S(2)}, u32[]{:S(2)}) collective-permute-start(bf16[128,1792]{1,0:T(8,128)(2,1)S(1)} %slice.55), channel_id=1, source_target_pairs={{0,224},{8,232},{16,240},{24,248},{32,0},{40,8},{48,16},{56,24},{6... | collective-permute-start | bytes 1376264 | tf_op jit(solution)/shard_map/ppermute | solution.py:24
  138.0 10.3 %shard_map.60.refs_2_ = f32[512,2560]{1,0:T(8,128)S(1)} custom-call(s32[4]{0:T(128)S(1)} %pad_add_fusion.place_ref, bf16[1024,1024]{1,0:T(8,128)(2,1)S(1)} %constant_dynamic-update-slice_fusion.2.mine_ref, bf16[1024,1024]{1,0:T(8,128)(2,1)} %collective-permute-done.4.other_ref, bf16[320,2560]{1,0:T(8,128)(2,1)} %collective-permute-done.17.refs_0_, ...), custom_call_target="tpu_custom_call" | custom-call | flops 1677721600 | bytes 9175040 | tf_op jit(solution)/shard_map/pallas_call | solution.py:124
  148.3 7.9 %shard_map.61 = (bf16[512,2304]{1,0:T(8,128)(2,1)}, bf16[512,256]{1,0:T(8,128)(2,1)S(1)}) custom-call(s32[4]{0:T(128)S(1)} %pad_add_fusion.place_ref, bf16[1024,1024]{1,0:T(8,128)(2,1)S(1)} %constant_dynamic-update-slice_fusion.2.mine_ref, bf16[1024,1024]{1,0:T(8,128)(2,1)} %collective-permute-done.4.other_ref, ...), custom_call_target="tpu_custom_call" | custom-call | flops 838860800 | bytes 7208960 | tf_op jit(solution)/shard_map/pallas_call | solution.py:124
  156.3 6.7 %shard_map.63.refs_2_ = f32[512,1792]{1,0:T(8,128)S(1)} custom-call(s32[4]{0:T(128)S(1)} %pad_add_fusion.place_ref, bf16[1024,1024]{1,0:T(8,128)(2,1)S(1)} %constant_dynamic-update-slice_fusion.2.mine_ref, bf16[1024,1024]{1,0:T(8,128)(2,1)} %collective-permute-done.4.other_ref, bf16[256,1792]{1,0:T(8,128)(2,1)} %collective-permute-done.27.refs_0_, ...), custom_call_target="tpu_custom_call" | custom-call | flops 939524096 | bytes 6029312 | tf_op jit(solution)/shard_map/pallas_call | solution.py:124
  163.0 4.9 %shard_map.64 = bf16[512,2048]{1,0:T(8,128)(2,1)} custom-call(s32[4]{0:T(128)S(1)} %pad_add_fusion.place_ref, bf16[1024,1024]{1,0:T(8,128)(2,1)S(1)} %constant_dynamic-update-slice_fusion.2.mine_ref, bf16[1024,1024]{1,0:T(8,128)(2,1)} %collective-permute-done.4.other_ref, bf16[128,1792]{1,0:T(8,128)(2,1)S(1)} %collective-permute-done.31.refs_0_, ...), custom_call_target="tpu_custom_call" | custom-call | flops 469762048 | bytes 4849664 | tf_op jit(solution)/shard_map/pallas_call | solution.py:124
  (103 shorter events, 25.7 us)
Async XLA Ops:
  2.7 26.7 %collective-permute-start = (bf16[256,1024]{1,0:T(8,128)(2,1)S(1)}, bf16[256,1024]{1,0:T(8,128)(2,1)S(1)}, u32[]{:S(2)}, u32[]{:S(2)}) collective-permute-start(bf16[256,1024]{1,0:T(8,128)(2,1)S(1)} %get-tuple-element.34), channel_id=1, source_target_pairs={{0,2},{1,3},{2,4},{3,5},{4,6},{5,7},{6,0},{7,1},{8,10},{9,11},{10,... | collective-permute-start | bytes 1572872 | tf_op jit(solution)/shard_map/ppermute | solution.py:29
  4.3 34.1 %collective-permute-start.1 = (bf16[256,1024]{1,0:T(8,128)(2,1)S(1)}, bf16[256,1024]{1,0:T(8,128)(2,1)S(1)}, u32[]{:S(2)}, u32[]{:S(2)}) collective-permute-start(bf16[256,1024]{1,0:T(8,128)(2,1)S(1)} %get-tuple-element.34), channel_id=1, source_target_pairs={{0,6},{1,7},{2,0},{3,1},{4,2},{5,3},{6,4},{7,5},{8,14},{9,15},{10,... | collective-permute-start | bytes 1572872 | tf_op jit(solution)/shard_map/ppermute | solution.py:29
  6.0 8.1 %collective-permute-start.13 = (bf16[64,1792]{1,0:T(8,128)(2,1)S(1)}, bf16[64,1792]{1,0:T(8,128)(2,1)S(1)}, u32[]{:S(2)}, u32[]{:S(2)}) collective-permute-start(bf16[64,1792]{1,0:T(8,128)(2,1)S(1)} %get-tuple-element.32), channel_id=1, source_target_pairs={{0,8},{8,16},{16,24},{24,0},{32,40},{40,48},{48,56},{56,32},{64,72... | collective-permute-start | bytes 688136 | tf_op jit(solution)/shard_map/ppermute | solution.py:24
  8.1 13.8 %collective-permute-start.5 = (bf16[64,2560]{1,0:T(8,128)(2,1)S(1)}, bf16[64,2560]{1,0:T(8,128)(2,1)S(1)}, u32[]{:S(2)}, u32[]{:S(2)}) collective-permute-start(bf16[64,2560]{1,0:T(8,128)(2,1)S(1)} %pad_maximum_fusion.1), channel_id=1, source_target_pairs={{0,32},{8,40},{16,48},{24,56},{32,64},{40,72},{48,80},{56,88},{64,... | collective-permute-start | bytes 983048 | tf_op jit(solution)/shard_map/ppermute | solution.py:24
  10.1 12.1 %collective-permute-start.7 = (bf16[64,2560]{1,0:T(8,128)(2,1)S(1)}, bf16[64,2560]{1,0:T(8,128)(2,1)S(1)}, u32[]{:S(2)}, u32[]{:S(2)}) collective-permute-start(bf16[64,2560]{1,0:T(8,128)(2,1)S(1)} %pad_maximum_fusion.1), channel_id=1, source_target_pairs={{0,224},{8,232},{16,240},{24,248},{32,0},{40,8},{48,16},{56,24},{6... | collective-permute-start | bytes 983048 | tf_op jit(solution)/shard_map/ppermute | solution.py:24
  14.1 6.2 %collective-permute-start.14 = (bf16[64,1792]{1,0:T(8,128)(2,1)S(1)}, bf16[64,1792]{1,0:T(8,128)(2,1)S(1)}, u32[]{:S(2)}, u32[]{:S(2)}) collective-permute-start(bf16[64,1792]{1,0:T(8,128)(2,1)S(1)} %get-tuple-element.32), channel_id=1, source_target_pairs={{0,24},{8,0},{16,8},{24,16},{32,56},{40,32},{48,40},{56,48},{64,88... | collective-permute-start | bytes 688136 | tf_op jit(solution)/shard_map/ppermute | solution.py:24
  20.4 6.0 %collective-permute-start.15 = (bf16[32,1792]{1,0:T(8,128)(2,1)S(1)}, bf16[32,1792]{1,0:T(8,128)(2,1)S(1)}, u32[]{:S(2)}, u32[]{:S(2)}) collective-permute-start(bf16[32,1792]{1,0:T(8,128)(2,1)S(1)} %slice.60), channel_id=1, source_target_pairs={{0,8},{8,16},{16,24},{24,0},{32,40},{40,48},{48,56},{56,32},{64,72... | collective-permute-start | bytes 344072 | tf_op jit(solution)/shard_map/ppermute | solution.py:24
  21.9 11.4 %collective-permute-start.6 = (bf16[64,2560]{1,0:T(8,128)(2,1)S(1)}, bf16[64,2560]{1,0:T(8,128)(2,1)S(1)}, u32[]{:S(2)}, u32[]{:S(2)}) collective-permute-start(bf16[64,2560]{1,0:T(8,128)(2,1)S(1)} %collective-permute-done.5), channel_id=1, source_target_pairs={{0,32},{8,40},{16,48},{24,56},{32,64},{40,72},{48,80},{56,88},{64,... | collective-permute-start | bytes 983048 | tf_op jit(solution)/shard_map/ppermute | solution.py:24
  22.2 12.3 %collective-permute-start.8 = (bf16[64,2560]{1,0:T(8,128)(2,1)S(1)}, bf16[64,2560]{1,0:T(8,128)(2,1)S(1)}, u32[]{:S(2)}, u32[]{:S(2)}) collective-permute-start(bf16[64,2560]{1,0:T(8,128)(2,1)S(1)} %collective-permute-done.7), channel_id=1, source_target_pairs={{0,224},{8,232},{16,240},{24,248},{32,0},{40,8},{48,16},{56,24},{6... | collective-permute-start | bytes 983048 | tf_op jit(solution)/shard_map/ppermute | solution.py:24
  29.3 32.4 %collective-permute-start.19 = (bf16[192,2560]{1,0:T(8,128)(2,1)S(1)}, bf16[192,2560]{1,0:T(8,128)(2,1)S(1)}, u32[]{:S(2)}, u32[]{:S(2)}) collective-permute-start(bf16[192,2560]{1,0:T(8,128)(2,1)S(1)} %pad_maximum_fusion.refs_0_), channel_id=1, source_target_pairs={{0,8},{8,16},{16,24},{24,0},{32,40},{40,48},{48,56},{56,32},{64,72... | collective-permute-start | bytes 2949128 | tf_op jit(solution)/shard_map/ppermute | solution.py:24
  31.7 17.2 %collective-permute-start.2 = (bf16[128,1024]{1,0:T(8,128)(2,1)S(1)}, bf16[128,1024]{1,0:T(8,128)(2,1)S(1)}, u32[]{:S(2)}, u32[]{:S(2)}) collective-permute-start(bf16[128,1024]{1,0:T(8,128)(2,1)S(1)} %slice.56), channel_id=1, source_target_pairs={{0,2},{1,3},{2,4},{3,5},{4,6},{5,7},{6,0},{7,1},{8,10},{9,11},{10,... | collective-permute-start | bytes 786440 | tf_op jit(solution)/shard_map/ppermute | solution.py:29
  33.3 10.1 %collective-permute-start.9 = (bf16[64,2560]{1,0:T(8,128)(2,1)S(1)}, bf16[64,2560]{1,0:T(8,128)(2,1)S(1)}, u32[]{:S(2)}, u32[]{:S(2)}) collective-permute-start(bf16[64,2560]{1,0:T(8,128)(2,1)S(1)} %collective-permute-done.6), channel_id=1, source_target_pairs={{0,32},{8,40},{16,48},{24,56},{32,64},{40,72},{48,80},{56,88},{64,... | collective-permute-start | bytes 983048 | tf_op jit(solution)/shard_map/ppermute | solution.py:24
  34.5 14.3 %collective-permute-start.10 = (bf16[64,2560]{1,0:T(8,128)(2,1)S(1)}, bf16[64,2560]{1,0:T(8,128)(2,1)S(1)}, u32[]{:S(2)}, u32[]{:S(2)}) collective-permute-start(bf16[64,2560]{1,0:T(8,128)(2,1)S(1)} %collective-permute-done.8), channel_id=1, source_target_pairs={{0,224},{8,232},{16,240},{24,248},{32,0},{40,8},{48,16},{56,24},{6... | collective-permute-start | bytes 983048 | tf_op jit(solution)/shard_map/ppermute | solution.py:24
  38.4 13.8 %collective-permute-start.3 = (bf16[128,1024]{1,0:T(8,128)(2,1)S(1)}, bf16[128,1024]{1,0:T(8,128)(2,1)S(1)}, u32[]{:S(2)}, u32[]{:S(2)}) collective-permute-start(bf16[128,1024]{1,0:T(8,128)(2,1)S(1)} %slice.57), channel_id=1, source_target_pairs={{0,6},{1,7},{2,0},{3,1},{4,2},{5,3},{6,4},{7,5},{8,14},{9,15},{10,... | collective-permute-start | bytes 786440 | tf_op jit(solution)/shard_map/ppermute | solution.py:29
  43.3 18.5 %collective-permute-start.20 = (bf16[192,2560]{1,0:T(8,128)(2,1)S(1)}, bf16[192,2560]{1,0:T(8,128)(2,1)S(1)}, u32[]{:S(2)}, u32[]{:S(2)}) collective-permute-start(bf16[192,2560]{1,0:T(8,128)(2,1)S(1)} %pad_maximum_fusion.refs_0_), channel_id=1, source_target_pairs={{0,24},{8,0},{16,8},{24,16},{32,56},{40,32},{48,40},{56,48},{64,88... | collective-permute-start | bytes 2949128 | tf_op jit(solution)/shard_map/ppermute | solution.py:24
  48.8 6.6 %collective-permute-start.11 = (bf16[32,2560]{1,0:T(8,128)(2,1)S(1)}, bf16[32,2560]{1,0:T(8,128)(2,1)S(1)}, u32[]{:S(2)}, u32[]{:S(2)}) collective-permute-start(bf16[32,2560]{1,0:T(8,128)(2,1)S(1)} %slice.58), channel_id=1, source_target_pairs={{0,32},{8,40},{16,48},{24,56},{32,64},{40,72},{48,80},{56,88},{64,... | collective-permute-start | bytes 491528 | tf_op jit(solution)/shard_map/ppermute | solution.py:24
  48.9 6.5 %collective-permute-start.12 = (bf16[32,2560]{1,0:T(8,128)(2,1)S(1)}, bf16[32,2560]{1,0:T(8,128)(2,1)S(1)}, u32[]{:S(2)}, u32[]{:S(2)}) collective-permute-start(bf16[32,2560]{1,0:T(8,128)(2,1)S(1)} %slice.59), channel_id=1, source_target_pairs={{0,224},{8,232},{16,240},{24,248},{32,0},{40,8},{48,16},{56,24},{6... | collective-permute-start | bytes 491528 | tf_op jit(solution)/shard_map/ppermute | solution.py:24
  52.2 50.1 %collective-permute-start.4 = (bf16[1024,1024]{1,0:T(8,128)(2,1)S(1)}, bf16[1024,1024]{1,0:T(8,128)(2,1)}, u32[]{:S(2)}, u32[]{:S(2)}) collective-permute-start(bf16[1024,1024]{1,0:T(8,128)(2,1)S(1)} %constant_dynamic-update-slice_fusion.2.mine_ref), channel_id=1, source_target_pairs={{0,1},{1,0},{2,3},{3,2},{4,5},{5,4},{6,7},{7,6},{8,9},{9,8},{10,11... | collective-permute-start | bytes 6291464 | tf_op jit(solution)/shard_map/ppermute | solution.py:29
  55.4 22.4 %collective-permute-start.25 = (bf16[256,1792]{1,0:T(8,128)(2,1)S(1)}, bf16[256,1792]{1,0:T(8,128)(2,1)S(1)}, u32[]{:S(2)}, u32[]{:S(2)}) collective-permute-start(bf16[256,1792]{1,0:T(8,128)(2,1)S(1)} %constant_dynamic-update-slice_fusion.8.refs_0_), channel_id=1, source_target_pairs={{0,32},{8,40},{16,48},{24,56},{32,64},{40,72},{48,80},{56,88},{64,... | collective-permute-start | bytes 2752520 | tf_op jit(solution)/shard_map/ppermute | solution.py:24
  55.4 23.4 %collective-permute-start.28 = (bf16[256,1792]{1,0:T(8,128)(2,1)S(1)}, bf16[256,1792]{1,0:T(8,128)(2,1)S(1)}, u32[]{:S(2)}, u32[]{:S(2)}) collective-permute-start(bf16[256,1792]{1,0:T(8,128)(2,1)S(1)} %constant_dynamic-update-slice_fusion.8.refs_0_), channel_id=1, source_target_pairs={{0,224},{8,232},{16,240},{24,248},{32,0},{40,8},{48,16},{56,24},{6... | collective-permute-start | bytes 2752520 | tf_op jit(solution)/shard_map/ppermute | solution.py:24
  61.7 11.2 %collective-permute-start.21 = (bf16[96,2560]{1,0:T(8,128)(2,1)S(1)}, bf16[96,2560]{1,0:T(8,128)(2,1)S(1)}, u32[]{:S(2)}, u32[]{:S(2)}) collective-permute-start(bf16[96,2560]{1,0:T(8,128)(2,1)S(1)} %slice.62), channel_id=1, source_target_pairs={{0,8},{8,16},{16,24},{24,0},{32,40},{40,48},{48,56},{56,32},{64,72... | collective-permute-start | bytes 1474568 | tf_op jit(solution)/shard_map/ppermute | solution.py:24
  63.6 10.2 %collective-permute-start.22 = (bf16[96,2560]{1,0:T(8,128)(2,1)S(1)}, bf16[96,2560]{1,0:T(8,128)(2,1)S(1)}, u32[]{:S(2)}, u32[]{:S(2)}) collective-permute-start(bf16[96,2560]{1,0:T(8,128)(2,1)S(1)} %slice.63), channel_id=1, source_target_pairs={{0,24},{8,0},{16,8},{24,16},{32,56},{40,32},{48,40},{56,48},{64,88... | collective-permute-start | bytes 1474568 | tf_op jit(solution)/shard_map/ppermute | solution.py:24
  73.7 44.6 %collective-permute-start.17 = (bf16[320,2560]{1,0:T(8,128)(2,1)}, bf16[320,2560]{1,0:T(8,128)(2,1)}, u32[]{:S(2)}, u32[]{:S(2)}) collective-permute-start(bf16[320,2560]{1,0:T(8,128)(2,1)} %constant_dynamic-update-slice_fusion.13.refs_5_), channel_id=1, source_target_pairs={{0,8},{8,16},{16,24},{24,0},{32,40},{40,48},{48,56},{56,32},{64,72... | collective-permute-start | bytes 4915208 | tf_op jit(solution)/shard_map/ppermute | solution.py:24
  74.5 43.8 %collective-permute-start.18 = (bf16[320,2560]{1,0:T(8,128)(2,1)}, bf16[320,2560]{1,0:T(8,128)(2,1)}, u32[]{:S(2)}, u32[]{:S(2)}) collective-permute-start(bf16[320,2560]{1,0:T(8,128)(2,1)} %constant_dynamic-update-slice_fusion.13.refs_5_), channel_id=1, source_target_pairs={{0,24},{8,0},{16,8},{24,16},{32,56},{40,32},{48,40},{56,48},{64,88... | collective-permute-start | bytes 4915208 | tf_op jit(solution)/shard_map/ppermute | solution.py:24
  77.8 20.3 %collective-permute-start.26 = (bf16[256,1792]{1,0:T(8,128)(2,1)S(1)}, bf16[256,1792]{1,0:T(8,128)(2,1)}, u32[]{:S(2)}, u32[]{:S(2)}) collective-permute-start(bf16[256,1792]{1,0:T(8,128)(2,1)S(1)} %collective-permute-done.25.refs_1_), channel_id=1, source_target_pairs={{0,32},{8,40},{16,48},{24,56},{32,64},{40,72},{48,80},{56,88},{64,... | collective-permute-start | bytes 2752520 | tf_op jit(solution)/shard_map/ppermute | solution.py:24
  78.7 20.1 %collective-permute-start.29 = (bf16[256,1792]{1,0:T(8,128)(2,1)S(1)}, bf16[256,1792]{1,0:T(8,128)(2,1)}, u32[]{:S(2)}, u32[]{:S(2)}) collective-permute-start(bf16[256,1792]{1,0:T(8,128)(2,1)S(1)} %collective-permute-done.28.refs_2_), channel_id=1, source_target_pairs={{0,224},{8,232},{16,240},{24,248},{32,0},{40,8},{48,16},{56,24},{6... | collective-permute-start | bytes 2752520 | tf_op jit(solution)/shard_map/ppermute | solution.py:24
  98.1 34.4 %collective-permute-start.27 = (bf16[256,1792]{1,0:T(8,128)(2,1)}, bf16[256,1792]{1,0:T(8,128)(2,1)}, u32[]{:S(2)}, u32[]{:S(2)}) collective-permute-start(bf16[256,1792]{1,0:T(8,128)(2,1)} %collective-permute-done.26.refs_3_), channel_id=1, source_target_pairs={{0,32},{8,40},{16,48},{24,56},{32,64},{40,72},{48,80},{56,88},{64,... | collective-permute-start | bytes 2752520 | tf_op jit(solution)/shard_map/ppermute | solution.py:24
  98.8 33.7 %collective-permute-start.30 = (bf16[256,1792]{1,0:T(8,128)(2,1)}, bf16[256,1792]{1,0:T(8,128)(2,1)}, u32[]{:S(2)}, u32[]{:S(2)}) collective-permute-start(bf16[256,1792]{1,0:T(8,128)(2,1)} %collective-permute-done.29.refs_4_), channel_id=1, source_target_pairs={{0,224},{8,232},{16,240},{24,248},{32,0},{40,8},{48,16},{56,24},{6... | collective-permute-start | bytes 2752520 | tf_op jit(solution)/shard_map/ppermute | solution.py:24
  119.7 28.6 %collective-permute-start.23 = (bf16[160,2560]{1,0:T(8,128)(2,1)S(1)}, bf16[160,2560]{1,0:T(8,128)(2,1)S(1)}, u32[]{:S(2)}, u32[]{:S(2)}) collective-permute-start(bf16[160,2560]{1,0:T(8,128)(2,1)S(1)} %slice.52), channel_id=1, source_target_pairs={{0,8},{8,16},{16,24},{24,0},{32,40},{40,48},{48,56},{56,32},{64,72... | collective-permute-start | bytes 2457608 | tf_op jit(solution)/shard_map/ppermute | solution.py:24
  121.0 27.3 %collective-permute-start.24 = (bf16[160,2560]{1,0:T(8,128)(2,1)S(1)}, bf16[160,2560]{1,0:T(8,128)(2,1)S(1)}, u32[]{:S(2)}, u32[]{:S(2)}) collective-permute-start(bf16[160,2560]{1,0:T(8,128)(2,1)S(1)} %slice.53), channel_id=1, source_target_pairs={{0,24},{8,0},{16,8},{24,16},{32,56},{40,32},{48,40},{56,48},{64,88... | collective-permute-start | bytes 2457608 | tf_op jit(solution)/shard_map/ppermute | solution.py:24
  133.6 29.4 %collective-permute-start.31 = (bf16[128,1792]{1,0:T(8,128)(2,1)S(1)}, bf16[128,1792]{1,0:T(8,128)(2,1)S(1)}, u32[]{:S(2)}, u32[]{:S(2)}) collective-permute-start(bf16[128,1792]{1,0:T(8,128)(2,1)S(1)} %slice.54), channel_id=1, source_target_pairs={{0,32},{8,40},{16,48},{24,56},{32,64},{40,72},{48,80},{56,88},{64,... | collective-permute-start | bytes 1376264 | tf_op jit(solution)/shard_map/ppermute | solution.py:24
  134.7 28.3 %collective-permute-start.32 = (bf16[128,1792]{1,0:T(8,128)(2,1)S(1)}, bf16[128,1792]{1,0:T(8,128)(2,1)S(1)}, u32[]{:S(2)}, u32[]{:S(2)}) collective-permute-start(bf16[128,1792]{1,0:T(8,128)(2,1)S(1)} %slice.55), channel_id=1, source_target_pairs={{0,224},{8,232},{16,240},{24,248},{32,0},{40,8},{48,16},{56,24},{6... | collective-permute-start | bytes 1376264 | tf_op jit(solution)/shard_map/ppermute | solution.py:24
  (16 other events, 57.6 us)

commit v3 on v2

v3 whole, which is shorter than its diff:
```python
import functools

import jax
import jax.numpy as jnp
from jax import lax
from jax.experimental import pallas as pl
from jax.experimental.pallas import tpu as pltpu
from jax.sharding import PartitionSpec as P

Z, X, Y, C = 8, 4, 4, 2
BLOCK = 64
FEATURES = 512
TILE = 256
SPLIT = 256

X_ORDER = (0, -1, 1, 2)
NEAR, FAR = (0, -1, 1), (-2, 2, -3, 3, 4)


def hop(value, dz, dx):
    pairs = [
        (z * X + x, ((z + dz) % Z) * X + (x + dx) % X) for z in range(Z) for x in range(X)
    ]
    return lax.ppermute(value, "row", pairs)


def hop_y(value, dy, swap=0):
    pairs = [(y * C + c, ((y + dy) % Y) * C + (c ^ swap)) for y in range(Y) for c in range(C)]
    return lax.ppermute(value, "col", pairs)


def halves(value):
    half = value.shape[0] // 2
    return value[:half], value[half:]


def arrange_kernel(groups, place_ref, mine_ref, other_ref, *refs):
    outs, (left, sems) = refs[: len(groups)], refs[len(groups) :]
    z, x, y, core = (place_ref[i] for i in range(4))
    at, copies = 0, []
    for rows, ops in groups:
        width = len(ops) * FEATURES
        for dz, dx, start, size in rows:
            group = lax.rem(z + (dz + Z), Z)
            away = lax.rem(group // C + Y - y, Y)
            slot = jnp.where(away == 0, 0, jnp.where(away == Y - 1, 1, jnp.where(away == 1, 2, 3)))
            row = slot * (X * BLOCK) + lax.rem(x + (dx + X), X) * BLOCK + start
            source = (pl.ds(pl.multiple_of(row, 32), size), pl.ds(ops[0] * FEATURES, width))
            target = left.at[pl.ds(at, size), pl.ds(0, width)]
            swapped, sem = lax.rem(group, C) != core, sems.at[len(copies)]

            @pl.when(swapped)
            def _():
                pltpu.make_async_copy(other_ref.at[source], target, sem).start()

            @pl.when(jnp.logical_not(swapped))
            def _():
                pltpu.make_async_copy(mine_ref.at[source], target, sem).start()

            copies.append(pltpu.make_async_copy(target, target, sem))
            at += size
    at = 0
    for (rows, ops), out in zip(groups, outs):
        size = depth_of(rows)
        for _ in rows:
            copies.pop(0).wait()
        for i in range(len(ops)):
            out[i] = left[at : at + size, i * FEATURES : (i + 1) * FEATURES].T
        at += size


def arrange(place, operand, groups):
    anywhere = pl.BlockSpec(memory_space=pl.ANY)
    depth = sum(depth_of(rows) for rows, _ in groups)
    return pl.pallas_call(
        functools.partial(arrange_kernel, groups),
        out_shape=[
            jax.ShapeDtypeStruct((len(ops), FEATURES, depth_of(rows)), jnp.bfloat16)
            for rows, ops in groups
        ],
        in_specs=[pl.BlockSpec(memory_space=pltpu.SMEM), anywhere, anywhere],
        out_specs=[pl.BlockSpec(memory_space=pltpu.VMEM)] * len(groups),
        scratch_shapes=[
            pltpu.VMEM((depth, 2 * FEATURES), jnp.bfloat16),
            pltpu.SemaphoreType.DMA((sum(len(rows) for rows, _ in groups),)),
        ],
        compiler_params=pltpu.CompilerParams(vmem_limit_bytes=24 << 20),
        cost_estimate=pl.CostEstimate(flops=0, bytes_accessed=16 << 20, transcendentals=0),
    )(place, *operand)


def kernel(sizes, added, cut, ahead, left_ref, *refs):
    grads, refs = refs[: len(sizes)], refs[len(sizes) :]
    if added:
        total_ref, *refs = refs
    if ahead:
        prefix_ref, *refs = refs
    *outs, right = refs
    tile = pl.program_id(0)

    def work(out_ref):
        at = 0
        for grad, size in zip(grads, sizes):
            right[pl.ds(at, size)] = grad[...]
            at += size
        part = jnp.dot(left_ref[0], right[...], preferred_element_type=jnp.float32)
        if added:
            part += total_ref[...]
        out_ref[...] = part.astype(out_ref.dtype)

    if ahead:
        pl.when(tile < ahead)(lambda: outs[0].__setitem__(..., prefix_ref[...]))
        pl.when(tile >= ahead)(lambda: work(outs[0]))
    elif len(outs) == 1:
        work(outs[0])
    else:
        pl.when(tile < cut)(lambda: work(outs[0]))
        pl.when(tile >= cut)(lambda: work(outs[1]))


def contract(left, grads, total=None, prefix=None, split=None, dtype=jnp.float32):
    sizes = [array.shape[0] for array in grads]
    depth, width = sum(sizes), grads[0].shape[1]
    assert depth == left.shape[2]
    ahead = 0 if prefix is None else prefix.shape[1] // TILE
    tiles = ahead + width // TILE
    cut = tiles if split is None else split // TILE
    here = lambda height: pl.BlockSpec((height, TILE), lambda t: (0, jnp.maximum(t - ahead, 0)))
    if dtype == jnp.float32 or split is None:
        widths, specs = [tiles * TILE], [pl.BlockSpec((FEATURES, TILE), lambda t: (0, t))]
    else:
        widths = [cut * TILE, (tiles - cut) * TILE]
        specs = [
            pl.BlockSpec((FEATURES, TILE), lambda t: (0, jnp.minimum(t, cut - 1))),
            pl.BlockSpec((FEATURES, TILE), lambda t: (0, jnp.maximum(t - cut, 0))),
        ]
    extra, extra_specs = [], []
    if total is not None:
        extra, extra_specs = [total], [here(FEATURES)]
    if prefix is not None:
        extra.append(prefix)
        extra_specs.append(
            pl.BlockSpec((FEATURES, TILE), lambda t: (0, jnp.minimum(t, ahead - 1)))
        )
    results = pl.pallas_call(
        functools.partial(kernel, sizes, total is not None, cut, ahead),
        grid=(tiles,),
        out_shape=[jax.ShapeDtypeStruct((FEATURES, w), dtype) for w in widths],
        in_specs=[pl.BlockSpec((1, FEATURES, depth), lambda t: (jnp.where(t >= cut, 1, 0), 0, 0))]
        + [here(size) for size in sizes]
        + extra_specs,
        out_specs=specs,
        scratch_shapes=[pltpu.VMEM((depth, TILE), jnp.bfloat16)],
        compiler_params=pltpu.CompilerParams(vmem_limit_bytes=16 << 20),
        cost_estimate=pl.CostEstimate(
            flops=2 * FEATURES * depth * width,
            bytes_accessed=2 * depth * (width + FEATURES) + 4 * FEATURES * width,
            transcendentals=0,
        ),
    )(left, *grads, *extra)
    return results if len(results) > 1 else results[0]


def depth_of(rows):
    return sum(row[3] for row in rows)


def whole(dzs, dx):
    return [(dz, dx, 0, BLOCK) for dz in dzs]


def parts(rows):
    half, first, second = depth_of(rows) // 2, [], []
    for dz, dx, start, size in rows:
        here = min(size, half)
        if here:
            first.append((dz, dx, start, here))
        if here < size:
            second.append((dz, dx, start + here, size - here))
        half -= here
    return first, second


def body(normed_input, attended, qkv_grad, proj_grad):
    row, col = lax.axis_index("row"), lax.axis_index("col")
    place = jnp.stack([row // X, row % X, col // C, col % C])

    tall = jnp.concatenate([qkv_grad, proj_grad[:, :SPLIT]], axis=1)
    wide = proj_grad[:, SPLIT:]

    below, above = hop(tall, 1, 0), hop(tall, -1, 0)
    left, right, opposite = hop(wide, 0, 1), hop(wide, 0, -1), hop(wide, 0, 2)
    below, above, left, right, opposite = lax.optimization_barrier(
        (below, above, left, right, opposite)
    )
    near = jnp.concatenate([tall, below, above])
    near_left, near_right = hop(near, 0, 1), hop(near, 0, -1)
    far = []
    for distance in (2, 3):
        below, above = hop(below, 1, 0), hop(above, -1, 0)
        far += [below, above]
    below, above, near_left, near_right = lax.optimization_barrier(
        (below, above, near_left, near_right)
    )
    far[2:] = [below, above, hop(halves(below)[0], 1, 0), hop(halves(above)[1], -1, 0)]
    wide = jnp.concatenate([wide, left, right, opposite])

    mine = jnp.concatenate([normed_input, attended], axis=1)
    mine, opposite = lax.optimization_barrier((mine, opposite))
    down = hop_y(mine, 1)
    mine, down = lax.optimization_barrier((mine, down))
    up = hop_y(mine, -1)
    mine, up = lax.optimization_barrier((mine, up))
    mine = jnp.concatenate([mine, down, up, hop_y(mine, 2)])
    near_rows = {dx: whole(NEAR, dx) for dx in X_ORDER}
    far_rows = {dx: whole(FAR, dx) for dx in X_ORDER}
    near_split, far_split = parts(near_rows[2]), parts(far_rows[2])
    wide_rows = {dz: [(dz, dx, 0, BLOCK) for dx in X_ORDER] for dz in range(-4, 5)}
    wide_split = parts(wide_rows[4])
    groups = [
        (sum([near_rows[0], near_rows[-1], near_rows[1], *near_split, far_rows[0]], []), (0, 1)),
        (far_rows[-1] + far_rows[1], (0, 1)),
        (far_split[0] + far_split[1], (0, 1)),
        (sum([wide_rows[d] for d in (0, -1, 1, -2, 2)], []), (1,)),
        (wide_rows[-3] + wide_rows[3], (1,)),
        (wide_split[0] + wide_split[1], (1,)),
    ]
    lefts = arrange(place, (mine, hop_y(mine, 0, 1)), groups)

    far, wide, below, above = lax.optimization_barrier((far, wide, below, above))
    near_halves = [hop(halves(near_left)[0], 0, 1), hop(halves(near_right)[1], 0, -1)]
    far = jnp.concatenate(far)
    far, near_halves = lax.optimization_barrier((far, near_halves))
    far_left, far_right = hop(far, 0, 1), hop(far, 0, -1)
    width = qkv_grad.shape[1]
    tall_sum = contract(lefts[0], [near, near_left, near_right, *near_halves, far], split=width)

    below = above = wide
    wide_first = [wide]
    for distance in (1, 2):
        below, above = hop(below, 1, 0), hop(above, -1, 0)
        wide_first += [below, above]
    below, above, tall_sum = lax.optimization_barrier((below, above, tall_sum))
    wide_sum = contract(lefts[3], wide_first)
    below, above = hop(below, 1, 0), hop(above, -1, 0)
    far_left, far_right, tall_sum = lax.optimization_barrier((far_left, far_right, tall_sum))
    far_halves = [hop(halves(far_left)[0], 0, 1), hop(halves(far_right)[1], 0, -1)]
    below, above, wide_sum = lax.optimization_barrier((below, above, wide_sum))
    wide_halves = [hop(halves(below)[0], 1, 0), hop(halves(above)[1], -1, 0)]

    tall_sum = contract(lefts[1], [far_left, far_right], tall_sum, split=width)
    wide_sum = contract(lefts[4], [below, above], wide_sum)
    qkv, low = contract(lefts[2], far_halves, tall_sum, split=width, dtype=jnp.bfloat16)
    out = contract(lefts[5], wide_halves, wide_sum, low, dtype=jnp.bfloat16)
    return qkv, out


def solution(mesh):
    placed = (P("col", "row"), P("col", "row"), P("row", "col"), P("row", "col"))
    return jax.shard_map(
        body,
        mesh=mesh,
        in_specs=placed,
        out_specs=(P("row", "col"), P("row", "col")),
        check_vma=False,
    )
```

time: 169 us -> 149 us (0.88)
  local copies, waits for them, and re-layouts: 22.8 us -> 12.4 us
  Pallas kernels: 49.5 us -> 39.7 us
  starting transfers between devices: 58.9 us -> 52.1 us
  waiting for transfers between devices: 35.6 us -> 40.4 us
  other arithmetic: 0.16 us -> 2.26 us
    pallas_call x6 -> x7, Pallas kernels: 49.5 us -> 39.7 us  [the longest x6 34.6 us: contract(): pl.pallas_call(functools.partial(kernel, sizes, total is not None, cut, a...]
    ppermute x5 -> x4, waiting for transfers between devices: 0.01 us -> 8.53 us  [hop_y(): return lax.ppermute(value, 'col', pairs)]
    unnamed x42 -> x26, local copies, waits for them, and re-layouts: 14.5 us -> 7.75 us
    ppermute x28 -> x27, starting transfers between devices: 54.3 us -> 47.8 us  [hop(): return lax.ppermute(value, 'row', pairs)]
    ppermute x28 -> x27, waiting for transfers between devices: 35.6 us -> 31.9 us  [hop(): return lax.ppermute(value, 'row', pairs)]
    slice x12 -> x8, local copies, waits for them, and re-layouts: 4.79 us -> 1.41 us  [halves(): return (value[:half], value[half:])]
    ppermute x5 -> x4, starting transfers between devices: 4.55 us -> 4.32 us  [hop_y(): return lax.ppermute(value, 'col', pairs)]
  transfers between devices with their start and end apart: 33 -> 31, of which waited for: 8 -> 10; matrix products, arithmetic and copies ran while one was open for 7% -> 8% of each run, Pallas kernels for 27% -> 24%
where the time goes in v3:
time: 149 us; the launch traced here: 148 us
  starting transfers between devices  52.1 us (35%)
  waiting for transfers between devices  40.4 us (27%)
  Pallas kernels  39.7 us (27%)
  local copies, waits for them, and re-layouts  12.4 us (8%)
  other arithmetic  2.26 us (2%)
    ppermute x27, starting transfers between devices, hop(): return lax.ppermute(value, 'row', pairs)  47.8 us
    pallas_call x6, Pallas kernels, contract(): pl.pallas_call(functools.partial(kernel, sizes, total is not None, cut, a...  34.6 us
    ppermute x27, waiting for transfers between devices, hop(): return lax.ppermute(value, 'row', pairs)  31.9 us
    ppermute x4, waiting for transfers between devices, hop_y(): return lax.ppermute(value, 'col', pairs)  8.53 us
    unnamed x26, local copies, waits for them, and re-layouts  7.75 us
    pallas_call x1, Pallas kernels, arrange(): pl.pallas_call(functools.partial(arrange_kernel, groups), out_shape=[jax....  5.18 us
    ppermute x4, starting transfers between devices, hop_y(): return lax.ppermute(value, 'col', pairs)  4.32 us
  transfers between devices with their start and end apart: 31, of which 10 were waited for; matrix products, arithmetic and copies ran while one was open for 8% of the time, Pallas kernels for 24%

profile of v3, /device:TPU:8, one launch (start us, length us, event | category | flops | bytes accessed | tf_op | source)
XLA Modules:
  0.0 147.9 jit_solution(11396096991394794441)
XLA Ops:
  2.4 2.0 %collective-permute-start = (bf16[64,2560]{1,0:T(8,128)(2,1)S(1)}, bf16[64,2560]{1,0:T(8,128)(2,1)S(1)}, u32[]{:S(2)}, u32[]{:S(2)}) collective-permute-start(bf16[64,2560]{1,0:T(8,128)(2,1)S(1)} %pad_maximum_fusion.3), channel_id=1, source_target_pairs={{0,32},{8,40},{16,48},{24,56},{32,64},{40,72},{48,80},{56,88},{64,... | collective-permute-start | bytes 983048 | tf_op jit(solution)/shard_map/ppermute | solution.py:24
  4.4 4.0 %collective-permute-start.1 = (bf16[64,2560]{1,0:T(8,128)(2,1)S(1)}, bf16[64,2560]{1,0:T(8,128)(2,1)S(1)}, u32[]{:S(2)}, u32[]{:S(2)}) collective-permute-start(bf16[64,2560]{1,0:T(8,128)(2,1)S(1)} %pad_maximum_fusion.3), channel_id=1, source_target_pairs={{0,224},{8,232},{16,240},{24,248},{32,0},{40,8},{48,16},{56,24},{6... | collective-permute-start | bytes 983048 | tf_op jit(solution)/shard_map/ppermute | solution.py:24
  11.0 1.7 %collective-permute-start.3 = (bf16[64,1792]{1,0:T(8,128)(2,1)S(1)}, bf16[64,1792]{1,0:T(8,128)(2,1)S(1)}, u32[]{:S(2)}, u32[]{:S(2)}) collective-permute-start(bf16[64,1792]{1,0:T(8,128)(2,1)S(1)} %slice.31), channel_id=1, source_target_pairs={{0,24},{8,0},{16,8},{24,16},{32,56},{40,32},{48,40},{56,48},{64,88... | collective-permute-start | bytes 688136 | tf_op jit(solution)/shard_map/ppermute | solution.py:24
  12.7 1.8 %collective-permute-start.4 = (bf16[64,1792]{1,0:T(8,128)(2,1)S(1)}, bf16[64,1792]{1,0:T(8,128)(2,1)S(1)}, u32[]{:S(2)}, u32[]{:S(2)}) collective-permute-start(bf16[64,1792]{1,0:T(8,128)(2,1)S(1)} %slice.31), channel_id=1, source_target_pairs={{0,16},{8,24},{16,0},{24,8},{32,48},{40,56},{48,32},{56,40},{64,80... | collective-permute-start | bytes 688136 | tf_op jit(solution)/shard_map/ppermute | solution.py:24
  15.6 2.6 %collective-permute-done.2 = bf16[64,1792]{1,0:T(8,128)(2,1)S(1)} collective-permute-done((bf16[64,1792]{1,0:T(8,128)(2,1)S(1)}, bf16[64,1792]{1,0:T(8,128)(2,1)S(1)}, u32[]{:S(2)}, u32[]{:S(2)}) %collective-permute-start.2) | collective-permute-done | bytes 229408 | tf_op jit(solution)/shard_map/ppermute | solution.py:24
  18.2 3.7 %collective-permute-done.3 = bf16[64,1792]{1,0:T(8,128)(2,1)S(1)} collective-permute-done((bf16[64,1792]{1,0:T(8,128)(2,1)S(1)}, bf16[64,1792]{1,0:T(8,128)(2,1)S(1)}, u32[]{:S(2)}, u32[]{:S(2)}) %collective-permute-start.3) | collective-permute-done | bytes 229408 | tf_op jit(solution)/shard_map/ppermute | solution.py:24
  26.5 2.1 %collective-permute-start.14 = (bf16[192,2560]{1,0:T(8,128)(2,1)S(1)}, bf16[192,2560]{1,0:T(8,128)(2,1)S(1)}, u32[]{:S(2)}, u32[]{:S(2)}) collective-permute-start(bf16[192,2560]{1,0:T(8,128)(2,1)S(1)} %pad_maximum_fusion.refs_0_), channel_id=1, source_target_pairs={{0,24},{8,0},{16,8},{24,16},{32,56},{40,32},{48,40},{56,48},{64,88... | collective-permute-start | bytes 2949128 | tf_op jit(solution)/shard_map/ppermute | solution.py:24
  28.6 3.2 %collective-permute-start.10 = (bf16[64,2560]{1,0:T(8,128)(2,1)S(1)}, bf16[64,2560]{1,0:T(8,128)(2,1)S(1)}, u32[]{:S(2)}, u32[]{:S(2)}) collective-permute-start(bf16[64,2560]{1,0:T(8,128)(2,1)S(1)} %collective-permute-done.1), channel_id=1, source_target_pairs={{0,224},{8,232},{16,240},{24,248},{32,0},{40,8},{48,16},{56,24},{6... | collective-permute-start | bytes 983048 | tf_op jit(solution)/shard_map/ppermute | solution.py:24
  31.9 4.3 %collective-permute-done.5 = bf16[256,1024]{1,0:T(8,128)(2,1)S(1)} collective-permute-done((bf16[256,1024]{1,0:T(8,128)(2,1)S(1)}, bf16[256,1024]{1,0:T(8,128)(2,1)S(1)}, u32[]{:S(2)}, u32[]{:S(2)}) %collective-permute-start.5) | collective-permute-done | bytes 524320 | tf_op jit(solution)/shard_map/ppermute | solution.py:29
  36.1 1.7 %collective-permute-start.6 = (bf16[256,1024]{1,0:T(8,128)(2,1)S(1)}, bf16[256,1024]{1,0:T(8,128)(2,1)S(1)}, u32[]{:S(2)}, u32[]{:S(2)}) collective-permute-start(bf16[256,1024]{1,0:T(8,128)(2,1)S(1)} %pad_maximum_fusion.2), channel_id=1, source_target_pairs={{0,6},{1,7},{2,0},{3,1},{4,2},{5,3},{6,4},{7,5},{8,14},{9,15},{10,... | collective-permute-start | bytes 1572872 | tf_op jit(solution)/shard_map/ppermute | solution.py:29
  37.9 3.2 %collective-permute-start.12 = (bf16[64,2560]{1,0:T(8,128)(2,1)S(1)}, bf16[64,2560]{1,0:T(8,128)(2,1)S(1)}, u32[]{:S(2)}, u32[]{:S(2)}) collective-permute-start(bf16[64,2560]{1,0:T(8,128)(2,1)S(1)} %collective-permute-done.10), channel_id=1, source_target_pairs={{0,224},{8,232},{16,240},{24,248},{32,0},{40,8},{48,16},{56,24},{6... | collective-permute-start | bytes 983048 | tf_op jit(solution)/shard_map/ppermute | solution.py:24
  41.2 5.0 %collective-permute-done.11 = bf16[64,2560]{1,0:T(8,128)(2,1)S(1)} collective-permute-done((bf16[64,2560]{1,0:T(8,128)(2,1)S(1)}, bf16[64,2560]{1,0:T(8,128)(2,1)S(1)}, u32[]{:S(2)}, u32[]{:S(2)}) %collective-permute-start.11) | collective-permute-done | bytes 327712 | tf_op jit(solution)/shard_map/ppermute | solution.py:24
  46.2 2.4 %collective-permute-done.13.refs_1_ = bf16[192,2560]{1,0:T(8,128)(2,1)S(1)} collective-permute-done((bf16[192,2560]{1,0:T(8,128)(2,1)S(1)}, bf16[192,2560]{1,0:T(8,128)(2,1)S(1)}, u32[]{:S(2)}, u32[]{:S(2)}) %collective-permute-start.13) | collective-permute-done | bytes 983072 | tf_op jit(solution)/shard_map/ppermute | solution.py:24
  48.8 3.3 %collective-permute-start.16 = (bf16[32,2560]{1,0:T(8,128)(2,1)S(1)}, bf16[32,2560]{1,0:T(8,128)(2,1)S(1)}, u32[]{:S(2)}, u32[]{:S(2)}) collective-permute-start(bf16[32,2560]{1,0:T(8,128)(2,1)S(1)} %slice.33), channel_id=1, source_target_pairs={{0,224},{8,232},{16,240},{24,248},{32,0},{40,8},{48,16},{56,24},{6... | collective-permute-start | bytes 491528 | tf_op jit(solution)/shard_map/ppermute | solution.py:24
  52.4 3.3 %collective-permute-start.18 = (bf16[96,2560]{1,0:T(8,128)(2,1)S(1)}, bf16[96,2560]{1,0:T(8,128)(2,1)S(1)}, u32[]{:S(2)}, u32[]{:S(2)}) collective-permute-start(bf16[96,2560]{1,0:T(8,128)(2,1)S(1)} %slice.35), channel_id=1, source_target_pairs={{0,24},{8,0},{16,8},{24,16},{32,56},{40,32},{48,40},{56,48},{64,88... | collective-permute-start | bytes 1474568 | tf_op jit(solution)/shard_map/ppermute | solution.py:24
  59.2 3.2 %collective-permute-start.23 = (bf16[256,1792]{1,0:T(8,128)(2,1)S(1)}, bf16[256,1792]{1,0:T(8,128)(2,1)}, u32[]{:S(2)}, u32[]{:S(2)}) collective-permute-start(bf16[256,1792]{1,0:T(8,128)(2,1)S(1)} %pad_maximum_fusion.1.refs_0_), channel_id=1, source_target_pairs={{0,224},{8,232},{16,240},{24,248},{32,0},{40,8},{48,16},{56,24},{6... | collective-permute-start | bytes 2752520 | tf_op jit(solution)/shard_map/ppermute | solution.py:24
  64.0 4.2 %collective-permute-done.7 = bf16[256,1024]{1,0:T(8,128)(2,1)S(1)} collective-permute-done((bf16[256,1024]{1,0:T(8,128)(2,1)S(1)}, bf16[256,1024]{1,0:T(8,128)(2,1)S(1)}, u32[]{:S(2)}, u32[]{:S(2)}) %collective-permute-start.7) | collective-permute-done | bytes 524320 | tf_op jit(solution)/shard_map/ppermute | solution.py:29
  73.5 3.2 %collective-permute-start.20 = (bf16[320,2560]{1,0:T(8,128)(2,1)}, bf16[320,2560]{1,0:T(8,128)(2,1)}, u32[]{:S(2)}, u32[]{:S(2)}) collective-permute-start(bf16[320,2560]{1,0:T(8,128)(2,1)} %constant_dynamic-update-slice_fusion.4.refs_5_), channel_id=1, source_target_pairs={{0,24},{8,0},{16,8},{24,16},{32,56},{40,32},{48,40},{56,48},{64,88... | collective-permute-start | bytes 4915208 | tf_op jit(solution)/shard_map/ppermute | solution.py:24
  76.7 2.2 %collective-permute-done.21.refs_1_ = bf16[256,1792]{1,0:T(8,128)(2,1)} collective-permute-done((bf16[256,1792]{1,0:T(8,128)(2,1)S(1)}, bf16[256,1792]{1,0:T(8,128)(2,1)}, u32[]{:S(2)}, u32[]{:S(2)}) %collective-permute-start.21) | collective-permute-done | bytes 917536 | tf_op jit(solution)/shard_map/ppermute | solution.py:24
  78.9 3.2 %collective-permute-start.24 = (bf16[256,1792]{1,0:T(8,128)(2,1)}, bf16[256,1792]{1,0:T(8,128)(2,1)}, u32[]{:S(2)}, u32[]{:S(2)}) collective-permute-start(bf16[256,1792]{1,0:T(8,128)(2,1)} %collective-permute-done.23.refs_2_), channel_id=1, source_target_pairs={{0,224},{8,232},{16,240},{24,248},{32,0},{40,8},{48,16},{56,24},{6... | collective-permute-start | bytes 2752520 | tf_op jit(solution)/shard_map/ppermute | solution.py:24
  82.3 5.2 %shard_map.59 = (bf16[2,512,1088]{2,1,0:T(8,128)(2,1)S(1)}, bf16[2,512,640]{2,1,0:T(8,128)(2,1)S(1)}, bf16[2,512,320]{2,1,0:T(8,128)(2,1)S(1)}, bf16[1,512,1280]...) custom-call(s32[4]{0:T(128)S(1)} %pad_add_fusion.place_ref, ...), custom_call_target="tpu_custom_call" | custom-call | bytes 16777216 | tf_op jit(solution)/shard_map/pallas_call | solution.py:75
  87.5 8.2 %shard_map.60.refs_2_ = f32[512,2560]{1,0:T(8,128)S(1)} custom-call(bf16[2,512,1088]{2,1,0:T(8,128)(2,1)S(1)} %get-tuple-element.66.left_ref, bf16[192,2560]{1,0:T(8,128)(2,1)S(1)} %pad_maximum_fusion.refs_0_, bf16[192,2560]{1,0:T(8,128)(2,1)S(1)} %copy-done.1, bf16[192,2560]{1,0:T(8,128)(2,1)S(1)} %copy-done.3, bf16[96,2560]{1,0:T(8,128)(2,1)S(1)} %copy-done.5, ...), custom_call_target="tpu_custom_call" | custom-call | flops 2852126720 | bytes 11927552 | tf_op jit(solution)/shard_map/pallas_call | solution.py:145
  95.7 4.7 %collective-permute-done.22.refs_3_ = bf16[256,1792]{1,0:T(8,128)(2,1)} collective-permute-done((bf16[256,1792]{1,0:T(8,128)(2,1)}, bf16[256,1792]{1,0:T(8,128)(2,1)}, u32[]{:S(2)}, u32[]{:S(2)}) %collective-permute-start.22) | collective-permute-done | bytes 917536 | tf_op jit(solution)/shard_map/ppermute | solution.py:24
  100.4 3.2 %collective-permute-start.28 = (bf16[256,1792]{1,0:T(8,128)(2,1)}, bf16[256,1792]{1,0:T(8,128)(2,1)S(1)}, u32[]{:S(2)}, u32[]{:S(2)}) collective-permute-start(bf16[256,1792]{1,0:T(8,128)(2,1)} %collective-permute-done.24.refs_4_), channel_id=1, source_target_pairs={{0,224},{8,232},{16,240},{24,248},{32,0},{40,8},{48,16},{56,24},{6... | collective-permute-start | bytes 2752520 | tf_op jit(solution)/shard_map/ppermute | solution.py:24
  103.7 9.4 %collective-permute-done.19.refs_0_ = bf16[320,2560]{1,0:T(8,128)(2,1)S(1)} collective-permute-done((bf16[320,2560]{1,0:T(8,128)(2,1)}, bf16[320,2560]{1,0:T(8,128)(2,1)S(1)}, u32[]{:S(2)}, u32[]{:S(2)}) %collective-permute-start.19) | collective-permute-done | bytes 1638432 | tf_op jit(solution)/shard_map/ppermute | solution.py:24
  114.5 3.5 %collective-permute-start.26 = (bf16[160,2560]{1,0:T(8,128)(2,1)S(1)}, bf16[160,2560]{1,0:T(8,128)(2,1)S(1)}, u32[]{:S(2)}, u32[]{:S(2)}) collective-permute-start(bf16[160,2560]{1,0:T(8,128)(2,1)S(1)} %slice.37), channel_id=1, source_target_pairs={{0,24},{8,0},{16,8},{24,16},{32,56},{40,32},{48,40},{56,48},{64,88... | collective-permute-start | bytes 2457608 | tf_op jit(solution)/shard_map/ppermute | solution.py:24
  118.0 6.6 %shard_map.63.refs_2_ = f32[512,1792]{1,0:T(8,128)S(1)} custom-call(bf16[1,512,1280]{2,1,0:T(8,128)(2,1)S(1)} %get-tuple-element.78.left_ref, bf16[256,1792]{1,0:T(8,128)(2,1)S(1)} %pad_maximum_fusion.1.refs_0_, bf16[256,1792]{1,0:T(8,128)(2,1)} %collective-permute-done.21.refs_1_, bf16[256,1792]{1,0:T(8,128)(2,1)} %collective-permute-done.23.refs_2_, ...), custom_call_target="tpu_custom_call" | custom-call | flops 2348810240 | bytes 9568256 | tf_op jit(solution)/shard_map/pallas_call | solution.py:145
  124.8 3.3 %collective-permute-start.30 = (bf16[128,1792]{1,0:T(8,128)(2,1)S(1)}, bf16[128,1792]{1,0:T(8,128)(2,1)S(1)}, u32[]{:S(2)}, u32[]{:S(2)}) collective-permute-start(bf16[128,1792]{1,0:T(8,128)(2,1)S(1)} %slice.39), channel_id=1, source_target_pairs={{0,224},{8,232},{16,240},{24,248},{32,0},{40,8},{48,16},{56,24},{6... | collective-permute-start | bytes 1376264 | tf_op jit(solution)/shard_map/ppermute | solution.py:24
  128.1 7.3 %shard_map.61.refs_2_ = f32[512,2560]{1,0:T(8,128)S(1)} custom-call(bf16[2,512,640]{2,1,0:T(8,128)(2,1)S(1)} %get-tuple-element.72.left_ref, bf16[320,2560]{1,0:T(8,128)(2,1)S(1)} %collective-permute-done.19.refs_0_, bf16[320,2560]{1,0:T(8,128)(2,1)} %collective-permute-done.20.refs_1_, f32[512,2560]{1,0:T(8,128)S(1)} %shard_map.60.refs_2_), custom_call_target="tpu_custom_call" | custom-call | flops 1677721600 | bytes 9175040 | tf_op jit(solution)/shard_map/pallas_call | solution.py:145
  135.4 5.7 %shard_map.62 = (bf16[512,2304]{1,0:T(8,128)(2,1)}, bf16[512,256]{1,0:T(8,128)(2,1)S(1)}) custom-call(bf16[2,512,320]{2,1,0:T(8,128)(2,1)S(1)} %get-tuple-element.49.left_ref, bf16[160,2560]{1,0:T(8,128)(2,1)S(1)} %collective-permute-done.25.refs_0_, bf16[160,2560]{1,0:T(8,128)(2,1)S(1)} %collective-permute-done.26.refs_1_, f32[512,2560]{1,0:T(8,128)S(1)} %shard_map.61.refs_2_), custom_call_target="tpu_custom_call" | custom-call | flops 838860800 | bytes 7208960 | tf_op jit(solution)/shard_map/pallas_call | solution.py:145
  141.1 2.7 %shard_map.64.refs_2_ = f32[512,1792]{1,0:T(8,128)S(1)} custom-call(bf16[1,512,512]{2,1,0:T(8,128)(2,1)S(1)} %get-tuple-element.81.left_ref, bf16[256,1792]{1,0:T(8,128)(2,1)S(1)} %collective-permute-done.27.refs_0_, bf16[256,1792]{1,0:T(8,128)(2,1)S(1)} %collective-permute-done.28.refs_1_, f32[512,1792]{1,0:T(8,128)S(1)} %shard_map.63.refs_2_), custom_call_target="tpu_custom_call" | custom-call | flops 939524096 | bytes 6029312 | tf_op jit(solution)/shard_map/pallas_call | solution.py:145
  143.9 4.0 %shard_map.65 = bf16[512,2048]{1,0:T(8,128)(2,1)} custom-call(bf16[1,512,256]{2,1,0:T(8,128)(2,1)S(1)} %get-tuple-element.75.left_ref, bf16[128,1792]{1,0:T(8,128)(2,1)S(1)} %collective-permute-done.29.refs_0_, bf16[128,1792]{1,0:T(8,128)(2,1)S(1)} %collective-permute-done.30.refs_1_, f32[512,1792]{1,0:T(8,128)S(1)} %shard_map.64.refs_2_, ...), custom_call_target="tpu_custom_call" | custom-call | flops 469762048 | bytes 4849664 | tf_op jit(solution)/shard_map/pallas_call | solution.py:145
  (80 shorter events, 22.3 us)
Async XLA Ops:
  0.6 24.6 %copy-start.8 = (bf16[64,2304]{1,0:T(8,128)(2,1)S(1)}, bf16[64,2304]{1,0:T(8,128)(2,1)}, u32[]{:S(2)}) copy-start(bf16[64,2304]{1,0:T(8,128)(2,1)} %param.6) | copy-start | bytes 884740
  2.4 21.2 %collective-permute-start = (bf16[64,2560]{1,0:T(8,128)(2,1)S(1)}, bf16[64,2560]{1,0:T(8,128)(2,1)S(1)}, u32[]{:S(2)}, u32[]{:S(2)}) collective-permute-start(bf16[64,2560]{1,0:T(8,128)(2,1)S(1)} %pad_maximum_fusion.3), channel_id=1, source_target_pairs={{0,32},{8,40},{16,48},{24,56},{32,64},{40,72},{48,80},{56,88},{64,... | collective-permute-start | bytes 983048 | tf_op jit(solution)/shard_map/ppermute | solution.py:24
  4.4 19.2 %collective-permute-start.1 = (bf16[64,2560]{1,0:T(8,128)(2,1)S(1)}, bf16[64,2560]{1,0:T(8,128)(2,1)S(1)}, u32[]{:S(2)}, u32[]{:S(2)}) collective-permute-start(bf16[64,2560]{1,0:T(8,128)(2,1)S(1)} %pad_maximum_fusion.3), channel_id=1, source_target_pairs={{0,224},{8,232},{16,240},{24,248},{32,0},{40,8},{48,16},{56,24},{6... | collective-permute-start | bytes 983048 | tf_op jit(solution)/shard_map/ppermute | solution.py:24
  9.4 8.8 %collective-permute-start.2 = (bf16[64,1792]{1,0:T(8,128)(2,1)S(1)}, bf16[64,1792]{1,0:T(8,128)(2,1)S(1)}, u32[]{:S(2)}, u32[]{:S(2)}) collective-permute-start(bf16[64,1792]{1,0:T(8,128)(2,1)S(1)} %slice.31), channel_id=1, source_target_pairs={{0,8},{8,16},{16,24},{24,0},{32,40},{40,48},{48,56},{56,32},{64,72... | collective-permute-start | bytes 688136 | tf_op jit(solution)/shard_map/ppermute | solution.py:24
  11.0 11.0 %collective-permute-start.3 = (bf16[64,1792]{1,0:T(8,128)(2,1)S(1)}, bf16[64,1792]{1,0:T(8,128)(2,1)S(1)}, u32[]{:S(2)}, u32[]{:S(2)}) collective-permute-start(bf16[64,1792]{1,0:T(8,128)(2,1)S(1)} %slice.31), channel_id=1, source_target_pairs={{0,24},{8,0},{16,8},{24,16},{32,56},{40,32},{48,40},{56,48},{64,88... | collective-permute-start | bytes 688136 | tf_op jit(solution)/shard_map/ppermute | solution.py:24
  12.7 10.9 %collective-permute-start.4 = (bf16[64,1792]{1,0:T(8,128)(2,1)S(1)}, bf16[64,1792]{1,0:T(8,128)(2,1)S(1)}, u32[]{:S(2)}, u32[]{:S(2)}) collective-permute-start(bf16[64,1792]{1,0:T(8,128)(2,1)S(1)} %slice.31), channel_id=1, source_target_pairs={{0,16},{8,24},{16,0},{24,8},{32,48},{40,56},{48,32},{56,40},{64,80... | collective-permute-start | bytes 688136 | tf_op jit(solution)/shard_map/ppermute | solution.py:24
  23.7 12.5 %collective-permute-start.5 = (bf16[256,1024]{1,0:T(8,128)(2,1)S(1)}, bf16[256,1024]{1,0:T(8,128)(2,1)S(1)}, u32[]{:S(2)}, u32[]{:S(2)}) collective-permute-start(bf16[256,1024]{1,0:T(8,128)(2,1)S(1)} %pad_maximum_fusion.2), channel_id=1, source_target_pairs={{0,2},{1,3},{2,4},{3,5},{4,6},{5,7},{6,0},{7,1},{8,10},{9,11},{10,... | collective-permute-start | bytes 1572872 | tf_op jit(solution)/shard_map/ppermute | solution.py:29
  25.3 23.3 %collective-permute-start.13 = (bf16[192,2560]{1,0:T(8,128)(2,1)S(1)}, bf16[192,2560]{1,0:T(8,128)(2,1)S(1)}, u32[]{:S(2)}, u32[]{:S(2)}) collective-permute-start(bf16[192,2560]{1,0:T(8,128)(2,1)S(1)} %pad_maximum_fusion.refs_0_), channel_id=1, source_target_pairs={{0,8},{8,16},{16,24},{24,0},{32,40},{40,48},{48,56},{56,32},{64,72... | collective-permute-start | bytes 2949128 | tf_op jit(solution)/shard_map/ppermute | solution.py:24
  26.5 22.1 %collective-permute-start.14 = (bf16[192,2560]{1,0:T(8,128)(2,1)S(1)}, bf16[192,2560]{1,0:T(8,128)(2,1)S(1)}, u32[]{:S(2)}, u32[]{:S(2)}) collective-permute-start(bf16[192,2560]{1,0:T(8,128)(2,1)S(1)} %pad_maximum_fusion.refs_0_), channel_id=1, source_target_pairs={{0,24},{8,0},{16,8},{24,16},{32,56},{40,32},{48,40},{56,48},{64,88... | collective-permute-start | bytes 2949128 | tf_op jit(solution)/shard_map/ppermute | solution.py:24
  28.6 9.2 %collective-permute-start.9 = (bf16[64,2560]{1,0:T(8,128)(2,1)S(1)}, bf16[64,2560]{1,0:T(8,128)(2,1)S(1)}, u32[]{:S(2)}, u32[]{:S(2)}) collective-permute-start(bf16[64,2560]{1,0:T(8,128)(2,1)S(1)} %collective-permute-done), channel_id=1, source_target_pairs={{0,32},{8,40},{16,48},{24,56},{32,64},{40,72},{48,80},{56,88},{64,... | collective-permute-start | bytes 983048 | tf_op jit(solution)/shard_map/ppermute | solution.py:24
  28.6 9.2 %collective-permute-start.10 = (bf16[64,2560]{1,0:T(8,128)(2,1)S(1)}, bf16[64,2560]{1,0:T(8,128)(2,1)S(1)}, u32[]{:S(2)}, u32[]{:S(2)}) collective-permute-start(bf16[64,2560]{1,0:T(8,128)(2,1)S(1)} %collective-permute-done.1), channel_id=1, source_target_pairs={{0,224},{8,232},{16,240},{24,248},{32,0},{40,8},{48,16},{56,24},{6... | collective-permute-start | bytes 983048 | tf_op jit(solution)/shard_map/ppermute | solution.py:24
  36.1 19.6 %collective-permute-start.6 = (bf16[256,1024]{1,0:T(8,128)(2,1)S(1)}, bf16[256,1024]{1,0:T(8,128)(2,1)S(1)}, u32[]{:S(2)}, u32[]{:S(2)}) collective-permute-start(bf16[256,1024]{1,0:T(8,128)(2,1)S(1)} %pad_maximum_fusion.2), channel_id=1, source_target_pairs={{0,6},{1,7},{2,0},{3,1},{4,2},{5,3},{6,4},{7,5},{8,14},{9,15},{10,... | collective-permute-start | bytes 1572872 | tf_op jit(solution)/shard_map/ppermute | solution.py:29
  37.9 8.3 %collective-permute-start.11 = (bf16[64,2560]{1,0:T(8,128)(2,1)S(1)}, bf16[64,2560]{1,0:T(8,128)(2,1)S(1)}, u32[]{:S(2)}, u32[]{:S(2)}) collective-permute-start(bf16[64,2560]{1,0:T(8,128)(2,1)S(1)} %collective-permute-done.9), channel_id=1, source_target_pairs={{0,32},{8,40},{16,48},{24,56},{32,64},{40,72},{48,80},{56,88},{64,... | collective-permute-start | bytes 983048 | tf_op jit(solution)/shard_map/ppermute | solution.py:24
  37.9 8.3 %collective-permute-start.12 = (bf16[64,2560]{1,0:T(8,128)(2,1)S(1)}, bf16[64,2560]{1,0:T(8,128)(2,1)S(1)}, u32[]{:S(2)}, u32[]{:S(2)}) collective-permute-start(bf16[64,2560]{1,0:T(8,128)(2,1)S(1)} %collective-permute-done.10), channel_id=1, source_target_pairs={{0,224},{8,232},{16,240},{24,248},{32,0},{40,8},{48,16},{56,24},{6... | collective-permute-start | bytes 983048 | tf_op jit(solution)/shard_map/ppermute | solution.py:24
  48.7 10.6 %collective-permute-start.15 = (bf16[32,2560]{1,0:T(8,128)(2,1)S(1)}, bf16[32,2560]{1,0:T(8,128)(2,1)S(1)}, u32[]{:S(2)}, u32[]{:S(2)}) collective-permute-start(bf16[32,2560]{1,0:T(8,128)(2,1)S(1)} %slice.32), channel_id=1, source_target_pairs={{0,32},{8,40},{16,48},{24,56},{32,64},{40,72},{48,80},{56,88},{64,... | collective-permute-start | bytes 491528 | tf_op jit(solution)/shard_map/ppermute | solution.py:24
  48.8 10.5 %collective-permute-start.16 = (bf16[32,2560]{1,0:T(8,128)(2,1)S(1)}, bf16[32,2560]{1,0:T(8,128)(2,1)S(1)}, u32[]{:S(2)}, u32[]{:S(2)}) collective-permute-start(bf16[32,2560]{1,0:T(8,128)(2,1)S(1)} %slice.33), channel_id=1, source_target_pairs={{0,224},{8,232},{16,240},{24,248},{32,0},{40,8},{48,16},{56,24},{6... | collective-permute-start | bytes 491528 | tf_op jit(solution)/shard_map/ppermute | solution.py:24
  52.1 19.8 %collective-permute-start.17 = (bf16[96,2560]{1,0:T(8,128)(2,1)S(1)}, bf16[96,2560]{1,0:T(8,128)(2,1)S(1)}, u32[]{:S(2)}, u32[]{:S(2)}) collective-permute-start(bf16[96,2560]{1,0:T(8,128)(2,1)S(1)} %slice.34), channel_id=1, source_target_pairs={{0,8},{8,16},{16,24},{24,0},{32,40},{40,48},{48,56},{56,32},{64,72... | collective-permute-start | bytes 1474568 | tf_op jit(solution)/shard_map/ppermute | solution.py:24
  52.4 20.2 %collective-permute-start.18 = (bf16[96,2560]{1,0:T(8,128)(2,1)S(1)}, bf16[96,2560]{1,0:T(8,128)(2,1)S(1)}, u32[]{:S(2)}, u32[]{:S(2)}) collective-permute-start(bf16[96,2560]{1,0:T(8,128)(2,1)S(1)} %slice.35), channel_id=1, source_target_pairs={{0,24},{8,0},{16,8},{24,16},{32,56},{40,32},{48,40},{56,48},{64,88... | collective-permute-start | bytes 1474568 | tf_op jit(solution)/shard_map/ppermute | solution.py:24
  56.5 11.7 %collective-permute-start.7 = (bf16[256,1024]{1,0:T(8,128)(2,1)S(1)}, bf16[256,1024]{1,0:T(8,128)(2,1)S(1)}, u32[]{:S(2)}, u32[]{:S(2)}) collective-permute-start(bf16[256,1024]{1,0:T(8,128)(2,1)S(1)} %pad_maximum_fusion.2), channel_id=1, source_target_pairs={{0,4},{1,5},{2,6},{3,7},{4,0},{5,1},{6,2},{7,3},{8,12},{9,13},{10,... | collective-permute-start | bytes 1572872 | tf_op jit(solution)/shard_map/ppermute | solution.py:29
  59.2 19.7 %collective-permute-start.21 = (bf16[256,1792]{1,0:T(8,128)(2,1)S(1)}, bf16[256,1792]{1,0:T(8,128)(2,1)}, u32[]{:S(2)}, u32[]{:S(2)}) collective-permute-start(bf16[256,1792]{1,0:T(8,128)(2,1)S(1)} %pad_maximum_fusion.1.refs_0_), channel_id=1, source_target_pairs={{0,32},{8,40},{16,48},{24,56},{32,64},{40,72},{48,80},{56,88},{64,... | collective-permute-start | bytes 2752520 | tf_op jit(solution)/shard_map/ppermute | solution.py:24
  59.2 19.7 %collective-permute-start.23 = (bf16[256,1792]{1,0:T(8,128)(2,1)S(1)}, bf16[256,1792]{1,0:T(8,128)(2,1)}, u32[]{:S(2)}, u32[]{:S(2)}) collective-permute-start(bf16[256,1792]{1,0:T(8,128)(2,1)S(1)} %pad_maximum_fusion.1.refs_0_), channel_id=1, source_target_pairs={{0,224},{8,232},{16,240},{24,248},{32,0},{40,8},{48,16},{56,24},{6... | collective-permute-start | bytes 2752520 | tf_op jit(solution)/shard_map/ppermute | solution.py:24
  69.0 13.2 %collective-permute-start.8 = (bf16[1024,1024]{1,0:T(8,128)(2,1)}, bf16[1024,1024]{1,0:T(8,128)(2,1)}, u32[]{:S(2)}, u32[]{:S(2)}) collective-permute-start(bf16[1024,1024]{1,0:T(8,128)(2,1)} %constant_dynamic-update-slice_fusion.mine_ref), channel_id=1, source_target_pairs={{0,1},{1,0},{2,3},{3,2},{4,5},{5,4},{6,7},{7,6},{8,9},{9,8},{10,11... | collective-permute-start | bytes 6291464 | tf_op jit(solution)/shard_map/ppermute | solution.py:29
  73.5 39.6 %collective-permute-start.19 = (bf16[320,2560]{1,0:T(8,128)(2,1)}, bf16[320,2560]{1,0:T(8,128)(2,1)S(1)}, u32[]{:S(2)}, u32[]{:S(2)}) collective-permute-start(bf16[320,2560]{1,0:T(8,128)(2,1)} %constant_dynamic-update-slice_fusion.4.refs_5_), channel_id=1, source_target_pairs={{0,8},{8,16},{16,24},{24,0},{32,40},{40,48},{48,56},{56,32},{64,72... | collective-permute-start | bytes 4915208 | tf_op jit(solution)/shard_map/ppermute | solution.py:24
  73.5 39.6 %collective-permute-start.20 = (bf16[320,2560]{1,0:T(8,128)(2,1)}, bf16[320,2560]{1,0:T(8,128)(2,1)}, u32[]{:S(2)}, u32[]{:S(2)}) collective-permute-start(bf16[320,2560]{1,0:T(8,128)(2,1)} %constant_dynamic-update-slice_fusion.4.refs_5_), channel_id=1, source_target_pairs={{0,24},{8,0},{16,8},{24,16},{32,56},{40,32},{48,40},{56,48},{64,88... | collective-permute-start | bytes 4915208 | tf_op jit(solution)/shard_map/ppermute | solution.py:24
  78.9 21.5 %collective-permute-start.22 = (bf16[256,1792]{1,0:T(8,128)(2,1)}, bf16[256,1792]{1,0:T(8,128)(2,1)}, u32[]{:S(2)}, u32[]{:S(2)}) collective-permute-start(bf16[256,1792]{1,0:T(8,128)(2,1)} %collective-permute-done.21.refs_1_), channel_id=1, source_target_pairs={{0,32},{8,40},{16,48},{24,56},{32,64},{40,72},{48,80},{56,88},{64,... | collective-permute-start | bytes 2752520 | tf_op jit(solution)/shard_map/ppermute | solution.py:24
  78.9 21.5 %collective-permute-start.24 = (bf16[256,1792]{1,0:T(8,128)(2,1)}, bf16[256,1792]{1,0:T(8,128)(2,1)}, u32[]{:S(2)}, u32[]{:S(2)}) collective-permute-start(bf16[256,1792]{1,0:T(8,128)(2,1)} %collective-permute-done.23.refs_2_), channel_id=1, source_target_pairs={{0,224},{8,232},{16,240},{24,248},{32,0},{40,8},{48,16},{56,24},{6... | collective-permute-start | bytes 2752520 | tf_op jit(solution)/shard_map/ppermute | solution.py:24
  100.4 24.2 %collective-permute-start.27 = (bf16[256,1792]{1,0:T(8,128)(2,1)}, bf16[256,1792]{1,0:T(8,128)(2,1)S(1)}, u32[]{:S(2)}, u32[]{:S(2)}) collective-permute-start(bf16[256,1792]{1,0:T(8,128)(2,1)} %collective-permute-done.22.refs_3_), channel_id=1, source_target_pairs={{0,32},{8,40},{16,48},{24,56},{32,64},{40,72},{48,80},{56,88},{64,... | collective-permute-start | bytes 2752520 | tf_op jit(solution)/shard_map/ppermute | solution.py:24
  100.4 24.2 %collective-permute-start.28 = (bf16[256,1792]{1,0:T(8,128)(2,1)}, bf16[256,1792]{1,0:T(8,128)(2,1)S(1)}, u32[]{:S(2)}, u32[]{:S(2)}) collective-permute-start(bf16[256,1792]{1,0:T(8,128)(2,1)} %collective-permute-done.24.refs_4_), channel_id=1, source_target_pairs={{0,224},{8,232},{16,240},{24,248},{32,0},{40,8},{48,16},{56,24},{6... | collective-permute-start | bytes 2752520 | tf_op jit(solution)/shard_map/ppermute | solution.py:24
  113.2 22.2 %collective-permute-start.25 = (bf16[160,2560]{1,0:T(8,128)(2,1)S(1)}, bf16[160,2560]{1,0:T(8,128)(2,1)S(1)}, u32[]{:S(2)}, u32[]{:S(2)}) collective-permute-start(bf16[160,2560]{1,0:T(8,128)(2,1)S(1)} %slice.36), channel_id=1, source_target_pairs={{0,8},{8,16},{16,24},{24,0},{32,40},{40,48},{48,56},{56,32},{64,72... | collective-permute-start | bytes 2457608 | tf_op jit(solution)/shard_map/ppermute | solution.py:24
  114.5 20.9 %collective-permute-start.26 = (bf16[160,2560]{1,0:T(8,128)(2,1)S(1)}, bf16[160,2560]{1,0:T(8,128)(2,1)S(1)}, u32[]{:S(2)}, u32[]{:S(2)}) collective-permute-start(bf16[160,2560]{1,0:T(8,128)(2,1)S(1)} %slice.37), channel_id=1, source_target_pairs={{0,24},{8,0},{16,8},{24,16},{32,56},{40,32},{48,40},{56,48},{64,88... | collective-permute-start | bytes 2457608 | tf_op jit(solution)/shard_map/ppermute | solution.py:24
  124.7 19.2 %collective-permute-start.29 = (bf16[128,1792]{1,0:T(8,128)(2,1)S(1)}, bf16[128,1792]{1,0:T(8,128)(2,1)S(1)}, u32[]{:S(2)}, u32[]{:S(2)}) collective-permute-start(bf16[128,1792]{1,0:T(8,128)(2,1)S(1)} %slice.38), channel_id=1, source_target_pairs={{0,32},{8,40},{16,48},{24,56},{32,64},{40,72},{48,80},{56,88},{64,... | collective-permute-start | bytes 1376264 | tf_op jit(solution)/shard_map/ppermute | solution.py:24
  124.8 19.0 %collective-permute-start.30 = (bf16[128,1792]{1,0:T(8,128)(2,1)S(1)}, bf16[128,1792]{1,0:T(8,128)(2,1)S(1)}, u32[]{:S(2)}, u32[]{:S(2)}) collective-permute-start(bf16[128,1792]{1,0:T(8,128)(2,1)S(1)} %slice.39), channel_id=1, source_target_pairs={{0,224},{8,232},{16,240},{24,248},{32,0},{40,8},{48,16},{56,24},{6... | collective-permute-start | bytes 1376264 | tf_op jit(solution)/shard_map/ppermute | solution.py:24
  (8 other events, 38.3 us)

commit v4 on v0

v4 whole, which is shorter than its diff:
```python
import functools

import jax
import jax.numpy as jnp
from jax import lax
from jax.experimental import pallas as pl
from jax.experimental.pallas import tpu as pltpu
from jax.sharding import PartitionSpec as P

Z, X, Y, C = 8, 4, 4, 2
BLOCK = 64
FEATURES = 512

X_ORDER = (0, -1, 1, 2)
NEAR, FAR = (0, -1, 1), (-2, 2, -3, 3, 4)


def hop(value, dz, dx):
    pairs = [
        (z * X + x, ((z + dz) % Z) * X + (x + dx) % X) for z in range(Z) for x in range(X)
    ]
    return lax.ppermute(value, "row", pairs)


def hop_y(value, dy, swap=0):
    pairs = [(y * C + c, ((y + dy) % Y) * C + (c ^ swap)) for y in range(Y) for c in range(C)]
    return lax.ppermute(value, "col", pairs)


def halves(value):
    half = value.shape[0] // 2
    return value[:half], value[half:]


def arrange_kernel(groups, place_ref, mine_ref, other_ref, *refs):
    outs, (left, sems) = refs[: len(groups)], refs[len(groups) :]
    z, x, y, core = (place_ref[i] for i in range(4))
    at, copies = 0, []
    for rows, op in groups:
        for dz, dx, start, size in rows:
            group = lax.rem(z + (dz + Z), Z)
            away = lax.rem(group // C + Y - y, Y)
            slot = jnp.where(away == 0, 0, jnp.where(away == Y - 1, 1, jnp.where(away == 1, 2, 3)))
            row = slot * (X * BLOCK) + lax.rem(x + (dx + X), X) * BLOCK + start
            source = (pl.ds(pl.multiple_of(row, 32), size), pl.ds(op * FEATURES, FEATURES))
            target = left.at[pl.ds(at, size)]
            swapped, sem = lax.rem(group, C) != core, sems.at[len(copies)]

            @pl.when(swapped)
            def _():
                pltpu.make_async_copy(other_ref.at[source], target, sem).start()

            @pl.when(jnp.logical_not(swapped))
            def _():
                pltpu.make_async_copy(mine_ref.at[source], target, sem).start()

            copies.append(pltpu.make_async_copy(target, target, sem))
            at += size
    at = 0
    for (rows, _), out in zip(groups, outs):
        size = depth_of(rows)
        for _ in rows:
            copies.pop(0).wait()
        out[...] = left[at : at + size].T
        at += size


def arrange(place, operand, groups):
    anywhere = pl.BlockSpec(memory_space=pl.ANY)
    depth = sum(depth_of(rows) for rows, _ in groups)
    return pl.pallas_call(
        functools.partial(arrange_kernel, groups),
        out_shape=[
            jax.ShapeDtypeStruct((FEATURES, depth_of(rows)), jnp.bfloat16) for rows, _ in groups
        ],
        in_specs=[pl.BlockSpec(memory_space=pltpu.SMEM), anywhere, anywhere],
        out_specs=[pl.BlockSpec(memory_space=pltpu.VMEM)] * len(groups),
        scratch_shapes=[
            pltpu.VMEM((depth, FEATURES), jnp.bfloat16),
            pltpu.SemaphoreType.DMA((sum(len(rows) for rows, _ in groups),)),
        ],
        compiler_params=pltpu.CompilerParams(vmem_limit_bytes=16 << 20),
        cost_estimate=pl.CostEstimate(flops=0, bytes_accessed=12 << 20, transcendentals=0),
    )(place, *operand)


def contract(left, grads, total=None, dtype=jnp.float32):
    part = jnp.dot(left, jnp.concatenate(grads), preferred_element_type=jnp.float32)
    if total is not None:
        part += total
    return part.astype(dtype)


def depth_of(rows):
    return sum(row[3] for row in rows)


def whole(dzs, dx):
    return [(dz, dx, 0, BLOCK) for dz in dzs]


def parts(rows):
    half, first, second = depth_of(rows) // 2, [], []
    for dz, dx, start, size in rows:
        here = min(size, half)
        if here:
            first.append((dz, dx, start, here))
        if here < size:
            second.append((dz, dx, start + here, size - here))
        half -= here
    return first, second


def body(normed_input, attended, qkv_grad, proj_grad):
    together = lax.optimization_barrier
    row, col = lax.axis_index("row"), lax.axis_index("col")
    place = jnp.stack([row // X, row % X, col // C, col % C])

    tall, wide = qkv_grad, proj_grad
    mine = jnp.concatenate([normed_input, attended], axis=1)

    below, above = hop(tall, 1, 0), hop(tall, -1, 0)
    left, right = hop(wide, 0, 1), hop(wide, 0, -1)
    down = hop_y(mine, 1)
    below, above, left, right = together((below, above, left, right))
    opposite = hop(wide, 0, 2)
    near = jnp.concatenate([tall, below, above])
    near, opposite = together((near, opposite))
    near_left, near_right = hop(near, 0, 1), hop(near, 0, -1)
    below, above = hop(below, 1, 0), hop(above, -1, 0)
    below, above, opposite, down = together((below, above, opposite, down))
    far = [below, above]
    below, above = hop(below, 1, 0), hop(above, -1, 0)
    far = jnp.concatenate([*far, below, above])
    mine, down = together((mine, down))
    up = hop_y(mine, -1)
    below, above, near_left, near_right, far, up = together(
        (below, above, near_left, near_right, far, up)
    )
    mine, up = together((mine, up))
    across = hop_y(mine, 2)
    far = [far, hop(halves(below)[0], 1, 0), hop(halves(above)[1], -1, 0)]
    near_halves = [hop(halves(near_left)[0], 0, 1), hop(halves(near_right)[1], 0, -1)]
    wide = jnp.concatenate([wide, left, right, opposite])
    far, wide = together((far, wide))
    far = jnp.concatenate(far)
    far, near_halves, across = together((far, near_halves, across))
    far_left, far_right = hop(far, 0, 1), hop(far, 0, -1)
    below, above = hop(wide, 1, 0), hop(wide, -1, 0)
    wide_first = [wide, below, above]
    mine = jnp.concatenate([mine, down, up, across])

    near_rows = {dx: whole(NEAR, dx) for dx in X_ORDER}
    far_rows = {dx: whole(FAR, dx) for dx in X_ORDER}
    near_split, far_split = parts(near_rows[2]), parts(far_rows[2])
    wide_rows = {dz: [(dz, dx, 0, BLOCK) for dx in X_ORDER] for dz in range(-4, 5)}
    wide_split = parts(wide_rows[4])
    groups = [
        (sum([near_rows[0], near_rows[-1], near_rows[1], *near_split, far_rows[0]], []), 0),
        (far_rows[-1] + far_rows[1], 0),
        (far_split[0] + far_split[1], 0),
        (sum([wide_rows[d] for d in (0, -1, 1, -2, 2)], []), 1),
        (wide_rows[-3] + wide_rows[3], 1),
        (wide_split[0] + wide_split[1], 1),
    ]
    lefts = arrange(place, (mine, hop_y(mine, 0, 1)), groups)
    tall_sum = contract(lefts[0], [near, near_left, near_right, *near_halves, far])

    below, above = hop(below, 1, 0), hop(above, -1, 0)
    wide_first += [below, above]
    below, above, far_left, far_right, tall_sum = together(
        (below, above, far_left, far_right, tall_sum)
    )
    wide_sum = contract(lefts[3], wide_first)
    below, above = hop(below, 1, 0), hop(above, -1, 0)
    far_halves = [hop(halves(far_left)[0], 0, 1), hop(halves(far_right)[1], 0, -1)]
    below, above, wide_sum = together((below, above, wide_sum))
    wide_halves = [hop(halves(below)[0], 1, 0), hop(halves(above)[1], -1, 0)]

    tall_sum = contract(lefts[1], [far_left, far_right], tall_sum)
    wide_sum = contract(lefts[4], [below, above], wide_sum)
    qkv = contract(lefts[2], far_halves, tall_sum, dtype=jnp.bfloat16)
    out = contract(lefts[5], wide_halves, wide_sum, dtype=jnp.bfloat16)
    return qkv, out


def solution(mesh):
    placed = (P("col", "row"), P("col", "row"), P("row", "col"), P("row", "col"))
    return jax.shard_map(
        body,
        mesh=mesh,
        in_specs=placed,
        out_specs=(P("row", "col"), P("row", "col")),
        check_vma=False,
    )
```

time: 292 us -> 146 us (0.50)
  waiting for transfers between devices: 257 us -> 61.9 us
  starting transfers between devices: 0.15 us -> 52.6 us
  between operations: 13.8 us -> 0.95 us
  local copies, waits for them, and re-layouts: 0 us -> 5.82 us
  matrix products: 20.2 us -> 15.6 us
  Pallas kernels: 0 us -> 4.22 us
  other arithmetic: 0 us -> 3.42 us
    all_gather x4 -> x0, waiting for transfers between devices: 255 us -> none  [the longest x1 107 us: body(): lax.all_gather(qkv_grad, 'row', axis=0, tiled=True)]
    ppermute x0 -> x31, waiting for transfers between devices: none -> 61.9 us  [the longest x27 56.1 us: hop(): return lax.ppermute(value, 'row', pairs)]
    ppermute x0 -> x31, starting transfers between devices: none -> 52.6 us  [the longest x27 48.1 us: hop(): return lax.ppermute(value, 'row', pairs)]
    dot_general x2 -> x6, matrix products: 20.2 us -> 15.6 us  [contract(): jnp.dot(left, jnp.concatenate(grads), preferred_element_type=jnp.float32)]
    pallas_call x0 -> x1, Pallas kernels: none -> 4.22 us  [arrange(): pl.pallas_call(functools.partial(arrange_kernel, groups), out_shape=[jax....]
  transfers between devices with their start and end apart: 4 -> 31, of which waited for: 4 -> 12; matrix products, arithmetic and copies ran while one was open for 3% -> 14% of each run, Pallas kernels for 0% -> 3%
where the time goes in v4:
time: 146 us; the launch traced here: 144 us
  waiting for transfers between devices  61.9 us (42%)
  starting transfers between devices  52.6 us (36%)
  matrix products  15.6 us (11%)
  local copies, waits for them, and re-layouts  5.82 us (4%)
  Pallas kernels  4.22 us (3%)
  other arithmetic  3.42 us (2%)
    ppermute x27, waiting for transfers between devices, hop(): return lax.ppermute(value, 'row', pairs)  56.1 us
    ppermute x27, starting transfers between devices, hop(): return lax.ppermute(value, 'row', pairs)  48.1 us
    dot_general x6, matrix products, contract(): jnp.dot(left, jnp.concatenate(grads), preferred_element_type=jnp.float32)  15.6 us
    ppermute x4, waiting for transfers between devices, hop_y(): return lax.ppermute(value, 'col', pairs)  5.8 us
    ppermute x4, starting transfers between devices, hop_y(): return lax.ppermute(value, 'col', pairs)  4.57 us
    pallas_call x1, Pallas kernels, arrange(): pl.pallas_call(functools.partial(arrange_kernel, groups), out_shape=[jax....  4.22 us
  transfers between devices with their start and end apart: 31, of which 12 were waited for; matrix products, arithmetic and copies ran while one was open for 14% of the time, Pallas kernels for 3%

profile of v4, /device:TPU:8, one launch (start us, length us, event | category | flops | bytes accessed | tf_op | source)
XLA Modules:
  0.0 144.5 jit_solution(8897057560244108114)
XLA Ops:
  0.6 2.0 %collective-permute-start = (bf16[64,2304]{1,0:T(8,128)(2,1)}, bf16[64,2304]{1,0:T(8,128)(2,1)S(1)}, u32[]{:S(2)}, u32[]{:S(2)}) collective-permute-start(bf16[64,2304]{1,0:T(8,128)(2,1)} %param.6), channel_id=1, source_target_pairs={{0,32},{8,40},{16,48},{24,56},{32,64},{40,72},{48,80},{56,88},{64,... | collective-permute-start | bytes 884744 | tf_op jit(solution)/shard_map/ppermute | solution.py:22
  2.6 4.0 %collective-permute-start.1 = (bf16[64,2304]{1,0:T(8,128)(2,1)}, bf16[64,2304]{1,0:T(8,128)(2,1)S(1)}, u32[]{:S(2)}, u32[]{:S(2)}) collective-permute-start(bf16[64,2304]{1,0:T(8,128)(2,1)} %param.6), channel_id=1, source_target_pairs={{0,224},{8,232},{16,240},{24,248},{32,0},{40,8},{48,16},{56,24},{6... | collective-permute-start | bytes 884744 | tf_op jit(solution)/shard_map/ppermute | solution.py:22
  13.6 2.3 %collective-permute-done.2 = bf16[64,2048]{1,0:T(8,128)(2,1)S(1)} collective-permute-done((bf16[64,2048]{1,0:T(8,128)(2,1)}, bf16[64,2048]{1,0:T(8,128)(2,1)S(1)}, u32[]{:S(2)}, u32[]{:S(2)}) %collective-permute-start.2) | collective-permute-done | bytes 262176 | tf_op jit(solution)/shard_map/ppermute | solution.py:22
  15.9 1.8 %collective-permute-start.6 = (bf16[64,2048]{1,0:T(8,128)(2,1)}, bf16[64,2048]{1,0:T(8,128)(2,1)S(1)}, u32[]{:S(2)}, u32[]{:S(2)}) collective-permute-start(bf16[64,2048]{1,0:T(8,128)(2,1)} %param.7), channel_id=1, source_target_pairs={{0,16},{8,24},{16,0},{24,8},{32,48},{40,56},{48,32},{56,40},{64,80... | collective-permute-start | bytes 786440 | tf_op jit(solution)/shard_map/ppermute | solution.py:22
  17.8 3.2 %collective-permute-start.5 = (bf16[64,2304]{1,0:T(8,128)(2,1)S(1)}, bf16[64,2304]{1,0:T(8,128)(2,1)S(1)}, u32[]{:S(2)}, u32[]{:S(2)}) collective-permute-start(bf16[64,2304]{1,0:T(8,128)(2,1)S(1)} %collective-permute-done.1), channel_id=1, source_target_pairs={{0,224},{8,232},{16,240},{24,248},{32,0},{40,8},{48,16},{56,24},{6... | collective-permute-start | bytes 884744 | tf_op jit(solution)/shard_map/ppermute | solution.py:22
  22.0 2.4 %collective-permute-done.6 = bf16[64,2048]{1,0:T(8,128)(2,1)S(1)} collective-permute-done((bf16[64,2048]{1,0:T(8,128)(2,1)}, bf16[64,2048]{1,0:T(8,128)(2,1)S(1)}, u32[]{:S(2)}, u32[]{:S(2)}) %collective-permute-start.6) | collective-permute-done | bytes 262176 | tf_op jit(solution)/shard_map/ppermute | solution.py:22
  24.7 3.0 %collective-permute-start.11 = (bf16[192,2304]{1,0:T(8,128)(2,1)S(1)}, bf16[192,2304]{1,0:T(8,128)(2,1)S(1)}, u32[]{:S(2)}, u32[]{:S(2)}) collective-permute-start(bf16[192,2304]{1,0:T(8,128)(2,1)S(1)} %pad_maximum_fusion.3), channel_id=1, source_target_pairs={{0,24},{8,0},{16,8},{24,16},{32,56},{40,32},{48,40},{56,48},{64,88... | collective-permute-start | bytes 2654216 | tf_op jit(solution)/shard_map/ppermute | solution.py:22
  27.8 3.2 %collective-permute-start.9 = (bf16[64,2304]{1,0:T(8,128)(2,1)S(1)}, bf16[64,2304]{1,0:T(8,128)(2,1)S(1)}, u32[]{:S(2)}, u32[]{:S(2)}) collective-permute-start(bf16[64,2304]{1,0:T(8,128)(2,1)S(1)} %collective-permute-done.5), channel_id=1, source_target_pairs={{0,224},{8,232},{16,240},{24,248},{32,0},{40,8},{48,16},{56,24},{6... | collective-permute-start | bytes 884744 | tf_op jit(solution)/shard_map/ppermute | solution.py:22
  31.7 4.0 %collective-permute-done.8 = bf16[64,2304]{1,0:T(8,128)(2,1)S(1)} collective-permute-done((bf16[64,2304]{1,0:T(8,128)(2,1)S(1)}, bf16[64,2304]{1,0:T(8,128)(2,1)S(1)}, u32[]{:S(2)}, u32[]{:S(2)}) %collective-permute-start.8) | collective-permute-done | bytes 294944 | tf_op jit(solution)/shard_map/ppermute | solution.py:22
  35.8 5.8 %collective-permute-done.12 = bf16[256,1024]{1,0:T(8,128)(2,1)S(1)} collective-permute-done((bf16[256,1024]{1,0:T(8,128)(2,1)S(1)}, bf16[256,1024]{1,0:T(8,128)(2,1)S(1)}, u32[]{:S(2)}, u32[]{:S(2)}) %collective-permute-start.12) | collective-permute-done | bytes 524320 | tf_op jit(solution)/shard_map/ppermute | solution.py:27
  41.6 3.4 %collective-permute-done.10 = bf16[192,2304]{1,0:T(8,128)(2,1)S(1)} collective-permute-done((bf16[192,2304]{1,0:T(8,128)(2,1)S(1)}, bf16[192,2304]{1,0:T(8,128)(2,1)S(1)}, u32[]{:S(2)}, u32[]{:S(2)}) %collective-permute-start.10) | collective-permute-done | bytes 884768 | tf_op jit(solution)/shard_map/ppermute | solution.py:22
  44.9 2.3 %collective-permute-start.17 = (bf16[256,1024]{1,0:T(8,128)(2,1)S(1)}, bf16[256,1024]{1,0:T(8,128)(2,1)S(1)}, u32[]{:S(2)}, u32[]{:S(2)}) collective-permute-start(bf16[256,1024]{1,0:T(8,128)(2,1)S(1)} %constant_dynamic-update-slice_fusion), channel_id=1, source_target_pairs={{0,4},{1,5},{2,6},{3,7},{4,0},{5,1},{6,2},{7,3},{8,12},{9,13},{10,... | collective-permute-start | bytes 1572872 | tf_op jit(solution)/shard_map/ppermute | solution.py:27
  47.4 3.5 %collective-permute-start.14 = (bf16[32,2304]{1,0:T(8,128)(2,1)S(1)}, bf16[32,2304]{1,0:T(8,128)(2,1)S(1)}, u32[]{:S(2)}, u32[]{:S(2)}) collective-permute-start(bf16[32,2304]{1,0:T(8,128)(2,1)S(1)} %slice.25), channel_id=1, source_target_pairs={{0,224},{8,232},{16,240},{24,248},{32,0},{40,8},{48,16},{56,24},{6... | collective-permute-start | bytes 442376 | tf_op jit(solution)/shard_map/ppermute | solution.py:22
  51.3 3.0 %collective-permute-start.16 = (bf16[96,2304]{1,0:T(8,128)(2,1)S(1)}, bf16[96,2304]{1,0:T(8,128)(2,1)S(1)}, u32[]{:S(2)}, u32[]{:S(2)}) collective-permute-start(bf16[96,2304]{1,0:T(8,128)(2,1)S(1)} %slice.27), channel_id=1, source_target_pairs={{0,24},{8,0},{16,8},{24,16},{32,56},{40,32},{48,40},{56,48},{64,88... | collective-permute-start | bytes 1327112 | tf_op jit(solution)/shard_map/ppermute | solution.py:22
  54.6 3.2 %collective-permute-start.21 = (bf16[256,2048]{1,0:T(8,128)(2,1)S(1)}, bf16[256,2048]{1,0:T(8,128)(2,1)S(1)}, u32[]{:S(2)}, u32[]{:S(2)}) collective-permute-start(bf16[256,2048]{1,0:T(8,128)(2,1)S(1)} %pad_maximum_fusion.2), channel_id=1, source_target_pairs={{0,224},{8,232},{16,240},{24,248},{32,0},{40,8},{48,16},{56,24},{6... | collective-permute-start | bytes 3145736 | tf_op jit(solution)/shard_map/ppermute | solution.py:22
  58.0 2.5 %collective-permute-done.15 = bf16[96,2304]{1,0:T(8,128)(2,1)S(1)} collective-permute-done((bf16[96,2304]{1,0:T(8,128)(2,1)S(1)}, bf16[96,2304]{1,0:T(8,128)(2,1)S(1)}, u32[]{:S(2)}, u32[]{:S(2)}) %collective-permute-start.15) | collective-permute-done | bytes 442400 | tf_op jit(solution)/shard_map/ppermute | solution.py:22
  62.1 2.2 %collective-permute-start.24 = (bf16[320,2304]{1,0:T(8,128)(2,1)S(1)}, bf16[320,2304]{1,0:T(8,128)(2,1)S(1)}, u32[]{:S(2)}, u32[]{:S(2)}) collective-permute-start(bf16[320,2304]{1,0:T(8,128)(2,1)S(1)} %pad_maximum_fusion), channel_id=1, source_target_pairs={{0,24},{8,0},{16,8},{24,16},{32,56},{40,32},{48,40},{56,48},{64,88... | collective-permute-start | bytes 4423688 | tf_op jit(solution)/shard_map/ppermute | solution.py:22
  64.3 13.7 %collective-permute-done.19 = bf16[256,2048]{1,0:T(8,128)(2,1)S(1)} collective-permute-done((bf16[256,2048]{1,0:T(8,128)(2,1)S(1)}, bf16[256,2048]{1,0:T(8,128)(2,1)S(1)}, u32[]{:S(2)}, u32[]{:S(2)}) %collective-permute-start.19) | collective-permute-done | bytes 1048608 | tf_op jit(solution)/shard_map/ppermute | solution.py:22
  78.0 3.3 %collective-permute-start.22 = (bf16[256,2048]{1,0:T(8,128)(2,1)S(1)}, bf16[256,2048]{1,0:T(8,128)(2,1)S(1)}, u32[]{:S(2)}, u32[]{:S(2)}) collective-permute-start(bf16[256,2048]{1,0:T(8,128)(2,1)S(1)} %collective-permute-done.21), channel_id=1, source_target_pairs={{0,224},{8,232},{16,240},{24,248},{32,0},{40,8},{48,16},{56,24},{6... | collective-permute-start | bytes 3145736 | tf_op jit(solution)/shard_map/ppermute | solution.py:22
  81.6 17.1 %collective-permute-done.20 = bf16[256,2048]{1,0:T(8,128)(2,1)S(1)} collective-permute-done((bf16[256,2048]{1,0:T(8,128)(2,1)S(1)}, bf16[256,2048]{1,0:T(8,128)(2,1)S(1)}, u32[]{:S(2)}, u32[]{:S(2)}) %collective-permute-start.20) | collective-permute-done | bytes 1048608 | tf_op jit(solution)/shard_map/ppermute | solution.py:22
  99.0 4.2 %shard_map.59 = (bf16[512,1088]{1,0:T(8,128)(2,1)S(1)}, bf16[512,640]{1,0:T(8,128)(2,1)S(1)}, bf16[512,320]{1,0:T(8,128)(2,1)S(1)}, bf16[512,1280]{1,0:T(8,128)(...) custom-call(s32[4]{0:T(128)S(1)} %pad_add_fusion.place_ref, ...), custom_call_target="tpu_custom_call" | custom-call | bytes 12582912 | tf_op jit(solution)/shard_map/pallas_call | solution.py:71
  103.2 3.2 %fusion.19 = f32[512,2304]{1,0:T(8,128)S(1)} fusion(bf16[512,1088]{1,0:T(8,128)(2,1)S(1)} %get-tuple-element.71, bf16[1088,2304]{1,0:T(8,128)(2,1)S(1)} %constant_dynamic-update-slice_fusion.6), kind=kOutput, calls=%fused_computation.43 | convolution fusion | flops 2566914048 | bytes 10846208 | tf_op jit(solution)/shard_map/dot_general | solution.py:88
  107.4 2.5 %collective-permute-start.28 = (bf16[256,2048]{1,0:T(8,128)(2,1)S(1)}, bf16[256,2048]{1,0:T(8,128)(2,1)S(1)}, u32[]{:S(2)}, u32[]{:S(2)}) collective-permute-start(bf16[256,2048]{1,0:T(8,128)(2,1)S(1)} %collective-permute-done.22), channel_id=1, source_target_pairs={{0,224},{8,232},{16,240},{24,248},{32,0},{40,8},{48,16},{56,24},{6... | collective-permute-start | bytes 3145736 | tf_op jit(solution)/shard_map/ppermute | solution.py:22
  110.4 3.0 %collective-permute-start.26 = (bf16[160,2304]{1,0:T(8,128)(2,1)S(1)}, bf16[160,2304]{1,0:T(8,128)(2,1)S(1)}, u32[]{:S(2)}, u32[]{:S(2)}) collective-permute-start(bf16[160,2304]{1,0:T(8,128)(2,1)S(1)} %slice.29), channel_id=1, source_target_pairs={{0,24},{8,0},{16,8},{24,16},{32,56},{40,32},{48,40},{56,48},{64,88... | collective-permute-start | bytes 2211848 | tf_op jit(solution)/shard_map/ppermute | solution.py:22
  113.4 2.0 %fusion = f32[512,2304]{1,0:T(8,128)S(1)} fusion(bf16[512,640]{1,0:T(8,128)(2,1)S(1)} %get-tuple-element.76, bf16[320,2304]{1,0:T(8,128)(2,1)S(1)} %collective-permute-done.24, bf16[320,2304]{1,0:T(8,128)(2,1)S(1)} %collective-permute-done.23), kind=kOutput, calls=%fused_computation.2 | convolution fusion | flops 1515847680 | bytes 8323072 | tf_op jit(solution)/shard_map/dot_general | solution.py:88
  115.4 2.9 %fusion.20 = f32[512,2048]{1,0:T(8,128)S(1)} fusion(bf16[512,1280]{1,0:T(8,128)(2,1)S(1)} %get-tuple-element.81, bf16[1280,2048]{1,0:T(8,128)(2,1)S(1)} %constant_dynamic-update-slice_fusion.12), kind=kOutput, calls=%fused_computation.44 | convolution fusion | flops 2684354560 | bytes 10747904 | tf_op jit(solution)/shard_map/dot_general | solution.py:88
  118.3 4.7 %collective-permute-done.25 = bf16[160,2304]{1,0:T(8,128)(2,1)S(1)} collective-permute-done((bf16[160,2304]{1,0:T(8,128)(2,1)S(1)}, bf16[160,2304]{1,0:T(8,128)(2,1)S(1)}, u32[]{:S(2)}, u32[]{:S(2)}) %collective-permute-start.25) | collective-permute-done | bytes 737312 | tf_op jit(solution)/shard_map/ppermute | solution.py:22
  124.4 3.4 %collective-permute-done.27 = bf16[256,2048]{1,0:T(8,128)(2,1)S(1)} collective-permute-done((bf16[256,2048]{1,0:T(8,128)(2,1)S(1)}, bf16[256,2048]{1,0:T(8,128)(2,1)S(1)}, u32[]{:S(2)}, u32[]{:S(2)}) %collective-permute-start.27) | collective-permute-done | bytes 1048608 | tf_op jit(solution)/shard_map/ppermute | solution.py:22
  131.7 2.1 %collective-permute-start.30 = (bf16[128,2048]{1,0:T(8,128)(2,1)}, bf16[128,2048]{1,0:T(8,128)(2,1)}, u32[]{:S(2)}, u32[]{:S(2)}) collective-permute-start(bf16[128,2048]{1,0:T(8,128)(2,1)} %slice.31), channel_id=1, source_target_pairs={{0,224},{8,232},{16,240},{24,248},{32,0},{40,8},{48,16},{56,24},{6... | collective-permute-start | bytes 1572872 | tf_op jit(solution)/shard_map/ppermute | solution.py:22
  133.8 2.1 %add_convert_fusion = bf16[512,2304]{1,0:T(8,128)(2,1)} fusion(f32[512,2304]{1,0:T(8,128)S(1)} %fusion.8, f32[512,2304]{1,0:T(8,128)S(1)} %fusion, f32[512,2304]{1,0:T(8,128)S(1)} %fusion.19), kind=kLoop, calls=%fused_computation | loop fusion | flops 3538944 | bytes 16515072 | tf_op jit(solution)/shard_map/convert_element_type | solution.py:91
  135.8 2.8 %fusion.4 = f32[512,2048]{1,0:T(8,128)S(1)} fusion(bf16[512,512]{1,0:T(8,128)(2,1)S(1)} %get-tuple-element.84, bf16[256,2048]{1,0:T(8,128)(2,1)} %copy-done.1, bf16[256,2048]{1,0:T(8,128)(2,1)} %copy-done), kind=kOutput, calls=%fused_computation.6 | convolution fusion | flops 1077936128 | bytes 6815744 | tf_op jit(solution)/shard_map/dot_general | solution.py:88
  141.2 3.3 %add_convert_fusion.1 = bf16[512,2048]{1,0:T(8,128)(2,1)} fusion(f32[512,2048]{1,0:T(8,128)S(1)} %fusion.4, f32[512,2048]{1,0:T(8,128)S(1)} %fusion.20, bf16[512,256]{1,0:T(8,128)(2,1)S(1)} %get-tuple-element.78, bf16[128,2048]{1,0:T(8,128)(2,1)} %collective-permute-done.30, bf16[128,2048]{1,0:T(8,128)(2,1)} %collective-permute-done.29), kind=kOutput, calls=%fused_computation.1 | convolution fusion | flops 542113792 | bytes 11796480 | tf_op jit(solution)/shard_map/dot_general | solution.py:88
  (74 shorter events, 21.3 us)
Async XLA Ops:
  0.6 31.0 %copy-start.2 = (bf16[64,2048]{1,0:T(8,128)(2,1)S(1)}, bf16[64,2048]{1,0:T(8,128)(2,1)}, u32[]{:S(2)}) copy-start(bf16[64,2048]{1,0:T(8,128)(2,1)} %param.7) | copy-start | bytes 786436
  0.6 17.0 %collective-permute-start = (bf16[64,2304]{1,0:T(8,128)(2,1)}, bf16[64,2304]{1,0:T(8,128)(2,1)S(1)}, u32[]{:S(2)}, u32[]{:S(2)}) collective-permute-start(bf16[64,2304]{1,0:T(8,128)(2,1)} %param.6), channel_id=1, source_target_pairs={{0,32},{8,40},{16,48},{24,56},{32,64},{40,72},{48,80},{56,88},{64,... | collective-permute-start | bytes 884744 | tf_op jit(solution)/shard_map/ppermute | solution.py:22
  2.6 15.0 %collective-permute-start.1 = (bf16[64,2304]{1,0:T(8,128)(2,1)}, bf16[64,2304]{1,0:T(8,128)(2,1)S(1)}, u32[]{:S(2)}, u32[]{:S(2)}) collective-permute-start(bf16[64,2304]{1,0:T(8,128)(2,1)} %param.6), channel_id=1, source_target_pairs={{0,224},{8,232},{16,240},{24,248},{32,0},{40,8},{48,16},{56,24},{6... | collective-permute-start | bytes 884744 | tf_op jit(solution)/shard_map/ppermute | solution.py:22
  6.7 9.2 %collective-permute-start.2 = (bf16[64,2048]{1,0:T(8,128)(2,1)}, bf16[64,2048]{1,0:T(8,128)(2,1)S(1)}, u32[]{:S(2)}, u32[]{:S(2)}) collective-permute-start(bf16[64,2048]{1,0:T(8,128)(2,1)} %param.7), channel_id=1, source_target_pairs={{0,8},{8,16},{16,24},{24,0},{32,40},{40,48},{48,56},{56,32},{64,72... | collective-permute-start | bytes 786440 | tf_op jit(solution)/shard_map/ppermute | solution.py:22
  8.2 9.5 %collective-permute-start.3 = (bf16[64,2048]{1,0:T(8,128)(2,1)}, bf16[64,2048]{1,0:T(8,128)(2,1)S(1)}, u32[]{:S(2)}, u32[]{:S(2)}) collective-permute-start(bf16[64,2048]{1,0:T(8,128)(2,1)} %param.7), channel_id=1, source_target_pairs={{0,24},{8,0},{16,8},{24,16},{32,56},{40,32},{48,40},{56,48},{64,88... | collective-permute-start | bytes 786440 | tf_op jit(solution)/shard_map/ppermute | solution.py:22
  11.9 15.8 %collective-permute-start.7 = (bf16[256,1024]{1,0:T(8,128)(2,1)S(1)}, bf16[256,1024]{1,0:T(8,128)(2,1)S(1)}, u32[]{:S(2)}, u32[]{:S(2)}) collective-permute-start(bf16[256,1024]{1,0:T(8,128)(2,1)S(1)} %constant_dynamic-update-slice_fusion), channel_id=1, source_target_pairs={{0,2},{1,3},{2,4},{3,5},{4,6},{5,7},{6,0},{7,1},{8,10},{9,11},{10,... | collective-permute-start | bytes 1572872 | tf_op jit(solution)/shard_map/ppermute | solution.py:27
  15.9 8.6 %collective-permute-start.6 = (bf16[64,2048]{1,0:T(8,128)(2,1)}, bf16[64,2048]{1,0:T(8,128)(2,1)S(1)}, u32[]{:S(2)}, u32[]{:S(2)}) collective-permute-start(bf16[64,2048]{1,0:T(8,128)(2,1)} %param.7), channel_id=1, source_target_pairs={{0,16},{8,24},{16,0},{24,8},{32,48},{40,56},{48,32},{56,40},{64,80... | collective-permute-start | bytes 786440 | tf_op jit(solution)/shard_map/ppermute | solution.py:22
  17.7 10.0 %collective-permute-start.4 = (bf16[64,2304]{1,0:T(8,128)(2,1)S(1)}, bf16[64,2304]{1,0:T(8,128)(2,1)S(1)}, u32[]{:S(2)}, u32[]{:S(2)}) collective-permute-start(bf16[64,2304]{1,0:T(8,128)(2,1)S(1)} %collective-permute-done), channel_id=1, source_target_pairs={{0,32},{8,40},{16,48},{24,56},{32,64},{40,72},{48,80},{56,88},{64,... | collective-permute-start | bytes 884744 | tf_op jit(solution)/shard_map/ppermute | solution.py:22
  17.8 9.9 %collective-permute-start.5 = (bf16[64,2304]{1,0:T(8,128)(2,1)S(1)}, bf16[64,2304]{1,0:T(8,128)(2,1)S(1)}, u32[]{:S(2)}, u32[]{:S(2)}) collective-permute-start(bf16[64,2304]{1,0:T(8,128)(2,1)S(1)} %collective-permute-done.1), channel_id=1, source_target_pairs={{0,224},{8,232},{16,240},{24,248},{32,0},{40,8},{48,16},{56,24},{6... | collective-permute-start | bytes 884744 | tf_op jit(solution)/shard_map/ppermute | solution.py:22
  24.4 20.5 %collective-permute-start.10 = (bf16[192,2304]{1,0:T(8,128)(2,1)S(1)}, bf16[192,2304]{1,0:T(8,128)(2,1)S(1)}, u32[]{:S(2)}, u32[]{:S(2)}) collective-permute-start(bf16[192,2304]{1,0:T(8,128)(2,1)S(1)} %pad_maximum_fusion.3), channel_id=1, source_target_pairs={{0,8},{8,16},{16,24},{24,0},{32,40},{40,48},{48,56},{56,32},{64,72... | collective-permute-start | bytes 2654216 | tf_op jit(solution)/shard_map/ppermute | solution.py:22
  24.7 20.2 %collective-permute-start.11 = (bf16[192,2304]{1,0:T(8,128)(2,1)S(1)}, bf16[192,2304]{1,0:T(8,128)(2,1)S(1)}, u32[]{:S(2)}, u32[]{:S(2)}) collective-permute-start(bf16[192,2304]{1,0:T(8,128)(2,1)S(1)} %pad_maximum_fusion.3), channel_id=1, source_target_pairs={{0,24},{8,0},{16,8},{24,16},{32,56},{40,32},{48,40},{56,48},{64,88... | collective-permute-start | bytes 2654216 | tf_op jit(solution)/shard_map/ppermute | solution.py:22
  27.7 8.0 %collective-permute-start.8 = (bf16[64,2304]{1,0:T(8,128)(2,1)S(1)}, bf16[64,2304]{1,0:T(8,128)(2,1)S(1)}, u32[]{:S(2)}, u32[]{:S(2)}) collective-permute-start(bf16[64,2304]{1,0:T(8,128)(2,1)S(1)} %collective-permute-done.4), channel_id=1, source_target_pairs={{0,32},{8,40},{16,48},{24,56},{32,64},{40,72},{48,80},{56,88},{64,... | collective-permute-start | bytes 884744 | tf_op jit(solution)/shard_map/ppermute | solution.py:22
  27.8 7.9 %collective-permute-start.9 = (bf16[64,2304]{1,0:T(8,128)(2,1)S(1)}, bf16[64,2304]{1,0:T(8,128)(2,1)S(1)}, u32[]{:S(2)}, u32[]{:S(2)}) collective-permute-start(bf16[64,2304]{1,0:T(8,128)(2,1)S(1)} %collective-permute-done.5), channel_id=1, source_target_pairs={{0,224},{8,232},{16,240},{24,248},{32,0},{40,8},{48,16},{56,24},{6... | collective-permute-start | bytes 884744 | tf_op jit(solution)/shard_map/ppermute | solution.py:22
  31.1 10.5 %collective-permute-start.12 = (bf16[256,1024]{1,0:T(8,128)(2,1)S(1)}, bf16[256,1024]{1,0:T(8,128)(2,1)S(1)}, u32[]{:S(2)}, u32[]{:S(2)}) collective-permute-start(bf16[256,1024]{1,0:T(8,128)(2,1)S(1)} %constant_dynamic-update-slice_fusion), channel_id=1, source_target_pairs={{0,6},{1,7},{2,0},{3,1},{4,2},{5,3},{6,4},{7,5},{8,14},{9,15},{10,... | collective-permute-start | bytes 1572872 | tf_op jit(solution)/shard_map/ppermute | solution.py:27
  44.9 15.6 %collective-permute-start.17 = (bf16[256,1024]{1,0:T(8,128)(2,1)S(1)}, bf16[256,1024]{1,0:T(8,128)(2,1)S(1)}, u32[]{:S(2)}, u32[]{:S(2)}) collective-permute-start(bf16[256,1024]{1,0:T(8,128)(2,1)S(1)} %constant_dynamic-update-slice_fusion), channel_id=1, source_target_pairs={{0,4},{1,5},{2,6},{3,7},{4,0},{5,1},{6,2},{7,3},{8,12},{9,13},{10,... | collective-permute-start | bytes 1572872 | tf_op jit(solution)/shard_map/ppermute | solution.py:27
  47.3 7.3 %collective-permute-start.13 = (bf16[32,2304]{1,0:T(8,128)(2,1)S(1)}, bf16[32,2304]{1,0:T(8,128)(2,1)S(1)}, u32[]{:S(2)}, u32[]{:S(2)}) collective-permute-start(bf16[32,2304]{1,0:T(8,128)(2,1)S(1)} %slice.24), channel_id=1, source_target_pairs={{0,32},{8,40},{16,48},{24,56},{32,64},{40,72},{48,80},{56,88},{64,... | collective-permute-start | bytes 442376 | tf_op jit(solution)/shard_map/ppermute | solution.py:22
  47.4 7.2 %collective-permute-start.14 = (bf16[32,2304]{1,0:T(8,128)(2,1)S(1)}, bf16[32,2304]{1,0:T(8,128)(2,1)S(1)}, u32[]{:S(2)}, u32[]{:S(2)}) collective-permute-start(bf16[32,2304]{1,0:T(8,128)(2,1)S(1)} %slice.25), channel_id=1, source_target_pairs={{0,224},{8,232},{16,240},{24,248},{32,0},{40,8},{48,16},{56,24},{6... | collective-permute-start | bytes 442376 | tf_op jit(solution)/shard_map/ppermute | solution.py:22
  50.9 9.6 %collective-permute-start.15 = (bf16[96,2304]{1,0:T(8,128)(2,1)S(1)}, bf16[96,2304]{1,0:T(8,128)(2,1)S(1)}, u32[]{:S(2)}, u32[]{:S(2)}) collective-permute-start(bf16[96,2304]{1,0:T(8,128)(2,1)S(1)} %slice.26), channel_id=1, source_target_pairs={{0,8},{8,16},{16,24},{24,0},{32,40},{40,48},{48,56},{56,32},{64,72... | collective-permute-start | bytes 1327112 | tf_op jit(solution)/shard_map/ppermute | solution.py:22
  51.3 9.2 %collective-permute-start.16 = (bf16[96,2304]{1,0:T(8,128)(2,1)S(1)}, bf16[96,2304]{1,0:T(8,128)(2,1)S(1)}, u32[]{:S(2)}, u32[]{:S(2)}) collective-permute-start(bf16[96,2304]{1,0:T(8,128)(2,1)S(1)} %slice.27), channel_id=1, source_target_pairs={{0,24},{8,0},{16,8},{24,16},{32,56},{40,32},{48,40},{56,48},{64,88... | collective-permute-start | bytes 1327112 | tf_op jit(solution)/shard_map/ppermute | solution.py:22
  54.6 23.4 %collective-permute-start.19 = (bf16[256,2048]{1,0:T(8,128)(2,1)S(1)}, bf16[256,2048]{1,0:T(8,128)(2,1)S(1)}, u32[]{:S(2)}, u32[]{:S(2)}) collective-permute-start(bf16[256,2048]{1,0:T(8,128)(2,1)S(1)} %pad_maximum_fusion.2), channel_id=1, source_target_pairs={{0,32},{8,40},{16,48},{24,56},{32,64},{40,72},{48,80},{56,88},{64,... | collective-permute-start | bytes 3145736 | tf_op jit(solution)/shard_map/ppermute | solution.py:22
  54.6 23.4 %collective-permute-start.21 = (bf16[256,2048]{1,0:T(8,128)(2,1)S(1)}, bf16[256,2048]{1,0:T(8,128)(2,1)S(1)}, u32[]{:S(2)}, u32[]{:S(2)}) collective-permute-start(bf16[256,2048]{1,0:T(8,128)(2,1)S(1)} %pad_maximum_fusion.2), channel_id=1, source_target_pairs={{0,224},{8,232},{16,240},{24,248},{32,0},{40,8},{48,16},{56,24},{6... | collective-permute-start | bytes 3145736 | tf_op jit(solution)/shard_map/ppermute | solution.py:22
  60.5 38.5 %collective-permute-start.18 = (bf16[1024,1024]{1,0:T(8,128)(2,1)S(1)}, bf16[1024,1024]{1,0:T(8,128)(2,1)S(1)}, u32[]{:S(2)}, u32[]{:S(2)}) collective-permute-start(bf16[1024,1024]{1,0:T(8,128)(2,1)S(1)} %constant_dynamic-update-slice_fusion.2.mine_ref), channel_id=1, source_target_pairs={{0,1},{1,0},{2,3},{3,2},{4,5},{5,4},{6,7},{7,6},{8,9},{9,8},{10,11... | collective-permute-start | bytes 6291464 | tf_op jit(solution)/shard_map/ppermute | solution.py:27
  60.7 45.7 %collective-permute-start.23 = (bf16[320,2304]{1,0:T(8,128)(2,1)S(1)}, bf16[320,2304]{1,0:T(8,128)(2,1)S(1)}, u32[]{:S(2)}, u32[]{:S(2)}) collective-permute-start(bf16[320,2304]{1,0:T(8,128)(2,1)S(1)} %pad_maximum_fusion), channel_id=1, source_target_pairs={{0,8},{8,16},{16,24},{24,0},{32,40},{40,48},{48,56},{56,32},{64,72... | collective-permute-start | bytes 4423688 | tf_op jit(solution)/shard_map/ppermute | solution.py:22
  62.1 44.4 %collective-permute-start.24 = (bf16[320,2304]{1,0:T(8,128)(2,1)S(1)}, bf16[320,2304]{1,0:T(8,128)(2,1)S(1)}, u32[]{:S(2)}, u32[]{:S(2)}) collective-permute-start(bf16[320,2304]{1,0:T(8,128)(2,1)S(1)} %pad_maximum_fusion), channel_id=1, source_target_pairs={{0,24},{8,0},{16,8},{24,16},{32,56},{40,32},{48,40},{56,48},{64,88... | collective-permute-start | bytes 4423688 | tf_op jit(solution)/shard_map/ppermute | solution.py:22
  78.0 20.8 %collective-permute-start.20 = (bf16[256,2048]{1,0:T(8,128)(2,1)S(1)}, bf16[256,2048]{1,0:T(8,128)(2,1)S(1)}, u32[]{:S(2)}, u32[]{:S(2)}) collective-permute-start(bf16[256,2048]{1,0:T(8,128)(2,1)S(1)} %collective-permute-done.19), channel_id=1, source_target_pairs={{0,32},{8,40},{16,48},{24,56},{32,64},{40,72},{48,80},{56,88},{64,... | collective-permute-start | bytes 3145736 | tf_op jit(solution)/shard_map/ppermute | solution.py:22
  78.0 20.9 %collective-permute-start.22 = (bf16[256,2048]{1,0:T(8,128)(2,1)S(1)}, bf16[256,2048]{1,0:T(8,128)(2,1)S(1)}, u32[]{:S(2)}, u32[]{:S(2)}) collective-permute-start(bf16[256,2048]{1,0:T(8,128)(2,1)S(1)} %collective-permute-done.21), channel_id=1, source_target_pairs={{0,224},{8,232},{16,240},{24,248},{32,0},{40,8},{48,16},{56,24},{6... | collective-permute-start | bytes 3145736 | tf_op jit(solution)/shard_map/ppermute | solution.py:22
  106.5 21.3 %collective-permute-start.27 = (bf16[256,2048]{1,0:T(8,128)(2,1)S(1)}, bf16[256,2048]{1,0:T(8,128)(2,1)S(1)}, u32[]{:S(2)}, u32[]{:S(2)}) collective-permute-start(bf16[256,2048]{1,0:T(8,128)(2,1)S(1)} %collective-permute-done.20), channel_id=1, source_target_pairs={{0,32},{8,40},{16,48},{24,56},{32,64},{40,72},{48,80},{56,88},{64,... | collective-permute-start | bytes 3145736 | tf_op jit(solution)/shard_map/ppermute | solution.py:22
  107.4 20.4 %collective-permute-start.28 = (bf16[256,2048]{1,0:T(8,128)(2,1)S(1)}, bf16[256,2048]{1,0:T(8,128)(2,1)S(1)}, u32[]{:S(2)}, u32[]{:S(2)}) collective-permute-start(bf16[256,2048]{1,0:T(8,128)(2,1)S(1)} %collective-permute-done.22), channel_id=1, source_target_pairs={{0,224},{8,232},{16,240},{24,248},{32,0},{40,8},{48,16},{56,24},{6... | collective-permute-start | bytes 3145736 | tf_op jit(solution)/shard_map/ppermute | solution.py:22
  110.0 13.0 %collective-permute-start.25 = (bf16[160,2304]{1,0:T(8,128)(2,1)S(1)}, bf16[160,2304]{1,0:T(8,128)(2,1)S(1)}, u32[]{:S(2)}, u32[]{:S(2)}) collective-permute-start(bf16[160,2304]{1,0:T(8,128)(2,1)S(1)} %slice.28), channel_id=1, source_target_pairs={{0,8},{8,16},{16,24},{24,0},{32,40},{40,48},{48,56},{56,32},{64,72... | collective-permute-start | bytes 2211848 | tf_op jit(solution)/shard_map/ppermute | solution.py:22
  110.4 12.6 %collective-permute-start.26 = (bf16[160,2304]{1,0:T(8,128)(2,1)S(1)}, bf16[160,2304]{1,0:T(8,128)(2,1)S(1)}, u32[]{:S(2)}, u32[]{:S(2)}) collective-permute-start(bf16[160,2304]{1,0:T(8,128)(2,1)S(1)} %slice.29), channel_id=1, source_target_pairs={{0,24},{8,0},{16,8},{24,16},{32,56},{40,32},{48,40},{56,48},{64,88... | collective-permute-start | bytes 2211848 | tf_op jit(solution)/shard_map/ppermute | solution.py:22
  129.7 10.7 %collective-permute-start.29 = (bf16[128,2048]{1,0:T(8,128)(2,1)}, bf16[128,2048]{1,0:T(8,128)(2,1)}, u32[]{:S(2)}, u32[]{:S(2)}) collective-permute-start(bf16[128,2048]{1,0:T(8,128)(2,1)} %slice.30), channel_id=1, source_target_pairs={{0,32},{8,40},{16,48},{24,56},{32,64},{40,72},{48,80},{56,88},{64,... | collective-permute-start | bytes 1572872 | tf_op jit(solution)/shard_map/ppermute | solution.py:22
  131.7 9.5 %collective-permute-start.30 = (bf16[128,2048]{1,0:T(8,128)(2,1)}, bf16[128,2048]{1,0:T(8,128)(2,1)}, u32[]{:S(2)}, u32[]{:S(2)}) collective-permute-start(bf16[128,2048]{1,0:T(8,128)(2,1)} %slice.31), channel_id=1, source_target_pairs={{0,224},{8,232},{16,240},{24,248},{32,0},{40,8},{48,16},{56,24},{6... | collective-permute-start | bytes 1572872 | tf_op jit(solution)/shard_map/ppermute | solution.py:22
  (2 other events, 3.0 us)

commit v5 on v4

--- a/solution.py
+++ b/solution.py
@@ -128,21 +128,18 @@
     near, opposite = together((near, opposite))
     near_left, near_right = hop(near, 0, 1), hop(near, 0, -1)
     below, above = hop(below, 1, 0), hop(above, -1, 0)
-    below, above, opposite, down = together((below, above, opposite, down))
+    below, above, opposite, mine, down = together((below, above, opposite, mine, down))
+    up = hop_y(mine, -1)
     far = [below, above]
     below, above = hop(below, 1, 0), hop(above, -1, 0)
     far = jnp.concatenate([*far, below, above])
-    mine, down = together((mine, down))
-    up = hop_y(mine, -1)
-    below, above, near_left, near_right, far, up = together(
-        (below, above, near_left, near_right, far, up)
-    )
+    below, above, far = together((below, above, far))
     mine, up = together((mine, up))
     across = hop_y(mine, 2)
     far = [far, hop(halves(below)[0], 1, 0), hop(halves(above)[1], -1, 0)]
+    wide = jnp.concatenate([wide, left, right, opposite])
+    far, wide, near_left, near_right = together((far, wide, near_left, near_right))
     near_halves = [hop(halves(near_left)[0], 0, 1), hop(halves(near_right)[1], 0, -1)]
-    wide = jnp.concatenate([wide, left, right, opposite])
-    far, wide = together((far, wide))
     far = jnp.concatenate(far)
     far, near_halves, across = together((far, near_halves, across))
     far_left, far_right = hop(far, 0, 1), hop(far, 0, -1)
@@ -168,9 +165,7 @@
 
     below, above = hop(below, 1, 0), hop(above, -1, 0)
     wide_first += [below, above]
-    below, above, far_left, far_right, tall_sum = together(
-        (below, above, far_left, far_right, tall_sum)
-    )
+    below, above, far_left, far_right = together((below, above, far_left, far_right))
     wide_sum = contract(lefts[3], wide_first)
     below, above = hop(below, 1, 0), hop(above, -1, 0)
     far_halves = [hop(halves(far_left)[0], 0, 1), hop(halves(far_right)[1], 0, -1)]
@@ -179,6 +174,7 @@
 
     tall_sum = contract(lefts[1], [far_left, far_right], tall_sum)
     wide_sum = contract(lefts[4], [below, above], wide_sum)
+    tall_sum, wide_sum = together((tall_sum, wide_sum))
     qkv = contract(lefts[2], far_halves, tall_sum, dtype=jnp.bfloat16)
     out = contract(lefts[5], wide_halves, wide_sum, dtype=jnp.bfloat16)
     return qkv, out

time: 146 us -> 142 us (0.973)
  starting transfers between devices: 52.6 us -> 57.7 us
  local copies, waits for them, and re-layouts: 5.82 us -> 3.21 us
  other arithmetic: 3.42 us -> 1.34 us
  waiting for transfers between devices: 61.9 us -> 60 us
    ppermute x4, starting transfers between devices: 4.57 us -> 11.1 us  [hop_y(): return lax.ppermute(value, 'col', pairs)]
    ppermute x4, waiting for transfers between devices: 5.8 us -> 0.01 us  [hop_y(): return lax.ppermute(value, 'col', pairs)]
    ppermute x27, waiting for transfers between devices: 56.1 us -> 60 us  [hop(): return lax.ppermute(value, 'row', pairs)]
    convert_element_type x1 -> x0, other arithmetic: 2.07 us -> none  [contract(): return part.astype(dtype)]
    slice x8, local copies, waits for them, and re-layouts: 1.91 us -> 0.26 us  [halves(): return (value[:half], value[half:])]
  transfers between devices with their start and end apart: 31 -> 31, of which waited for: 12 -> 9; matrix products, arithmetic and copies ran while one was open for 14% -> 12% of each run, Pallas kernels for 3% -> 3%
where the time goes in v5:
time: 142 us
  waiting for transfers between devices  60 us (42%)
  starting transfers between devices  57.7 us (41%)
  matrix products  14.2 us (10%)
  Pallas kernels  4.22 us (3%)
  local copies, waits for them, and re-layouts  3.21 us (2%)
    ppermute x27, waiting for transfers between devices, hop(): return lax.ppermute(value, 'row', pairs)  60 us
    ppermute x27, starting transfers between devices, hop(): return lax.ppermute(value, 'row', pairs)  46.6 us
    dot_general x6, matrix products, contract(): jnp.dot(left, jnp.concatenate(grads), preferred_element_type=jnp.float32)  14.2 us
    ppermute x4, starting transfers between devices, hop_y(): return lax.ppermute(value, 'col', pairs)  11.1 us
    pallas_call x1, Pallas kernels, arrange(): pl.pallas_call(functools.partial(arrange_kernel, groups), out_shape=[jax....  4.22 us
  transfers between devices with their start and end apart: 31, of which 9 were waited for; matrix products, arithmetic and copies ran while one was open for 12% of the time, Pallas kernels for 3%

profile of v5, /device:TPU:8, one launch (start us, length us, event | category | flops | bytes accessed | tf_op | source)
XLA Modules:
  0.0 141.8 jit_solution(14213145524116194261)
XLA Ops:
  0.6 2.0 %collective-permute-start = (bf16[64,2304]{1,0:T(8,128)(2,1)}, bf16[64,2304]{1,0:T(8,128)(2,1)S(1)}, u32[]{:S(2)}, u32[]{:S(2)}) collective-permute-start(bf16[64,2304]{1,0:T(8,128)(2,1)} %param.6), channel_id=1, source_target_pairs={{0,32},{8,40},{16,48},{24,56},{32,64},{40,72},{48,80},{56,88},{64,... | collective-permute-start | bytes 884744 | tf_op jit(solution)/shard_map/ppermute | solution.py:22
  2.6 4.0 %collective-permute-start.1 = (bf16[64,2304]{1,0:T(8,128)(2,1)}, bf16[64,2304]{1,0:T(8,128)(2,1)S(1)}, u32[]{:S(2)}, u32[]{:S(2)}) collective-permute-start(bf16[64,2304]{1,0:T(8,128)(2,1)} %param.6), channel_id=1, source_target_pairs={{0,224},{8,232},{16,240},{24,248},{32,0},{40,8},{48,16},{56,24},{6... | collective-permute-start | bytes 884744 | tf_op jit(solution)/shard_map/ppermute | solution.py:22
  8.2 1.7 %collective-permute-start.3 = (bf16[64,2048]{1,0:T(8,128)(2,1)}, bf16[64,2048]{1,0:T(8,128)(2,1)S(1)}, u32[]{:S(2)}, u32[]{:S(2)}) collective-permute-start(bf16[64,2048]{1,0:T(8,128)(2,1)} %param.7), channel_id=1, source_target_pairs={{0,24},{8,0},{16,8},{24,16},{32,56},{40,32},{48,40},{56,48},{64,88... | collective-permute-start | bytes 786440 | tf_op jit(solution)/shard_map/ppermute | solution.py:22
  11.9 1.7 %collective-permute-start.7 = (bf16[256,1024]{1,0:T(8,128)(2,1)S(1)}, bf16[256,1024]{1,0:T(8,128)(2,1)S(1)}, u32[]{:S(2)}, u32[]{:S(2)}) collective-permute-start(bf16[256,1024]{1,0:T(8,128)(2,1)S(1)} %constant_dynamic-update-slice_fusion), channel_id=1, source_target_pairs={{0,2},{1,3},{2,4},{3,5},{4,6},{5,7},{6,0},{7,1},{8,10},{9,11},{10,... | collective-permute-start | bytes 1572872 | tf_op jit(solution)/shard_map/ppermute | solution.py:27
  13.6 2.3 %collective-permute-done.2 = bf16[64,2048]{1,0:T(8,128)(2,1)S(1)} collective-permute-done((bf16[64,2048]{1,0:T(8,128)(2,1)}, bf16[64,2048]{1,0:T(8,128)(2,1)S(1)}, u32[]{:S(2)}, u32[]{:S(2)}) %collective-permute-start.2) | collective-permute-done | bytes 262176 | tf_op jit(solution)/shard_map/ppermute | solution.py:22
  15.9 1.8 %collective-permute-start.6 = (bf16[64,2048]{1,0:T(8,128)(2,1)}, bf16[64,2048]{1,0:T(8,128)(2,1)S(1)}, u32[]{:S(2)}, u32[]{:S(2)}) collective-permute-start(bf16[64,2048]{1,0:T(8,128)(2,1)} %param.7), channel_id=1, source_target_pairs={{0,16},{8,24},{16,0},{24,8},{32,48},{40,56},{48,32},{56,40},{64,80... | collective-permute-start | bytes 786440 | tf_op jit(solution)/shard_map/ppermute | solution.py:22
  17.8 3.2 %collective-permute-start.5 = (bf16[64,2304]{1,0:T(8,128)(2,1)S(1)}, bf16[64,2304]{1,0:T(8,128)(2,1)S(1)}, u32[]{:S(2)}, u32[]{:S(2)}) collective-permute-start(bf16[64,2304]{1,0:T(8,128)(2,1)S(1)} %collective-permute-done.1), channel_id=1, source_target_pairs={{0,224},{8,232},{16,240},{24,248},{32,0},{40,8},{48,16},{56,24},{6... | collective-permute-start | bytes 884744 | tf_op jit(solution)/shard_map/ppermute | solution.py:22
  22.0 2.4 %collective-permute-done.6 = bf16[64,2048]{1,0:T(8,128)(2,1)S(1)} collective-permute-done((bf16[64,2048]{1,0:T(8,128)(2,1)}, bf16[64,2048]{1,0:T(8,128)(2,1)S(1)}, u32[]{:S(2)}, u32[]{:S(2)}) %collective-permute-start.6) | collective-permute-done | bytes 262176 | tf_op jit(solution)/shard_map/ppermute | solution.py:22
  24.7 3.0 %collective-permute-start.14 = (bf16[192,2304]{1,0:T(8,128)(2,1)S(1)}, bf16[192,2304]{1,0:T(8,128)(2,1)S(1)}, u32[]{:S(2)}, u32[]{:S(2)}) collective-permute-start(bf16[192,2304]{1,0:T(8,128)(2,1)S(1)} %pad_maximum_fusion.3), channel_id=1, source_target_pairs={{0,24},{8,0},{16,8},{24,16},{32,56},{40,32},{48,40},{56,48},{64,88... | collective-permute-start | bytes 2654216 | tf_op jit(solution)/shard_map/ppermute | solution.py:22
  27.7 1.5 %collective-permute-start.10 = (bf16[64,2304]{1,0:T(8,128)(2,1)S(1)}, bf16[64,2304]{1,0:T(8,128)(2,1)S(1)}, u32[]{:S(2)}, u32[]{:S(2)}) collective-permute-start(bf16[64,2304]{1,0:T(8,128)(2,1)S(1)} %collective-permute-done.5), channel_id=1, source_target_pairs={{0,224},{8,232},{16,240},{24,248},{32,0},{40,8},{48,16},{56,24},{6... | collective-permute-start | bytes 884744 | tf_op jit(solution)/shard_map/ppermute | solution.py:22
  30.5 4.0 %collective-permute-done.10 = bf16[64,2304]{1,0:T(8,128)(2,1)S(1)} collective-permute-done((bf16[64,2304]{1,0:T(8,128)(2,1)S(1)}, bf16[64,2304]{1,0:T(8,128)(2,1)S(1)}, u32[]{:S(2)}, u32[]{:S(2)}) %collective-permute-start.10) | collective-permute-done | bytes 294944 | tf_op jit(solution)/shard_map/ppermute | solution.py:22
  34.5 2.7 %collective-permute-done.9 = bf16[64,2304]{1,0:T(8,128)(2,1)S(1)} collective-permute-done((bf16[64,2304]{1,0:T(8,128)(2,1)S(1)}, bf16[64,2304]{1,0:T(8,128)(2,1)S(1)}, u32[]{:S(2)}, u32[]{:S(2)}) %collective-permute-start.9) | collective-permute-done | bytes 294944 | tf_op jit(solution)/shard_map/ppermute | solution.py:22
  37.3 3.3 %collective-permute-start.12 = (bf16[32,2304]{1,0:T(8,128)(2,1)S(1)}, bf16[32,2304]{1,0:T(8,128)(2,1)S(1)}, u32[]{:S(2)}, u32[]{:S(2)}) collective-permute-start(bf16[32,2304]{1,0:T(8,128)(2,1)S(1)} %slice.25), channel_id=1, source_target_pairs={{0,224},{8,232},{16,240},{24,248},{32,0},{40,8},{48,16},{56,24},{6... | collective-permute-start | bytes 442376 | tf_op jit(solution)/shard_map/ppermute | solution.py:22
  40.6 8.8 %collective-permute-start.17 = (bf16[256,1024]{1,0:T(8,128)(2,1)S(1)}, bf16[256,1024]{1,0:T(8,128)(2,1)S(1)}, u32[]{:S(2)}, u32[]{:S(2)}) collective-permute-start(bf16[256,1024]{1,0:T(8,128)(2,1)S(1)} %constant_dynamic-update-slice_fusion), channel_id=1, source_target_pairs={{0,4},{1,5},{2,6},{3,7},{4,0},{5,1},{6,2},{7,3},{8,12},{9,13},{10,... | collective-permute-start | bytes 1572872 | tf_op jit(solution)/shard_map/ppermute | solution.py:27
  49.7 3.2 %collective-permute-start.21 = (bf16[256,2048]{1,0:T(8,128)(2,1)S(1)}, bf16[256,2048]{1,0:T(8,128)(2,1)S(1)}, u32[]{:S(2)}, u32[]{:S(2)}) collective-permute-start(bf16[256,2048]{1,0:T(8,128)(2,1)S(1)} %pad_maximum_fusion.2), channel_id=1, source_target_pairs={{0,224},{8,232},{16,240},{24,248},{32,0},{40,8},{48,16},{56,24},{6... | collective-permute-start | bytes 3145736 | tf_op jit(solution)/shard_map/ppermute | solution.py:22
  53.2 3.2 %collective-permute-start.16 = (bf16[96,2304]{1,0:T(8,128)(2,1)S(1)}, bf16[96,2304]{1,0:T(8,128)(2,1)S(1)}, u32[]{:S(2)}, u32[]{:S(2)}) collective-permute-start(bf16[96,2304]{1,0:T(8,128)(2,1)S(1)} %slice.27), channel_id=1, source_target_pairs={{0,24},{8,0},{16,8},{24,16},{32,56},{40,32},{48,40},{56,48},{64,88... | collective-permute-start | bytes 1327112 | tf_op jit(solution)/shard_map/ppermute | solution.py:22
  56.6 5.9 %collective-permute-done.15 = bf16[96,2304]{1,0:T(8,128)(2,1)S(1)} collective-permute-done((bf16[96,2304]{1,0:T(8,128)(2,1)S(1)}, bf16[96,2304]{1,0:T(8,128)(2,1)S(1)}, u32[]{:S(2)}, u32[]{:S(2)}) %collective-permute-start.15) | collective-permute-done | bytes 442400 | tf_op jit(solution)/shard_map/ppermute | solution.py:22
  63.0 3.3 %collective-permute-start.24 = (bf16[320,2304]{1,0:T(8,128)(2,1)S(1)}, bf16[320,2304]{1,0:T(8,128)(2,1)S(1)}, u32[]{:S(2)}, u32[]{:S(2)}) collective-permute-start(bf16[320,2304]{1,0:T(8,128)(2,1)S(1)} %pad_maximum_fusion), channel_id=1, source_target_pairs={{0,24},{8,0},{16,8},{24,16},{32,56},{40,32},{48,40},{56,48},{64,88... | collective-permute-start | bytes 4423688 | tf_op jit(solution)/shard_map/ppermute | solution.py:22
  66.4 1.6 %collective-permute-done.19 = bf16[256,2048]{1,0:T(8,128)(2,1)S(1)} collective-permute-done((bf16[256,2048]{1,0:T(8,128)(2,1)S(1)}, bf16[256,2048]{1,0:T(8,128)(2,1)S(1)}, u32[]{:S(2)}, u32[]{:S(2)}) %collective-permute-start.19) | collective-permute-done | bytes 1048608 | tf_op jit(solution)/shard_map/ppermute | solution.py:22
  68.0 3.2 %collective-permute-start.22 = (bf16[256,2048]{1,0:T(8,128)(2,1)S(1)}, bf16[256,2048]{1,0:T(8,128)(2,1)S(1)}, u32[]{:S(2)}, u32[]{:S(2)}) collective-permute-start(bf16[256,2048]{1,0:T(8,128)(2,1)S(1)} %collective-permute-done.21), channel_id=1, source_target_pairs={{0,224},{8,232},{16,240},{24,248},{32,0},{40,8},{48,16},{56,24},{6... | collective-permute-start | bytes 3145736 | tf_op jit(solution)/shard_map/ppermute | solution.py:22
  71.6 27.6 %collective-permute-done.23 = bf16[320,2304]{1,0:T(8,128)(2,1)S(1)} collective-permute-done((bf16[320,2304]{1,0:T(8,128)(2,1)S(1)}, bf16[320,2304]{1,0:T(8,128)(2,1)S(1)}, u32[]{:S(2)}, u32[]{:S(2)}) %collective-permute-start.23) | collective-permute-done | bytes 1474592 | tf_op jit(solution)/shard_map/ppermute | solution.py:22
  99.3 3.2 %collective-permute-start.28 = (bf16[256,2048]{1,0:T(8,128)(2,1)S(1)}, bf16[256,2048]{1,0:T(8,128)(2,1)S(1)}, u32[]{:S(2)}, u32[]{:S(2)}) collective-permute-start(bf16[256,2048]{1,0:T(8,128)(2,1)S(1)} %collective-permute-done.22), channel_id=1, source_target_pairs={{0,224},{8,232},{16,240},{24,248},{32,0},{40,8},{48,16},{56,24},{6... | collective-permute-start | bytes 3145736 | tf_op jit(solution)/shard_map/ppermute | solution.py:22
  103.8 2.3 %collective-permute-start.26 = (bf16[160,2304]{1,0:T(8,128)(2,1)S(1)}, bf16[160,2304]{1,0:T(8,128)(2,1)S(1)}, u32[]{:S(2)}, u32[]{:S(2)}) collective-permute-start(bf16[160,2304]{1,0:T(8,128)(2,1)S(1)} %slice.29), channel_id=1, source_target_pairs={{0,24},{8,0},{16,8},{24,16},{32,56},{40,32},{48,40},{56,48},{64,88... | collective-permute-start | bytes 2211848 | tf_op jit(solution)/shard_map/ppermute | solution.py:22
  106.3 4.2 %shard_map.59 = (bf16[512,1088]{1,0:T(8,128)(2,1)S(1)}, bf16[512,640]{1,0:T(8,128)(2,1)S(1)}, bf16[512,320]{1,0:T(8,128)(2,1)S(1)}, bf16[512,1280]{1,0:T(8,128)(...) custom-call(s32[4]{0:T(128)S(1)} %pad_add_fusion.place_ref, ...), custom_call_target="tpu_custom_call" | custom-call | bytes 12582912 | tf_op jit(solution)/shard_map/pallas_call | solution.py:71
  110.5 2.9 %fusion.18 = f32[512,2048]{1,0:T(8,128)S(1)} fusion(bf16[512,1280]{1,0:T(8,128)(2,1)S(1)} %get-tuple-element.77, bf16[1280,2048]{1,0:T(8,128)(2,1)S(1)} %constant_dynamic-update-slice_fusion.12), kind=kOutput, calls=%fused_computation.44 | convolution fusion | flops 2684354560 | bytes 10747904 | tf_op jit(solution)/shard_map/dot_general | solution.py:88
  113.5 3.2 %fusion.17 = f32[512,2304]{1,0:T(8,128)S(1)} fusion(bf16[512,1088]{1,0:T(8,128)(2,1)S(1)} %get-tuple-element.71, bf16[1088,2304]{1,0:T(8,128)(2,1)S(1)} %bitcast.13), kind=kOutput, calls=%fused_computation.43 | convolution fusion | flops 2566914048 | bytes 10846208 | tf_op jit(solution)/shard_map/dot_general | solution.py:88
  116.7 2.0 %convolution_add_fusion.1 = f32[512,2304]{1,0:T(8,128)S(1)} fusion(f32[512,2304]{1,0:T(8,128)S(1)} %fusion.17, bf16[512,640]{1,0:T(8,128)(2,1)S(1)} %get-tuple-element.70, bf16[320,2304]{1,0:T(8,128)(2,1)S(1)} %collective-permute-done.24, bf16[320,2304]{1,0:T(8,128)(2,1)S(1)} %collective-permute-done.23), kind=kOutput, calls=%fused_computation.1 | convolution fusion | flops 1517027328 | bytes 13041664 | tf_op jit(solution)/shard_map/dot_general | solution.py:88
  118.7 6.8 %collective-permute-done.27 = bf16[256,2048]{1,0:T(8,128)(2,1)S(1)} collective-permute-done((bf16[256,2048]{1,0:T(8,128)(2,1)S(1)}, bf16[256,2048]{1,0:T(8,128)(2,1)S(1)}, u32[]{:S(2)}, u32[]{:S(2)}) %collective-permute-start.27) | collective-permute-done | bytes 1048608 | tf_op jit(solution)/shard_map/ppermute | solution.py:22
  125.7 3.3 %collective-permute-start.30 = (bf16[128,2048]{1,0:T(8,128)(2,1)S(1)}, bf16[128,2048]{1,0:T(8,128)(2,1)S(1)}, u32[]{:S(2)}, u32[]{:S(2)}) collective-permute-start(bf16[128,2048]{1,0:T(8,128)(2,1)S(1)} %slice.31), channel_id=1, source_target_pairs={{0,224},{8,232},{16,240},{24,248},{32,0},{40,8},{48,16},{56,24},{6... | collective-permute-start | bytes 1572872 | tf_op jit(solution)/shard_map/ppermute | solution.py:22
  130.3 2.8 %fusion = bf16[512,2304]{1,0:T(8,128)(2,1)} fusion(f32[512,2304]{1,0:T(8,128)S(1)} %convolution_add_fusion.1, bf16[512,320]{1,0:T(8,128)(2,1)S(1)} %get-tuple-element.65, bf16[160,2304]{1,0:T(8,128)(2,1)S(1)} %collective-permute-done.26, bf16[160,2304]{1,0:T(8,128)(2,1)S(1)} %collective-permute-done.25), kind=kOutput, calls=%fused_computation.2 | convolution fusion | flops 760283136 | bytes 8880128 | tf_op jit(solution)/shard_map/dot_general | solution.py:88
  133.1 6.7 %collective-permute-done.29 = bf16[128,2048]{1,0:T(8,128)(2,1)S(1)} collective-permute-done((bf16[128,2048]{1,0:T(8,128)(2,1)S(1)}, bf16[128,2048]{1,0:T(8,128)(2,1)S(1)}, u32[]{:S(2)}, u32[]{:S(2)}) %collective-permute-start.29) | collective-permute-done | bytes 524320 | tf_op jit(solution)/shard_map/ppermute | solution.py:22
  139.7 2.0 %add_convert_fusion = bf16[512,2048]{1,0:T(8,128)(2,1)} fusion(f32[512,2048]{1,0:T(8,128)S(1)} %convolution_add_fusion.2, bf16[512,256]{1,0:T(8,128)(2,1)S(1)} %get-tuple-element.82, bf16[128,2048]{1,0:T(8,128)(2,1)S(1)} %collective-permute-done.30, bf16[128,2048]{1,0:T(8,128)(2,1)S(1)} %collective-permute-done.29), kind=kOutput, calls=%fused_computation.3 | convolution fusion | flops 541065216 | bytes 7602176 | tf_op jit(solution)/shard_map/dot_general | solution.py:88
  (76 shorter events, 10.8 us)
Async XLA Ops:
  0.6 17.0 %collective-permute-start = (bf16[64,2304]{1,0:T(8,128)(2,1)}, bf16[64,2304]{1,0:T(8,128)(2,1)S(1)}, u32[]{:S(2)}, u32[]{:S(2)}) collective-permute-start(bf16[64,2304]{1,0:T(8,128)(2,1)} %param.6), channel_id=1, source_target_pairs={{0,32},{8,40},{16,48},{24,56},{32,64},{40,72},{48,80},{56,88},{64,... | collective-permute-start | bytes 884744 | tf_op jit(solution)/shard_map/ppermute | solution.py:22
  2.6 15.0 %collective-permute-start.1 = (bf16[64,2304]{1,0:T(8,128)(2,1)}, bf16[64,2304]{1,0:T(8,128)(2,1)S(1)}, u32[]{:S(2)}, u32[]{:S(2)}) collective-permute-start(bf16[64,2304]{1,0:T(8,128)(2,1)} %param.6), channel_id=1, source_target_pairs={{0,224},{8,232},{16,240},{24,248},{32,0},{40,8},{48,16},{56,24},{6... | collective-permute-start | bytes 884744 | tf_op jit(solution)/shard_map/ppermute | solution.py:22
  6.7 9.2 %collective-permute-start.2 = (bf16[64,2048]{1,0:T(8,128)(2,1)}, bf16[64,2048]{1,0:T(8,128)(2,1)S(1)}, u32[]{:S(2)}, u32[]{:S(2)}) collective-permute-start(bf16[64,2048]{1,0:T(8,128)(2,1)} %param.7), channel_id=1, source_target_pairs={{0,8},{8,16},{16,24},{24,0},{32,40},{40,48},{48,56},{56,32},{64,72... | collective-permute-start | bytes 786440 | tf_op jit(solution)/shard_map/ppermute | solution.py:22
  8.2 9.5 %collective-permute-start.3 = (bf16[64,2048]{1,0:T(8,128)(2,1)}, bf16[64,2048]{1,0:T(8,128)(2,1)S(1)}, u32[]{:S(2)}, u32[]{:S(2)}) collective-permute-start(bf16[64,2048]{1,0:T(8,128)(2,1)} %param.7), channel_id=1, source_target_pairs={{0,24},{8,0},{16,8},{24,16},{32,56},{40,32},{48,40},{56,48},{64,88... | collective-permute-start | bytes 786440 | tf_op jit(solution)/shard_map/ppermute | solution.py:22
  11.9 15.8 %collective-permute-start.7 = (bf16[256,1024]{1,0:T(8,128)(2,1)S(1)}, bf16[256,1024]{1,0:T(8,128)(2,1)S(1)}, u32[]{:S(2)}, u32[]{:S(2)}) collective-permute-start(bf16[256,1024]{1,0:T(8,128)(2,1)S(1)} %constant_dynamic-update-slice_fusion), channel_id=1, source_target_pairs={{0,2},{1,3},{2,4},{3,5},{4,6},{5,7},{6,0},{7,1},{8,10},{9,11},{10,... | collective-permute-start | bytes 1572872 | tf_op jit(solution)/shard_map/ppermute | solution.py:27
  15.9 8.6 %collective-permute-start.6 = (bf16[64,2048]{1,0:T(8,128)(2,1)}, bf16[64,2048]{1,0:T(8,128)(2,1)S(1)}, u32[]{:S(2)}, u32[]{:S(2)}) collective-permute-start(bf16[64,2048]{1,0:T(8,128)(2,1)} %param.7), channel_id=1, source_target_pairs={{0,16},{8,24},{16,0},{24,8},{32,48},{40,56},{48,32},{56,40},{64,80... | collective-permute-start | bytes 786440 | tf_op jit(solution)/shard_map/ppermute | solution.py:22
  17.7 10.0 %collective-permute-start.4 = (bf16[64,2304]{1,0:T(8,128)(2,1)S(1)}, bf16[64,2304]{1,0:T(8,128)(2,1)S(1)}, u32[]{:S(2)}, u32[]{:S(2)}) collective-permute-start(bf16[64,2304]{1,0:T(8,128)(2,1)S(1)} %collective-permute-done), channel_id=1, source_target_pairs={{0,32},{8,40},{16,48},{24,56},{32,64},{40,72},{48,80},{56,88},{64,... | collective-permute-start | bytes 884744 | tf_op jit(solution)/shard_map/ppermute | solution.py:22
  17.8 9.9 %collective-permute-start.5 = (bf16[64,2304]{1,0:T(8,128)(2,1)S(1)}, bf16[64,2304]{1,0:T(8,128)(2,1)S(1)}, u32[]{:S(2)}, u32[]{:S(2)}) collective-permute-start(bf16[64,2304]{1,0:T(8,128)(2,1)S(1)} %collective-permute-done.1), channel_id=1, source_target_pairs={{0,224},{8,232},{16,240},{24,248},{32,0},{40,8},{48,16},{56,24},{6... | collective-permute-start | bytes 884744 | tf_op jit(solution)/shard_map/ppermute | solution.py:22
  24.4 25.2 %collective-permute-start.13 = (bf16[192,2304]{1,0:T(8,128)(2,1)S(1)}, bf16[192,2304]{1,0:T(8,128)(2,1)S(1)}, u32[]{:S(2)}, u32[]{:S(2)}) collective-permute-start(bf16[192,2304]{1,0:T(8,128)(2,1)S(1)} %pad_maximum_fusion.3), channel_id=1, source_target_pairs={{0,8},{8,16},{16,24},{24,0},{32,40},{40,48},{48,56},{56,32},{64,72... | collective-permute-start | bytes 2654216 | tf_op jit(solution)/shard_map/ppermute | solution.py:22
  24.7 24.9 %collective-permute-start.14 = (bf16[192,2304]{1,0:T(8,128)(2,1)S(1)}, bf16[192,2304]{1,0:T(8,128)(2,1)S(1)}, u32[]{:S(2)}, u32[]{:S(2)}) collective-permute-start(bf16[192,2304]{1,0:T(8,128)(2,1)S(1)} %pad_maximum_fusion.3), channel_id=1, source_target_pairs={{0,24},{8,0},{16,8},{24,16},{32,56},{40,32},{48,40},{56,48},{64,88... | collective-permute-start | bytes 2654216 | tf_op jit(solution)/shard_map/ppermute | solution.py:22
  27.7 6.8 %collective-permute-start.10 = (bf16[64,2304]{1,0:T(8,128)(2,1)S(1)}, bf16[64,2304]{1,0:T(8,128)(2,1)S(1)}, u32[]{:S(2)}, u32[]{:S(2)}) collective-permute-start(bf16[64,2304]{1,0:T(8,128)(2,1)S(1)} %collective-permute-done.5), channel_id=1, source_target_pairs={{0,224},{8,232},{16,240},{24,248},{32,0},{40,8},{48,16},{56,24},{6... | collective-permute-start | bytes 884744 | tf_op jit(solution)/shard_map/ppermute | solution.py:22
  29.2 7.9 %collective-permute-start.9 = (bf16[64,2304]{1,0:T(8,128)(2,1)S(1)}, bf16[64,2304]{1,0:T(8,128)(2,1)S(1)}, u32[]{:S(2)}, u32[]{:S(2)}) collective-permute-start(bf16[64,2304]{1,0:T(8,128)(2,1)S(1)} %collective-permute-done.4), channel_id=1, source_target_pairs={{0,32},{8,40},{16,48},{24,56},{32,64},{40,72},{48,80},{56,88},{64,... | collective-permute-start | bytes 884744 | tf_op jit(solution)/shard_map/ppermute | solution.py:22
  29.8 10.8 %collective-permute-start.8 = (bf16[256,1024]{1,0:T(8,128)(2,1)S(1)}, bf16[256,1024]{1,0:T(8,128)(2,1)S(1)}, u32[]{:S(2)}, u32[]{:S(2)}) collective-permute-start(bf16[256,1024]{1,0:T(8,128)(2,1)S(1)} %constant_dynamic-update-slice_fusion), channel_id=1, source_target_pairs={{0,6},{1,7},{2,0},{3,1},{4,2},{5,3},{6,4},{7,5},{8,14},{9,15},{10,... | collective-permute-start | bytes 1572872 | tf_op jit(solution)/shard_map/ppermute | solution.py:27
  37.2 12.4 %collective-permute-start.11 = (bf16[32,2304]{1,0:T(8,128)(2,1)S(1)}, bf16[32,2304]{1,0:T(8,128)(2,1)S(1)}, u32[]{:S(2)}, u32[]{:S(2)}) collective-permute-start(bf16[32,2304]{1,0:T(8,128)(2,1)S(1)} %slice.24), channel_id=1, source_target_pairs={{0,32},{8,40},{16,48},{24,56},{32,64},{40,72},{48,80},{56,88},{64,... | collective-permute-start | bytes 442376 | tf_op jit(solution)/shard_map/ppermute | solution.py:22
  37.3 12.3 %collective-permute-start.12 = (bf16[32,2304]{1,0:T(8,128)(2,1)S(1)}, bf16[32,2304]{1,0:T(8,128)(2,1)S(1)}, u32[]{:S(2)}, u32[]{:S(2)}) collective-permute-start(bf16[32,2304]{1,0:T(8,128)(2,1)S(1)} %slice.25), channel_id=1, source_target_pairs={{0,224},{8,232},{16,240},{24,248},{32,0},{40,8},{48,16},{56,24},{6... | collective-permute-start | bytes 442376 | tf_op jit(solution)/shard_map/ppermute | solution.py:22
  40.6 21.9 %collective-permute-start.17 = (bf16[256,1024]{1,0:T(8,128)(2,1)S(1)}, bf16[256,1024]{1,0:T(8,128)(2,1)S(1)}, u32[]{:S(2)}, u32[]{:S(2)}) collective-permute-start(bf16[256,1024]{1,0:T(8,128)(2,1)S(1)} %constant_dynamic-update-slice_fusion), channel_id=1, source_target_pairs={{0,4},{1,5},{2,6},{3,7},{4,0},{5,1},{6,2},{7,3},{8,12},{9,13},{10,... | collective-permute-start | bytes 1572872 | tf_op jit(solution)/shard_map/ppermute | solution.py:27
  49.6 18.4 %collective-permute-start.19 = (bf16[256,2048]{1,0:T(8,128)(2,1)S(1)}, bf16[256,2048]{1,0:T(8,128)(2,1)S(1)}, u32[]{:S(2)}, u32[]{:S(2)}) collective-permute-start(bf16[256,2048]{1,0:T(8,128)(2,1)S(1)} %pad_maximum_fusion.2), channel_id=1, source_target_pairs={{0,32},{8,40},{16,48},{24,56},{32,64},{40,72},{48,80},{56,88},{64,... | collective-permute-start | bytes 3145736 | tf_op jit(solution)/shard_map/ppermute | solution.py:22
  49.7 18.3 %collective-permute-start.21 = (bf16[256,2048]{1,0:T(8,128)(2,1)S(1)}, bf16[256,2048]{1,0:T(8,128)(2,1)S(1)}, u32[]{:S(2)}, u32[]{:S(2)}) collective-permute-start(bf16[256,2048]{1,0:T(8,128)(2,1)S(1)} %pad_maximum_fusion.2), channel_id=1, source_target_pairs={{0,224},{8,232},{16,240},{24,248},{32,0},{40,8},{48,16},{56,24},{6... | collective-permute-start | bytes 3145736 | tf_op jit(solution)/shard_map/ppermute | solution.py:22
  53.0 9.6 %collective-permute-start.15 = (bf16[96,2304]{1,0:T(8,128)(2,1)S(1)}, bf16[96,2304]{1,0:T(8,128)(2,1)S(1)}, u32[]{:S(2)}, u32[]{:S(2)}) collective-permute-start(bf16[96,2304]{1,0:T(8,128)(2,1)S(1)} %slice.26), channel_id=1, source_target_pairs={{0,8},{8,16},{16,24},{24,0},{32,40},{40,48},{48,56},{56,32},{64,72... | collective-permute-start | bytes 1327112 | tf_op jit(solution)/shard_map/ppermute | solution.py:22
  53.2 9.4 %collective-permute-start.16 = (bf16[96,2304]{1,0:T(8,128)(2,1)S(1)}, bf16[96,2304]{1,0:T(8,128)(2,1)S(1)}, u32[]{:S(2)}, u32[]{:S(2)}) collective-permute-start(bf16[96,2304]{1,0:T(8,128)(2,1)S(1)} %slice.27), channel_id=1, source_target_pairs={{0,24},{8,0},{16,8},{24,16},{32,56},{40,32},{48,40},{56,48},{64,88... | collective-permute-start | bytes 1327112 | tf_op jit(solution)/shard_map/ppermute | solution.py:22
  62.6 43.6 %collective-permute-start.18 = (bf16[1024,1024]{1,0:T(8,128)(2,1)S(1)}, bf16[1024,1024]{1,0:T(8,128)(2,1)S(1)}, u32[]{:S(2)}, u32[]{:S(2)}) collective-permute-start(bf16[1024,1024]{1,0:T(8,128)(2,1)S(1)} %constant_dynamic-update-slice_fusion.2.mine_ref), channel_id=1, source_target_pairs={{0,1},{1,0},{2,3},{3,2},{4,5},{5,4},{6,7},{7,6},{8,9},{9,8},{10,11... | collective-permute-start | bytes 6291464 | tf_op jit(solution)/shard_map/ppermute | solution.py:27
  62.8 36.4 %collective-permute-start.23 = (bf16[320,2304]{1,0:T(8,128)(2,1)S(1)}, bf16[320,2304]{1,0:T(8,128)(2,1)S(1)}, u32[]{:S(2)}, u32[]{:S(2)}) collective-permute-start(bf16[320,2304]{1,0:T(8,128)(2,1)S(1)} %pad_maximum_fusion), channel_id=1, source_target_pairs={{0,8},{8,16},{16,24},{24,0},{32,40},{40,48},{48,56},{56,32},{64,72... | collective-permute-start | bytes 4423688 | tf_op jit(solution)/shard_map/ppermute | solution.py:22
  63.0 36.2 %collective-permute-start.24 = (bf16[320,2304]{1,0:T(8,128)(2,1)S(1)}, bf16[320,2304]{1,0:T(8,128)(2,1)S(1)}, u32[]{:S(2)}, u32[]{:S(2)}) collective-permute-start(bf16[320,2304]{1,0:T(8,128)(2,1)S(1)} %pad_maximum_fusion), channel_id=1, source_target_pairs={{0,24},{8,0},{16,8},{24,16},{32,56},{40,32},{48,40},{56,48},{64,88... | collective-permute-start | bytes 4423688 | tf_op jit(solution)/shard_map/ppermute | solution.py:22
  68.0 31.2 %collective-permute-start.20 = (bf16[256,2048]{1,0:T(8,128)(2,1)S(1)}, bf16[256,2048]{1,0:T(8,128)(2,1)S(1)}, u32[]{:S(2)}, u32[]{:S(2)}) collective-permute-start(bf16[256,2048]{1,0:T(8,128)(2,1)S(1)} %collective-permute-done.19), channel_id=1, source_target_pairs={{0,32},{8,40},{16,48},{24,56},{32,64},{40,72},{48,80},{56,88},{64,... | collective-permute-start | bytes 3145736 | tf_op jit(solution)/shard_map/ppermute | solution.py:22
  68.0 31.2 %collective-permute-start.22 = (bf16[256,2048]{1,0:T(8,128)(2,1)S(1)}, bf16[256,2048]{1,0:T(8,128)(2,1)S(1)}, u32[]{:S(2)}, u32[]{:S(2)}) collective-permute-start(bf16[256,2048]{1,0:T(8,128)(2,1)S(1)} %collective-permute-done.21), channel_id=1, source_target_pairs={{0,224},{8,232},{16,240},{24,248},{32,0},{40,8},{48,16},{56,24},{6... | collective-permute-start | bytes 3145736 | tf_op jit(solution)/shard_map/ppermute | solution.py:22
  71.4 32.4 %copy-start.1 = (bf16[1088,2304]{1,0:T(8,128)(2,1)}, bf16[1088,2304]{1,0:T(8,128)(2,1)S(1)}, u32[]{:S(2)}) copy-start(bf16[1088,2304]{1,0:T(8,128)(2,1)S(1)} %constant_dynamic-update-slice_fusion.6) | copy-start | bytes 15040516
  99.2 26.3 %collective-permute-start.27 = (bf16[256,2048]{1,0:T(8,128)(2,1)S(1)}, bf16[256,2048]{1,0:T(8,128)(2,1)S(1)}, u32[]{:S(2)}, u32[]{:S(2)}) collective-permute-start(bf16[256,2048]{1,0:T(8,128)(2,1)S(1)} %collective-permute-done.20), channel_id=1, source_target_pairs={{0,32},{8,40},{16,48},{24,56},{32,64},{40,72},{48,80},{56,88},{64,... | collective-permute-start | bytes 3145736 | tf_op jit(solution)/shard_map/ppermute | solution.py:22
  99.3 26.2 %collective-permute-start.28 = (bf16[256,2048]{1,0:T(8,128)(2,1)S(1)}, bf16[256,2048]{1,0:T(8,128)(2,1)S(1)}, u32[]{:S(2)}, u32[]{:S(2)}) collective-permute-start(bf16[256,2048]{1,0:T(8,128)(2,1)S(1)} %collective-permute-done.22), channel_id=1, source_target_pairs={{0,224},{8,232},{16,240},{24,248},{32,0},{40,8},{48,16},{56,24},{6... | collective-permute-start | bytes 3145736 | tf_op jit(solution)/shard_map/ppermute | solution.py:22
  102.6 27.7 %collective-permute-start.25 = (bf16[160,2304]{1,0:T(8,128)(2,1)S(1)}, bf16[160,2304]{1,0:T(8,128)(2,1)S(1)}, u32[]{:S(2)}, u32[]{:S(2)}) collective-permute-start(bf16[160,2304]{1,0:T(8,128)(2,1)S(1)} %slice.28), channel_id=1, source_target_pairs={{0,8},{8,16},{16,24},{24,0},{32,40},{40,48},{48,56},{56,32},{64,72... | collective-permute-start | bytes 2211848 | tf_op jit(solution)/shard_map/ppermute | solution.py:22
  103.8 26.5 %collective-permute-start.26 = (bf16[160,2304]{1,0:T(8,128)(2,1)S(1)}, bf16[160,2304]{1,0:T(8,128)(2,1)S(1)}, u32[]{:S(2)}, u32[]{:S(2)}) collective-permute-start(bf16[160,2304]{1,0:T(8,128)(2,1)S(1)} %slice.29), channel_id=1, source_target_pairs={{0,24},{8,0},{16,8},{24,16},{32,56},{40,32},{48,40},{56,48},{64,88... | collective-permute-start | bytes 2211848 | tf_op jit(solution)/shard_map/ppermute | solution.py:22
  125.5 14.2 %collective-permute-start.29 = (bf16[128,2048]{1,0:T(8,128)(2,1)S(1)}, bf16[128,2048]{1,0:T(8,128)(2,1)S(1)}, u32[]{:S(2)}, u32[]{:S(2)}) collective-permute-start(bf16[128,2048]{1,0:T(8,128)(2,1)S(1)} %slice.30), channel_id=1, source_target_pairs={{0,32},{8,40},{16,48},{24,56},{32,64},{40,72},{48,80},{56,88},{64,... | collective-permute-start | bytes 1572872 | tf_op jit(solution)/shard_map/ppermute | solution.py:22
  125.7 14.0 %collective-permute-start.30 = (bf16[128,2048]{1,0:T(8,128)(2,1)S(1)}, bf16[128,2048]{1,0:T(8,128)(2,1)S(1)}, u32[]{:S(2)}, u32[]{:S(2)}) collective-permute-start(bf16[128,2048]{1,0:T(8,128)(2,1)S(1)} %slice.31), channel_id=1, source_target_pairs={{0,224},{8,232},{16,240},{24,248},{32,0},{40,8},{48,16},{56,24},{6... | collective-permute-start | bytes 1572872 | tf_op jit(solution)/shard_map/ppermute | solution.py:22
  (3 other events, 39.8 us)

commit v6 on v5

--- a/solution.py
+++ b/solution.py
@@ -134,17 +134,18 @@
     below, above = hop(below, 1, 0), hop(above, -1, 0)
     far = jnp.concatenate([*far, below, above])
     below, above, far = together((below, above, far))
-    mine, up = together((mine, up))
+    mine, up, near_left, near_right = together((mine, up, near_left, near_right))
     across = hop_y(mine, 2)
     far = [far, hop(halves(below)[0], 1, 0), hop(halves(above)[1], -1, 0)]
     wide = jnp.concatenate([wide, left, right, opposite])
-    far, wide, near_left, near_right = together((far, wide, near_left, near_right))
-    near_halves = [hop(halves(near_left)[0], 0, 1), hop(halves(near_right)[1], 0, -1)]
+    far, wide = together((far, wide))
     far = jnp.concatenate(far)
-    far, near_halves, across = together((far, near_halves, across))
+    far, near_left, near_right = together((far, near_left, near_right))
     far_left, far_right = hop(far, 0, 1), hop(far, 0, -1)
     below, above = hop(wide, 1, 0), hop(wide, -1, 0)
     wide_first = [wide, below, above]
+    tall_first = [near, near_left, near_right, far]
+    below, above, tall_first = together((below, above, tall_first))
     mine = jnp.concatenate([mine, down, up, across])
 
     near_rows = {dx: whole(NEAR, dx) for dx in X_ORDER}
@@ -153,29 +154,31 @@
     wide_rows = {dz: [(dz, dx, 0, BLOCK) for dx in X_ORDER] for dz in range(-4, 5)}
     wide_split = parts(wide_rows[4])
     groups = [
-        (sum([near_rows[0], near_rows[-1], near_rows[1], *near_split, far_rows[0]], []), 0),
+        (sum([near_rows[0], near_rows[-1], near_rows[1], far_rows[0]], []), 0),
         (far_rows[-1] + far_rows[1], 0),
-        (far_split[0] + far_split[1], 0),
-        (sum([wide_rows[d] for d in (0, -1, 1, -2, 2)], []), 1),
-        (wide_rows[-3] + wide_rows[3], 1),
+        (near_split[0] + far_split[0] + near_split[1] + far_split[1], 0),
+        (wide_rows[0] + wide_rows[-1] + wide_rows[1], 1),
+        (sum([wide_rows[d] for d in (-2, 2, -3, 3)], []), 1),
         (wide_split[0] + wide_split[1], 1),
     ]
     lefts = arrange(place, (mine, hop_y(mine, 0, 1)), groups)
-    tall_sum = contract(lefts[0], [near, near_left, near_right, *near_halves, far])
+    tall_sum = contract(lefts[0], tall_first)
 
     below, above = hop(below, 1, 0), hop(above, -1, 0)
-    wide_first += [below, above]
+    wide_second = [below, above]
     below, above, far_left, far_right = together((below, above, far_left, far_right))
     wide_sum = contract(lefts[3], wide_first)
     below, above = hop(below, 1, 0), hop(above, -1, 0)
-    far_halves = [hop(halves(far_left)[0], 0, 1), hop(halves(far_right)[1], 0, -1)]
+    first = jnp.concatenate([halves(near_left)[0], halves(far_left)[0]])
+    second = jnp.concatenate([halves(near_right)[1], halves(far_right)[1]])
+    tall_halves = [hop(first, 0, 1), hop(second, 0, -1)]
     below, above, wide_sum = together((below, above, wide_sum))
     wide_halves = [hop(halves(below)[0], 1, 0), hop(halves(above)[1], -1, 0)]
 
     tall_sum = contract(lefts[1], [far_left, far_right], tall_sum)
-    wide_sum = contract(lefts[4], [below, above], wide_sum)
+    wide_sum = contract(lefts[4], [*wide_second, below, above], wide_sum)
     tall_sum, wide_sum = together((tall_sum, wide_sum))
-    qkv = contract(lefts[2], far_halves, tall_sum, dtype=jnp.bfloat16)
+    qkv = contract(lefts[2], tall_halves, tall_sum, dtype=jnp.bfloat16)
     out = contract(lefts[5], wide_halves, wide_sum, dtype=jnp.bfloat16)
     return qkv, out
 

time: 142 us -> 130 us (0.915)
  the two profiles are of different devices: /device:TPU:8 before, /device:TPU:32 now
where the time goes in v6:
time: 130 us; the launch traced here: 129 us
  waiting for transfers between devices  54.4 us (42%)
  starting transfers between devices  41.6 us (32%)
  matrix products  20.3 us (16%)
  local copies, waits for them, and re-layouts  5.6 us (4%)
  Pallas kernels  3.81 us (3%)
  other arithmetic  2.63 us (2%)
    ppermute x25, waiting for transfers between devices, hop(): return lax.ppermute(value, 'row', pairs)  48 us
    ppermute x25, starting transfers between devices, hop(): return lax.ppermute(value, 'row', pairs)  34.2 us
    dot_general x6, matrix products, contract(): jnp.dot(left, jnp.concatenate(grads), preferred_element_type=jnp.float32)  20.3 us
    ppermute x4, starting transfers between devices, hop_y(): return lax.ppermute(value, 'col', pairs)  7.36 us
    ppermute x4, waiting for transfers between devices, hop_y(): return lax.ppermute(value, 'col', pairs)  6.46 us
    pallas_call x1, Pallas kernels, arrange(): pl.pallas_call(functools.partial(arrange_kernel, groups), out_shape=[jax....  3.81 us
    slice x9, local copies, waits for them, and re-layouts, halves(): return (value[:half], value[half:])  3.48 us
  transfers between devices with their start and end apart: 29, of which 19 were waited for; matrix products, arithmetic and copies ran while one was open for 20% of the time, Pallas kernels for 3%

profile of v6, /device:TPU:32, one launch (start us, length us, event | category | flops | bytes accessed | tf_op | source)
XLA Modules:
  0.0 129.3 jit_solution(9785905744572558870)
XLA Ops:
  0.6 2.0 %collective-permute-start = (bf16[64,2304]{1,0:T(8,128)(2,1)}, bf16[64,2304]{1,0:T(8,128)(2,1)S(1)}, u32[]{:S(2)}, u32[]{:S(2)}) collective-permute-start(bf16[64,2304]{1,0:T(8,128)(2,1)} %param.6), channel_id=1, source_target_pairs={{0,32},{8,40},{16,48},{24,56},{32,64},{40,72},{48,80},{56,88},{64,... | collective-permute-start | bytes 884744 | tf_op jit(solution)/shard_map/ppermute | solution.py:22
  4.2 1.7 %collective-permute-start.3 = (bf16[64,2048]{1,0:T(8,128)(2,1)}, bf16[64,2048]{1,0:T(8,128)(2,1)S(1)}, u32[]{:S(2)}, u32[]{:S(2)}) collective-permute-start(bf16[64,2048]{1,0:T(8,128)(2,1)} %param.7), channel_id=1, source_target_pairs={{0,24},{8,0},{16,8},{24,16},{32,56},{40,32},{48,40},{56,48},{64,88... | collective-permute-start | bytes 786440 | tf_op jit(solution)/shard_map/ppermute | solution.py:22
  9.6 2.2 %collective-permute-done.2 = bf16[64,2048]{1,0:T(8,128)(2,1)S(1)} collective-permute-done((bf16[64,2048]{1,0:T(8,128)(2,1)}, bf16[64,2048]{1,0:T(8,128)(2,1)S(1)}, u32[]{:S(2)}, u32[]{:S(2)}) %collective-permute-start.2) | collective-permute-done | bytes 262176 | tf_op jit(solution)/shard_map/ppermute | solution.py:22
  11.8 1.8 %collective-permute-start.6 = (bf16[64,2048]{1,0:T(8,128)(2,1)}, bf16[64,2048]{1,0:T(8,128)(2,1)S(1)}, u32[]{:S(2)}, u32[]{:S(2)}) collective-permute-start(bf16[64,2048]{1,0:T(8,128)(2,1)} %param.7), channel_id=1, source_target_pairs={{0,16},{8,24},{16,0},{24,8},{32,48},{40,56},{48,32},{56,40},{64,80... | collective-permute-start | bytes 786440 | tf_op jit(solution)/shard_map/ppermute | solution.py:22
  13.6 2.0 %collective-permute-start.4 = (bf16[64,2304]{1,0:T(8,128)(2,1)S(1)}, bf16[64,2304]{1,0:T(8,128)(2,1)S(1)}, u32[]{:S(2)}, u32[]{:S(2)}) collective-permute-start(bf16[64,2304]{1,0:T(8,128)(2,1)S(1)} %collective-permute-done), channel_id=1, source_target_pairs={{0,32},{8,40},{16,48},{24,56},{32,64},{40,72},{48,80},{56,88},{64,... | collective-permute-start | bytes 884744 | tf_op jit(solution)/shard_map/ppermute | solution.py:22
  15.6 2.3 %collective-permute-start.5 = (bf16[64,2304]{1,0:T(8,128)(2,1)S(1)}, bf16[64,2304]{1,0:T(8,128)(2,1)S(1)}, u32[]{:S(2)}, u32[]{:S(2)}) collective-permute-start(bf16[64,2304]{1,0:T(8,128)(2,1)S(1)} %collective-permute-done.1), channel_id=1, source_target_pairs={{0,224},{8,232},{16,240},{24,248},{32,0},{40,8},{48,16},{56,24},{6... | collective-permute-start | bytes 884744 | tf_op jit(solution)/shard_map/ppermute | solution.py:22
  24.0 2.7 %collective-permute-start.13 = (bf16[64,2304]{1,0:T(8,128)(2,1)S(1)}, bf16[64,2304]{1,0:T(8,128)(2,1)S(1)}, u32[]{:S(2)}, u32[]{:S(2)}) collective-permute-start(bf16[64,2304]{1,0:T(8,128)(2,1)S(1)} %collective-permute-done.4), channel_id=1, source_target_pairs={{0,32},{8,40},{16,48},{24,56},{32,64},{40,72},{48,80},{56,88},{64,... | collective-permute-start | bytes 884744 | tf_op jit(solution)/shard_map/ppermute | solution.py:22
  28.7 3.0 %collective-permute-start.8 = (bf16[256,1024]{1,0:T(8,128)(2,1)S(1)}, bf16[256,1024]{1,0:T(8,128)(2,1)S(1)}, u32[]{:S(2)}, u32[]{:S(2)}) collective-permute-start(bf16[256,1024]{1,0:T(8,128)(2,1)S(1)} %constant_dynamic-update-slice_fusion), channel_id=1, source_target_pairs={{0,6},{1,7},{2,0},{3,1},{4,2},{5,3},{6,4},{7,5},{8,14},{9,15},{10,... | collective-permute-start | bytes 1572872 | tf_op jit(solution)/shard_map/ppermute | solution.py:27
  31.7 2.6 %collective-permute-done.14 = bf16[64,2304]{1,0:T(8,128)(2,1)S(1)} collective-permute-done((bf16[64,2304]{1,0:T(8,128)(2,1)S(1)}, bf16[64,2304]{1,0:T(8,128)(2,1)S(1)}, u32[]{:S(2)}, u32[]{:S(2)}) %collective-permute-start.14) | collective-permute-done | bytes 294944 | tf_op jit(solution)/shard_map/ppermute | solution.py:22
  34.5 2.1 %collective-permute-start.15 = (bf16[32,2304]{1,0:T(8,128)(2,1)S(1)}, bf16[32,2304]{1,0:T(8,128)(2,1)S(1)}, u32[]{:S(2)}, u32[]{:S(2)}) collective-permute-start(bf16[32,2304]{1,0:T(8,128)(2,1)S(1)} %slice.24), channel_id=1, source_target_pairs={{0,32},{8,40},{16,48},{24,56},{32,64},{40,72},{48,80},{56,88},{64,... | collective-permute-start | bytes 442376 | tf_op jit(solution)/shard_map/ppermute | solution.py:22
  36.8 2.9 %collective-permute-done.15 = bf16[32,2304]{1,0:T(8,128)(2,1)S(1)} collective-permute-done((bf16[32,2304]{1,0:T(8,128)(2,1)S(1)}, bf16[32,2304]{1,0:T(8,128)(2,1)S(1)}, u32[]{:S(2)}, u32[]{:S(2)}) %collective-permute-start.15) | collective-permute-done | bytes 147488 | tf_op jit(solution)/shard_map/ppermute | solution.py:22
  39.7 2.8 %collective-permute-done.16 = bf16[32,2304]{1,0:T(8,128)(2,1)S(1)} collective-permute-done((bf16[32,2304]{1,0:T(8,128)(2,1)S(1)}, bf16[32,2304]{1,0:T(8,128)(2,1)S(1)}, u32[]{:S(2)}, u32[]{:S(2)}) %collective-permute-start.16) | collective-permute-done | bytes 147488 | tf_op jit(solution)/shard_map/ppermute | solution.py:22
  45.6 2.6 %collective-permute-done.9 = bf16[192,2304]{1,0:T(8,128)(2,1)} collective-permute-done((bf16[192,2304]{1,0:T(8,128)(2,1)S(1)}, bf16[192,2304]{1,0:T(8,128)(2,1)}, u32[]{:S(2)}, u32[]{:S(2)}) %collective-permute-start.9) | collective-permute-done | bytes 884768 | tf_op jit(solution)/shard_map/ppermute | solution.py:22
  48.2 2.6 %collective-permute-start.11 = (bf16[256,1024]{1,0:T(8,128)(2,1)S(1)}, bf16[256,1024]{1,0:T(8,128)(2,1)S(1)}, u32[]{:S(2)}, u32[]{:S(2)}) collective-permute-start(bf16[256,1024]{1,0:T(8,128)(2,1)S(1)} %constant_dynamic-update-slice_fusion), channel_id=1, source_target_pairs={{0,4},{1,5},{2,6},{3,7},{4,0},{5,1},{6,2},{7,3},{8,12},{9,13},{10,... | collective-permute-start | bytes 1572872 | tf_op jit(solution)/shard_map/ppermute | solution.py:27
  52.0 3.2 %collective-permute-start.22 = (bf16[320,2304]{1,0:T(8,128)(2,1)}, bf16[320,2304]{1,0:T(8,128)(2,1)}, u32[]{:S(2)}, u32[]{:S(2)}) collective-permute-start(bf16[320,2304]{1,0:T(8,128)(2,1)} %pad_maximum_fusion), channel_id=1, source_target_pairs={{0,24},{8,0},{16,8},{24,16},{32,56},{40,32},{48,40},{56,48},{64,88... | collective-permute-start | bytes 4423688 | tf_op jit(solution)/shard_map/ppermute | solution.py:22
  55.4 4.7 %collective-permute-done.11 = bf16[256,1024]{1,0:T(8,128)(2,1)S(1)} collective-permute-done((bf16[256,1024]{1,0:T(8,128)(2,1)S(1)}, bf16[256,1024]{1,0:T(8,128)(2,1)S(1)}, u32[]{:S(2)}, u32[]{:S(2)}) %collective-permute-start.11) | collective-permute-done | bytes 524320 | tf_op jit(solution)/shard_map/ppermute | solution.py:27
  60.3 2.0 %collective-permute-done.17 = bf16[256,2048]{1,0:T(8,128)(2,1)} collective-permute-done((bf16[256,2048]{1,0:T(8,128)(2,1)S(1)}, bf16[256,2048]{1,0:T(8,128)(2,1)}, u32[]{:S(2)}, u32[]{:S(2)}) %collective-permute-start.17) | collective-permute-done | bytes 1048608 | tf_op jit(solution)/shard_map/ppermute | solution.py:22
  62.2 2.3 %collective-permute-done.18 = bf16[256,2048]{1,0:T(8,128)(2,1)} collective-permute-done((bf16[256,2048]{1,0:T(8,128)(2,1)S(1)}, bf16[256,2048]{1,0:T(8,128)(2,1)}, u32[]{:S(2)}, u32[]{:S(2)}) %collective-permute-start.18) | collective-permute-done | bytes 1048608 | tf_op jit(solution)/shard_map/ppermute | solution.py:22
  67.7 15.7 %collective-permute-done.21 = bf16[320,2304]{1,0:T(8,128)(2,1)} collective-permute-done((bf16[320,2304]{1,0:T(8,128)(2,1)}, bf16[320,2304]{1,0:T(8,128)(2,1)}, u32[]{:S(2)}, u32[]{:S(2)}) %collective-permute-start.21) | collective-permute-done | bytes 1474592 | tf_op jit(solution)/shard_map/ppermute | solution.py:22
  83.4 3.7 %collective-permute-done.19 = bf16[256,2048]{1,0:T(8,128)(2,1)} collective-permute-done((bf16[256,2048]{1,0:T(8,128)(2,1)}, bf16[256,2048]{1,0:T(8,128)(2,1)}, u32[]{:S(2)}, u32[]{:S(2)}) %collective-permute-start.19) | collective-permute-done | bytes 1048608 | tf_op jit(solution)/shard_map/ppermute | solution.py:22
  87.1 3.0 %collective-permute-start.25 = (bf16[256,2048]{1,0:T(8,128)(2,1)}, bf16[256,2048]{1,0:T(8,128)(2,1)S(1)}, u32[]{:S(2)}, u32[]{:S(2)}) collective-permute-start(bf16[256,2048]{1,0:T(8,128)(2,1)} %collective-permute-done.19), channel_id=1, source_target_pairs={{0,32},{8,40},{16,48},{24,56},{32,64},{40,72},{48,80},{56,88},{64,... | collective-permute-start | bytes 3145736 | tf_op jit(solution)/shard_map/ppermute | solution.py:22
  92.7 3.3 %collective-permute-start.24 = (bf16[256,2304]{1,0:T(8,128)(2,1)S(1)}, bf16[256,2304]{1,0:T(8,128)(2,1)S(1)}, u32[]{:S(2)}, u32[]{:S(2)}) collective-permute-start(bf16[256,2304]{1,0:T(8,128)(2,1)S(1)} %pad_maximum_fusion.3), channel_id=1, source_target_pairs={{0,24},{8,0},{16,8},{24,16},{32,56},{40,32},{48,40},{56,48},{64,88... | collective-permute-start | bytes 3538952 | tf_op jit(solution)/shard_map/ppermute | solution.py:22
  96.1 3.8 %shard_map.59 = (bf16[512,896]{1,0:T(8,128)(2,1)S(1)}, bf16[512,640]{1,0:T(8,128)(2,1)S(1)}, bf16[512,512]{1,0:T(8,128)(2,1)S(1)}, bf16[512,768]{1,0:T(8,128)(2,...) custom-call(s32[4]{0:T(128)S(1)} %pad_add_fusion.place_ref, ...), custom_call_target="tpu_custom_call" | custom-call | bytes 12582912 | tf_op jit(solution)/shard_map/pallas_call | solution.py:71
  99.9 4.3 %fusion.9 = f32[512,2304]{1,0:T(8,128)S(1)} fusion(bf16[512,896]{1,0:T(8,128)(2,1)S(1)} %get-tuple-element.79, bf16[320,2304]{1,0:T(8,128)(2,1)} %pad_maximum_fusion, bf16[192,2304]{1,0:T(8,128)(2,1)S(1)} %copy-done.1, bf16[192,2304]{1,0:T(8,128)(2,1)} %collective-permute-done.9, bf16[192,2304]{1,0:T(8,128)(2,1)S(1)} %copy-done.5), kind=kOutput, calls=%fused_computation.12 | convolution fusion | flops 2130444288 | bytes 9764864 | tf_op jit(solution)/shard_map/dot_general | solution.py:88
  104.2 4.0 %convolution_add_fusion.1 = f32[512,2304]{1,0:T(8,128)S(1)} fusion(f32[512,2304]{1,0:T(8,128)S(1)} %fusion.9, bf16[512,640]{1,0:T(8,128)(2,1)S(1)} %get-tuple-element.78, bf16[320,2304]{1,0:T(8,128)(2,1)} %collective-permute-done.22, bf16[320,2304]{1,0:T(8,128)(2,1)} %collective-permute-done.21), kind=kOutput, calls=%fused_computation.1 | convolution fusion | flops 1517027328 | bytes 13041664 | tf_op jit(solution)/shard_map/dot_general | solution.py:88
  108.2 3.4 %fusion.20 = f32[512,2048]{1,0:T(8,128)S(1)} fusion(bf16[512,768]{1,0:T(8,128)(2,1)S(1)} %get-tuple-element.87, bf16[256,2048]{1,0:T(8,128)(2,1)} %collective-permute-done.18, bf16[256,2048]{1,0:T(8,128)(2,1)} %collective-permute-done.17, bf16[256,2048]{1,0:T(8,128)(2,1)S(1)} %copy-done.3), kind=kOutput, calls=%fused_computation.21 | convolution fusion | flops 1620049920 | bytes 8126464 | tf_op jit(solution)/shard_map/dot_general | solution.py:88
  111.7 2.7 %collective-permute-done.26 = bf16[256,2048]{1,0:T(8,128)(2,1)S(1)} collective-permute-done((bf16[256,2048]{1,0:T(8,128)(2,1)}, bf16[256,2048]{1,0:T(8,128)(2,1)S(1)}, u32[]{:S(2)}, u32[]{:S(2)}) %collective-permute-start.26) | collective-permute-done | bytes 1048608 | tf_op jit(solution)/shard_map/ppermute | solution.py:22
  114.5 1.8 %collective-permute-start.27 = (bf16[128,2048]{1,0:T(8,128)(2,1)S(1)}, bf16[128,2048]{1,0:T(8,128)(2,1)S(1)}, u32[]{:S(2)}, u32[]{:S(2)}) collective-permute-start(bf16[128,2048]{1,0:T(8,128)(2,1)S(1)} %slice.30), channel_id=1, source_target_pairs={{0,32},{8,40},{16,48},{24,56},{32,64},{40,72},{48,80},{56,88},{64,... | collective-permute-start | bytes 1572872 | tf_op jit(solution)/shard_map/ppermute | solution.py:22
  116.8 3.8 %fusion.17 = f32[512,2048]{1,0:T(8,128)S(1)} fusion(f32[512,2048]{1,0:T(8,128)S(1)} %fusion.20, bf16[512,1024]{1,0:T(8,128)(2,1)S(1)} %get-tuple-element.84, bf16[256,2048]{1,0:T(8,128)(2,1)S(1)} %collective-permute-done.26, bf16[256,2048]{1,0:T(8,128)(2,1)S(1)} %collective-permute-done.25, bf16[256,2048]{1,0:T(8,128)(2,1)} %collective-permute-done.20, ...), kind=kOutput, calls=%fused_computation.20 | convolution fusion | flops 2165309440 | bytes 13631488 | tf_op jit(solution)/shard_map/dot_general | solution.py:88
  120.6 2.8 %fusion = bf16[512,2304]{1,0:T(8,128)(2,1)} fusion(f32[512,2304]{1,0:T(8,128)S(1)} %convolution_add_fusion.1, bf16[512,512]{1,0:T(8,128)(2,1)S(1)} %get-tuple-element.56, bf16[256,2304]{1,0:T(8,128)(2,1)S(1)} %collective-permute-done.24, bf16[256,2304]{1,0:T(8,128)(2,1)S(1)} %collective-permute-done.23), kind=kOutput, calls=%fused_computation.2 | convolution fusion | flops 1215037440 | bytes 9961472 | tf_op jit(solution)/shard_map/dot_general | solution.py:88
  123.4 2.3 %collective-permute-done.27 = bf16[128,2048]{1,0:T(8,128)(2,1)S(1)} collective-permute-done((bf16[128,2048]{1,0:T(8,128)(2,1)S(1)}, bf16[128,2048]{1,0:T(8,128)(2,1)S(1)}, u32[]{:S(2)}, u32[]{:S(2)}) %collective-permute-start.27) | collective-permute-done | bytes 524320 | tf_op jit(solution)/shard_map/ppermute | solution.py:22
  127.3 2.0 %add_convert_fusion = bf16[512,2048]{1,0:T(8,128)(2,1)} fusion(f32[512,2048]{1,0:T(8,128)S(1)} %fusion.17, bf16[512,256]{1,0:T(8,128)(2,1)S(1)} %get-tuple-element.92, bf16[128,2048]{1,0:T(8,128)(2,1)S(1)} %collective-permute-done.28, bf16[128,2048]{1,0:T(8,128)(2,1)S(1)} %collective-permute-done.27), kind=kOutput, calls=%fused_computation.11 | convolution fusion | flops 541065216 | bytes 7602176 | tf_op jit(solution)/shard_map/dot_general | solution.py:88
  (69 shorter events, 26.1 us)
Async XLA Ops:
  0.6 13.0 %collective-permute-start = (bf16[64,2304]{1,0:T(8,128)(2,1)}, bf16[64,2304]{1,0:T(8,128)(2,1)S(1)}, u32[]{:S(2)}, u32[]{:S(2)}) collective-permute-start(bf16[64,2304]{1,0:T(8,128)(2,1)} %param.6), channel_id=1, source_target_pairs={{0,32},{8,40},{16,48},{24,56},{32,64},{40,72},{48,80},{56,88},{64,... | collective-permute-start | bytes 884744 | tf_op jit(solution)/shard_map/ppermute | solution.py:22
  2.6 11.0 %collective-permute-start.1 = (bf16[64,2304]{1,0:T(8,128)(2,1)}, bf16[64,2304]{1,0:T(8,128)(2,1)S(1)}, u32[]{:S(2)}, u32[]{:S(2)}) collective-permute-start(bf16[64,2304]{1,0:T(8,128)(2,1)} %param.6), channel_id=1, source_target_pairs={{0,224},{8,232},{16,240},{24,248},{32,0},{40,8},{48,16},{56,24},{6... | collective-permute-start | bytes 884744 | tf_op jit(solution)/shard_map/ppermute | solution.py:22
  2.7 9.1 %collective-permute-start.2 = (bf16[64,2048]{1,0:T(8,128)(2,1)}, bf16[64,2048]{1,0:T(8,128)(2,1)S(1)}, u32[]{:S(2)}, u32[]{:S(2)}) collective-permute-start(bf16[64,2048]{1,0:T(8,128)(2,1)} %param.7), channel_id=1, source_target_pairs={{0,8},{8,16},{16,24},{24,0},{32,40},{40,48},{48,56},{56,32},{64,72... | collective-permute-start | bytes 786440 | tf_op jit(solution)/shard_map/ppermute | solution.py:22
  4.2 9.4 %collective-permute-start.3 = (bf16[64,2048]{1,0:T(8,128)(2,1)}, bf16[64,2048]{1,0:T(8,128)(2,1)S(1)}, u32[]{:S(2)}, u32[]{:S(2)}) collective-permute-start(bf16[64,2048]{1,0:T(8,128)(2,1)} %param.7), channel_id=1, source_target_pairs={{0,24},{8,0},{16,8},{24,16},{32,56},{40,32},{48,40},{56,48},{64,88... | collective-permute-start | bytes 786440 | tf_op jit(solution)/shard_map/ppermute | solution.py:22
  7.9 28.7 %copy-start.6 = (bf16[64,2048]{1,0:T(8,128)(2,1)S(1)}, bf16[64,2048]{1,0:T(8,128)(2,1)}, u32[]{:S(2)}) copy-start(bf16[64,2048]{1,0:T(8,128)(2,1)} %param.7) | copy-start | bytes 786436
  7.9 14.1 %collective-permute-start.7 = (bf16[256,1024]{1,0:T(8,128)(2,1)S(1)}, bf16[256,1024]{1,0:T(8,128)(2,1)S(1)}, u32[]{:S(2)}, u32[]{:S(2)}) collective-permute-start(bf16[256,1024]{1,0:T(8,128)(2,1)S(1)} %constant_dynamic-update-slice_fusion), channel_id=1, source_target_pairs={{0,2},{1,3},{2,4},{3,5},{4,6},{5,7},{6,0},{7,1},{8,10},{9,11},{10,... | collective-permute-start | bytes 1572872 | tf_op jit(solution)/shard_map/ppermute | solution.py:27
  11.8 8.4 %collective-permute-start.6 = (bf16[64,2048]{1,0:T(8,128)(2,1)}, bf16[64,2048]{1,0:T(8,128)(2,1)S(1)}, u32[]{:S(2)}, u32[]{:S(2)}) collective-permute-start(bf16[64,2048]{1,0:T(8,128)(2,1)} %param.7), channel_id=1, source_target_pairs={{0,16},{8,24},{16,0},{24,8},{32,48},{40,56},{48,32},{56,40},{64,80... | collective-permute-start | bytes 786440 | tf_op jit(solution)/shard_map/ppermute | solution.py:22
  13.6 9.8 %collective-permute-start.4 = (bf16[64,2304]{1,0:T(8,128)(2,1)S(1)}, bf16[64,2304]{1,0:T(8,128)(2,1)S(1)}, u32[]{:S(2)}, u32[]{:S(2)}) collective-permute-start(bf16[64,2304]{1,0:T(8,128)(2,1)S(1)} %collective-permute-done), channel_id=1, source_target_pairs={{0,32},{8,40},{16,48},{24,56},{32,64},{40,72},{48,80},{56,88},{64,... | collective-permute-start | bytes 884744 | tf_op jit(solution)/shard_map/ppermute | solution.py:22
  15.6 8.4 %collective-permute-start.5 = (bf16[64,2304]{1,0:T(8,128)(2,1)S(1)}, bf16[64,2304]{1,0:T(8,128)(2,1)S(1)}, u32[]{:S(2)}, u32[]{:S(2)}) collective-permute-start(bf16[64,2304]{1,0:T(8,128)(2,1)S(1)} %collective-permute-done.1), channel_id=1, source_target_pairs={{0,224},{8,232},{16,240},{24,248},{32,0},{40,8},{48,16},{56,24},{6... | collective-permute-start | bytes 884744 | tf_op jit(solution)/shard_map/ppermute | solution.py:22
  24.0 7.7 %collective-permute-start.13 = (bf16[64,2304]{1,0:T(8,128)(2,1)S(1)}, bf16[64,2304]{1,0:T(8,128)(2,1)S(1)}, u32[]{:S(2)}, u32[]{:S(2)}) collective-permute-start(bf16[64,2304]{1,0:T(8,128)(2,1)S(1)} %collective-permute-done.4), channel_id=1, source_target_pairs={{0,32},{8,40},{16,48},{24,56},{32,64},{40,72},{48,80},{56,88},{64,... | collective-permute-start | bytes 884744 | tf_op jit(solution)/shard_map/ppermute | solution.py:22
  26.7 7.7 %collective-permute-start.14 = (bf16[64,2304]{1,0:T(8,128)(2,1)S(1)}, bf16[64,2304]{1,0:T(8,128)(2,1)S(1)}, u32[]{:S(2)}, u32[]{:S(2)}) collective-permute-start(bf16[64,2304]{1,0:T(8,128)(2,1)S(1)} %collective-permute-done.5), channel_id=1, source_target_pairs={{0,224},{8,232},{16,240},{24,248},{32,0},{40,8},{48,16},{56,24},{6... | collective-permute-start | bytes 884744 | tf_op jit(solution)/shard_map/ppermute | solution.py:22
  26.7 19.0 %collective-permute-start.10 = (bf16[192,2304]{1,0:T(8,128)(2,1)S(1)}, bf16[192,2304]{1,0:T(8,128)(2,1)S(1)}, u32[]{:S(2)}, u32[]{:S(2)}) collective-permute-start(bf16[192,2304]{1,0:T(8,128)(2,1)S(1)} %pad_maximum_fusion.5), channel_id=1, source_target_pairs={{0,24},{8,0},{16,8},{24,16},{32,56},{40,32},{48,40},{56,48},{64,88... | collective-permute-start | bytes 2654216 | tf_op jit(solution)/shard_map/ppermute | solution.py:22
  27.9 20.3 %collective-permute-start.9 = (bf16[192,2304]{1,0:T(8,128)(2,1)S(1)}, bf16[192,2304]{1,0:T(8,128)(2,1)}, u32[]{:S(2)}, u32[]{:S(2)}) collective-permute-start(bf16[192,2304]{1,0:T(8,128)(2,1)S(1)} %pad_maximum_fusion.5), channel_id=1, source_target_pairs={{0,8},{8,16},{16,24},{24,0},{32,40},{40,48},{48,56},{56,32},{64,72... | collective-permute-start | bytes 2654216 | tf_op jit(solution)/shard_map/ppermute | solution.py:22
  28.7 15.8 %collective-permute-start.8 = (bf16[256,1024]{1,0:T(8,128)(2,1)S(1)}, bf16[256,1024]{1,0:T(8,128)(2,1)S(1)}, u32[]{:S(2)}, u32[]{:S(2)}) collective-permute-start(bf16[256,1024]{1,0:T(8,128)(2,1)S(1)} %constant_dynamic-update-slice_fusion), channel_id=1, source_target_pairs={{0,6},{1,7},{2,0},{3,1},{4,2},{5,3},{6,4},{7,5},{8,14},{9,15},{10,... | collective-permute-start | bytes 1572872 | tf_op jit(solution)/shard_map/ppermute | solution.py:27
  34.5 5.2 %collective-permute-start.15 = (bf16[32,2304]{1,0:T(8,128)(2,1)S(1)}, bf16[32,2304]{1,0:T(8,128)(2,1)S(1)}, u32[]{:S(2)}, u32[]{:S(2)}) collective-permute-start(bf16[32,2304]{1,0:T(8,128)(2,1)S(1)} %slice.24), channel_id=1, source_target_pairs={{0,32},{8,40},{16,48},{24,56},{32,64},{40,72},{48,80},{56,88},{64,... | collective-permute-start | bytes 442376 | tf_op jit(solution)/shard_map/ppermute | solution.py:22
  36.6 6.0 %collective-permute-start.16 = (bf16[32,2304]{1,0:T(8,128)(2,1)S(1)}, bf16[32,2304]{1,0:T(8,128)(2,1)S(1)}, u32[]{:S(2)}, u32[]{:S(2)}) collective-permute-start(bf16[32,2304]{1,0:T(8,128)(2,1)S(1)} %slice.25), channel_id=1, source_target_pairs={{0,224},{8,232},{16,240},{24,248},{32,0},{40,8},{48,16},{56,24},{6... | collective-permute-start | bytes 442376 | tf_op jit(solution)/shard_map/ppermute | solution.py:22
  42.5 19.7 %collective-permute-start.17 = (bf16[256,2048]{1,0:T(8,128)(2,1)S(1)}, bf16[256,2048]{1,0:T(8,128)(2,1)}, u32[]{:S(2)}, u32[]{:S(2)}) collective-permute-start(bf16[256,2048]{1,0:T(8,128)(2,1)S(1)} %pad_maximum_fusion.4), channel_id=1, source_target_pairs={{0,32},{8,40},{16,48},{24,56},{32,64},{40,72},{48,80},{56,88},{64,... | collective-permute-start | bytes 3145736 | tf_op jit(solution)/shard_map/ppermute | solution.py:22
  44.2 20.4 %collective-permute-start.18 = (bf16[256,2048]{1,0:T(8,128)(2,1)S(1)}, bf16[256,2048]{1,0:T(8,128)(2,1)}, u32[]{:S(2)}, u32[]{:S(2)}) collective-permute-start(bf16[256,2048]{1,0:T(8,128)(2,1)S(1)} %pad_maximum_fusion.4), channel_id=1, source_target_pairs={{0,224},{8,232},{16,240},{24,248},{32,0},{40,8},{48,16},{56,24},{6... | collective-permute-start | bytes 3145736 | tf_op jit(solution)/shard_map/ppermute | solution.py:22
  45.6 22.1 %copy-start = (bf16[192,2304]{1,0:T(8,128)(2,1)}, bf16[192,2304]{1,0:T(8,128)(2,1)S(1)}, u32[]{:S(2)}) copy-start(bf16[192,2304]{1,0:T(8,128)(2,1)S(1)} %collective-permute-done.10) | copy-start | bytes 2654212
  48.2 11.9 %collective-permute-start.11 = (bf16[256,1024]{1,0:T(8,128)(2,1)S(1)}, bf16[256,1024]{1,0:T(8,128)(2,1)S(1)}, u32[]{:S(2)}, u32[]{:S(2)}) collective-permute-start(bf16[256,1024]{1,0:T(8,128)(2,1)S(1)} %constant_dynamic-update-slice_fusion), channel_id=1, source_target_pairs={{0,4},{1,5},{2,6},{3,7},{4,0},{5,1},{6,2},{7,3},{8,12},{9,13},{10,... | collective-permute-start | bytes 1572872 | tf_op jit(solution)/shard_map/ppermute | solution.py:27
  52.0 31.4 %collective-permute-start.21 = (bf16[320,2304]{1,0:T(8,128)(2,1)}, bf16[320,2304]{1,0:T(8,128)(2,1)}, u32[]{:S(2)}, u32[]{:S(2)}) collective-permute-start(bf16[320,2304]{1,0:T(8,128)(2,1)} %pad_maximum_fusion), channel_id=1, source_target_pairs={{0,8},{8,16},{16,24},{24,0},{32,40},{40,48},{48,56},{56,32},{64,72... | collective-permute-start | bytes 4423688 | tf_op jit(solution)/shard_map/ppermute | solution.py:22
  52.0 31.4 %collective-permute-start.22 = (bf16[320,2304]{1,0:T(8,128)(2,1)}, bf16[320,2304]{1,0:T(8,128)(2,1)}, u32[]{:S(2)}, u32[]{:S(2)}) collective-permute-start(bf16[320,2304]{1,0:T(8,128)(2,1)} %pad_maximum_fusion), channel_id=1, source_target_pairs={{0,24},{8,0},{16,8},{24,16},{32,56},{40,32},{48,40},{56,48},{64,88... | collective-permute-start | bytes 4423688 | tf_op jit(solution)/shard_map/ppermute | solution.py:22
  60.2 35.9 %collective-permute-start.12 = (bf16[1024,1024]{1,0:T(8,128)(2,1)S(1)}, bf16[1024,1024]{1,0:T(8,128)(2,1)}, u32[]{:S(2)}, u32[]{:S(2)}) collective-permute-start(bf16[1024,1024]{1,0:T(8,128)(2,1)S(1)} %constant_dynamic-update-slice_fusion.2.mine_ref), channel_id=1, source_target_pairs={{0,1},{1,0},{2,3},{3,2},{4,5},{5,4},{6,7},{7,6},{8,9},{9,8},{10,11... | collective-permute-start | bytes 6291464 | tf_op jit(solution)/shard_map/ppermute | solution.py:27
  64.6 22.5 %collective-permute-start.19 = (bf16[256,2048]{1,0:T(8,128)(2,1)}, bf16[256,2048]{1,0:T(8,128)(2,1)}, u32[]{:S(2)}, u32[]{:S(2)}) collective-permute-start(bf16[256,2048]{1,0:T(8,128)(2,1)} %collective-permute-done.17), channel_id=1, source_target_pairs={{0,32},{8,40},{16,48},{24,56},{32,64},{40,72},{48,80},{56,88},{64,... | collective-permute-start | bytes 3145736 | tf_op jit(solution)/shard_map/ppermute | solution.py:22
  65.9 21.2 %collective-permute-start.20 = (bf16[256,2048]{1,0:T(8,128)(2,1)}, bf16[256,2048]{1,0:T(8,128)(2,1)}, u32[]{:S(2)}, u32[]{:S(2)}) collective-permute-start(bf16[256,2048]{1,0:T(8,128)(2,1)} %collective-permute-done.18), channel_id=1, source_target_pairs={{0,224},{8,232},{16,240},{24,248},{32,0},{40,8},{48,16},{56,24},{6... | collective-permute-start | bytes 3145736 | tf_op jit(solution)/shard_map/ppermute | solution.py:22
  67.7 24.9 %slice-start = ((bf16[192,2304]{1,0:T(8,128)(2,1)}), bf16[96,2304]{1,0:T(8,128)(2,1)S(1)}, s32[]{:S(2)}) async-start(bf16[192,2304]{1,0:T(8,128)(2,1)} %copy-done), calls=%async_computation | async-start | bytes 884736 | tf_op jit(solution)/shard_map/slice | solution.py:32
  87.1 24.6 %collective-permute-start.25 = (bf16[256,2048]{1,0:T(8,128)(2,1)}, bf16[256,2048]{1,0:T(8,128)(2,1)S(1)}, u32[]{:S(2)}, u32[]{:S(2)}) collective-permute-start(bf16[256,2048]{1,0:T(8,128)(2,1)} %collective-permute-done.19), channel_id=1, source_target_pairs={{0,32},{8,40},{16,48},{24,56},{32,64},{40,72},{48,80},{56,88},{64,... | collective-permute-start | bytes 3145736 | tf_op jit(solution)/shard_map/ppermute | solution.py:22
  90.1 24.4 %collective-permute-start.26 = (bf16[256,2048]{1,0:T(8,128)(2,1)}, bf16[256,2048]{1,0:T(8,128)(2,1)S(1)}, u32[]{:S(2)}, u32[]{:S(2)}) collective-permute-start(bf16[256,2048]{1,0:T(8,128)(2,1)} %collective-permute-done.20), channel_id=1, source_target_pairs={{0,224},{8,232},{16,240},{24,248},{32,0},{40,8},{48,16},{56,24},{6... | collective-permute-start | bytes 3145736 | tf_op jit(solution)/shard_map/ppermute | solution.py:22
  91.4 29.2 %collective-permute-start.23 = (bf16[256,2304]{1,0:T(8,128)(2,1)S(1)}, bf16[256,2304]{1,0:T(8,128)(2,1)S(1)}, u32[]{:S(2)}, u32[]{:S(2)}) collective-permute-start(bf16[256,2304]{1,0:T(8,128)(2,1)S(1)} %pad_maximum_fusion.2), channel_id=1, source_target_pairs={{0,8},{8,16},{16,24},{24,0},{32,40},{40,48},{48,56},{56,32},{64,72... | collective-permute-start | bytes 3538952 | tf_op jit(solution)/shard_map/ppermute | solution.py:22
  92.7 27.8 %collective-permute-start.24 = (bf16[256,2304]{1,0:T(8,128)(2,1)S(1)}, bf16[256,2304]{1,0:T(8,128)(2,1)S(1)}, u32[]{:S(2)}, u32[]{:S(2)}) collective-permute-start(bf16[256,2304]{1,0:T(8,128)(2,1)S(1)} %pad_maximum_fusion.3), channel_id=1, source_target_pairs={{0,24},{8,0},{16,8},{24,16},{32,56},{40,32},{48,40},{56,48},{64,88... | collective-permute-start | bytes 3538952 | tf_op jit(solution)/shard_map/ppermute | solution.py:22
  114.5 11.1 %collective-permute-start.27 = (bf16[128,2048]{1,0:T(8,128)(2,1)S(1)}, bf16[128,2048]{1,0:T(8,128)(2,1)S(1)}, u32[]{:S(2)}, u32[]{:S(2)}) collective-permute-start(bf16[128,2048]{1,0:T(8,128)(2,1)S(1)} %slice.30), channel_id=1, source_target_pairs={{0,32},{8,40},{16,48},{24,56},{32,64},{40,72},{48,80},{56,88},{64,... | collective-permute-start | bytes 1572872 | tf_op jit(solution)/shard_map/ppermute | solution.py:22
  116.4 10.9 %collective-permute-start.28 = (bf16[128,2048]{1,0:T(8,128)(2,1)S(1)}, bf16[128,2048]{1,0:T(8,128)(2,1)S(1)}, u32[]{:S(2)}, u32[]{:S(2)}) collective-permute-start(bf16[128,2048]{1,0:T(8,128)(2,1)S(1)} %slice.31), channel_id=1, source_target_pairs={{0,224},{8,232},{16,240},{24,248},{32,0},{40,8},{48,16},{56,24},{6... | collective-permute-start | bytes 1572872 | tf_op jit(solution)/shard_map/ppermute | solution.py:22
  (5 other events, 54.7 us)

commit v7 on v6

--- a/solution.py
+++ b/solution.py
@@ -120,20 +120,19 @@
     mine = jnp.concatenate([normed_input, attended], axis=1)
 
     below, above = hop(tall, 1, 0), hop(tall, -1, 0)
-    left, right = hop(wide, 0, 1), hop(wide, 0, -1)
-    down = hop_y(mine, 1)
-    below, above, left, right = together((below, above, left, right))
-    opposite = hop(wide, 0, 2)
+    left, right, opposite = hop(wide, 0, 1), hop(wide, 0, -1), hop(wide, 0, 2)
     near = jnp.concatenate([tall, below, above])
     near, opposite = together((near, opposite))
     near_left, near_right = hop(near, 0, 1), hop(near, 0, -1)
     below, above = hop(below, 1, 0), hop(above, -1, 0)
-    below, above, opposite, mine, down = together((below, above, opposite, mine, down))
-    up = hop_y(mine, -1)
+    below, above, left, right = together((below, above, left, right))
     far = [below, above]
     below, above = hop(below, 1, 0), hop(above, -1, 0)
     far = jnp.concatenate([*far, below, above])
+    down = hop_y(mine, 1)
     below, above, far = together((below, above, far))
+    mine, down = together((mine, down))
+    up = hop_y(mine, -1)
     mine, up, near_left, near_right = together((mine, up, near_left, near_right))
     across = hop_y(mine, 2)
     far = [far, hop(halves(below)[0], 1, 0), hop(halves(above)[1], -1, 0)]

time: 130 us -> 131 us (level)
  the two profiles are of different devices: /device:TPU:32 before, /device:TPU:8 now
where the time goes in v7:
time: 131 us; the launch traced here: 128 us
  starting transfers between devices  49.4 us (38%)
  waiting for transfers between devices  45.7 us (35%)
  matrix products  20.2 us (15%)
  local copies, waits for them, and re-layouts  5.49 us (4%)
  Pallas kernels  3.79 us (3%)
  other arithmetic  2.64 us (2%)
    ppermute x25, starting transfers between devices, hop(): return lax.ppermute(value, 'row', pairs)  45 us
    ppermute x25, waiting for transfers between devices, hop(): return lax.ppermute(value, 'row', pairs)  41.9 us
    dot_general x6, matrix products, contract(): jnp.dot(left, jnp.concatenate(grads), preferred_element_type=jnp.float32)  20.2 us
    ppermute x4, starting transfers between devices, hop_y(): return lax.ppermute(value, 'col', pairs)  4.42 us
    ppermute x4, waiting for transfers between devices, hop_y(): return lax.ppermute(value, 'col', pairs)  3.82 us
    pallas_call x1, Pallas kernels, arrange(): pl.pallas_call(functools.partial(arrange_kernel, groups), out_shape=[jax....  3.79 us
  transfers between devices with their start and end apart: 29, of which 10 were waited for; matrix products, arithmetic and copies ran while one was open for 20% of the time, Pallas kernels for 3%

profile of v7, /device:TPU:8, one launch (start us, length us, event | category | flops | bytes accessed | tf_op | source)
XLA Modules:
  0.0 128.2 jit_solution(17736457463880143931)
XLA Ops:
  0.6 5.9 %collective-permute-start.3 = (bf16[64,2304]{1,0:T(8,128)(2,1)}, bf16[64,2304]{1,0:T(8,128)(2,1)S(1)}, u32[]{:S(2)}, u32[]{:S(2)}) collective-permute-start(bf16[64,2304]{1,0:T(8,128)(2,1)} %param.6), channel_id=1, source_target_pairs={{0,224},{8,232},{16,240},{24,248},{32,0},{40,8},{48,16},{56,24},{6... | collective-permute-start | bytes 884744 | tf_op jit(solution)/shard_map/ppermute | solution.py:22
  6.6 6.6 %collective-permute-done.3 = bf16[64,2304]{1,0:T(8,128)(2,1)S(1)} collective-permute-done((bf16[64,2304]{1,0:T(8,128)(2,1)}, bf16[64,2304]{1,0:T(8,128)(2,1)S(1)}, u32[]{:S(2)}, u32[]{:S(2)}) %collective-permute-start.3) | collective-permute-done | bytes 294944 | tf_op jit(solution)/shard_map/ppermute | solution.py:22
  13.1 3.6 %collective-permute-start.10 = (bf16[64,2304]{1,0:T(8,128)(2,1)S(1)}, bf16[64,2304]{1,0:T(8,128)(2,1)S(1)}, u32[]{:S(2)}, u32[]{:S(2)}) collective-permute-start(bf16[64,2304]{1,0:T(8,128)(2,1)S(1)} %collective-permute-done.3), channel_id=1, source_target_pairs={{0,224},{8,232},{16,240},{24,248},{32,0},{40,8},{48,16},{56,24},{6... | collective-permute-start | bytes 884744 | tf_op jit(solution)/shard_map/ppermute | solution.py:22
  16.7 1.5 %collective-permute-start.11 = (bf16[64,2048]{1,0:T(8,128)(2,1)}, bf16[64,2048]{1,0:T(8,128)(2,1)S(1)}, u32[]{:S(2)}, u32[]{:S(2)}) collective-permute-start(bf16[64,2048]{1,0:T(8,128)(2,1)} %param.7), channel_id=1, source_target_pairs={{0,8},{8,16},{16,24},{24,0},{32,40},{40,48},{48,56},{56,32},{64,72... | collective-permute-start | bytes 786440 | tf_op jit(solution)/shard_map/ppermute | solution.py:22
  18.2 1.7 %collective-permute-start.12 = (bf16[64,2048]{1,0:T(8,128)(2,1)}, bf16[64,2048]{1,0:T(8,128)(2,1)S(1)}, u32[]{:S(2)}, u32[]{:S(2)}) collective-permute-start(bf16[64,2048]{1,0:T(8,128)(2,1)} %param.7), channel_id=1, source_target_pairs={{0,24},{8,0},{16,8},{24,16},{32,56},{40,32},{48,40},{56,48},{64,88... | collective-permute-start | bytes 786440 | tf_op jit(solution)/shard_map/ppermute | solution.py:22
  20.0 1.8 %collective-permute-start.4 = (bf16[64,2048]{1,0:T(8,128)(2,1)}, bf16[64,2048]{1,0:T(8,128)(2,1)S(1)}, u32[]{:S(2)}, u32[]{:S(2)}) collective-permute-start(bf16[64,2048]{1,0:T(8,128)(2,1)} %param.7), channel_id=1, source_target_pairs={{0,16},{8,24},{16,0},{24,8},{32,48},{40,56},{48,32},{56,40},{64,80... | collective-permute-start | bytes 786440 | tf_op jit(solution)/shard_map/ppermute | solution.py:22
  23.8 2.7 %collective-permute-done.11 = bf16[64,2048]{1,0:T(8,128)(2,1)S(1)} collective-permute-done((bf16[64,2048]{1,0:T(8,128)(2,1)}, bf16[64,2048]{1,0:T(8,128)(2,1)S(1)}, u32[]{:S(2)}, u32[]{:S(2)}) %collective-permute-start.11) | collective-permute-done | bytes 262176 | tf_op jit(solution)/shard_map/ppermute | solution.py:22
  26.4 1.6 %collective-permute-start = (bf16[256,1024]{1,0:T(8,128)(2,1)S(1)}, bf16[256,1024]{1,0:T(8,128)(2,1)S(1)}, u32[]{:S(2)}, u32[]{:S(2)}) collective-permute-start(bf16[256,1024]{1,0:T(8,128)(2,1)S(1)} %constant_dynamic-update-slice_fusion), channel_id=1, source_target_pairs={{0,2},{1,3},{2,4},{3,5},{4,6},{5,7},{6,0},{7,1},{8,10},{9,11},{10,... | collective-permute-start | bytes 1572872 | tf_op jit(solution)/shard_map/ppermute | solution.py:27
  28.0 2.1 %collective-permute-done.12 = bf16[64,2048]{1,0:T(8,128)(2,1)S(1)} collective-permute-done((bf16[64,2048]{1,0:T(8,128)(2,1)}, bf16[64,2048]{1,0:T(8,128)(2,1)S(1)}, u32[]{:S(2)}, u32[]{:S(2)}) %collective-permute-start.12) | collective-permute-done | bytes 262176 | tf_op jit(solution)/shard_map/ppermute | solution.py:22
  30.1 3.2 %collective-permute-start.14 = (bf16[64,2304]{1,0:T(8,128)(2,1)S(1)}, bf16[64,2304]{1,0:T(8,128)(2,1)S(1)}, u32[]{:S(2)}, u32[]{:S(2)}) collective-permute-start(bf16[64,2304]{1,0:T(8,128)(2,1)S(1)} %collective-permute-done.10), channel_id=1, source_target_pairs={{0,224},{8,232},{16,240},{24,248},{32,0},{40,8},{48,16},{56,24},{6... | collective-permute-start | bytes 884744 | tf_op jit(solution)/shard_map/ppermute | solution.py:22
  34.4 3.6 %collective-permute-start.6 = (bf16[192,2304]{1,0:T(8,128)(2,1)S(1)}, bf16[192,2304]{1,0:T(8,128)(2,1)S(1)}, u32[]{:S(2)}, u32[]{:S(2)}) collective-permute-start(bf16[192,2304]{1,0:T(8,128)(2,1)S(1)} %pad_maximum_fusion.5), channel_id=1, source_target_pairs={{0,24},{8,0},{16,8},{24,16},{32,56},{40,32},{48,40},{56,48},{64,88... | collective-permute-start | bytes 2654216 | tf_op jit(solution)/shard_map/ppermute | solution.py:22
  38.8 3.3 %collective-permute-start.16 = (bf16[32,2304]{1,0:T(8,128)(2,1)S(1)}, bf16[32,2304]{1,0:T(8,128)(2,1)S(1)}, u32[]{:S(2)}, u32[]{:S(2)}) collective-permute-start(bf16[32,2304]{1,0:T(8,128)(2,1)S(1)} %slice.25), channel_id=1, source_target_pairs={{0,224},{8,232},{16,240},{24,248},{32,0},{40,8},{48,16},{56,24},{6... | collective-permute-start | bytes 442376 | tf_op jit(solution)/shard_map/ppermute | solution.py:22
  42.2 4.2 %collective-permute-done.15 = bf16[32,2304]{1,0:T(8,128)(2,1)S(1)} collective-permute-done((bf16[32,2304]{1,0:T(8,128)(2,1)S(1)}, bf16[32,2304]{1,0:T(8,128)(2,1)S(1)}, u32[]{:S(2)}, u32[]{:S(2)}) %collective-permute-start.15) | collective-permute-done | bytes 147488 | tf_op jit(solution)/shard_map/ppermute | solution.py:22
  47.7 2.3 %collective-permute-start.18 = (bf16[256,2048]{1,0:T(8,128)(2,1)S(1)}, bf16[256,2048]{1,0:T(8,128)(2,1)}, u32[]{:S(2)}, u32[]{:S(2)}) collective-permute-start(bf16[256,2048]{1,0:T(8,128)(2,1)S(1)} %pad_maximum_fusion.4), channel_id=1, source_target_pairs={{0,224},{8,232},{16,240},{24,248},{32,0},{40,8},{48,16},{56,24},{6... | collective-permute-start | bytes 3145736 | tf_op jit(solution)/shard_map/ppermute | solution.py:22
  50.0 2.2 %collective-permute-done.5 = bf16[192,2304]{1,0:T(8,128)(2,1)S(1)} collective-permute-done((bf16[192,2304]{1,0:T(8,128)(2,1)S(1)}, bf16[192,2304]{1,0:T(8,128)(2,1)S(1)}, u32[]{:S(2)}, u32[]{:S(2)}) %collective-permute-start.5) | collective-permute-done | bytes 884768 | tf_op jit(solution)/shard_map/ppermute | solution.py:22
  53.1 2.3 %collective-permute-start.7 = (bf16[256,1024]{1,0:T(8,128)(2,1)S(1)}, bf16[256,1024]{1,0:T(8,128)(2,1)S(1)}, u32[]{:S(2)}, u32[]{:S(2)}) collective-permute-start(bf16[256,1024]{1,0:T(8,128)(2,1)S(1)} %constant_dynamic-update-slice_fusion), channel_id=1, source_target_pairs={{0,4},{1,5},{2,6},{3,7},{4,0},{5,1},{6,2},{7,3},{8,12},{9,13},{10,... | collective-permute-start | bytes 1572872 | tf_op jit(solution)/shard_map/ppermute | solution.py:27
  56.6 3.2 %collective-permute-start.22 = (bf16[320,2304]{1,0:T(8,128)(2,1)}, bf16[320,2304]{1,0:T(8,128)(2,1)}, u32[]{:S(2)}, u32[]{:S(2)}) collective-permute-start(bf16[320,2304]{1,0:T(8,128)(2,1)} %pad_maximum_fusion), channel_id=1, source_target_pairs={{0,24},{8,0},{16,8},{24,16},{32,56},{40,32},{48,40},{56,48},{64,88... | collective-permute-start | bytes 4423688 | tf_op jit(solution)/shard_map/ppermute | solution.py:22
  60.0 3.8 %collective-permute-done.7 = bf16[256,1024]{1,0:T(8,128)(2,1)S(1)} collective-permute-done((bf16[256,1024]{1,0:T(8,128)(2,1)S(1)}, bf16[256,1024]{1,0:T(8,128)(2,1)S(1)}, u32[]{:S(2)}, u32[]{:S(2)}) %collective-permute-start.7) | collective-permute-done | bytes 524320 | tf_op jit(solution)/shard_map/ppermute | solution.py:27
  63.9 3.7 %collective-permute-done.17 = bf16[256,2048]{1,0:T(8,128)(2,1)} collective-permute-done((bf16[256,2048]{1,0:T(8,128)(2,1)S(1)}, bf16[256,2048]{1,0:T(8,128)(2,1)}, u32[]{:S(2)}, u32[]{:S(2)}) %collective-permute-start.17) | collective-permute-done | bytes 1048608 | tf_op jit(solution)/shard_map/ppermute | solution.py:22
  68.2 2.7 %collective-permute-start.20 = (bf16[256,2048]{1,0:T(8,128)(2,1)}, bf16[256,2048]{1,0:T(8,128)(2,1)}, u32[]{:S(2)}, u32[]{:S(2)}) collective-permute-start(bf16[256,2048]{1,0:T(8,128)(2,1)} %collective-permute-done.18), channel_id=1, source_target_pairs={{0,224},{8,232},{16,240},{24,248},{32,0},{40,8},{48,16},{56,24},{6... | collective-permute-start | bytes 3145736 | tf_op jit(solution)/shard_map/ppermute | solution.py:22
  71.0 14.8 %collective-permute-done.21 = bf16[320,2304]{1,0:T(8,128)(2,1)} collective-permute-done((bf16[320,2304]{1,0:T(8,128)(2,1)}, bf16[320,2304]{1,0:T(8,128)(2,1)}, u32[]{:S(2)}, u32[]{:S(2)}) %collective-permute-start.21) | collective-permute-done | bytes 1474592 | tf_op jit(solution)/shard_map/ppermute | solution.py:22
  85.8 5.3 %collective-permute-done.19 = bf16[256,2048]{1,0:T(8,128)(2,1)} collective-permute-done((bf16[256,2048]{1,0:T(8,128)(2,1)}, bf16[256,2048]{1,0:T(8,128)(2,1)}, u32[]{:S(2)}, u32[]{:S(2)}) %collective-permute-start.19) | collective-permute-done | bytes 1048608 | tf_op jit(solution)/shard_map/ppermute | solution.py:22
  91.4 2.9 %collective-permute-start.26 = (bf16[256,2048]{1,0:T(8,128)(2,1)}, bf16[256,2048]{1,0:T(8,128)(2,1)S(1)}, u32[]{:S(2)}, u32[]{:S(2)}) collective-permute-start(bf16[256,2048]{1,0:T(8,128)(2,1)} %collective-permute-done.20), channel_id=1, source_target_pairs={{0,224},{8,232},{16,240},{24,248},{32,0},{40,8},{48,16},{56,24},{6... | collective-permute-start | bytes 3145736 | tf_op jit(solution)/shard_map/ppermute | solution.py:22
  96.9 3.3 %collective-permute-start.24 = (bf16[256,2304]{1,0:T(8,128)(2,1)S(1)}, bf16[256,2304]{1,0:T(8,128)(2,1)S(1)}, u32[]{:S(2)}, u32[]{:S(2)}) collective-permute-start(bf16[256,2304]{1,0:T(8,128)(2,1)S(1)} %pad_maximum_fusion.3), channel_id=1, source_target_pairs={{0,24},{8,0},{16,8},{24,16},{32,56},{40,32},{48,40},{56,48},{64,88... | collective-permute-start | bytes 3538952 | tf_op jit(solution)/shard_map/ppermute | solution.py:22
  100.2 3.8 %shard_map.59 = (bf16[512,896]{1,0:T(8,128)(2,1)S(1)}, bf16[512,640]{1,0:T(8,128)(2,1)S(1)}, bf16[512,512]{1,0:T(8,128)(2,1)S(1)}, bf16[512,768]{1,0:T(8,128)(2,...) custom-call(s32[4]{0:T(128)S(1)} %pad_add_fusion.place_ref, ...), custom_call_target="tpu_custom_call" | custom-call | bytes 12582912 | tf_op jit(solution)/shard_map/pallas_call | solution.py:71
  104.1 4.2 %fusion.9 = f32[512,2304]{1,0:T(8,128)S(1)} fusion(bf16[512,896]{1,0:T(8,128)(2,1)S(1)} %get-tuple-element.73, bf16[320,2304]{1,0:T(8,128)(2,1)} %pad_maximum_fusion, bf16[192,2304]{1,0:T(8,128)(2,1)S(1)} %copy-done.1, bf16[192,2304]{1,0:T(8,128)(2,1)S(1)} %copy-done.3, bf16[192,2304]{1,0:T(8,128)(2,1)S(1)} %copy-done.7), kind=kOutput, calls=%fused_computation.12 | convolution fusion | flops 2130444288 | bytes 9764864 | tf_op jit(solution)/shard_map/dot_general | solution.py:88
  108.3 4.0 %convolution_add_fusion.1 = f32[512,2304]{1,0:T(8,128)S(1)} fusion(f32[512,2304]{1,0:T(8,128)S(1)} %fusion.9, bf16[512,640]{1,0:T(8,128)(2,1)S(1)} %get-tuple-element.72, bf16[320,2304]{1,0:T(8,128)(2,1)} %collective-permute-done.22, bf16[320,2304]{1,0:T(8,128)(2,1)} %collective-permute-done.21), kind=kOutput, calls=%fused_computation.1 | convolution fusion | flops 1517027328 | bytes 13041664 | tf_op jit(solution)/shard_map/dot_general | solution.py:88
  112.3 3.4 %fusion.20 = f32[512,2048]{1,0:T(8,128)S(1)} fusion(bf16[512,768]{1,0:T(8,128)(2,1)S(1)} %get-tuple-element.81, bf16[256,2048]{1,0:T(8,128)(2,1)} %collective-permute-done.18, bf16[256,2048]{1,0:T(8,128)(2,1)} %collective-permute-done.17, bf16[256,2048]{1,0:T(8,128)(2,1)S(1)} %copy-done.5), kind=kOutput, calls=%fused_computation.21 | convolution fusion | flops 1620049920 | bytes 8126464 | tf_op jit(solution)/shard_map/dot_general | solution.py:88
  115.9 3.3 %collective-permute-start.28 = (bf16[128,2048]{1,0:T(8,128)(2,1)S(1)}, bf16[128,2048]{1,0:T(8,128)(2,1)S(1)}, u32[]{:S(2)}, u32[]{:S(2)}) collective-permute-start(bf16[128,2048]{1,0:T(8,128)(2,1)S(1)} %slice.31), channel_id=1, source_target_pairs={{0,224},{8,232},{16,240},{24,248},{32,0},{40,8},{48,16},{56,24},{6... | collective-permute-start | bytes 1572872 | tf_op jit(solution)/shard_map/ppermute | solution.py:22
  119.2 3.8 %fusion.17 = f32[512,2048]{1,0:T(8,128)S(1)} fusion(f32[512,2048]{1,0:T(8,128)S(1)} %fusion.20, bf16[512,1024]{1,0:T(8,128)(2,1)S(1)} %get-tuple-element.78, bf16[256,2048]{1,0:T(8,128)(2,1)S(1)} %collective-permute-done.26, bf16[256,2048]{1,0:T(8,128)(2,1)S(1)} %collective-permute-done.25, bf16[256,2048]{1,0:T(8,128)(2,1)} %collective-permute-done.20, ...), kind=kOutput, calls=%fused_computation.20 | convolution fusion | flops 2165309440 | bytes 13631488 | tf_op jit(solution)/shard_map/dot_general | solution.py:88
  123.0 2.8 %fusion = bf16[512,2304]{1,0:T(8,128)(2,1)} fusion(f32[512,2304]{1,0:T(8,128)S(1)} %convolution_add_fusion.1, bf16[512,512]{1,0:T(8,128)(2,1)S(1)} %get-tuple-element.50, bf16[256,2304]{1,0:T(8,128)(2,1)S(1)} %collective-permute-done.24, bf16[256,2304]{1,0:T(8,128)(2,1)S(1)} %collective-permute-done.23), kind=kOutput, calls=%fused_computation.2 | convolution fusion | flops 1215037440 | bytes 9961472 | tf_op jit(solution)/shard_map/dot_general | solution.py:88
  126.2 2.0 %add_convert_fusion = bf16[512,2048]{1,0:T(8,128)(2,1)} fusion(f32[512,2048]{1,0:T(8,128)S(1)} %fusion.17, bf16[512,256]{1,0:T(8,128)(2,1)S(1)} %get-tuple-element.86, bf16[128,2048]{1,0:T(8,128)(2,1)S(1)} %collective-permute-done.28, bf16[128,2048]{1,0:T(8,128)(2,1)S(1)} %collective-permute-done.27), kind=kOutput, calls=%fused_computation.11 | convolution fusion | flops 541065216 | bytes 7602176 | tf_op jit(solution)/shard_map/dot_general | solution.py:88
  (74 shorter events, 11.7 us)
Async XLA Ops:
  0.6 12.5 %collective-permute-start.3 = (bf16[64,2304]{1,0:T(8,128)(2,1)}, bf16[64,2304]{1,0:T(8,128)(2,1)S(1)}, u32[]{:S(2)}, u32[]{:S(2)}) collective-permute-start(bf16[64,2304]{1,0:T(8,128)(2,1)} %param.6), channel_id=1, source_target_pairs={{0,224},{8,232},{16,240},{24,248},{32,0},{40,8},{48,16},{56,24},{6... | collective-permute-start | bytes 884744 | tf_op jit(solution)/shard_map/ppermute | solution.py:22
  6.6 10.2 %collective-permute-start.2 = (bf16[64,2304]{1,0:T(8,128)(2,1)}, bf16[64,2304]{1,0:T(8,128)(2,1)S(1)}, u32[]{:S(2)}, u32[]{:S(2)}) collective-permute-start(bf16[64,2304]{1,0:T(8,128)(2,1)} %param.6), channel_id=1, source_target_pairs={{0,32},{8,40},{16,48},{24,56},{32,64},{40,72},{48,80},{56,88},{64,... | collective-permute-start | bytes 884744 | tf_op jit(solution)/shard_map/ppermute | solution.py:22
  13.1 16.9 %collective-permute-start.10 = (bf16[64,2304]{1,0:T(8,128)(2,1)S(1)}, bf16[64,2304]{1,0:T(8,128)(2,1)S(1)}, u32[]{:S(2)}, u32[]{:S(2)}) collective-permute-start(bf16[64,2304]{1,0:T(8,128)(2,1)S(1)} %collective-permute-done.3), channel_id=1, source_target_pairs={{0,224},{8,232},{16,240},{24,248},{32,0},{40,8},{48,16},{56,24},{6... | collective-permute-start | bytes 884744 | tf_op jit(solution)/shard_map/ppermute | solution.py:22
  16.7 13.3 %collective-permute-start.9 = (bf16[64,2304]{1,0:T(8,128)(2,1)S(1)}, bf16[64,2304]{1,0:T(8,128)(2,1)S(1)}, u32[]{:S(2)}, u32[]{:S(2)}) collective-permute-start(bf16[64,2304]{1,0:T(8,128)(2,1)S(1)} %collective-permute-done.2), channel_id=1, source_target_pairs={{0,32},{8,40},{16,48},{24,56},{32,64},{40,72},{48,80},{56,88},{64,... | collective-permute-start | bytes 884744 | tf_op jit(solution)/shard_map/ppermute | solution.py:22
  16.7 9.7 %collective-permute-start.11 = (bf16[64,2048]{1,0:T(8,128)(2,1)}, bf16[64,2048]{1,0:T(8,128)(2,1)S(1)}, u32[]{:S(2)}, u32[]{:S(2)}) collective-permute-start(bf16[64,2048]{1,0:T(8,128)(2,1)} %param.7), channel_id=1, source_target_pairs={{0,8},{8,16},{16,24},{24,0},{32,40},{40,48},{48,56},{56,32},{64,72... | collective-permute-start | bytes 786440 | tf_op jit(solution)/shard_map/ppermute | solution.py:22
  18.2 11.8 %collective-permute-start.12 = (bf16[64,2048]{1,0:T(8,128)(2,1)}, bf16[64,2048]{1,0:T(8,128)(2,1)S(1)}, u32[]{:S(2)}, u32[]{:S(2)}) collective-permute-start(bf16[64,2048]{1,0:T(8,128)(2,1)} %param.7), channel_id=1, source_target_pairs={{0,24},{8,0},{16,8},{24,16},{32,56},{40,32},{48,40},{56,48},{64,88... | collective-permute-start | bytes 786440 | tf_op jit(solution)/shard_map/ppermute | solution.py:22
  20.0 14.4 %collective-permute-start.4 = (bf16[64,2048]{1,0:T(8,128)(2,1)}, bf16[64,2048]{1,0:T(8,128)(2,1)S(1)}, u32[]{:S(2)}, u32[]{:S(2)}) collective-permute-start(bf16[64,2048]{1,0:T(8,128)(2,1)} %param.7), channel_id=1, source_target_pairs={{0,16},{8,24},{16,0},{24,8},{32,48},{40,56},{48,32},{56,40},{64,80... | collective-permute-start | bytes 786440 | tf_op jit(solution)/shard_map/ppermute | solution.py:22
  26.4 11.7 %collective-permute-start = (bf16[256,1024]{1,0:T(8,128)(2,1)S(1)}, bf16[256,1024]{1,0:T(8,128)(2,1)S(1)}, u32[]{:S(2)}, u32[]{:S(2)}) collective-permute-start(bf16[256,1024]{1,0:T(8,128)(2,1)S(1)} %constant_dynamic-update-slice_fusion), channel_id=1, source_target_pairs={{0,2},{1,3},{2,4},{3,5},{4,6},{5,7},{6,0},{7,1},{8,10},{9,11},{10,... | collective-permute-start | bytes 1572872 | tf_op jit(solution)/shard_map/ppermute | solution.py:27
  30.1 8.5 %collective-permute-start.13 = (bf16[64,2304]{1,0:T(8,128)(2,1)S(1)}, bf16[64,2304]{1,0:T(8,128)(2,1)S(1)}, u32[]{:S(2)}, u32[]{:S(2)}) collective-permute-start(bf16[64,2304]{1,0:T(8,128)(2,1)S(1)} %collective-permute-done.9), channel_id=1, source_target_pairs={{0,32},{8,40},{16,48},{24,56},{32,64},{40,72},{48,80},{56,88},{64,... | collective-permute-start | bytes 884744 | tf_op jit(solution)/shard_map/ppermute | solution.py:22
  30.1 8.5 %collective-permute-start.14 = (bf16[64,2304]{1,0:T(8,128)(2,1)S(1)}, bf16[64,2304]{1,0:T(8,128)(2,1)S(1)}, u32[]{:S(2)}, u32[]{:S(2)}) collective-permute-start(bf16[64,2304]{1,0:T(8,128)(2,1)S(1)} %collective-permute-done.10), channel_id=1, source_target_pairs={{0,224},{8,232},{16,240},{24,248},{32,0},{40,8},{48,16},{56,24},{6... | collective-permute-start | bytes 884744 | tf_op jit(solution)/shard_map/ppermute | solution.py:22
  34.4 17.8 %collective-permute-start.5 = (bf16[192,2304]{1,0:T(8,128)(2,1)S(1)}, bf16[192,2304]{1,0:T(8,128)(2,1)S(1)}, u32[]{:S(2)}, u32[]{:S(2)}) collective-permute-start(bf16[192,2304]{1,0:T(8,128)(2,1)S(1)} %pad_maximum_fusion.5), channel_id=1, source_target_pairs={{0,8},{8,16},{16,24},{24,0},{32,40},{40,48},{48,56},{56,32},{64,72... | collective-permute-start | bytes 2654216 | tf_op jit(solution)/shard_map/ppermute | solution.py:22
  34.4 17.7 %collective-permute-start.6 = (bf16[192,2304]{1,0:T(8,128)(2,1)S(1)}, bf16[192,2304]{1,0:T(8,128)(2,1)S(1)}, u32[]{:S(2)}, u32[]{:S(2)}) collective-permute-start(bf16[192,2304]{1,0:T(8,128)(2,1)S(1)} %pad_maximum_fusion.5), channel_id=1, source_target_pairs={{0,24},{8,0},{16,8},{24,16},{32,56},{40,32},{48,40},{56,48},{64,88... | collective-permute-start | bytes 2654216 | tf_op jit(solution)/shard_map/ppermute | solution.py:22
  38.1 11.9 %collective-permute-start.1 = (bf16[256,1024]{1,0:T(8,128)(2,1)S(1)}, bf16[256,1024]{1,0:T(8,128)(2,1)S(1)}, u32[]{:S(2)}, u32[]{:S(2)}) collective-permute-start(bf16[256,1024]{1,0:T(8,128)(2,1)S(1)} %constant_dynamic-update-slice_fusion), channel_id=1, source_target_pairs={{0,6},{1,7},{2,0},{3,1},{4,2},{5,3},{6,4},{7,5},{8,14},{9,15},{10,... | collective-permute-start | bytes 1572872 | tf_op jit(solution)/shard_map/ppermute | solution.py:27
  38.6 7.7 %collective-permute-start.15 = (bf16[32,2304]{1,0:T(8,128)(2,1)S(1)}, bf16[32,2304]{1,0:T(8,128)(2,1)S(1)}, u32[]{:S(2)}, u32[]{:S(2)}) collective-permute-start(bf16[32,2304]{1,0:T(8,128)(2,1)S(1)} %slice.24), channel_id=1, source_target_pairs={{0,32},{8,40},{16,48},{24,56},{32,64},{40,72},{48,80},{56,88},{64,... | collective-permute-start | bytes 442376 | tf_op jit(solution)/shard_map/ppermute | solution.py:22
  38.8 7.6 %collective-permute-start.16 = (bf16[32,2304]{1,0:T(8,128)(2,1)S(1)}, bf16[32,2304]{1,0:T(8,128)(2,1)S(1)}, u32[]{:S(2)}, u32[]{:S(2)}) collective-permute-start(bf16[32,2304]{1,0:T(8,128)(2,1)S(1)} %slice.25), channel_id=1, source_target_pairs={{0,224},{8,232},{16,240},{24,248},{32,0},{40,8},{48,16},{56,24},{6... | collective-permute-start | bytes 442376 | tf_op jit(solution)/shard_map/ppermute | solution.py:22
  42.2 21.7 %copy-start.4 = (bf16[256,2048]{1,0:T(8,128)(2,1)}, bf16[256,2048]{1,0:T(8,128)(2,1)S(1)}, u32[]{:S(2)}) copy-start(bf16[256,2048]{1,0:T(8,128)(2,1)S(1)} %pad_maximum_fusion.4) | copy-start | bytes 3145732
  46.4 21.3 %collective-permute-start.17 = (bf16[256,2048]{1,0:T(8,128)(2,1)S(1)}, bf16[256,2048]{1,0:T(8,128)(2,1)}, u32[]{:S(2)}, u32[]{:S(2)}) collective-permute-start(bf16[256,2048]{1,0:T(8,128)(2,1)S(1)} %pad_maximum_fusion.4), channel_id=1, source_target_pairs={{0,32},{8,40},{16,48},{24,56},{32,64},{40,72},{48,80},{56,88},{64,... | collective-permute-start | bytes 3145736 | tf_op jit(solution)/shard_map/ppermute | solution.py:22
  47.7 20.0 %collective-permute-start.18 = (bf16[256,2048]{1,0:T(8,128)(2,1)S(1)}, bf16[256,2048]{1,0:T(8,128)(2,1)}, u32[]{:S(2)}, u32[]{:S(2)}) collective-permute-start(bf16[256,2048]{1,0:T(8,128)(2,1)S(1)} %pad_maximum_fusion.4), channel_id=1, source_target_pairs={{0,224},{8,232},{16,240},{24,248},{32,0},{40,8},{48,16},{56,24},{6... | collective-permute-start | bytes 3145736 | tf_op jit(solution)/shard_map/ppermute | solution.py:22
  53.1 10.7 %collective-permute-start.7 = (bf16[256,1024]{1,0:T(8,128)(2,1)S(1)}, bf16[256,1024]{1,0:T(8,128)(2,1)S(1)}, u32[]{:S(2)}, u32[]{:S(2)}) collective-permute-start(bf16[256,1024]{1,0:T(8,128)(2,1)S(1)} %constant_dynamic-update-slice_fusion), channel_id=1, source_target_pairs={{0,4},{1,5},{2,6},{3,7},{4,0},{5,1},{6,2},{7,3},{8,12},{9,13},{10,... | collective-permute-start | bytes 1572872 | tf_op jit(solution)/shard_map/ppermute | solution.py:27
  56.6 29.2 %collective-permute-start.21 = (bf16[320,2304]{1,0:T(8,128)(2,1)}, bf16[320,2304]{1,0:T(8,128)(2,1)}, u32[]{:S(2)}, u32[]{:S(2)}) collective-permute-start(bf16[320,2304]{1,0:T(8,128)(2,1)} %pad_maximum_fusion), channel_id=1, source_target_pairs={{0,8},{8,16},{16,24},{24,0},{32,40},{40,48},{48,56},{56,32},{64,72... | collective-permute-start | bytes 4423688 | tf_op jit(solution)/shard_map/ppermute | solution.py:22
  56.6 29.2 %collective-permute-start.22 = (bf16[320,2304]{1,0:T(8,128)(2,1)}, bf16[320,2304]{1,0:T(8,128)(2,1)}, u32[]{:S(2)}, u32[]{:S(2)}) collective-permute-start(bf16[320,2304]{1,0:T(8,128)(2,1)} %pad_maximum_fusion), channel_id=1, source_target_pairs={{0,24},{8,0},{16,8},{24,16},{32,56},{40,32},{48,40},{56,48},{64,88... | collective-permute-start | bytes 4423688 | tf_op jit(solution)/shard_map/ppermute | solution.py:22
  60.0 35.5 %slice-start.1 = ((bf16[192,2304]{1,0:T(8,128)(2,1)}), bf16[96,2304]{1,0:T(8,128)(2,1)S(1)}, s32[]{:S(2)}) async-start(bf16[192,2304]{1,0:T(8,128)(2,1)} %copy-done.2), calls=%async_computation.1 | async-start | bytes 884736 | tf_op jit(solution)/shard_map/slice | solution.py:32
  63.8 36.4 %collective-permute-start.8 = (bf16[1024,1024]{1,0:T(8,128)(2,1)S(1)}, bf16[1024,1024]{1,0:T(8,128)(2,1)}, u32[]{:S(2)}, u32[]{:S(2)}) collective-permute-start(bf16[1024,1024]{1,0:T(8,128)(2,1)S(1)} %constant_dynamic-update-slice_fusion.2.mine_ref), channel_id=1, source_target_pairs={{0,1},{1,0},{2,3},{3,2},{4,5},{5,4},{6,7},{7,6},{8,9},{9,8},{10,11... | collective-permute-start | bytes 6291464 | tf_op jit(solution)/shard_map/ppermute | solution.py:27
  67.7 23.4 %collective-permute-start.19 = (bf16[256,2048]{1,0:T(8,128)(2,1)}, bf16[256,2048]{1,0:T(8,128)(2,1)}, u32[]{:S(2)}, u32[]{:S(2)}) collective-permute-start(bf16[256,2048]{1,0:T(8,128)(2,1)} %collective-permute-done.17), channel_id=1, source_target_pairs={{0,32},{8,40},{16,48},{24,56},{32,64},{40,72},{48,80},{56,88},{64,... | collective-permute-start | bytes 3145736 | tf_op jit(solution)/shard_map/ppermute | solution.py:22
  68.2 22.8 %collective-permute-start.20 = (bf16[256,2048]{1,0:T(8,128)(2,1)}, bf16[256,2048]{1,0:T(8,128)(2,1)}, u32[]{:S(2)}, u32[]{:S(2)}) collective-permute-start(bf16[256,2048]{1,0:T(8,128)(2,1)} %collective-permute-done.18), channel_id=1, source_target_pairs={{0,224},{8,232},{16,240},{24,248},{32,0},{40,8},{48,16},{56,24},{6... | collective-permute-start | bytes 3145736 | tf_op jit(solution)/shard_map/ppermute | solution.py:22
  71.0 25.8 %slice-start = ((bf16[192,2304]{1,0:T(8,128)(2,1)}), bf16[96,2304]{1,0:T(8,128)(2,1)S(1)}, s32[]{:S(2)}) async-start(bf16[192,2304]{1,0:T(8,128)(2,1)} %copy-done), calls=%async_computation | async-start | bytes 884736 | tf_op jit(solution)/shard_map/slice | solution.py:32
  91.0 24.6 %collective-permute-start.25 = (bf16[256,2048]{1,0:T(8,128)(2,1)}, bf16[256,2048]{1,0:T(8,128)(2,1)S(1)}, u32[]{:S(2)}, u32[]{:S(2)}) collective-permute-start(bf16[256,2048]{1,0:T(8,128)(2,1)} %collective-permute-done.19), channel_id=1, source_target_pairs={{0,32},{8,40},{16,48},{24,56},{32,64},{40,72},{48,80},{56,88},{64,... | collective-permute-start | bytes 3145736 | tf_op jit(solution)/shard_map/ppermute | solution.py:22
  91.4 24.3 %collective-permute-start.26 = (bf16[256,2048]{1,0:T(8,128)(2,1)}, bf16[256,2048]{1,0:T(8,128)(2,1)S(1)}, u32[]{:S(2)}, u32[]{:S(2)}) collective-permute-start(bf16[256,2048]{1,0:T(8,128)(2,1)} %collective-permute-done.20), channel_id=1, source_target_pairs={{0,224},{8,232},{16,240},{24,248},{32,0},{40,8},{48,16},{56,24},{6... | collective-permute-start | bytes 3145736 | tf_op jit(solution)/shard_map/ppermute | solution.py:22
  95.5 27.4 %collective-permute-start.23 = (bf16[256,2304]{1,0:T(8,128)(2,1)S(1)}, bf16[256,2304]{1,0:T(8,128)(2,1)S(1)}, u32[]{:S(2)}, u32[]{:S(2)}) collective-permute-start(bf16[256,2304]{1,0:T(8,128)(2,1)S(1)} %pad_maximum_fusion.2), channel_id=1, source_target_pairs={{0,8},{8,16},{16,24},{24,0},{32,40},{40,48},{48,56},{56,32},{64,72... | collective-permute-start | bytes 3538952 | tf_op jit(solution)/shard_map/ppermute | solution.py:22
  96.9 26.1 %collective-permute-start.24 = (bf16[256,2304]{1,0:T(8,128)(2,1)S(1)}, bf16[256,2304]{1,0:T(8,128)(2,1)S(1)}, u32[]{:S(2)}, u32[]{:S(2)}) collective-permute-start(bf16[256,2304]{1,0:T(8,128)(2,1)S(1)} %pad_maximum_fusion.3), channel_id=1, source_target_pairs={{0,24},{8,0},{16,8},{24,16},{32,56},{40,32},{48,40},{56,48},{64,88... | collective-permute-start | bytes 3538952 | tf_op jit(solution)/shard_map/ppermute | solution.py:22
  115.7 10.5 %collective-permute-start.27 = (bf16[128,2048]{1,0:T(8,128)(2,1)S(1)}, bf16[128,2048]{1,0:T(8,128)(2,1)S(1)}, u32[]{:S(2)}, u32[]{:S(2)}) collective-permute-start(bf16[128,2048]{1,0:T(8,128)(2,1)S(1)} %slice.30), channel_id=1, source_target_pairs={{0,32},{8,40},{16,48},{24,56},{32,64},{40,72},{48,80},{56,88},{64,... | collective-permute-start | bytes 1572872 | tf_op jit(solution)/shard_map/ppermute | solution.py:22
  115.9 10.3 %collective-permute-start.28 = (bf16[128,2048]{1,0:T(8,128)(2,1)S(1)}, bf16[128,2048]{1,0:T(8,128)(2,1)S(1)}, u32[]{:S(2)}, u32[]{:S(2)}) collective-permute-start(bf16[128,2048]{1,0:T(8,128)(2,1)S(1)} %slice.31), channel_id=1, source_target_pairs={{0,224},{8,232},{16,240},{24,248},{32,0},{40,8},{48,16},{56,24},{6... | collective-permute-start | bytes 1572872 | tf_op jit(solution)/shard_map/ppermute | solution.py:22
  (8 other events, 70.4 us)

commit v8 on v6

--- a/solution.py
+++ b/solution.py
@@ -120,19 +120,18 @@
     mine = jnp.concatenate([normed_input, attended], axis=1)
 
     below, above = hop(tall, 1, 0), hop(tall, -1, 0)
-    left, right = hop(wide, 0, 1), hop(wide, 0, -1)
+    left, right, opposite = hop(wide, 0, 1), hop(wide, 0, -1), hop(wide, 0, 2)
     down = hop_y(mine, 1)
     below, above, left, right = together((below, above, left, right))
-    opposite = hop(wide, 0, 2)
     near = jnp.concatenate([tall, below, above])
     near, opposite = together((near, opposite))
+    below, above = hop(below, 1, 0), hop(above, -1, 0)
     near_left, near_right = hop(near, 0, 1), hop(near, 0, -1)
-    below, above = hop(below, 1, 0), hop(above, -1, 0)
     below, above, opposite, mine, down = together((below, above, opposite, mine, down))
-    up = hop_y(mine, -1)
     far = [below, above]
     below, above = hop(below, 1, 0), hop(above, -1, 0)
     far = jnp.concatenate([*far, below, above])
+    up = hop_y(mine, -1)
     below, above, far = together((below, above, far))
     mine, up, near_left, near_right = together((mine, up, near_left, near_right))
     across = hop_y(mine, 2)
@@ -145,7 +144,6 @@
     below, above = hop(wide, 1, 0), hop(wide, -1, 0)
     wide_first = [wide, below, above]
     tall_first = [near, near_left, near_right, far]
-    below, above, tall_first = together((below, above, tall_first))
     mine = jnp.concatenate([mine, down, up, across])
 
     near_rows = {dx: whole(NEAR, dx) for dx in X_ORDER}
@@ -154,7 +152,7 @@
     wide_rows = {dz: [(dz, dx, 0, BLOCK) for dx in X_ORDER] for dz in range(-4, 5)}
     wide_split = parts(wide_rows[4])
     groups = [
-        (sum([near_rows[0], near_rows[-1], near_rows[1], far_rows[0]], []), 0),
+        (near_rows[0] + near_rows[-1] + near_rows[1] + far_rows[0], 0),
         (far_rows[-1] + far_rows[1], 0),
         (near_split[0] + far_split[0] + near_split[1] + far_split[1], 0),
         (wide_rows[0] + wide_rows[-1] + wide_rows[1], 1),
@@ -166,15 +164,14 @@
 
     below, above = hop(below, 1, 0), hop(above, -1, 0)
     wide_second = [below, above]
+    wide_sum = contract(lefts[3], wide_first)
     below, above, far_left, far_right = together((below, above, far_left, far_right))
-    wide_sum = contract(lefts[3], wide_first)
     below, above = hop(below, 1, 0), hop(above, -1, 0)
     first = jnp.concatenate([halves(near_left)[0], halves(far_left)[0]])
     second = jnp.concatenate([halves(near_right)[1], halves(far_right)[1]])
     tall_halves = [hop(first, 0, 1), hop(second, 0, -1)]
-    below, above, wide_sum = together((below, above, wide_sum))
+    below, above, wide_sum, tall_sum = together((below, above, wide_sum, tall_sum))
     wide_halves = [hop(halves(below)[0], 1, 0), hop(halves(above)[1], -1, 0)]
-
     tall_sum = contract(lefts[1], [far_left, far_right], tall_sum)
     wide_sum = contract(lefts[4], [*wide_second, below, above], wide_sum)
     tall_sum, wide_sum = together((tall_sum, wide_sum))

time: 130 us -> 130 us (level)
  the two profiles are of different devices: /device:TPU:32 before, /device:TPU:8 now
where the time goes in v8:
time: 130 us; the launch traced here: 128 us
  waiting for transfers between devices  48 us (37%)
  starting transfers between devices  47.1 us (36%)
  matrix products  20.4 us (16%)
  local copies, waits for them, and re-layouts  5.6 us (4%)
  Pallas kernels  3.79 us (3%)
  other arithmetic  2.63 us (2%)
    ppermute x25, waiting for transfers between devices, hop(): return lax.ppermute(value, 'row', pairs)  43.5 us
    ppermute x25, starting transfers between devices, hop(): return lax.ppermute(value, 'row', pairs)  42.6 us
    dot_general x6, matrix products, contract(): jnp.dot(left, jnp.concatenate(grads), preferred_element_type=jnp.float32)  20.4 us
    ppermute x4, waiting for transfers between devices, hop_y(): return lax.ppermute(value, 'col', pairs)  4.49 us
    ppermute x4, starting transfers between devices, hop_y(): return lax.ppermute(value, 'col', pairs)  4.49 us
    pallas_call x1, Pallas kernels, arrange(): pl.pallas_call(functools.partial(arrange_kernel, groups), out_shape=[jax....  3.79 us
    slice x9, local copies, waits for them, and re-layouts, halves(): return (value[:half], value[half:])  3.48 us
  transfers between devices with their start and end apart: 29, of which 15 were waited for; matrix products, arithmetic and copies ran while one was open for 21% of the time, Pallas kernels for 3%

profile of v8, /device:TPU:8, one launch (start us, length us, event | category | flops | bytes accessed | tf_op | source)
XLA Modules:
  0.0 128.5 jit_solution(5145701063944075638)
XLA Ops:
  0.6 2.0 %collective-permute-start = (bf16[64,2304]{1,0:T(8,128)(2,1)}, bf16[64,2304]{1,0:T(8,128)(2,1)S(1)}, u32[]{:S(2)}, u32[]{:S(2)}) collective-permute-start(bf16[64,2304]{1,0:T(8,128)(2,1)} %param.6), channel_id=1, source_target_pairs={{0,32},{8,40},{16,48},{24,56},{32,64},{40,72},{48,80},{56,88},{64,... | collective-permute-start | bytes 884744 | tf_op jit(solution)/shard_map/ppermute | solution.py:22
  2.6 4.0 %collective-permute-start.1 = (bf16[64,2304]{1,0:T(8,128)(2,1)}, bf16[64,2304]{1,0:T(8,128)(2,1)S(1)}, u32[]{:S(2)}, u32[]{:S(2)}) collective-permute-start(bf16[64,2304]{1,0:T(8,128)(2,1)} %param.6), channel_id=1, source_target_pairs={{0,224},{8,232},{16,240},{24,248},{32,0},{40,8},{48,16},{56,24},{6... | collective-permute-start | bytes 884744 | tf_op jit(solution)/shard_map/ppermute | solution.py:22
  8.1 1.7 %collective-permute-start.3 = (bf16[64,2048]{1,0:T(8,128)(2,1)}, bf16[64,2048]{1,0:T(8,128)(2,1)S(1)}, u32[]{:S(2)}, u32[]{:S(2)}) collective-permute-start(bf16[64,2048]{1,0:T(8,128)(2,1)} %param.7), channel_id=1, source_target_pairs={{0,24},{8,0},{16,8},{24,16},{32,56},{40,32},{48,40},{56,48},{64,88... | collective-permute-start | bytes 786440 | tf_op jit(solution)/shard_map/ppermute | solution.py:22
  13.5 2.3 %collective-permute-done.2 = bf16[64,2048]{1,0:T(8,128)(2,1)S(1)} collective-permute-done((bf16[64,2048]{1,0:T(8,128)(2,1)}, bf16[64,2048]{1,0:T(8,128)(2,1)S(1)}, u32[]{:S(2)}, u32[]{:S(2)}) %collective-permute-start.2) | collective-permute-done | bytes 262176 | tf_op jit(solution)/shard_map/ppermute | solution.py:22
  15.8 1.8 %collective-permute-start.6 = (bf16[64,2048]{1,0:T(8,128)(2,1)}, bf16[64,2048]{1,0:T(8,128)(2,1)S(1)}, u32[]{:S(2)}, u32[]{:S(2)}) collective-permute-start(bf16[64,2048]{1,0:T(8,128)(2,1)} %param.7), channel_id=1, source_target_pairs={{0,16},{8,24},{16,0},{24,8},{32,48},{40,56},{48,32},{56,40},{64,80... | collective-permute-start | bytes 786440 | tf_op jit(solution)/shard_map/ppermute | solution.py:22
  17.8 3.2 %collective-permute-start.5 = (bf16[64,2304]{1,0:T(8,128)(2,1)S(1)}, bf16[64,2304]{1,0:T(8,128)(2,1)S(1)}, u32[]{:S(2)}, u32[]{:S(2)}) collective-permute-start(bf16[64,2304]{1,0:T(8,128)(2,1)S(1)} %collective-permute-done.1), channel_id=1, source_target_pairs={{0,224},{8,232},{16,240},{24,248},{32,0},{40,8},{48,16},{56,24},{6... | collective-permute-start | bytes 884744 | tf_op jit(solution)/shard_map/ppermute | solution.py:22
  22.0 2.4 %collective-permute-done.6 = bf16[64,2048]{1,0:T(8,128)(2,1)S(1)} collective-permute-done((bf16[64,2048]{1,0:T(8,128)(2,1)}, bf16[64,2048]{1,0:T(8,128)(2,1)S(1)}, u32[]{:S(2)}, u32[]{:S(2)}) %collective-permute-start.6) | collective-permute-done | bytes 262176 | tf_op jit(solution)/shard_map/ppermute | solution.py:22
  26.2 3.2 %collective-permute-start.14 = (bf16[64,2304]{1,0:T(8,128)(2,1)S(1)}, bf16[64,2304]{1,0:T(8,128)(2,1)S(1)}, u32[]{:S(2)}, u32[]{:S(2)}) collective-permute-start(bf16[64,2304]{1,0:T(8,128)(2,1)S(1)} %collective-permute-done.5), channel_id=1, source_target_pairs={{0,224},{8,232},{16,240},{24,248},{32,0},{40,8},{48,16},{56,24},{6... | collective-permute-start | bytes 884744 | tf_op jit(solution)/shard_map/ppermute | solution.py:22
  32.0 2.2 %collective-permute-done.13 = bf16[64,2304]{1,0:T(8,128)(2,1)S(1)} collective-permute-done((bf16[64,2304]{1,0:T(8,128)(2,1)S(1)}, bf16[64,2304]{1,0:T(8,128)(2,1)S(1)}, u32[]{:S(2)}, u32[]{:S(2)}) %collective-permute-start.13) | collective-permute-done | bytes 294944 | tf_op jit(solution)/shard_map/ppermute | solution.py:22
  34.3 2.2 %collective-permute-start.15 = (bf16[32,2304]{1,0:T(8,128)(2,1)S(1)}, bf16[32,2304]{1,0:T(8,128)(2,1)S(1)}, u32[]{:S(2)}, u32[]{:S(2)}) collective-permute-start(bf16[32,2304]{1,0:T(8,128)(2,1)S(1)} %slice.24), channel_id=1, source_target_pairs={{0,32},{8,40},{16,48},{24,56},{32,64},{40,72},{48,80},{56,88},{64,... | collective-permute-start | bytes 442376 | tf_op jit(solution)/shard_map/ppermute | solution.py:22
  37.8 3.3 %collective-permute-done.15 = bf16[32,2304]{1,0:T(8,128)(2,1)S(1)} collective-permute-done((bf16[32,2304]{1,0:T(8,128)(2,1)S(1)}, bf16[32,2304]{1,0:T(8,128)(2,1)S(1)}, u32[]{:S(2)}, u32[]{:S(2)}) %collective-permute-start.15) | collective-permute-done | bytes 147488 | tf_op jit(solution)/shard_map/ppermute | solution.py:22
  41.2 2.0 %collective-permute-done.16 = bf16[32,2304]{1,0:T(8,128)(2,1)S(1)} collective-permute-done((bf16[32,2304]{1,0:T(8,128)(2,1)S(1)}, bf16[32,2304]{1,0:T(8,128)(2,1)S(1)}, u32[]{:S(2)}, u32[]{:S(2)}) %collective-permute-start.16) | collective-permute-done | bytes 147488 | tf_op jit(solution)/shard_map/ppermute | solution.py:22
  43.1 2.2 %collective-permute-start.17 = (bf16[256,2048]{1,0:T(8,128)(2,1)S(1)}, bf16[256,2048]{1,0:T(8,128)(2,1)}, u32[]{:S(2)}, u32[]{:S(2)}) collective-permute-start(bf16[256,2048]{1,0:T(8,128)(2,1)S(1)} %pad_maximum_fusion.4), channel_id=1, source_target_pairs={{0,32},{8,40},{16,48},{24,56},{32,64},{40,72},{48,80},{56,88},{64,... | collective-permute-start | bytes 3145736 | tf_op jit(solution)/shard_map/ppermute | solution.py:22
  47.9 2.2 %collective-permute-done.9 = bf16[192,2304]{1,0:T(8,128)(2,1)} collective-permute-done((bf16[192,2304]{1,0:T(8,128)(2,1)S(1)}, bf16[192,2304]{1,0:T(8,128)(2,1)}, u32[]{:S(2)}, u32[]{:S(2)}) %collective-permute-start.9) | collective-permute-done | bytes 884768 | tf_op jit(solution)/shard_map/ppermute | solution.py:22
  50.1 2.3 %collective-permute-start.11 = (bf16[256,1024]{1,0:T(8,128)(2,1)S(1)}, bf16[256,1024]{1,0:T(8,128)(2,1)S(1)}, u32[]{:S(2)}, u32[]{:S(2)}) collective-permute-start(bf16[256,1024]{1,0:T(8,128)(2,1)S(1)} %constant_dynamic-update-slice_fusion), channel_id=1, source_target_pairs={{0,4},{1,5},{2,6},{3,7},{4,0},{5,1},{6,2},{7,3},{8,12},{9,13},{10,... | collective-permute-start | bytes 1572872 | tf_op jit(solution)/shard_map/ppermute | solution.py:27
  53.6 3.2 %collective-permute-start.22 = (bf16[320,2304]{1,0:T(8,128)(2,1)}, bf16[320,2304]{1,0:T(8,128)(2,1)}, u32[]{:S(2)}, u32[]{:S(2)}) collective-permute-start(bf16[320,2304]{1,0:T(8,128)(2,1)} %pad_maximum_fusion), channel_id=1, source_target_pairs={{0,24},{8,0},{16,8},{24,16},{32,56},{40,32},{48,40},{56,48},{64,88... | collective-permute-start | bytes 4423688 | tf_op jit(solution)/shard_map/ppermute | solution.py:22
  57.0 4.1 %collective-permute-done.11 = bf16[256,1024]{1,0:T(8,128)(2,1)S(1)} collective-permute-done((bf16[256,1024]{1,0:T(8,128)(2,1)S(1)}, bf16[256,1024]{1,0:T(8,128)(2,1)S(1)}, u32[]{:S(2)}, u32[]{:S(2)}) %collective-permute-start.11) | collective-permute-done | bytes 524320 | tf_op jit(solution)/shard_map/ppermute | solution.py:27
  61.2 2.0 %collective-permute-done.17 = bf16[256,2048]{1,0:T(8,128)(2,1)} collective-permute-done((bf16[256,2048]{1,0:T(8,128)(2,1)S(1)}, bf16[256,2048]{1,0:T(8,128)(2,1)}, u32[]{:S(2)}, u32[]{:S(2)}) %collective-permute-start.17) | collective-permute-done | bytes 1048608 | tf_op jit(solution)/shard_map/ppermute | solution.py:22
  64.4 2.2 %collective-permute-start.20 = (bf16[256,2048]{1,0:T(8,128)(2,1)}, bf16[256,2048]{1,0:T(8,128)(2,1)}, u32[]{:S(2)}, u32[]{:S(2)}) collective-permute-start(bf16[256,2048]{1,0:T(8,128)(2,1)} %collective-permute-done.19), channel_id=1, source_target_pairs={{0,224},{8,232},{16,240},{24,248},{32,0},{40,8},{48,16},{56,24},{6... | collective-permute-start | bytes 3145736 | tf_op jit(solution)/shard_map/ppermute | solution.py:22
  67.8 16.9 %collective-permute-done.21 = bf16[320,2304]{1,0:T(8,128)(2,1)} collective-permute-done((bf16[320,2304]{1,0:T(8,128)(2,1)}, bf16[320,2304]{1,0:T(8,128)(2,1)}, u32[]{:S(2)}, u32[]{:S(2)}) %collective-permute-start.21) | collective-permute-done | bytes 1474592 | tf_op jit(solution)/shard_map/ppermute | solution.py:22
  84.7 3.6 %collective-permute-done.18 = bf16[256,2048]{1,0:T(8,128)(2,1)} collective-permute-done((bf16[256,2048]{1,0:T(8,128)(2,1)}, bf16[256,2048]{1,0:T(8,128)(2,1)}, u32[]{:S(2)}, u32[]{:S(2)}) %collective-permute-start.18) | collective-permute-done | bytes 1048608 | tf_op jit(solution)/shard_map/ppermute | solution.py:22
  88.9 2.7 %collective-permute-start.26 = (bf16[256,2048]{1,0:T(8,128)(2,1)}, bf16[256,2048]{1,0:T(8,128)(2,1)S(1)}, u32[]{:S(2)}, u32[]{:S(2)}) collective-permute-start(bf16[256,2048]{1,0:T(8,128)(2,1)} %collective-permute-done.20), channel_id=1, source_target_pairs={{0,224},{8,232},{16,240},{24,248},{32,0},{40,8},{48,16},{56,24},{6... | collective-permute-start | bytes 3145736 | tf_op jit(solution)/shard_map/ppermute | solution.py:22
  94.2 3.3 %collective-permute-start.24 = (bf16[256,2304]{1,0:T(8,128)(2,1)S(1)}, bf16[256,2304]{1,0:T(8,128)(2,1)S(1)}, u32[]{:S(2)}, u32[]{:S(2)}) collective-permute-start(bf16[256,2304]{1,0:T(8,128)(2,1)S(1)} %pad_maximum_fusion.3), channel_id=1, source_target_pairs={{0,24},{8,0},{16,8},{24,16},{32,56},{40,32},{48,40},{56,48},{64,88... | collective-permute-start | bytes 3538952 | tf_op jit(solution)/shard_map/ppermute | solution.py:22
  97.5 3.8 %shard_map.59 = (bf16[512,896]{1,0:T(8,128)(2,1)S(1)}, bf16[512,640]{1,0:T(8,128)(2,1)S(1)}, bf16[512,512]{1,0:T(8,128)(2,1)S(1)}, bf16[512,768]{1,0:T(8,128)(2,...) custom-call(s32[4]{0:T(128)S(1)} %pad_add_fusion.place_ref, ...), custom_call_target="tpu_custom_call" | custom-call | bytes 12582912 | tf_op jit(solution)/shard_map/pallas_call | solution.py:71
  101.3 3.5 %fusion.20 = f32[512,2048]{1,0:T(8,128)S(1)} fusion(bf16[512,768]{1,0:T(8,128)(2,1)S(1)} %get-tuple-element.74, bf16[256,2048]{1,0:T(8,128)(2,1)} %collective-permute-done.19, bf16[256,2048]{1,0:T(8,128)(2,1)} %collective-permute-done.17, bf16[256,2048]{1,0:T(8,128)(2,1)S(1)} %copy-done.3), kind=kOutput, calls=%fused_computation.21 | convolution fusion | flops 1620049920 | bytes 8126464 | tf_op jit(solution)/shard_map/dot_general | solution.py:88
  104.8 4.3 %fusion.9 = f32[512,2304]{1,0:T(8,128)S(1)} fusion(bf16[512,896]{1,0:T(8,128)(2,1)S(1)} %get-tuple-element.75, bf16[320,2304]{1,0:T(8,128)(2,1)} %pad_maximum_fusion, bf16[192,2304]{1,0:T(8,128)(2,1)S(1)} %copy-done.1, bf16[192,2304]{1,0:T(8,128)(2,1)} %collective-permute-done.9, bf16[192,2304]{1,0:T(8,128)(2,1)S(1)} %copy-done.5), kind=kOutput, calls=%fused_computation.12 | convolution fusion | flops 2130444288 | bytes 9764864 | tf_op jit(solution)/shard_map/dot_general | solution.py:88
  109.1 3.2 %collective-permute-done.25 = bf16[256,2048]{1,0:T(8,128)(2,1)S(1)} collective-permute-done((bf16[256,2048]{1,0:T(8,128)(2,1)}, bf16[256,2048]{1,0:T(8,128)(2,1)S(1)}, u32[]{:S(2)}, u32[]{:S(2)}) %collective-permute-start.25) | collective-permute-done | bytes 1048608 | tf_op jit(solution)/shard_map/ppermute | solution.py:22
  112.9 2.9 %collective-permute-start.28 = (bf16[128,2048]{1,0:T(8,128)(2,1)S(1)}, bf16[128,2048]{1,0:T(8,128)(2,1)S(1)}, u32[]{:S(2)}, u32[]{:S(2)}) collective-permute-start(bf16[128,2048]{1,0:T(8,128)(2,1)S(1)} %slice.31), channel_id=1, source_target_pairs={{0,224},{8,232},{16,240},{24,248},{32,0},{40,8},{48,16},{56,24},{6... | collective-permute-start | bytes 1572872 | tf_op jit(solution)/shard_map/ppermute | solution.py:22
  115.9 3.8 %fusion.17 = f32[512,2048]{1,0:T(8,128)S(1)} fusion(f32[512,2048]{1,0:T(8,128)S(1)} %fusion.20, bf16[512,1024]{1,0:T(8,128)(2,1)S(1)} %get-tuple-element.77, bf16[256,2048]{1,0:T(8,128)(2,1)S(1)} %collective-permute-done.26, bf16[256,2048]{1,0:T(8,128)(2,1)S(1)} %collective-permute-done.25, bf16[256,2048]{1,0:T(8,128)(2,1)} %collective-permute-done.20, ...), kind=kOutput, calls=%fused_computation.20 | convolution fusion | flops 2165309440 | bytes 13631488 | tf_op jit(solution)/shard_map/dot_general | solution.py:88
  119.7 3.9 %convolution_add_fusion.1 = f32[512,2304]{1,0:T(8,128)S(1)} fusion(f32[512,2304]{1,0:T(8,128)S(1)} %fusion.9, bf16[512,640]{1,0:T(8,128)(2,1)S(1)} %get-tuple-element.71, bf16[320,2304]{1,0:T(8,128)(2,1)} %collective-permute-done.22, bf16[320,2304]{1,0:T(8,128)(2,1)} %collective-permute-done.21), kind=kOutput, calls=%fused_computation.1 | convolution fusion | flops 1517027328 | bytes 13041664 | tf_op jit(solution)/shard_map/dot_general | solution.py:88
  123.6 2.8 %fusion = bf16[512,2304]{1,0:T(8,128)(2,1)} fusion(f32[512,2304]{1,0:T(8,128)S(1)} %convolution_add_fusion.1, bf16[512,512]{1,0:T(8,128)(2,1)S(1)} %get-tuple-element.51, bf16[256,2304]{1,0:T(8,128)(2,1)S(1)} %collective-permute-done.24, bf16[256,2304]{1,0:T(8,128)(2,1)S(1)} %collective-permute-done.23), kind=kOutput, calls=%fused_computation.2 | convolution fusion | flops 1215037440 | bytes 9961472 | tf_op jit(solution)/shard_map/dot_general | solution.py:88
  126.5 2.0 %add_convert_fusion = bf16[512,2048]{1,0:T(8,128)(2,1)} fusion(f32[512,2048]{1,0:T(8,128)S(1)} %fusion.17, bf16[512,256]{1,0:T(8,128)(2,1)S(1)} %get-tuple-element.82, bf16[128,2048]{1,0:T(8,128)(2,1)S(1)} %collective-permute-done.28, bf16[128,2048]{1,0:T(8,128)(2,1)S(1)} %collective-permute-done.27), kind=kOutput, calls=%fused_computation.11 | convolution fusion | flops 541065216 | bytes 7602176 | tf_op jit(solution)/shard_map/dot_general | solution.py:88
  (69 shorter events, 22.0 us)
Async XLA Ops:
  0.6 17.0 %collective-permute-start = (bf16[64,2304]{1,0:T(8,128)(2,1)}, bf16[64,2304]{1,0:T(8,128)(2,1)S(1)}, u32[]{:S(2)}, u32[]{:S(2)}) collective-permute-start(bf16[64,2304]{1,0:T(8,128)(2,1)} %param.6), channel_id=1, source_target_pairs={{0,32},{8,40},{16,48},{24,56},{32,64},{40,72},{48,80},{56,88},{64,... | collective-permute-start | bytes 884744 | tf_op jit(solution)/shard_map/ppermute | solution.py:22
  2.6 15.0 %collective-permute-start.1 = (bf16[64,2304]{1,0:T(8,128)(2,1)}, bf16[64,2304]{1,0:T(8,128)(2,1)S(1)}, u32[]{:S(2)}, u32[]{:S(2)}) collective-permute-start(bf16[64,2304]{1,0:T(8,128)(2,1)} %param.6), channel_id=1, source_target_pairs={{0,224},{8,232},{16,240},{24,248},{32,0},{40,8},{48,16},{56,24},{6... | collective-permute-start | bytes 884744 | tf_op jit(solution)/shard_map/ppermute | solution.py:22
  6.7 9.2 %collective-permute-start.2 = (bf16[64,2048]{1,0:T(8,128)(2,1)}, bf16[64,2048]{1,0:T(8,128)(2,1)S(1)}, u32[]{:S(2)}, u32[]{:S(2)}) collective-permute-start(bf16[64,2048]{1,0:T(8,128)(2,1)} %param.7), channel_id=1, source_target_pairs={{0,8},{8,16},{16,24},{24,0},{32,40},{40,48},{48,56},{56,32},{64,72... | collective-permute-start | bytes 786440 | tf_op jit(solution)/shard_map/ppermute | solution.py:22
  8.1 9.5 %collective-permute-start.3 = (bf16[64,2048]{1,0:T(8,128)(2,1)}, bf16[64,2048]{1,0:T(8,128)(2,1)S(1)}, u32[]{:S(2)}, u32[]{:S(2)}) collective-permute-start(bf16[64,2048]{1,0:T(8,128)(2,1)} %param.7), channel_id=1, source_target_pairs={{0,24},{8,0},{16,8},{24,16},{32,56},{40,32},{48,40},{56,48},{64,88... | collective-permute-start | bytes 786440 | tf_op jit(solution)/shard_map/ppermute | solution.py:22
  11.8 25.9 %copy-start.6 = (bf16[64,2048]{1,0:T(8,128)(2,1)S(1)}, bf16[64,2048]{1,0:T(8,128)(2,1)}, u32[]{:S(2)}) copy-start(bf16[64,2048]{1,0:T(8,128)(2,1)} %param.7) | copy-start | bytes 786436
  11.9 12.9 %collective-permute-start.7 = (bf16[256,1024]{1,0:T(8,128)(2,1)S(1)}, bf16[256,1024]{1,0:T(8,128)(2,1)S(1)}, u32[]{:S(2)}, u32[]{:S(2)}) collective-permute-start(bf16[256,1024]{1,0:T(8,128)(2,1)S(1)} %constant_dynamic-update-slice_fusion), channel_id=1, source_target_pairs={{0,2},{1,3},{2,4},{3,5},{4,6},{5,7},{6,0},{7,1},{8,10},{9,11},{10,... | collective-permute-start | bytes 1572872 | tf_op jit(solution)/shard_map/ppermute | solution.py:27
  15.8 8.6 %collective-permute-start.6 = (bf16[64,2048]{1,0:T(8,128)(2,1)}, bf16[64,2048]{1,0:T(8,128)(2,1)S(1)}, u32[]{:S(2)}, u32[]{:S(2)}) collective-permute-start(bf16[64,2048]{1,0:T(8,128)(2,1)} %param.7), channel_id=1, source_target_pairs={{0,16},{8,24},{16,0},{24,8},{32,48},{40,56},{48,32},{56,40},{64,80... | collective-permute-start | bytes 786440 | tf_op jit(solution)/shard_map/ppermute | solution.py:22
  17.7 8.6 %collective-permute-start.4 = (bf16[64,2304]{1,0:T(8,128)(2,1)S(1)}, bf16[64,2304]{1,0:T(8,128)(2,1)S(1)}, u32[]{:S(2)}, u32[]{:S(2)}) collective-permute-start(bf16[64,2304]{1,0:T(8,128)(2,1)S(1)} %collective-permute-done), channel_id=1, source_target_pairs={{0,32},{8,40},{16,48},{24,56},{32,64},{40,72},{48,80},{56,88},{64,... | collective-permute-start | bytes 884744 | tf_op jit(solution)/shard_map/ppermute | solution.py:22
  17.8 8.5 %collective-permute-start.5 = (bf16[64,2304]{1,0:T(8,128)(2,1)S(1)}, bf16[64,2304]{1,0:T(8,128)(2,1)S(1)}, u32[]{:S(2)}, u32[]{:S(2)}) collective-permute-start(bf16[64,2304]{1,0:T(8,128)(2,1)S(1)} %collective-permute-done.1), channel_id=1, source_target_pairs={{0,224},{8,232},{16,240},{24,248},{32,0},{40,8},{48,16},{56,24},{6... | collective-permute-start | bytes 884744 | tf_op jit(solution)/shard_map/ppermute | solution.py:22
  26.2 7.9 %collective-permute-start.13 = (bf16[64,2304]{1,0:T(8,128)(2,1)S(1)}, bf16[64,2304]{1,0:T(8,128)(2,1)S(1)}, u32[]{:S(2)}, u32[]{:S(2)}) collective-permute-start(bf16[64,2304]{1,0:T(8,128)(2,1)S(1)} %collective-permute-done.4), channel_id=1, source_target_pairs={{0,32},{8,40},{16,48},{24,56},{32,64},{40,72},{48,80},{56,88},{64,... | collective-permute-start | bytes 884744 | tf_op jit(solution)/shard_map/ppermute | solution.py:22
  26.2 7.9 %collective-permute-start.14 = (bf16[64,2304]{1,0:T(8,128)(2,1)S(1)}, bf16[64,2304]{1,0:T(8,128)(2,1)S(1)}, u32[]{:S(2)}, u32[]{:S(2)}) collective-permute-start(bf16[64,2304]{1,0:T(8,128)(2,1)S(1)} %collective-permute-done.5), channel_id=1, source_target_pairs={{0,224},{8,232},{16,240},{24,248},{32,0},{40,8},{48,16},{56,24},{6... | collective-permute-start | bytes 884744 | tf_op jit(solution)/shard_map/ppermute | solution.py:22
  29.5 18.4 %collective-permute-start.10 = (bf16[192,2304]{1,0:T(8,128)(2,1)S(1)}, bf16[192,2304]{1,0:T(8,128)(2,1)S(1)}, u32[]{:S(2)}, u32[]{:S(2)}) collective-permute-start(bf16[192,2304]{1,0:T(8,128)(2,1)S(1)} %pad_maximum_fusion.5), channel_id=1, source_target_pairs={{0,24},{8,0},{16,8},{24,16},{32,56},{40,32},{48,40},{56,48},{64,88... | collective-permute-start | bytes 2654216 | tf_op jit(solution)/shard_map/ppermute | solution.py:22
  30.6 19.5 %collective-permute-start.9 = (bf16[192,2304]{1,0:T(8,128)(2,1)S(1)}, bf16[192,2304]{1,0:T(8,128)(2,1)}, u32[]{:S(2)}, u32[]{:S(2)}) collective-permute-start(bf16[192,2304]{1,0:T(8,128)(2,1)S(1)} %pad_maximum_fusion.5), channel_id=1, source_target_pairs={{0,8},{8,16},{16,24},{24,0},{32,40},{40,48},{48,56},{56,32},{64,72... | collective-permute-start | bytes 2654216 | tf_op jit(solution)/shard_map/ppermute | solution.py:22
  31.5 14.8 %collective-permute-start.8 = (bf16[256,1024]{1,0:T(8,128)(2,1)S(1)}, bf16[256,1024]{1,0:T(8,128)(2,1)S(1)}, u32[]{:S(2)}, u32[]{:S(2)}) collective-permute-start(bf16[256,1024]{1,0:T(8,128)(2,1)S(1)} %constant_dynamic-update-slice_fusion), channel_id=1, source_target_pairs={{0,6},{1,7},{2,0},{3,1},{4,2},{5,3},{6,4},{7,5},{8,14},{9,15},{10,... | collective-permute-start | bytes 1572872 | tf_op jit(solution)/shard_map/ppermute | solution.py:27
  34.3 6.9 %collective-permute-start.15 = (bf16[32,2304]{1,0:T(8,128)(2,1)S(1)}, bf16[32,2304]{1,0:T(8,128)(2,1)S(1)}, u32[]{:S(2)}, u32[]{:S(2)}) collective-permute-start(bf16[32,2304]{1,0:T(8,128)(2,1)S(1)} %slice.24), channel_id=1, source_target_pairs={{0,32},{8,40},{16,48},{24,56},{32,64},{40,72},{48,80},{56,88},{64,... | collective-permute-start | bytes 442376 | tf_op jit(solution)/shard_map/ppermute | solution.py:22
  36.5 6.6 %collective-permute-start.16 = (bf16[32,2304]{1,0:T(8,128)(2,1)S(1)}, bf16[32,2304]{1,0:T(8,128)(2,1)S(1)}, u32[]{:S(2)}, u32[]{:S(2)}) collective-permute-start(bf16[32,2304]{1,0:T(8,128)(2,1)S(1)} %slice.25), channel_id=1, source_target_pairs={{0,224},{8,232},{16,240},{24,248},{32,0},{40,8},{48,16},{56,24},{6... | collective-permute-start | bytes 442376 | tf_op jit(solution)/shard_map/ppermute | solution.py:22
  43.1 20.2 %collective-permute-start.17 = (bf16[256,2048]{1,0:T(8,128)(2,1)S(1)}, bf16[256,2048]{1,0:T(8,128)(2,1)}, u32[]{:S(2)}, u32[]{:S(2)}) collective-permute-start(bf16[256,2048]{1,0:T(8,128)(2,1)S(1)} %pad_maximum_fusion.4), channel_id=1, source_target_pairs={{0,32},{8,40},{16,48},{24,56},{32,64},{40,72},{48,80},{56,88},{64,... | collective-permute-start | bytes 3145736 | tf_op jit(solution)/shard_map/ppermute | solution.py:22
  45.3 19.1 %collective-permute-start.19 = (bf16[256,2048]{1,0:T(8,128)(2,1)S(1)}, bf16[256,2048]{1,0:T(8,128)(2,1)}, u32[]{:S(2)}, u32[]{:S(2)}) collective-permute-start(bf16[256,2048]{1,0:T(8,128)(2,1)S(1)} %pad_maximum_fusion.4), channel_id=1, source_target_pairs={{0,224},{8,232},{16,240},{24,248},{32,0},{40,8},{48,16},{56,24},{6... | collective-permute-start | bytes 3145736 | tf_op jit(solution)/shard_map/ppermute | solution.py:22
  47.9 19.8 %copy-start = (bf16[192,2304]{1,0:T(8,128)(2,1)}, bf16[192,2304]{1,0:T(8,128)(2,1)S(1)}, u32[]{:S(2)}) copy-start(bf16[192,2304]{1,0:T(8,128)(2,1)S(1)} %collective-permute-done.10) | copy-start | bytes 2654212
  50.1 11.0 %collective-permute-start.11 = (bf16[256,1024]{1,0:T(8,128)(2,1)S(1)}, bf16[256,1024]{1,0:T(8,128)(2,1)S(1)}, u32[]{:S(2)}, u32[]{:S(2)}) collective-permute-start(bf16[256,1024]{1,0:T(8,128)(2,1)S(1)} %constant_dynamic-update-slice_fusion), channel_id=1, source_target_pairs={{0,4},{1,5},{2,6},{3,7},{4,0},{5,1},{6,2},{7,3},{8,12},{9,13},{10,... | collective-permute-start | bytes 1572872 | tf_op jit(solution)/shard_map/ppermute | solution.py:27
  53.6 31.1 %collective-permute-start.21 = (bf16[320,2304]{1,0:T(8,128)(2,1)}, bf16[320,2304]{1,0:T(8,128)(2,1)}, u32[]{:S(2)}, u32[]{:S(2)}) collective-permute-start(bf16[320,2304]{1,0:T(8,128)(2,1)} %pad_maximum_fusion), channel_id=1, source_target_pairs={{0,8},{8,16},{16,24},{24,0},{32,40},{40,48},{48,56},{56,32},{64,72... | collective-permute-start | bytes 4423688 | tf_op jit(solution)/shard_map/ppermute | solution.py:22
  53.6 31.1 %collective-permute-start.22 = (bf16[320,2304]{1,0:T(8,128)(2,1)}, bf16[320,2304]{1,0:T(8,128)(2,1)}, u32[]{:S(2)}, u32[]{:S(2)}) collective-permute-start(bf16[320,2304]{1,0:T(8,128)(2,1)} %pad_maximum_fusion), channel_id=1, source_target_pairs={{0,24},{8,0},{16,8},{24,16},{32,56},{40,32},{48,40},{56,48},{64,88... | collective-permute-start | bytes 4423688 | tf_op jit(solution)/shard_map/ppermute | solution.py:22
  61.1 36.4 %collective-permute-start.12 = (bf16[1024,1024]{1,0:T(8,128)(2,1)S(1)}, bf16[1024,1024]{1,0:T(8,128)(2,1)}, u32[]{:S(2)}, u32[]{:S(2)}) collective-permute-start(bf16[1024,1024]{1,0:T(8,128)(2,1)S(1)} %constant_dynamic-update-slice_fusion.2.mine_ref), channel_id=1, source_target_pairs={{0,1},{1,0},{2,3},{3,2},{4,5},{5,4},{6,7},{7,6},{8,9},{9,8},{10,11... | collective-permute-start | bytes 6291464 | tf_op jit(solution)/shard_map/ppermute | solution.py:27
  63.3 25.1 %collective-permute-start.18 = (bf16[256,2048]{1,0:T(8,128)(2,1)}, bf16[256,2048]{1,0:T(8,128)(2,1)}, u32[]{:S(2)}, u32[]{:S(2)}) collective-permute-start(bf16[256,2048]{1,0:T(8,128)(2,1)} %collective-permute-done.17), channel_id=1, source_target_pairs={{0,32},{8,40},{16,48},{24,56},{32,64},{40,72},{48,80},{56,88},{64,... | collective-permute-start | bytes 3145736 | tf_op jit(solution)/shard_map/ppermute | solution.py:22
  64.4 23.9 %collective-permute-start.20 = (bf16[256,2048]{1,0:T(8,128)(2,1)}, bf16[256,2048]{1,0:T(8,128)(2,1)}, u32[]{:S(2)}, u32[]{:S(2)}) collective-permute-start(bf16[256,2048]{1,0:T(8,128)(2,1)} %collective-permute-done.19), channel_id=1, source_target_pairs={{0,224},{8,232},{16,240},{24,248},{32,0},{40,8},{48,16},{56,24},{6... | collective-permute-start | bytes 3145736 | tf_op jit(solution)/shard_map/ppermute | solution.py:22
  67.8 26.3 %slice-start = ((bf16[192,2304]{1,0:T(8,128)(2,1)}), bf16[96,2304]{1,0:T(8,128)(2,1)S(1)}, s32[]{:S(2)}) async-start(bf16[192,2304]{1,0:T(8,128)(2,1)} %copy-done), calls=%async_computation | async-start | bytes 884736 | tf_op jit(solution)/shard_map/slice | solution.py:32
  88.3 24.0 %collective-permute-start.25 = (bf16[256,2048]{1,0:T(8,128)(2,1)}, bf16[256,2048]{1,0:T(8,128)(2,1)S(1)}, u32[]{:S(2)}, u32[]{:S(2)}) collective-permute-start(bf16[256,2048]{1,0:T(8,128)(2,1)} %collective-permute-done.18), channel_id=1, source_target_pairs={{0,32},{8,40},{16,48},{24,56},{32,64},{40,72},{48,80},{56,88},{64,... | collective-permute-start | bytes 3145736 | tf_op jit(solution)/shard_map/ppermute | solution.py:22
  88.9 23.5 %collective-permute-start.26 = (bf16[256,2048]{1,0:T(8,128)(2,1)}, bf16[256,2048]{1,0:T(8,128)(2,1)S(1)}, u32[]{:S(2)}, u32[]{:S(2)}) collective-permute-start(bf16[256,2048]{1,0:T(8,128)(2,1)} %collective-permute-done.20), channel_id=1, source_target_pairs={{0,224},{8,232},{16,240},{24,248},{32,0},{40,8},{48,16},{56,24},{6... | collective-permute-start | bytes 3145736 | tf_op jit(solution)/shard_map/ppermute | solution.py:22
  92.8 30.8 %collective-permute-start.23 = (bf16[256,2304]{1,0:T(8,128)(2,1)S(1)}, bf16[256,2304]{1,0:T(8,128)(2,1)S(1)}, u32[]{:S(2)}, u32[]{:S(2)}) collective-permute-start(bf16[256,2304]{1,0:T(8,128)(2,1)S(1)} %pad_maximum_fusion.2), channel_id=1, source_target_pairs={{0,8},{8,16},{16,24},{24,0},{32,40},{40,48},{48,56},{56,32},{64,72... | collective-permute-start | bytes 3538952 | tf_op jit(solution)/shard_map/ppermute | solution.py:22
  94.2 29.4 %collective-permute-start.24 = (bf16[256,2304]{1,0:T(8,128)(2,1)S(1)}, bf16[256,2304]{1,0:T(8,128)(2,1)S(1)}, u32[]{:S(2)}, u32[]{:S(2)}) collective-permute-start(bf16[256,2304]{1,0:T(8,128)(2,1)S(1)} %pad_maximum_fusion.3), channel_id=1, source_target_pairs={{0,24},{8,0},{16,8},{24,16},{32,56},{40,32},{48,40},{56,48},{64,88... | collective-permute-start | bytes 3538952 | tf_op jit(solution)/shard_map/ppermute | solution.py:22
  112.4 14.0 %collective-permute-start.27 = (bf16[128,2048]{1,0:T(8,128)(2,1)S(1)}, bf16[128,2048]{1,0:T(8,128)(2,1)S(1)}, u32[]{:S(2)}, u32[]{:S(2)}) collective-permute-start(bf16[128,2048]{1,0:T(8,128)(2,1)S(1)} %slice.30), channel_id=1, source_target_pairs={{0,32},{8,40},{16,48},{24,56},{32,64},{40,72},{48,80},{56,88},{64,... | collective-permute-start | bytes 1572872 | tf_op jit(solution)/shard_map/ppermute | solution.py:22
  112.9 13.5 %collective-permute-start.28 = (bf16[128,2048]{1,0:T(8,128)(2,1)S(1)}, bf16[128,2048]{1,0:T(8,128)(2,1)S(1)}, u32[]{:S(2)}, u32[]{:S(2)}) collective-permute-start(bf16[128,2048]{1,0:T(8,128)(2,1)S(1)} %slice.31), channel_id=1, source_target_pairs={{0,224},{8,232},{16,240},{24,248},{32,0},{40,8},{48,16},{56,24},{6... | collective-permute-start | bytes 1572872 | tf_op jit(solution)/shard_map/ppermute | solution.py:22
  (5 other events, 49.0 us)

commit v9 on v8

--- a/solution.py
+++ b/solution.py
@@ -121,13 +121,12 @@
 
     below, above = hop(tall, 1, 0), hop(tall, -1, 0)
     left, right, opposite = hop(wide, 0, 1), hop(wide, 0, -1), hop(wide, 0, 2)
-    down = hop_y(mine, 1)
     below, above, left, right = together((below, above, left, right))
     near = jnp.concatenate([tall, below, above])
-    near, opposite = together((near, opposite))
     below, above = hop(below, 1, 0), hop(above, -1, 0)
     near_left, near_right = hop(near, 0, 1), hop(near, 0, -1)
-    below, above, opposite, mine, down = together((below, above, opposite, mine, down))
+    down = hop_y(mine, 1)
+    below, above, opposite = together((below, above, opposite))
     far = [below, above]
     below, above = hop(below, 1, 0), hop(above, -1, 0)
     far = jnp.concatenate([*far, below, above])
@@ -137,9 +136,8 @@
     across = hop_y(mine, 2)
     far = [far, hop(halves(below)[0], 1, 0), hop(halves(above)[1], -1, 0)]
     wide = jnp.concatenate([wide, left, right, opposite])
-    far, wide = together((far, wide))
     far = jnp.concatenate(far)
-    far, near_left, near_right = together((far, near_left, near_right))
+    far, mine, up = together((far, mine, up))
     far_left, far_right = hop(far, 0, 1), hop(far, 0, -1)
     below, above = hop(wide, 1, 0), hop(wide, -1, 0)
     wide_first = [wide, below, above]
@@ -169,6 +167,7 @@
     below, above = hop(below, 1, 0), hop(above, -1, 0)
     first = jnp.concatenate([halves(near_left)[0], halves(far_left)[0]])
     second = jnp.concatenate([halves(near_right)[1], halves(far_right)[1]])
+
     tall_halves = [hop(first, 0, 1), hop(second, 0, -1)]
     below, above, wide_sum, tall_sum = together((below, above, wide_sum, tall_sum))
     wide_halves = [hop(halves(below)[0], 1, 0), hop(halves(above)[1], -1, 0)]

time: 130 us -> 130 us (level)
  matrix products: 20.4 us -> 14.2 us
  waiting for transfers between devices: 48 us -> 51.9 us
  starting transfers between devices: 47.1 us -> 49.4 us
  other arithmetic: 2.63 us -> 0.41 us
  local copies, waits for them, and re-layouts: 5.6 us -> 7.02 us
    dot_general x6, matrix products: 20.4 us -> 14.2 us  [contract(): jnp.dot(left, jnp.concatenate(grads), preferred_element_type=jnp.float32)]
    ppermute x25, waiting for transfers between devices: 43.5 us -> 48.1 us  [hop(): return lax.ppermute(value, 'row', pairs)]
    unnamed x18 -> x20, local copies, waits for them, and re-layouts: 1.11 us -> 5.63 us
    ppermute x25, starting transfers between devices: 42.6 us -> 46.6 us  [hop(): return lax.ppermute(value, 'row', pairs)]
    slice x9 -> x10, local copies, waits for them, and re-layouts: 3.48 us -> 0.21 us  [halves(): return (value[:half], value[half:])]
    ppermute x4, starting transfers between devices: 4.49 us -> 2.79 us  [hop_y(): return lax.ppermute(value, 'col', pairs)]
  transfers between devices with their start and end apart: 29 -> 29, of which waited for: 15 -> 12; matrix products, arithmetic and copies ran while one was open for 21% -> 15% of each run, Pallas kernels for 3% -> 3%
where the time goes in v9:
time: 130 us; the launch traced here: 128 us
  waiting for transfers between devices  51.9 us (40%)
  starting transfers between devices  49.4 us (38%)
  matrix products  14.2 us (11%)
  local copies, waits for them, and re-layouts  7.02 us (5%)
  Pallas kernels  4.22 us (3%)
    ppermute x25, waiting for transfers between devices, hop(): return lax.ppermute(value, 'row', pairs)  48.1 us
    ppermute x25, starting transfers between devices, hop(): return lax.ppermute(value, 'row', pairs)  46.6 us
    dot_general x6, matrix products, contract(): jnp.dot(left, jnp.concatenate(grads), preferred_element_type=jnp.float32)  14.2 us
    unnamed x20, local copies, waits for them, and re-layouts  5.63 us
    pallas_call x1, Pallas kernels, arrange(): pl.pallas_call(functools.partial(arrange_kernel, groups), out_shape=[jax....  4.22 us
    ppermute x4, waiting for transfers between devices, hop_y(): return lax.ppermute(value, 'col', pairs)  3.83 us
    ppermute x4, starting transfers between devices, hop_y(): return lax.ppermute(value, 'col', pairs)  2.79 us
  transfers between devices with their start and end apart: 29, of which 12 were waited for; matrix products, arithmetic and copies ran while one was open for 15% of the time, Pallas kernels for 3%

profile of v9, /device:TPU:8, one launch (start us, length us, event | category | flops | bytes accessed | tf_op | source)
XLA Modules:
  0.0 128.2 jit_solution(1993468854576081062)
XLA Ops:
  0.6 2.0 %collective-permute-start = (bf16[64,2304]{1,0:T(8,128)(2,1)}, bf16[64,2304]{1,0:T(8,128)(2,1)S(1)}, u32[]{:S(2)}, u32[]{:S(2)}) collective-permute-start(bf16[64,2304]{1,0:T(8,128)(2,1)} %param.6), channel_id=1, source_target_pairs={{0,32},{8,40},{16,48},{24,56},{32,64},{40,72},{48,80},{56,88},{64,... | collective-permute-start | bytes 884744 | tf_op jit(solution)/shard_map/ppermute | solution.py:22
  2.6 4.0 %collective-permute-start.1 = (bf16[64,2304]{1,0:T(8,128)(2,1)}, bf16[64,2304]{1,0:T(8,128)(2,1)S(1)}, u32[]{:S(2)}, u32[]{:S(2)}) collective-permute-start(bf16[64,2304]{1,0:T(8,128)(2,1)} %param.6), channel_id=1, source_target_pairs={{0,224},{8,232},{16,240},{24,248},{32,0},{40,8},{48,16},{56,24},{6... | collective-permute-start | bytes 884744 | tf_op jit(solution)/shard_map/ppermute | solution.py:22
  8.1 1.7 %collective-permute-start.3 = (bf16[64,2048]{1,0:T(8,128)(2,1)}, bf16[64,2048]{1,0:T(8,128)(2,1)S(1)}, u32[]{:S(2)}, u32[]{:S(2)}) collective-permute-start(bf16[64,2048]{1,0:T(8,128)(2,1)} %param.7), channel_id=1, source_target_pairs={{0,24},{8,0},{16,8},{24,16},{32,56},{40,32},{48,40},{56,48},{64,88... | collective-permute-start | bytes 786440 | tf_op jit(solution)/shard_map/ppermute | solution.py:22
  9.9 1.8 %collective-permute-start.6 = (bf16[64,2048]{1,0:T(8,128)(2,1)}, bf16[64,2048]{1,0:T(8,128)(2,1)S(1)}, u32[]{:S(2)}, u32[]{:S(2)}) collective-permute-start(bf16[64,2048]{1,0:T(8,128)(2,1)} %param.7), channel_id=1, source_target_pairs={{0,16},{8,24},{16,0},{24,8},{32,48},{40,56},{48,32},{56,40},{64,80... | collective-permute-start | bytes 786440 | tf_op jit(solution)/shard_map/ppermute | solution.py:22
  11.7 1.7 %constant_dynamic-update-slice_fusion.24 = (bf16[896,2304]{1,0:T(8,128)(2,1)}, bf16[192,2304]{1,0:T(8,128)(2,1)S(1)}) fusion(bf16[64,2304]{1,0:T(8,128)(2,1)} %param.6), kind=kLoop, calls=%fused_computation.50 | loop fusion | bytes 884736
  17.0 3.8 %collective-permute-done.3 = bf16[64,2048]{1,0:T(8,128)(2,1)S(1)} collective-permute-done((bf16[64,2048]{1,0:T(8,128)(2,1)}, bf16[64,2048]{1,0:T(8,128)(2,1)S(1)}, u32[]{:S(2)}, u32[]{:S(2)}) %collective-permute-start.3) | collective-permute-done | bytes 262176 | tf_op jit(solution)/shard_map/ppermute | solution.py:22
  20.9 3.2 %collective-permute-start.5 = (bf16[64,2304]{1,0:T(8,128)(2,1)S(1)}, bf16[64,2304]{1,0:T(8,128)(2,1)S(1)}, u32[]{:S(2)}, u32[]{:S(2)}) collective-permute-start(bf16[64,2304]{1,0:T(8,128)(2,1)S(1)} %collective-permute-done.1), channel_id=1, source_target_pairs={{0,224},{8,232},{16,240},{24,248},{32,0},{40,8},{48,16},{56,24},{6... | collective-permute-start | bytes 884744 | tf_op jit(solution)/shard_map/ppermute | solution.py:22
  25.6 3.6 %collective-permute-start.13 = (bf16[192,2304]{1,0:T(8,128)(2,1)S(1)}, bf16[192,2304]{1,0:T(8,128)(2,1)S(1)}, u32[]{:S(2)}, u32[]{:S(2)}) collective-permute-start(bf16[192,2304]{1,0:T(8,128)(2,1)S(1)} %get-tuple-element.69), channel_id=1, source_target_pairs={{0,24},{8,0},{16,8},{24,16},{32,56},{40,32},{48,40},{56,48},{64,88... | collective-permute-start | bytes 2654216 | tf_op jit(solution)/shard_map/ppermute | solution.py:22
  29.2 2.1 %collective-permute-done.4 = bf16[64,2304]{1,0:T(8,128)(2,1)S(1)} collective-permute-done((bf16[64,2304]{1,0:T(8,128)(2,1)S(1)}, bf16[64,2304]{1,0:T(8,128)(2,1)S(1)}, u32[]{:S(2)}, u32[]{:S(2)}) %collective-permute-start.4) | collective-permute-done | bytes 294944 | tf_op jit(solution)/shard_map/ppermute | solution.py:22
  31.3 3.6 %collective-permute-start.8 = (bf16[64,2304]{1,0:T(8,128)(2,1)S(1)}, bf16[64,2304]{1,0:T(8,128)(2,1)S(1)}, u32[]{:S(2)}, u32[]{:S(2)}) collective-permute-start(bf16[64,2304]{1,0:T(8,128)(2,1)S(1)} %collective-permute-done.5), channel_id=1, source_target_pairs={{0,224},{8,232},{16,240},{24,248},{32,0},{40,8},{48,16},{56,24},{6... | collective-permute-start | bytes 884744 | tf_op jit(solution)/shard_map/ppermute | solution.py:22
  34.9 4.9 %collective-permute-done.7 = bf16[64,2304]{1,0:T(8,128)(2,1)S(1)} collective-permute-done((bf16[64,2304]{1,0:T(8,128)(2,1)S(1)}, bf16[64,2304]{1,0:T(8,128)(2,1)S(1)}, u32[]{:S(2)}, u32[]{:S(2)}) %collective-permute-start.7) | collective-permute-done | bytes 294944 | tf_op jit(solution)/shard_map/ppermute | solution.py:22
  41.5 4.8 %collective-permute-start.10 = (bf16[32,2304]{1,0:T(8,128)(2,1)S(1)}, bf16[32,2304]{1,0:T(8,128)(2,1)S(1)}, u32[]{:S(2)}, u32[]{:S(2)}) collective-permute-start(bf16[32,2304]{1,0:T(8,128)(2,1)S(1)} %slice.25), channel_id=1, source_target_pairs={{0,224},{8,232},{16,240},{24,248},{32,0},{40,8},{48,16},{56,24},{6... | collective-permute-start | bytes 442376 | tf_op jit(solution)/shard_map/ppermute | solution.py:22
  47.0 3.1 %collective-permute-start.19 = (bf16[256,2048]{1,0:T(8,128)(2,1)S(1)}, bf16[256,2048]{1,0:T(8,128)(2,1)S(1)}, u32[]{:S(2)}, u32[]{:S(2)}) collective-permute-start(bf16[256,2048]{1,0:T(8,128)(2,1)S(1)} %get-tuple-element.75), channel_id=1, source_target_pairs={{0,224},{8,232},{16,240},{24,248},{32,0},{40,8},{48,16},{56,24},{6... | collective-permute-start | bytes 3145736 | tf_op jit(solution)/shard_map/ppermute | solution.py:22
  51.3 2.6 %collective-permute-done.9 = bf16[32,2304]{1,0:T(8,128)(2,1)S(1)} collective-permute-done((bf16[32,2304]{1,0:T(8,128)(2,1)S(1)}, bf16[32,2304]{1,0:T(8,128)(2,1)S(1)}, u32[]{:S(2)}, u32[]{:S(2)}) %collective-permute-start.9) | collective-permute-done | bytes 147488 | tf_op jit(solution)/shard_map/ppermute | solution.py:22
  54.2 3.3 %collective-permute-start.22 = (bf16[320,2304]{1,0:T(8,128)(2,1)S(1)}, bf16[320,2304]{1,0:T(8,128)(2,1)S(1)}, u32[]{:S(2)}, u32[]{:S(2)}) collective-permute-start(bf16[320,2304]{1,0:T(8,128)(2,1)S(1)} %pad_maximum_fusion), channel_id=1, source_target_pairs={{0,24},{8,0},{16,8},{24,16},{32,56},{40,32},{48,40},{56,48},{64,88... | collective-permute-start | bytes 4423688 | tf_op jit(solution)/shard_map/ppermute | solution.py:22
  57.5 3.8 %collective-permute-done.15 = bf16[256,1024]{1,0:T(8,128)(2,1)S(1)} collective-permute-done((bf16[256,1024]{1,0:T(8,128)(2,1)S(1)}, bf16[256,1024]{1,0:T(8,128)(2,1)S(1)}, u32[]{:S(2)}, u32[]{:S(2)}) %collective-permute-start.15) | collective-permute-done | bytes 524320 | tf_op jit(solution)/shard_map/ppermute | solution.py:27
  61.6 3.6 %collective-permute-done.17 = bf16[256,2048]{1,0:T(8,128)(2,1)S(1)} collective-permute-done((bf16[256,2048]{1,0:T(8,128)(2,1)S(1)}, bf16[256,2048]{1,0:T(8,128)(2,1)S(1)}, u32[]{:S(2)}, u32[]{:S(2)}) %collective-permute-start.17) | collective-permute-done | bytes 1048608 | tf_op jit(solution)/shard_map/ppermute | solution.py:22
  65.2 3.2 %collective-permute-start.20 = (bf16[256,2048]{1,0:T(8,128)(2,1)S(1)}, bf16[256,2048]{1,0:T(8,128)(2,1)S(1)}, u32[]{:S(2)}, u32[]{:S(2)}) collective-permute-start(bf16[256,2048]{1,0:T(8,128)(2,1)S(1)} %collective-permute-done.19), channel_id=1, source_target_pairs={{0,224},{8,232},{16,240},{24,248},{32,0},{40,8},{48,16},{56,24},{6... | collective-permute-start | bytes 3145736 | tf_op jit(solution)/shard_map/ppermute | solution.py:22
  68.8 8.1 %collective-permute-done.21 = bf16[320,2304]{1,0:T(8,128)(2,1)S(1)} collective-permute-done((bf16[320,2304]{1,0:T(8,128)(2,1)S(1)}, bf16[320,2304]{1,0:T(8,128)(2,1)S(1)}, u32[]{:S(2)}, u32[]{:S(2)}) %collective-permute-start.21) | collective-permute-done | bytes 1474592 | tf_op jit(solution)/shard_map/ppermute | solution.py:22
  76.9 12.3 %collective-permute-done.18 = bf16[256,2048]{1,0:T(8,128)(2,1)S(1)} collective-permute-done((bf16[256,2048]{1,0:T(8,128)(2,1)S(1)}, bf16[256,2048]{1,0:T(8,128)(2,1)S(1)}, u32[]{:S(2)}, u32[]{:S(2)}) %collective-permute-start.18) | collective-permute-done | bytes 1048608 | tf_op jit(solution)/shard_map/ppermute | solution.py:22
  89.2 2.4 %collective-permute-start.25 = (bf16[256,2048]{1,0:T(8,128)(2,1)S(1)}, bf16[256,2048]{1,0:T(8,128)(2,1)S(1)}, u32[]{:S(2)}, u32[]{:S(2)}) collective-permute-start(bf16[256,2048]{1,0:T(8,128)(2,1)S(1)} %collective-permute-done.18), channel_id=1, source_target_pairs={{0,32},{8,40},{16,48},{24,56},{32,64},{40,72},{48,80},{56,88},{64,... | collective-permute-start | bytes 3145736 | tf_op jit(solution)/shard_map/ppermute | solution.py:22
  93.1 3.0 %collective-permute-start.24 = (bf16[256,2304]{1,0:T(8,128)(2,1)S(1)}, bf16[256,2304]{1,0:T(8,128)(2,1)S(1)}, u32[]{:S(2)}, u32[]{:S(2)}) collective-permute-start(bf16[256,2304]{1,0:T(8,128)(2,1)S(1)} %pad_maximum_fusion.3), channel_id=1, source_target_pairs={{0,24},{8,0},{16,8},{24,16},{32,56},{40,32},{48,40},{56,48},{64,88... | collective-permute-start | bytes 3538952 | tf_op jit(solution)/shard_map/ppermute | solution.py:22
  96.1 4.2 %shard_map.59 = (bf16[512,896]{1,0:T(8,128)(2,1)S(1)}, bf16[512,640]{1,0:T(8,128)(2,1)S(1)}, bf16[512,512]{1,0:T(8,128)(2,1)S(1)}, bf16[512,768]{1,0:T(8,128)(2,...) custom-call(s32[4]{0:T(128)S(1)} %pad_add_fusion.place_ref, ...), custom_call_target="tpu_custom_call" | custom-call | bytes 12582912 | tf_op jit(solution)/shard_map/pallas_call | solution.py:71
  100.3 1.8 %fusion.25 = f32[512,2048]{1,0:T(8,128)S(1)} fusion(bf16[512,768]{1,0:T(8,128)(2,1)S(1)} %get-tuple-element.58, bf16[768,2048]{1,0:T(8,128)(2,1)S(1)} %constant_dynamic-update-slice_fusion.13), kind=kOutput, calls=%fused_computation.56 | convolution fusion | flops 1610612736 | bytes 8126464 | tf_op jit(solution)/shard_map/dot_general | solution.py:88
  102.2 2.6 %fusion.26 = f32[512,2304]{1,0:T(8,128)S(1)} fusion(bf16[512,896]{1,0:T(8,128)(2,1)S(1)} %get-tuple-element.59, bf16[896,2304]{1,0:T(8,128)(2,1)S(1)} %constant_dynamic-update-slice_fusion.19), kind=kOutput, calls=%fused_computation.57 | convolution fusion | flops 2113929216 | bytes 9764864 | tf_op jit(solution)/shard_map/dot_general | solution.py:88
  104.8 7.5 %collective-permute-done.25 = bf16[256,2048]{1,0:T(8,128)(2,1)S(1)} collective-permute-done((bf16[256,2048]{1,0:T(8,128)(2,1)S(1)}, bf16[256,2048]{1,0:T(8,128)(2,1)S(1)}, u32[]{:S(2)}, u32[]{:S(2)}) %collective-permute-start.25) | collective-permute-done | bytes 1048608 | tf_op jit(solution)/shard_map/ppermute | solution.py:22
  112.3 2.0 %collective-permute-done.26 = bf16[256,2048]{1,0:T(8,128)(2,1)S(1)} collective-permute-done((bf16[256,2048]{1,0:T(8,128)(2,1)S(1)}, bf16[256,2048]{1,0:T(8,128)(2,1)S(1)}, u32[]{:S(2)}, u32[]{:S(2)}) %collective-permute-start.26) | collective-permute-done | bytes 1048608 | tf_op jit(solution)/shard_map/ppermute | solution.py:22
  114.3 1.9 %collective-permute-start.27 = (bf16[128,2048]{1,0:T(8,128)(2,1)S(1)}, bf16[128,2048]{1,0:T(8,128)(2,1)S(1)}, u32[]{:S(2)}, u32[]{:S(2)}) collective-permute-start(bf16[128,2048]{1,0:T(8,128)(2,1)S(1)} %slice.30), channel_id=1, source_target_pairs={{0,32},{8,40},{16,48},{24,56},{32,64},{40,72},{48,80},{56,88},{64,... | collective-permute-start | bytes 1572872 | tf_op jit(solution)/shard_map/ppermute | solution.py:22
  117.8 2.9 %fusion.9 = f32[512,2048]{1,0:T(8,128)S(1)} fusion(f32[512,2048]{1,0:T(8,128)S(1)} %fusion.25, bf16[512,1024]{1,0:T(8,128)(2,1)S(1)} %get-tuple-element.61, bf16[256,2048]{1,0:T(8,128)(2,1)S(1)} %collective-permute-done.26, bf16[256,2048]{1,0:T(8,128)(2,1)S(1)} %collective-permute-done.25, bf16[256,2048]{1,0:T(8,128)(2,1)S(1)} %collective-permute-done.20, ...), kind=kOutput, calls=%fused_computation.12 | convolution fusion | flops 2165309440 | bytes 13631488 | tf_op jit(solution)/shard_map/dot_general | solution.py:88
  120.7 2.0 %convolution_add_fusion.1 = f32[512,2304]{1,0:T(8,128)S(1)} fusion(f32[512,2304]{1,0:T(8,128)S(1)} %fusion.26, bf16[512,640]{1,0:T(8,128)(2,1)S(1)} %get-tuple-element.55, bf16[320,2304]{1,0:T(8,128)(2,1)S(1)} %collective-permute-done.22, bf16[320,2304]{1,0:T(8,128)(2,1)S(1)} %collective-permute-done.21), kind=kOutput, calls=%fused_computation.1 | convolution fusion | flops 1517027328 | bytes 13041664 | tf_op jit(solution)/shard_map/dot_general | solution.py:88
  122.7 2.8 %fusion = bf16[512,2304]{1,0:T(8,128)(2,1)} fusion(f32[512,2304]{1,0:T(8,128)S(1)} %convolution_add_fusion.1, bf16[512,512]{1,0:T(8,128)(2,1)S(1)} %get-tuple-element.46, bf16[256,2304]{1,0:T(8,128)(2,1)S(1)} %collective-permute-done.24, bf16[256,2304]{1,0:T(8,128)(2,1)S(1)} %collective-permute-done.23), kind=kOutput, calls=%fused_computation.2 | convolution fusion | flops 1215037440 | bytes 9961472 | tf_op jit(solution)/shard_map/dot_general | solution.py:88
  126.2 2.0 %add_convert_fusion = bf16[512,2048]{1,0:T(8,128)(2,1)} fusion(f32[512,2048]{1,0:T(8,128)S(1)} %fusion.9, bf16[512,256]{1,0:T(8,128)(2,1)S(1)} %get-tuple-element.66, bf16[128,2048]{1,0:T(8,128)(2,1)S(1)} %collective-permute-done.28, bf16[128,2048]{1,0:T(8,128)(2,1)S(1)} %collective-permute-done.27), kind=kOutput, calls=%fused_computation.11 | convolution fusion | flops 541065216 | bytes 7602176 | tf_op jit(solution)/shard_map/dot_general | solution.py:88
  (72 shorter events, 14.6 us)
Async XLA Ops:
  0.6 20.2 %collective-permute-start = (bf16[64,2304]{1,0:T(8,128)(2,1)}, bf16[64,2304]{1,0:T(8,128)(2,1)S(1)}, u32[]{:S(2)}, u32[]{:S(2)}) collective-permute-start(bf16[64,2304]{1,0:T(8,128)(2,1)} %param.6), channel_id=1, source_target_pairs={{0,32},{8,40},{16,48},{24,56},{32,64},{40,72},{48,80},{56,88},{64,... | collective-permute-start | bytes 884744 | tf_op jit(solution)/shard_map/ppermute | solution.py:22
  2.6 18.2 %collective-permute-start.1 = (bf16[64,2304]{1,0:T(8,128)(2,1)}, bf16[64,2304]{1,0:T(8,128)(2,1)S(1)}, u32[]{:S(2)}, u32[]{:S(2)}) collective-permute-start(bf16[64,2304]{1,0:T(8,128)(2,1)} %param.6), channel_id=1, source_target_pairs={{0,224},{8,232},{16,240},{24,248},{32,0},{40,8},{48,16},{56,24},{6... | collective-permute-start | bytes 884744 | tf_op jit(solution)/shard_map/ppermute | solution.py:22
  6.7 9.9 %collective-permute-start.2 = (bf16[64,2048]{1,0:T(8,128)(2,1)}, bf16[64,2048]{1,0:T(8,128)(2,1)S(1)}, u32[]{:S(2)}, u32[]{:S(2)}) collective-permute-start(bf16[64,2048]{1,0:T(8,128)(2,1)} %param.7), channel_id=1, source_target_pairs={{0,8},{8,16},{16,24},{24,0},{32,40},{40,48},{48,56},{56,32},{64,72... | collective-permute-start | bytes 786440 | tf_op jit(solution)/shard_map/ppermute | solution.py:22
  8.1 12.7 %collective-permute-start.3 = (bf16[64,2048]{1,0:T(8,128)(2,1)}, bf16[64,2048]{1,0:T(8,128)(2,1)S(1)}, u32[]{:S(2)}, u32[]{:S(2)}) collective-permute-start(bf16[64,2048]{1,0:T(8,128)(2,1)} %param.7), channel_id=1, source_target_pairs={{0,24},{8,0},{16,8},{24,16},{32,56},{40,32},{48,40},{56,48},{64,88... | collective-permute-start | bytes 786440 | tf_op jit(solution)/shard_map/ppermute | solution.py:22
  9.9 15.8 %collective-permute-start.6 = (bf16[64,2048]{1,0:T(8,128)(2,1)}, bf16[64,2048]{1,0:T(8,128)(2,1)S(1)}, u32[]{:S(2)}, u32[]{:S(2)}) collective-permute-start(bf16[64,2048]{1,0:T(8,128)(2,1)} %param.7), channel_id=1, source_target_pairs={{0,16},{8,24},{16,0},{24,8},{32,48},{40,56},{48,32},{56,40},{64,80... | collective-permute-start | bytes 786440 | tf_op jit(solution)/shard_map/ppermute | solution.py:22
  16.5 29.9 %collective-permute-start.11 = (bf16[256,1024]{1,0:T(8,128)(2,1)S(1)}, bf16[256,1024]{1,0:T(8,128)(2,1)S(1)}, u32[]{:S(2)}, u32[]{:S(2)}) collective-permute-start(bf16[256,1024]{1,0:T(8,128)(2,1)S(1)} %constant_dynamic-update-slice_fusion), channel_id=1, source_target_pairs={{0,6},{1,7},{2,0},{3,1},{4,2},{5,3},{6,4},{7,5},{8,14},{9,15},{10,... | collective-permute-start | bytes 1572872 | tf_op jit(solution)/shard_map/ppermute | solution.py:27
  20.9 10.4 %collective-permute-start.4 = (bf16[64,2304]{1,0:T(8,128)(2,1)S(1)}, bf16[64,2304]{1,0:T(8,128)(2,1)S(1)}, u32[]{:S(2)}, u32[]{:S(2)}) collective-permute-start(bf16[64,2304]{1,0:T(8,128)(2,1)S(1)} %collective-permute-done), channel_id=1, source_target_pairs={{0,32},{8,40},{16,48},{24,56},{32,64},{40,72},{48,80},{56,88},{64,... | collective-permute-start | bytes 884744 | tf_op jit(solution)/shard_map/ppermute | solution.py:22
  20.9 10.4 %collective-permute-start.5 = (bf16[64,2304]{1,0:T(8,128)(2,1)S(1)}, bf16[64,2304]{1,0:T(8,128)(2,1)S(1)}, u32[]{:S(2)}, u32[]{:S(2)}) collective-permute-start(bf16[64,2304]{1,0:T(8,128)(2,1)S(1)} %collective-permute-done.1), channel_id=1, source_target_pairs={{0,224},{8,232},{16,240},{24,248},{32,0},{40,8},{48,16},{56,24},{6... | collective-permute-start | bytes 884744 | tf_op jit(solution)/shard_map/ppermute | solution.py:22
  25.6 20.9 %collective-permute-start.12 = (bf16[192,2304]{1,0:T(8,128)(2,1)S(1)}, bf16[192,2304]{1,0:T(8,128)(2,1)S(1)}, u32[]{:S(2)}, u32[]{:S(2)}) collective-permute-start(bf16[192,2304]{1,0:T(8,128)(2,1)S(1)} %get-tuple-element.69), channel_id=1, source_target_pairs={{0,8},{8,16},{16,24},{24,0},{32,40},{40,48},{48,56},{56,32},{64,72... | collective-permute-start | bytes 2654216 | tf_op jit(solution)/shard_map/ppermute | solution.py:22
  25.6 21.4 %collective-permute-start.13 = (bf16[192,2304]{1,0:T(8,128)(2,1)S(1)}, bf16[192,2304]{1,0:T(8,128)(2,1)S(1)}, u32[]{:S(2)}, u32[]{:S(2)}) collective-permute-start(bf16[192,2304]{1,0:T(8,128)(2,1)S(1)} %get-tuple-element.69), channel_id=1, source_target_pairs={{0,24},{8,0},{16,8},{24,16},{32,56},{40,32},{48,40},{56,48},{64,88... | collective-permute-start | bytes 2654216 | tf_op jit(solution)/shard_map/ppermute | solution.py:22
  31.3 8.6 %collective-permute-start.7 = (bf16[64,2304]{1,0:T(8,128)(2,1)S(1)}, bf16[64,2304]{1,0:T(8,128)(2,1)S(1)}, u32[]{:S(2)}, u32[]{:S(2)}) collective-permute-start(bf16[64,2304]{1,0:T(8,128)(2,1)S(1)} %collective-permute-done.4), channel_id=1, source_target_pairs={{0,32},{8,40},{16,48},{24,56},{32,64},{40,72},{48,80},{56,88},{64,... | collective-permute-start | bytes 884744 | tf_op jit(solution)/shard_map/ppermute | solution.py:22
  31.3 10.2 %collective-permute-start.8 = (bf16[64,2304]{1,0:T(8,128)(2,1)S(1)}, bf16[64,2304]{1,0:T(8,128)(2,1)S(1)}, u32[]{:S(2)}, u32[]{:S(2)}) collective-permute-start(bf16[64,2304]{1,0:T(8,128)(2,1)S(1)} %collective-permute-done.5), channel_id=1, source_target_pairs={{0,224},{8,232},{16,240},{24,248},{32,0},{40,8},{48,16},{56,24},{6... | collective-permute-start | bytes 884744 | tf_op jit(solution)/shard_map/ppermute | solution.py:22
  39.9 14.3 %collective-permute-start.14 = (bf16[256,1024]{1,0:T(8,128)(2,1)S(1)}, bf16[256,1024]{1,0:T(8,128)(2,1)S(1)}, u32[]{:S(2)}, u32[]{:S(2)}) collective-permute-start(bf16[256,1024]{1,0:T(8,128)(2,1)S(1)} %constant_dynamic-update-slice_fusion), channel_id=1, source_target_pairs={{0,2},{1,3},{2,4},{3,5},{4,6},{5,7},{6,0},{7,1},{8,10},{9,11},{10,... | collective-permute-start | bytes 1572872 | tf_op jit(solution)/shard_map/ppermute | solution.py:27
  41.5 9.1 %collective-permute-start.10 = (bf16[32,2304]{1,0:T(8,128)(2,1)S(1)}, bf16[32,2304]{1,0:T(8,128)(2,1)S(1)}, u32[]{:S(2)}, u32[]{:S(2)}) collective-permute-start(bf16[32,2304]{1,0:T(8,128)(2,1)S(1)} %slice.25), channel_id=1, source_target_pairs={{0,224},{8,232},{16,240},{24,248},{32,0},{40,8},{48,16},{56,24},{6... | collective-permute-start | bytes 442376 | tf_op jit(solution)/shard_map/ppermute | solution.py:22
  46.4 7.5 %collective-permute-start.9 = (bf16[32,2304]{1,0:T(8,128)(2,1)S(1)}, bf16[32,2304]{1,0:T(8,128)(2,1)S(1)}, u32[]{:S(2)}, u32[]{:S(2)}) collective-permute-start(bf16[32,2304]{1,0:T(8,128)(2,1)S(1)} %slice.24), channel_id=1, source_target_pairs={{0,32},{8,40},{16,48},{24,56},{32,64},{40,72},{48,80},{56,88},{64,... | collective-permute-start | bytes 442376 | tf_op jit(solution)/shard_map/ppermute | solution.py:22
  46.5 21.9 %copy-start = (bf16[192,2304]{1,0:T(8,128)(2,1)}, bf16[192,2304]{1,0:T(8,128)(2,1)S(1)}, u32[]{:S(2)}) copy-start(bf16[192,2304]{1,0:T(8,128)(2,1)S(1)} %collective-permute-done.12) | copy-start | bytes 2654212
  46.6 18.6 %collective-permute-start.17 = (bf16[256,2048]{1,0:T(8,128)(2,1)S(1)}, bf16[256,2048]{1,0:T(8,128)(2,1)S(1)}, u32[]{:S(2)}, u32[]{:S(2)}) collective-permute-start(bf16[256,2048]{1,0:T(8,128)(2,1)S(1)} %get-tuple-element.75), channel_id=1, source_target_pairs={{0,32},{8,40},{16,48},{24,56},{32,64},{40,72},{48,80},{56,88},{64,... | collective-permute-start | bytes 3145736 | tf_op jit(solution)/shard_map/ppermute | solution.py:22
  47.0 18.1 %collective-permute-start.19 = (bf16[256,2048]{1,0:T(8,128)(2,1)S(1)}, bf16[256,2048]{1,0:T(8,128)(2,1)S(1)}, u32[]{:S(2)}, u32[]{:S(2)}) collective-permute-start(bf16[256,2048]{1,0:T(8,128)(2,1)S(1)} %get-tuple-element.75), channel_id=1, source_target_pairs={{0,224},{8,232},{16,240},{24,248},{32,0},{40,8},{48,16},{56,24},{6... | collective-permute-start | bytes 3145736 | tf_op jit(solution)/shard_map/ppermute | solution.py:22
  50.7 10.7 %collective-permute-start.15 = (bf16[256,1024]{1,0:T(8,128)(2,1)S(1)}, bf16[256,1024]{1,0:T(8,128)(2,1)S(1)}, u32[]{:S(2)}, u32[]{:S(2)}) collective-permute-start(bf16[256,1024]{1,0:T(8,128)(2,1)S(1)} %constant_dynamic-update-slice_fusion), channel_id=1, source_target_pairs={{0,4},{1,5},{2,6},{3,7},{4,0},{5,1},{6,2},{7,3},{8,12},{9,13},{10,... | collective-permute-start | bytes 1572872 | tf_op jit(solution)/shard_map/ppermute | solution.py:27
  54.0 22.9 %collective-permute-start.21 = (bf16[320,2304]{1,0:T(8,128)(2,1)S(1)}, bf16[320,2304]{1,0:T(8,128)(2,1)S(1)}, u32[]{:S(2)}, u32[]{:S(2)}) collective-permute-start(bf16[320,2304]{1,0:T(8,128)(2,1)S(1)} %pad_maximum_fusion), channel_id=1, source_target_pairs={{0,8},{8,16},{16,24},{24,0},{32,40},{40,48},{48,56},{56,32},{64,72... | collective-permute-start | bytes 4423688 | tf_op jit(solution)/shard_map/ppermute | solution.py:22
  54.2 22.7 %collective-permute-start.22 = (bf16[320,2304]{1,0:T(8,128)(2,1)S(1)}, bf16[320,2304]{1,0:T(8,128)(2,1)S(1)}, u32[]{:S(2)}, u32[]{:S(2)}) collective-permute-start(bf16[320,2304]{1,0:T(8,128)(2,1)S(1)} %pad_maximum_fusion), channel_id=1, source_target_pairs={{0,24},{8,0},{16,8},{24,16},{32,56},{40,32},{48,40},{56,48},{64,88... | collective-permute-start | bytes 4423688 | tf_op jit(solution)/shard_map/ppermute | solution.py:22
  61.4 34.7 %collective-permute-start.16 = (bf16[1024,1024]{1,0:T(8,128)(2,1)S(1)}, bf16[1024,1024]{1,0:T(8,128)(2,1)S(1)}, u32[]{:S(2)}, u32[]{:S(2)}) collective-permute-start(bf16[1024,1024]{1,0:T(8,128)(2,1)S(1)} %constant_dynamic-update-slice_fusion.5.mine_ref), channel_id=1, source_target_pairs={{0,1},{1,0},{2,3},{3,2},{4,5},{5,4},{6,7},{7,6},{8,9},{9,8},{10,11... | collective-permute-start | bytes 6291464 | tf_op jit(solution)/shard_map/ppermute | solution.py:27
  65.2 24.0 %collective-permute-start.18 = (bf16[256,2048]{1,0:T(8,128)(2,1)S(1)}, bf16[256,2048]{1,0:T(8,128)(2,1)S(1)}, u32[]{:S(2)}, u32[]{:S(2)}) collective-permute-start(bf16[256,2048]{1,0:T(8,128)(2,1)S(1)} %collective-permute-done.17), channel_id=1, source_target_pairs={{0,32},{8,40},{16,48},{24,56},{32,64},{40,72},{48,80},{56,88},{64,... | collective-permute-start | bytes 3145736 | tf_op jit(solution)/shard_map/ppermute | solution.py:22
  65.2 24.0 %collective-permute-start.20 = (bf16[256,2048]{1,0:T(8,128)(2,1)S(1)}, bf16[256,2048]{1,0:T(8,128)(2,1)S(1)}, u32[]{:S(2)}, u32[]{:S(2)}) collective-permute-start(bf16[256,2048]{1,0:T(8,128)(2,1)S(1)} %collective-permute-done.19), channel_id=1, source_target_pairs={{0,224},{8,232},{16,240},{24,248},{32,0},{40,8},{48,16},{56,24},{6... | collective-permute-start | bytes 3145736 | tf_op jit(solution)/shard_map/ppermute | solution.py:22
  68.6 23.9 %slice-start = ((bf16[192,2304]{1,0:T(8,128)(2,1)}), bf16[96,2304]{1,0:T(8,128)(2,1)S(1)}, s32[]{:S(2)}) async-start(bf16[192,2304]{1,0:T(8,128)(2,1)} %copy-done), calls=%async_computation | async-start | bytes 884736 | tf_op jit(solution)/shard_map/slice | solution.py:32
  68.7 24.3 %slice-start.1 = ((bf16[192,2304]{1,0:T(8,128)(2,1)}), bf16[96,2304]{1,0:T(8,128)(2,1)S(1)}, s32[]{:S(2)}) async-start(bf16[192,2304]{1,0:T(8,128)(2,1)} %copy-done.1), calls=%async_computation.1 | async-start | bytes 884736 | tf_op jit(solution)/shard_map/slice | solution.py:32
  89.2 23.1 %collective-permute-start.25 = (bf16[256,2048]{1,0:T(8,128)(2,1)S(1)}, bf16[256,2048]{1,0:T(8,128)(2,1)S(1)}, u32[]{:S(2)}, u32[]{:S(2)}) collective-permute-start(bf16[256,2048]{1,0:T(8,128)(2,1)S(1)} %collective-permute-done.18), channel_id=1, source_target_pairs={{0,32},{8,40},{16,48},{24,56},{32,64},{40,72},{48,80},{56,88},{64,... | collective-permute-start | bytes 3145736 | tf_op jit(solution)/shard_map/ppermute | solution.py:22
  91.5 22.7 %collective-permute-start.26 = (bf16[256,2048]{1,0:T(8,128)(2,1)S(1)}, bf16[256,2048]{1,0:T(8,128)(2,1)S(1)}, u32[]{:S(2)}, u32[]{:S(2)}) collective-permute-start(bf16[256,2048]{1,0:T(8,128)(2,1)S(1)} %collective-permute-done.20), channel_id=1, source_target_pairs={{0,224},{8,232},{16,240},{24,248},{32,0},{40,8},{48,16},{56,24},{6... | collective-permute-start | bytes 3145736 | tf_op jit(solution)/shard_map/ppermute | solution.py:22
  92.6 30.1 %collective-permute-start.23 = (bf16[256,2304]{1,0:T(8,128)(2,1)S(1)}, bf16[256,2304]{1,0:T(8,128)(2,1)S(1)}, u32[]{:S(2)}, u32[]{:S(2)}) collective-permute-start(bf16[256,2304]{1,0:T(8,128)(2,1)S(1)} %pad_maximum_fusion.2), channel_id=1, source_target_pairs={{0,8},{8,16},{16,24},{24,0},{32,40},{40,48},{48,56},{56,32},{64,72... | collective-permute-start | bytes 3538952 | tf_op jit(solution)/shard_map/ppermute | solution.py:22
  93.1 29.6 %collective-permute-start.24 = (bf16[256,2304]{1,0:T(8,128)(2,1)S(1)}, bf16[256,2304]{1,0:T(8,128)(2,1)S(1)}, u32[]{:S(2)}, u32[]{:S(2)}) collective-permute-start(bf16[256,2304]{1,0:T(8,128)(2,1)S(1)} %pad_maximum_fusion.3), channel_id=1, source_target_pairs={{0,24},{8,0},{16,8},{24,16},{32,56},{40,32},{48,40},{56,48},{64,88... | collective-permute-start | bytes 3538952 | tf_op jit(solution)/shard_map/ppermute | solution.py:22
  114.3 11.8 %collective-permute-start.27 = (bf16[128,2048]{1,0:T(8,128)(2,1)S(1)}, bf16[128,2048]{1,0:T(8,128)(2,1)S(1)}, u32[]{:S(2)}, u32[]{:S(2)}) collective-permute-start(bf16[128,2048]{1,0:T(8,128)(2,1)S(1)} %slice.30), channel_id=1, source_target_pairs={{0,32},{8,40},{16,48},{24,56},{32,64},{40,72},{48,80},{56,88},{64,... | collective-permute-start | bytes 1572872 | tf_op jit(solution)/shard_map/ppermute | solution.py:22
  116.3 9.9 %collective-permute-start.28 = (bf16[128,2048]{1,0:T(8,128)(2,1)S(1)}, bf16[128,2048]{1,0:T(8,128)(2,1)S(1)}, u32[]{:S(2)}, u32[]{:S(2)}) collective-permute-start(bf16[128,2048]{1,0:T(8,128)(2,1)S(1)} %slice.31), channel_id=1, source_target_pairs={{0,224},{8,232},{16,240},{24,248},{32,0},{40,8},{48,16},{56,24},{6... | collective-permute-start | bytes 1572872 | tf_op jit(solution)/shard_map/ppermute | solution.py:22
  (2 other events, 36.4 us)

commit v10 on v9

--- a/solution.py
+++ b/solution.py
@@ -123,10 +123,11 @@
     left, right, opposite = hop(wide, 0, 1), hop(wide, 0, -1), hop(wide, 0, 2)
     below, above, left, right = together((below, above, left, right))
     near = jnp.concatenate([tall, below, above])
+    near, opposite = together((near, opposite))
     below, above = hop(below, 1, 0), hop(above, -1, 0)
     near_left, near_right = hop(near, 0, 1), hop(near, 0, -1)
     down = hop_y(mine, 1)
-    below, above, opposite = together((below, above, opposite))
+    below, above, left, right, opposite, mine, down = together((below, above, left, right, opposite, mine, down))
     far = [below, above]
     below, above = hop(below, 1, 0), hop(above, -1, 0)
     far = jnp.concatenate([*far, below, above])

time: 130 us -> 130 us (level)
  local copies, waits for them, and re-layouts: 7.02 us -> 13.2 us
  waiting for transfers between devices: 51.9 us -> 45.9 us
  starting transfers between devices: 49.4 us -> 44.3 us
  matrix products: 14.2 us -> 18.6 us
  other arithmetic: 0.41 us -> 2.53 us
    ppermute x25, waiting for transfers between devices: 48.1 us -> 39.4 us  [hop(): return lax.ppermute(value, 'row', pairs)]
    ppermute x25, starting transfers between devices: 46.6 us -> 39.7 us  [hop(): return lax.ppermute(value, 'row', pairs)]
    dot_general x6, matrix products: 14.2 us -> 18.6 us  [contract(): jnp.dot(left, jnp.concatenate(grads), preferred_element_type=jnp.float32)]
    ppermute x4, waiting for transfers between devices: 3.83 us -> 6.48 us  [hop_y(): return lax.ppermute(value, 'col', pairs)]
    slice x10, local copies, waits for them, and re-layouts: 0.21 us -> 2.44 us  [halves(): return (value[:half], value[half:])]
    concatenate x2 -> x1, local copies, waits for them, and re-layouts: 0.17 us -> 2.32 us  [contract(): jnp.concatenate(grads)]
    unnamed x20 -> x23, local copies, waits for them, and re-layouts: 5.63 us -> 7.42 us
    ppermute x4, starting transfers between devices: 2.79 us -> 4.57 us  [hop_y(): return lax.ppermute(value, 'col', pairs)]
  transfers between devices with their start and end apart: 29 -> 29, of which waited for: 12 -> 13; matrix products, arithmetic and copies ran while one was open for 15% -> 25% of each run, Pallas kernels for 3% -> 3%
where the time goes in v10:
time: 130 us; the launch traced here: 129 us
  waiting for transfers between devices  45.9 us (35%)
  starting transfers between devices  44.3 us (34%)
  matrix products  18.6 us (14%)
  local copies, waits for them, and re-layouts  13.2 us (10%)
  Pallas kernels  3.79 us (3%)
  other arithmetic  2.53 us (2%)
    ppermute x25, starting transfers between devices, hop(): return lax.ppermute(value, 'row', pairs)  39.7 us
    ppermute x25, waiting for transfers between devices, hop(): return lax.ppermute(value, 'row', pairs)  39.4 us
    dot_general x6, matrix products, contract(): jnp.dot(left, jnp.concatenate(grads), preferred_element_type=jnp.float32)  18.6 us
    unnamed x23, local copies, waits for them, and re-layouts  7.42 us
    ppermute x4, waiting for transfers between devices, hop_y(): return lax.ppermute(value, 'col', pairs)  6.48 us
    ppermute x4, starting transfers between devices, hop_y(): return lax.ppermute(value, 'col', pairs)  4.57 us
    pallas_call x1, Pallas kernels, arrange(): pl.pallas_call(functools.partial(arrange_kernel, groups), out_shape=[jax....  3.79 us
  transfers between devices with their start and end apart: 29, of which 13 were waited for; matrix products, arithmetic and copies ran while one was open for 25% of the time, Pallas kernels for 3%

profile of v10, /device:TPU:8, one launch (start us, length us, event | category | flops | bytes accessed | tf_op | source)
XLA Modules:
  0.0 129.2 jit_solution(7014864380168576027)
XLA Ops:
  0.6 2.0 %collective-permute-start = (bf16[64,2304]{1,0:T(8,128)(2,1)}, bf16[64,2304]{1,0:T(8,128)(2,1)S(1)}, u32[]{:S(2)}, u32[]{:S(2)}) collective-permute-start(bf16[64,2304]{1,0:T(8,128)(2,1)} %param.6), channel_id=1, source_target_pairs={{0,32},{8,40},{16,48},{24,56},{32,64},{40,72},{48,80},{56,88},{64,... | collective-permute-start | bytes 884744 | tf_op jit(solution)/shard_map/ppermute | solution.py:22
  2.6 4.0 %collective-permute-start.1 = (bf16[64,2304]{1,0:T(8,128)(2,1)}, bf16[64,2304]{1,0:T(8,128)(2,1)S(1)}, u32[]{:S(2)}, u32[]{:S(2)}) collective-permute-start(bf16[64,2304]{1,0:T(8,128)(2,1)} %param.6), channel_id=1, source_target_pairs={{0,224},{8,232},{16,240},{24,248},{32,0},{40,8},{48,16},{56,24},{6... | collective-permute-start | bytes 884744 | tf_op jit(solution)/shard_map/ppermute | solution.py:22
  15.8 1.8 %collective-permute-start.6 = (bf16[64,2048]{1,0:T(8,128)(2,1)}, bf16[64,2048]{1,0:T(8,128)(2,1)S(1)}, u32[]{:S(2)}, u32[]{:S(2)}) collective-permute-start(bf16[64,2048]{1,0:T(8,128)(2,1)} %param.7), channel_id=1, source_target_pairs={{0,16},{8,24},{16,0},{24,8},{32,48},{40,56},{48,32},{56,40},{64,80... | collective-permute-start | bytes 786440 | tf_op jit(solution)/shard_map/ppermute | solution.py:22
  17.8 3.2 %collective-permute-start.5 = (bf16[64,2304]{1,0:T(8,128)(2,1)S(1)}, bf16[64,2304]{1,0:T(8,128)(2,1)S(1)}, u32[]{:S(2)}, u32[]{:S(2)}) collective-permute-start(bf16[64,2304]{1,0:T(8,128)(2,1)S(1)} %collective-permute-done.1), channel_id=1, source_target_pairs={{0,224},{8,232},{16,240},{24,248},{32,0},{40,8},{48,16},{56,24},{6... | collective-permute-start | bytes 884744 | tf_op jit(solution)/shard_map/ppermute | solution.py:22
  22.0 2.4 %collective-permute-done.6 = bf16[64,2048]{1,0:T(8,128)(2,1)S(1)} collective-permute-done((bf16[64,2048]{1,0:T(8,128)(2,1)}, bf16[64,2048]{1,0:T(8,128)(2,1)S(1)}, u32[]{:S(2)}, u32[]{:S(2)}) %collective-permute-start.6) | collective-permute-done | bytes 262176 | tf_op jit(solution)/shard_map/ppermute | solution.py:22
  24.7 3.0 %collective-permute-start.14 = (bf16[192,2304]{1,0:T(8,128)(2,1)S(1)}, bf16[192,2304]{1,0:T(8,128)(2,1)S(1)}, u32[]{:S(2)}, u32[]{:S(2)}) collective-permute-start(bf16[192,2304]{1,0:T(8,128)(2,1)S(1)} %pad_maximum_fusion.4), channel_id=1, source_target_pairs={{0,24},{8,0},{16,8},{24,16},{32,56},{40,32},{48,40},{56,48},{64,88... | collective-permute-start | bytes 2654216 | tf_op jit(solution)/shard_map/ppermute | solution.py:22
  27.8 3.2 %collective-permute-start.9 = (bf16[64,2304]{1,0:T(8,128)(2,1)S(1)}, bf16[64,2304]{1,0:T(8,128)(2,1)S(1)}, u32[]{:S(2)}, u32[]{:S(2)}) collective-permute-start(bf16[64,2304]{1,0:T(8,128)(2,1)S(1)} %collective-permute-done.5), channel_id=1, source_target_pairs={{0,224},{8,232},{16,240},{24,248},{32,0},{40,8},{48,16},{56,24},{6... | collective-permute-start | bytes 884744 | tf_op jit(solution)/shard_map/ppermute | solution.py:22
  32.9 2.7 %collective-permute-done.8 = bf16[64,2304]{1,0:T(8,128)(2,1)S(1)} collective-permute-done((bf16[64,2304]{1,0:T(8,128)(2,1)S(1)}, bf16[64,2304]{1,0:T(8,128)(2,1)S(1)}, u32[]{:S(2)}, u32[]{:S(2)}) %collective-permute-start.8) | collective-permute-done | bytes 294944 | tf_op jit(solution)/shard_map/ppermute | solution.py:22
  36.5 2.7 %collective-permute-start.11 = (bf16[32,2304]{1,0:T(8,128)(2,1)S(1)}, bf16[32,2304]{1,0:T(8,128)(2,1)S(1)}, u32[]{:S(2)}, u32[]{:S(2)}) collective-permute-start(bf16[32,2304]{1,0:T(8,128)(2,1)S(1)} %slice.25), channel_id=1, source_target_pairs={{0,224},{8,232},{16,240},{24,248},{32,0},{40,8},{48,16},{56,24},{6... | collective-permute-start | bytes 442376 | tf_op jit(solution)/shard_map/ppermute | solution.py:22
  41.4 3.5 %collective-permute-done.13 = bf16[192,2304]{1,0:T(8,128)(2,1)S(1)} collective-permute-done((bf16[192,2304]{1,0:T(8,128)(2,1)S(1)}, bf16[192,2304]{1,0:T(8,128)(2,1)S(1)}, u32[]{:S(2)}, u32[]{:S(2)}) %collective-permute-start.13) | collective-permute-done | bytes 884768 | tf_op jit(solution)/shard_map/ppermute | solution.py:22
  46.0 2.4 %collective-permute-start.15 = (bf16[256,1024]{1,0:T(8,128)(2,1)S(1)}, bf16[256,1024]{1,0:T(8,128)(2,1)S(1)}, u32[]{:S(2)}, u32[]{:S(2)}) collective-permute-start(bf16[256,1024]{1,0:T(8,128)(2,1)S(1)} %constant_dynamic-update-slice_fusion), channel_id=1, source_target_pairs={{0,4},{1,5},{2,6},{3,7},{4,0},{5,1},{6,2},{7,3},{8,12},{9,13},{10,... | collective-permute-start | bytes 1572872 | tf_op jit(solution)/shard_map/ppermute | solution.py:27
  49.6 3.2 %collective-permute-start.22 = (bf16[320,2304]{1,0:T(8,128)(2,1)}, bf16[320,2304]{1,0:T(8,128)(2,1)}, u32[]{:S(2)}, u32[]{:S(2)}) collective-permute-start(bf16[320,2304]{1,0:T(8,128)(2,1)} %pad_maximum_fusion), channel_id=1, source_target_pairs={{0,24},{8,0},{16,8},{24,16},{32,56},{40,32},{48,40},{56,48},{64,88... | collective-permute-start | bytes 4423688 | tf_op jit(solution)/shard_map/ppermute | solution.py:22
  52.9 5.0 %collective-permute-done.15 = bf16[256,1024]{1,0:T(8,128)(2,1)S(1)} collective-permute-done((bf16[256,1024]{1,0:T(8,128)(2,1)S(1)}, bf16[256,1024]{1,0:T(8,128)(2,1)S(1)}, u32[]{:S(2)}, u32[]{:S(2)}) %collective-permute-start.15) | collective-permute-done | bytes 524320 | tf_op jit(solution)/shard_map/ppermute | solution.py:27
  58.1 6.7 %collective-permute-done.17 = bf16[256,2048]{1,0:T(8,128)(2,1)} collective-permute-done((bf16[256,2048]{1,0:T(8,128)(2,1)S(1)}, bf16[256,2048]{1,0:T(8,128)(2,1)}, u32[]{:S(2)}, u32[]{:S(2)}) %collective-permute-start.17) | collective-permute-done | bytes 1048608 | tf_op jit(solution)/shard_map/ppermute | solution.py:22
  64.8 3.2 %collective-permute-done.19 = bf16[256,2048]{1,0:T(8,128)(2,1)} collective-permute-done((bf16[256,2048]{1,0:T(8,128)(2,1)S(1)}, bf16[256,2048]{1,0:T(8,128)(2,1)}, u32[]{:S(2)}, u32[]{:S(2)}) %collective-permute-start.19) | collective-permute-done | bytes 1048608 | tf_op jit(solution)/shard_map/ppermute | solution.py:22
  69.2 2.4 %constant_dynamic-update-slice_fusion.11 = bf16[768,2048]{1,0:T(8,128)(2,1)} fusion(bf16[768,2048]{1,0:T(8,128)(2,1)} %get-tuple-element.80, bf16[256,2048]{1,0:T(8,128)(2,1)} %collective-permute-done.17), kind=kLoop, calls=%fused_computation.46 | loop fusion | bytes 2097152
  71.5 2.3 %constant_dynamic-update-slice_fusion.10 = bf16[768,2048]{1,0:T(8,128)(2,1)} fusion(bf16[768,2048]{1,0:T(8,128)(2,1)} %constant_dynamic-update-slice_fusion.11, bf16[256,2048]{1,0:T(8,128)(2,1)} %collective-permute-done.19), kind=kLoop, calls=%fused_computation.45 | loop fusion | bytes 2097152 | tf_op jit(solution)/shard_map/concatenate | solution.py:88
  73.9 7.7 %collective-permute-done.21 = bf16[320,2304]{1,0:T(8,128)(2,1)} collective-permute-done((bf16[320,2304]{1,0:T(8,128)(2,1)}, bf16[320,2304]{1,0:T(8,128)(2,1)}, u32[]{:S(2)}, u32[]{:S(2)}) %collective-permute-start.21) | collective-permute-done | bytes 1474592 | tf_op jit(solution)/shard_map/ppermute | solution.py:22
  81.6 5.9 %collective-permute-done.18 = bf16[256,2048]{1,0:T(8,128)(2,1)} collective-permute-done((bf16[256,2048]{1,0:T(8,128)(2,1)}, bf16[256,2048]{1,0:T(8,128)(2,1)}, u32[]{:S(2)}, u32[]{:S(2)}) %collective-permute-start.18) | collective-permute-done | bytes 1048608 | tf_op jit(solution)/shard_map/ppermute | solution.py:22
  87.5 1.9 %collective-permute-done.20 = bf16[256,2048]{1,0:T(8,128)(2,1)} collective-permute-done((bf16[256,2048]{1,0:T(8,128)(2,1)}, bf16[256,2048]{1,0:T(8,128)(2,1)}, u32[]{:S(2)}, u32[]{:S(2)}) %collective-permute-start.20) | collective-permute-done | bytes 1048608 | tf_op jit(solution)/shard_map/ppermute | solution.py:22
  90.5 2.1 %collective-permute-start.26 = (bf16[256,2048]{1,0:T(8,128)(2,1)}, bf16[256,2048]{1,0:T(8,128)(2,1)S(1)}, u32[]{:S(2)}, u32[]{:S(2)}) collective-permute-start(bf16[256,2048]{1,0:T(8,128)(2,1)} %collective-permute-done.20), channel_id=1, source_target_pairs={{0,224},{8,232},{16,240},{24,248},{32,0},{40,8},{48,16},{56,24},{6... | collective-permute-start | bytes 3145736 | tf_op jit(solution)/shard_map/ppermute | solution.py:22
  95.2 3.3 %collective-permute-start.24 = (bf16[256,2304]{1,0:T(8,128)(2,1)S(1)}, bf16[256,2304]{1,0:T(8,128)(2,1)S(1)}, u32[]{:S(2)}, u32[]{:S(2)}) collective-permute-start(bf16[256,2304]{1,0:T(8,128)(2,1)S(1)} %pad_maximum_fusion.3), channel_id=1, source_target_pairs={{0,24},{8,0},{16,8},{24,16},{32,56},{40,32},{48,40},{56,48},{64,88... | collective-permute-start | bytes 3538952 | tf_op jit(solution)/shard_map/ppermute | solution.py:22
  98.5 3.8 %shard_map.59 = (bf16[512,896]{1,0:T(8,128)(2,1)S(1)}, bf16[512,640]{1,0:T(8,128)(2,1)S(1)}, bf16[512,512]{1,0:T(8,128)(2,1)S(1)}, bf16[512,768]{1,0:T(8,128)(2,...) custom-call(s32[4]{0:T(128)S(1)} %pad_add_fusion.place_ref, ...), custom_call_target="tpu_custom_call" | custom-call | bytes 12582912 | tf_op jit(solution)/shard_map/pallas_call | solution.py:71
  102.4 1.8 %fusion.34 = f32[512,2048]{1,0:T(8,128)S(1)} fusion(bf16[512,768]{1,0:T(8,128)(2,1)S(1)} %get-tuple-element.70, bf16[768,2048]{1,0:T(8,128)(2,1)S(1)} %copy-done.6), kind=kOutput, calls=%fused_computation.57 | convolution fusion | flops 1610612736 | bytes 8126464 | tf_op jit(solution)/shard_map/dot_general | solution.py:88
  104.2 4.2 %fusion.9 = f32[512,2304]{1,0:T(8,128)S(1)} fusion(bf16[512,896]{1,0:T(8,128)(2,1)S(1)} %get-tuple-element.71, bf16[320,2304]{1,0:T(8,128)(2,1)} %pad_maximum_fusion, bf16[192,2304]{1,0:T(8,128)(2,1)S(1)} %copy-done.1, bf16[192,2304]{1,0:T(8,128)(2,1)S(1)} %copy-done.3, bf16[192,2304]{1,0:T(8,128)(2,1)S(1)} %copy-done.5), kind=kOutput, calls=%fused_computation.12 | convolution fusion | flops 2130444288 | bytes 9764864 | tf_op jit(solution)/shard_map/dot_general | solution.py:88
  108.4 2.8 %collective-permute-done.25 = bf16[256,2048]{1,0:T(8,128)(2,1)S(1)} collective-permute-done((bf16[256,2048]{1,0:T(8,128)(2,1)}, bf16[256,2048]{1,0:T(8,128)(2,1)S(1)}, u32[]{:S(2)}, u32[]{:S(2)}) %collective-permute-start.25) | collective-permute-done | bytes 1048608 | tf_op jit(solution)/shard_map/ppermute | solution.py:22
  111.1 2.0 %collective-permute-done.26 = bf16[256,2048]{1,0:T(8,128)(2,1)S(1)} collective-permute-done((bf16[256,2048]{1,0:T(8,128)(2,1)}, bf16[256,2048]{1,0:T(8,128)(2,1)S(1)}, u32[]{:S(2)}, u32[]{:S(2)}) %collective-permute-start.26) | collective-permute-done | bytes 1048608 | tf_op jit(solution)/shard_map/ppermute | solution.py:22
  113.2 2.7 %collective-permute-start.27 = (bf16[128,2048]{1,0:T(8,128)(2,1)S(1)}, bf16[128,2048]{1,0:T(8,128)(2,1)S(1)}, u32[]{:S(2)}, u32[]{:S(2)}) collective-permute-start(bf16[128,2048]{1,0:T(8,128)(2,1)S(1)} %slice.30), channel_id=1, source_target_pairs={{0,32},{8,40},{16,48},{24,56},{32,64},{40,72},{48,80},{56,88},{64,... | collective-permute-start | bytes 1572872 | tf_op jit(solution)/shard_map/ppermute | solution.py:22
  116.6 3.8 %fusion.17 = f32[512,2048]{1,0:T(8,128)S(1)} fusion(f32[512,2048]{1,0:T(8,128)S(1)} %fusion.34, bf16[512,1024]{1,0:T(8,128)(2,1)S(1)} %get-tuple-element.73, bf16[256,2048]{1,0:T(8,128)(2,1)S(1)} %collective-permute-done.26, bf16[256,2048]{1,0:T(8,128)(2,1)S(1)} %collective-permute-done.25, bf16[256,2048]{1,0:T(8,128)(2,1)} %collective-permute-done.20, ...), kind=kOutput, calls=%fused_computation.20 | convolution fusion | flops 2165309440 | bytes 13631488 | tf_op jit(solution)/shard_map/dot_general | solution.py:88
  120.4 3.9 %convolution_add_fusion.1 = f32[512,2304]{1,0:T(8,128)S(1)} fusion(f32[512,2304]{1,0:T(8,128)S(1)} %fusion.9, bf16[512,640]{1,0:T(8,128)(2,1)S(1)} %get-tuple-element.67, bf16[320,2304]{1,0:T(8,128)(2,1)} %collective-permute-done.22, bf16[320,2304]{1,0:T(8,128)(2,1)} %collective-permute-done.21), kind=kOutput, calls=%fused_computation.1 | convolution fusion | flops 1517027328 | bytes 13041664 | tf_op jit(solution)/shard_map/dot_general | solution.py:88
  124.3 2.8 %fusion = bf16[512,2304]{1,0:T(8,128)(2,1)} fusion(f32[512,2304]{1,0:T(8,128)S(1)} %convolution_add_fusion.1, bf16[512,512]{1,0:T(8,128)(2,1)S(1)} %get-tuple-element.58, bf16[256,2304]{1,0:T(8,128)(2,1)S(1)} %collective-permute-done.24, bf16[256,2304]{1,0:T(8,128)(2,1)S(1)} %collective-permute-done.23), kind=kOutput, calls=%fused_computation.2 | convolution fusion | flops 1215037440 | bytes 9961472 | tf_op jit(solution)/shard_map/dot_general | solution.py:88
  127.2 2.0 %add_convert_fusion = bf16[512,2048]{1,0:T(8,128)(2,1)} fusion(f32[512,2048]{1,0:T(8,128)S(1)} %fusion.17, bf16[512,256]{1,0:T(8,128)(2,1)S(1)} %get-tuple-element.78, bf16[128,2048]{1,0:T(8,128)(2,1)S(1)} %collective-permute-done.28, bf16[128,2048]{1,0:T(8,128)(2,1)S(1)} %collective-permute-done.27), kind=kOutput, calls=%fused_computation.11 | convolution fusion | flops 541065216 | bytes 7602176 | tf_op jit(solution)/shard_map/dot_general | solution.py:88
  (75 shorter events, 23.8 us)
Async XLA Ops:
  0.6 17.0 %collective-permute-start = (bf16[64,2304]{1,0:T(8,128)(2,1)}, bf16[64,2304]{1,0:T(8,128)(2,1)S(1)}, u32[]{:S(2)}, u32[]{:S(2)}) collective-permute-start(bf16[64,2304]{1,0:T(8,128)(2,1)} %param.6), channel_id=1, source_target_pairs={{0,32},{8,40},{16,48},{24,56},{32,64},{40,72},{48,80},{56,88},{64,... | collective-permute-start | bytes 884744 | tf_op jit(solution)/shard_map/ppermute | solution.py:22
  2.6 15.0 %collective-permute-start.1 = (bf16[64,2304]{1,0:T(8,128)(2,1)}, bf16[64,2304]{1,0:T(8,128)(2,1)S(1)}, u32[]{:S(2)}, u32[]{:S(2)}) collective-permute-start(bf16[64,2304]{1,0:T(8,128)(2,1)} %param.6), channel_id=1, source_target_pairs={{0,224},{8,232},{16,240},{24,248},{32,0},{40,8},{48,16},{56,24},{6... | collective-permute-start | bytes 884744 | tf_op jit(solution)/shard_map/ppermute | solution.py:22
  6.7 9.2 %collective-permute-start.2 = (bf16[64,2048]{1,0:T(8,128)(2,1)}, bf16[64,2048]{1,0:T(8,128)(2,1)S(1)}, u32[]{:S(2)}, u32[]{:S(2)}) collective-permute-start(bf16[64,2048]{1,0:T(8,128)(2,1)} %param.7), channel_id=1, source_target_pairs={{0,8},{8,16},{16,24},{24,0},{32,40},{40,48},{48,56},{56,32},{64,72... | collective-permute-start | bytes 786440 | tf_op jit(solution)/shard_map/ppermute | solution.py:22
  8.1 9.5 %collective-permute-start.3 = (bf16[64,2048]{1,0:T(8,128)(2,1)}, bf16[64,2048]{1,0:T(8,128)(2,1)S(1)}, u32[]{:S(2)}, u32[]{:S(2)}) collective-permute-start(bf16[64,2048]{1,0:T(8,128)(2,1)} %param.7), channel_id=1, source_target_pairs={{0,24},{8,0},{16,8},{24,16},{32,56},{40,32},{48,40},{56,48},{64,88... | collective-permute-start | bytes 786440 | tf_op jit(solution)/shard_map/ppermute | solution.py:22
  11.8 15.8 %collective-permute-start.7 = (bf16[256,1024]{1,0:T(8,128)(2,1)S(1)}, bf16[256,1024]{1,0:T(8,128)(2,1)S(1)}, u32[]{:S(2)}, u32[]{:S(2)}) collective-permute-start(bf16[256,1024]{1,0:T(8,128)(2,1)S(1)} %constant_dynamic-update-slice_fusion), channel_id=1, source_target_pairs={{0,2},{1,3},{2,4},{3,5},{4,6},{5,7},{6,0},{7,1},{8,10},{9,11},{10,... | collective-permute-start | bytes 1572872 | tf_op jit(solution)/shard_map/ppermute | solution.py:27
  15.8 8.6 %collective-permute-start.6 = (bf16[64,2048]{1,0:T(8,128)(2,1)}, bf16[64,2048]{1,0:T(8,128)(2,1)S(1)}, u32[]{:S(2)}, u32[]{:S(2)}) collective-permute-start(bf16[64,2048]{1,0:T(8,128)(2,1)} %param.7), channel_id=1, source_target_pairs={{0,16},{8,24},{16,0},{24,8},{32,48},{40,56},{48,32},{56,40},{64,80... | collective-permute-start | bytes 786440 | tf_op jit(solution)/shard_map/ppermute | solution.py:22
  17.7 10.0 %collective-permute-start.4 = (bf16[64,2304]{1,0:T(8,128)(2,1)S(1)}, bf16[64,2304]{1,0:T(8,128)(2,1)S(1)}, u32[]{:S(2)}, u32[]{:S(2)}) collective-permute-start(bf16[64,2304]{1,0:T(8,128)(2,1)S(1)} %collective-permute-done), channel_id=1, source_target_pairs={{0,32},{8,40},{16,48},{24,56},{32,64},{40,72},{48,80},{56,88},{64,... | collective-permute-start | bytes 884744 | tf_op jit(solution)/shard_map/ppermute | solution.py:22
  17.8 9.9 %collective-permute-start.5 = (bf16[64,2304]{1,0:T(8,128)(2,1)S(1)}, bf16[64,2304]{1,0:T(8,128)(2,1)S(1)}, u32[]{:S(2)}, u32[]{:S(2)}) collective-permute-start(bf16[64,2304]{1,0:T(8,128)(2,1)S(1)} %collective-permute-done.1), channel_id=1, source_target_pairs={{0,224},{8,232},{16,240},{24,248},{32,0},{40,8},{48,16},{56,24},{6... | collective-permute-start | bytes 884744 | tf_op jit(solution)/shard_map/ppermute | solution.py:22
  22.0 26.3 %copy-start.4 = (bf16[192,2304]{1,0:T(8,128)(2,1)}, bf16[192,2304]{1,0:T(8,128)(2,1)S(1)}, u32[]{:S(2)}) copy-start(bf16[192,2304]{1,0:T(8,128)(2,1)S(1)} %pad_maximum_fusion.4) | copy-start | bytes 2654212
  24.4 20.5 %collective-permute-start.13 = (bf16[192,2304]{1,0:T(8,128)(2,1)S(1)}, bf16[192,2304]{1,0:T(8,128)(2,1)S(1)}, u32[]{:S(2)}, u32[]{:S(2)}) collective-permute-start(bf16[192,2304]{1,0:T(8,128)(2,1)S(1)} %pad_maximum_fusion.4), channel_id=1, source_target_pairs={{0,8},{8,16},{16,24},{24,0},{32,40},{40,48},{48,56},{56,32},{64,72... | collective-permute-start | bytes 2654216 | tf_op jit(solution)/shard_map/ppermute | solution.py:22
  24.7 21.3 %collective-permute-start.14 = (bf16[192,2304]{1,0:T(8,128)(2,1)S(1)}, bf16[192,2304]{1,0:T(8,128)(2,1)S(1)}, u32[]{:S(2)}, u32[]{:S(2)}) collective-permute-start(bf16[192,2304]{1,0:T(8,128)(2,1)S(1)} %pad_maximum_fusion.4), channel_id=1, source_target_pairs={{0,24},{8,0},{16,8},{24,16},{32,56},{40,32},{48,40},{56,48},{64,88... | collective-permute-start | bytes 2654216 | tf_op jit(solution)/shard_map/ppermute | solution.py:22
  27.7 8.0 %collective-permute-start.8 = (bf16[64,2304]{1,0:T(8,128)(2,1)S(1)}, bf16[64,2304]{1,0:T(8,128)(2,1)S(1)}, u32[]{:S(2)}, u32[]{:S(2)}) collective-permute-start(bf16[64,2304]{1,0:T(8,128)(2,1)S(1)} %collective-permute-done.4), channel_id=1, source_target_pairs={{0,32},{8,40},{16,48},{24,56},{32,64},{40,72},{48,80},{56,88},{64,... | collective-permute-start | bytes 884744 | tf_op jit(solution)/shard_map/ppermute | solution.py:22
  27.8 7.9 %collective-permute-start.9 = (bf16[64,2304]{1,0:T(8,128)(2,1)S(1)}, bf16[64,2304]{1,0:T(8,128)(2,1)S(1)}, u32[]{:S(2)}, u32[]{:S(2)}) collective-permute-start(bf16[64,2304]{1,0:T(8,128)(2,1)S(1)} %collective-permute-done.5), channel_id=1, source_target_pairs={{0,224},{8,232},{16,240},{24,248},{32,0},{40,8},{48,16},{56,24},{6... | collective-permute-start | bytes 884744 | tf_op jit(solution)/shard_map/ppermute | solution.py:22
  31.0 10.4 %collective-permute-start.12 = (bf16[256,1024]{1,0:T(8,128)(2,1)S(1)}, bf16[256,1024]{1,0:T(8,128)(2,1)S(1)}, u32[]{:S(2)}, u32[]{:S(2)}) collective-permute-start(bf16[256,1024]{1,0:T(8,128)(2,1)S(1)} %constant_dynamic-update-slice_fusion), channel_id=1, source_target_pairs={{0,6},{1,7},{2,0},{3,1},{4,2},{5,3},{6,4},{7,5},{8,14},{9,15},{10,... | collective-permute-start | bytes 1572872 | tf_op jit(solution)/shard_map/ppermute | solution.py:27
  35.8 12.6 %collective-permute-start.10 = (bf16[32,2304]{1,0:T(8,128)(2,1)S(1)}, bf16[32,2304]{1,0:T(8,128)(2,1)S(1)}, u32[]{:S(2)}, u32[]{:S(2)}) collective-permute-start(bf16[32,2304]{1,0:T(8,128)(2,1)S(1)} %slice.24), channel_id=1, source_target_pairs={{0,32},{8,40},{16,48},{24,56},{32,64},{40,72},{48,80},{56,88},{64,... | collective-permute-start | bytes 442376 | tf_op jit(solution)/shard_map/ppermute | solution.py:22
  36.5 11.9 %collective-permute-start.11 = (bf16[32,2304]{1,0:T(8,128)(2,1)S(1)}, bf16[32,2304]{1,0:T(8,128)(2,1)S(1)}, u32[]{:S(2)}, u32[]{:S(2)}) collective-permute-start(bf16[32,2304]{1,0:T(8,128)(2,1)S(1)} %slice.25), channel_id=1, source_target_pairs={{0,224},{8,232},{16,240},{24,248},{32,0},{40,8},{48,16},{56,24},{6... | collective-permute-start | bytes 442376 | tf_op jit(solution)/shard_map/ppermute | solution.py:22
  41.4 23.4 %collective-permute-start.17 = (bf16[256,2048]{1,0:T(8,128)(2,1)S(1)}, bf16[256,2048]{1,0:T(8,128)(2,1)}, u32[]{:S(2)}, u32[]{:S(2)}) collective-permute-start(bf16[256,2048]{1,0:T(8,128)(2,1)S(1)} %get-tuple-element.81), channel_id=1, source_target_pairs={{0,32},{8,40},{16,48},{24,56},{32,64},{40,72},{48,80},{56,88},{64,... | collective-permute-start | bytes 3145736 | tf_op jit(solution)/shard_map/ppermute | solution.py:22
  44.9 23.1 %collective-permute-start.19 = (bf16[256,2048]{1,0:T(8,128)(2,1)S(1)}, bf16[256,2048]{1,0:T(8,128)(2,1)}, u32[]{:S(2)}, u32[]{:S(2)}) collective-permute-start(bf16[256,2048]{1,0:T(8,128)(2,1)S(1)} %get-tuple-element.81), channel_id=1, source_target_pairs={{0,224},{8,232},{16,240},{24,248},{32,0},{40,8},{48,16},{56,24},{6... | collective-permute-start | bytes 3145736 | tf_op jit(solution)/shard_map/ppermute | solution.py:22
  46.0 23.2 %copy-start = (bf16[192,2304]{1,0:T(8,128)(2,1)}, bf16[192,2304]{1,0:T(8,128)(2,1)S(1)}, u32[]{:S(2)}) copy-start(bf16[192,2304]{1,0:T(8,128)(2,1)S(1)} %collective-permute-done.14) | copy-start | bytes 2654212
  46.0 12.0 %collective-permute-start.15 = (bf16[256,1024]{1,0:T(8,128)(2,1)S(1)}, bf16[256,1024]{1,0:T(8,128)(2,1)S(1)}, u32[]{:S(2)}, u32[]{:S(2)}) collective-permute-start(bf16[256,1024]{1,0:T(8,128)(2,1)S(1)} %constant_dynamic-update-slice_fusion), channel_id=1, source_target_pairs={{0,4},{1,5},{2,6},{3,7},{4,0},{5,1},{6,2},{7,3},{8,12},{9,13},{10,... | collective-permute-start | bytes 1572872 | tf_op jit(solution)/shard_map/ppermute | solution.py:27
  49.6 32.0 %collective-permute-start.21 = (bf16[320,2304]{1,0:T(8,128)(2,1)}, bf16[320,2304]{1,0:T(8,128)(2,1)}, u32[]{:S(2)}, u32[]{:S(2)}) collective-permute-start(bf16[320,2304]{1,0:T(8,128)(2,1)} %pad_maximum_fusion), channel_id=1, source_target_pairs={{0,8},{8,16},{16,24},{24,0},{32,40},{40,48},{48,56},{56,32},{64,72... | collective-permute-start | bytes 4423688 | tf_op jit(solution)/shard_map/ppermute | solution.py:22
  49.6 32.0 %collective-permute-start.22 = (bf16[320,2304]{1,0:T(8,128)(2,1)}, bf16[320,2304]{1,0:T(8,128)(2,1)}, u32[]{:S(2)}, u32[]{:S(2)}) collective-permute-start(bf16[320,2304]{1,0:T(8,128)(2,1)} %pad_maximum_fusion), channel_id=1, source_target_pairs={{0,24},{8,0},{16,8},{24,16},{32,56},{40,32},{48,40},{56,48},{64,88... | collective-permute-start | bytes 4423688 | tf_op jit(solution)/shard_map/ppermute | solution.py:22
  58.0 40.5 %collective-permute-start.16 = (bf16[1024,1024]{1,0:T(8,128)(2,1)S(1)}, bf16[1024,1024]{1,0:T(8,128)(2,1)}, u32[]{:S(2)}, u32[]{:S(2)}) collective-permute-start(bf16[1024,1024]{1,0:T(8,128)(2,1)S(1)} %constant_dynamic-update-slice_fusion.2.mine_ref), channel_id=1, source_target_pairs={{0,1},{1,0},{2,3},{3,2},{4,5},{5,4},{6,7},{7,6},{8,9},{9,8},{10,11... | collective-permute-start | bytes 6291464 | tf_op jit(solution)/shard_map/ppermute | solution.py:27
  64.8 22.7 %collective-permute-start.18 = (bf16[256,2048]{1,0:T(8,128)(2,1)}, bf16[256,2048]{1,0:T(8,128)(2,1)}, u32[]{:S(2)}, u32[]{:S(2)}) collective-permute-start(bf16[256,2048]{1,0:T(8,128)(2,1)} %collective-permute-done.17), channel_id=1, source_target_pairs={{0,32},{8,40},{16,48},{24,56},{32,64},{40,72},{48,80},{56,88},{64,... | collective-permute-start | bytes 3145736 | tf_op jit(solution)/shard_map/ppermute | solution.py:22
  68.0 21.3 %collective-permute-start.20 = (bf16[256,2048]{1,0:T(8,128)(2,1)}, bf16[256,2048]{1,0:T(8,128)(2,1)}, u32[]{:S(2)}, u32[]{:S(2)}) collective-permute-start(bf16[256,2048]{1,0:T(8,128)(2,1)} %collective-permute-done.19), channel_id=1, source_target_pairs={{0,224},{8,232},{16,240},{24,248},{32,0},{40,8},{48,16},{56,24},{6... | collective-permute-start | bytes 3145736 | tf_op jit(solution)/shard_map/ppermute | solution.py:22
  69.2 24.6 %slice-start.1 = ((bf16[192,2304]{1,0:T(8,128)(2,1)}), bf16[96,2304]{1,0:T(8,128)(2,1)S(1)}, s32[]{:S(2)}) async-start(bf16[192,2304]{1,0:T(8,128)(2,1)} %copy-done.2), calls=%async_computation.1 | async-start | bytes 884736 | tf_op jit(solution)/shard_map/slice | solution.py:32
  89.3 21.8 %collective-permute-start.25 = (bf16[256,2048]{1,0:T(8,128)(2,1)}, bf16[256,2048]{1,0:T(8,128)(2,1)S(1)}, u32[]{:S(2)}, u32[]{:S(2)}) collective-permute-start(bf16[256,2048]{1,0:T(8,128)(2,1)} %collective-permute-done.18), channel_id=1, source_target_pairs={{0,32},{8,40},{16,48},{24,56},{32,64},{40,72},{48,80},{56,88},{64,... | collective-permute-start | bytes 3145736 | tf_op jit(solution)/shard_map/ppermute | solution.py:22
  90.5 22.6 %collective-permute-start.26 = (bf16[256,2048]{1,0:T(8,128)(2,1)}, bf16[256,2048]{1,0:T(8,128)(2,1)S(1)}, u32[]{:S(2)}, u32[]{:S(2)}) collective-permute-start(bf16[256,2048]{1,0:T(8,128)(2,1)} %collective-permute-done.20), channel_id=1, source_target_pairs={{0,224},{8,232},{16,240},{24,248},{32,0},{40,8},{48,16},{56,24},{6... | collective-permute-start | bytes 3145736 | tf_op jit(solution)/shard_map/ppermute | solution.py:22
  93.8 30.5 %collective-permute-start.23 = (bf16[256,2304]{1,0:T(8,128)(2,1)S(1)}, bf16[256,2304]{1,0:T(8,128)(2,1)S(1)}, u32[]{:S(2)}, u32[]{:S(2)}) collective-permute-start(bf16[256,2304]{1,0:T(8,128)(2,1)S(1)} %pad_maximum_fusion.2), channel_id=1, source_target_pairs={{0,8},{8,16},{16,24},{24,0},{32,40},{40,48},{48,56},{56,32},{64,72... | collective-permute-start | bytes 3538952 | tf_op jit(solution)/shard_map/ppermute | solution.py:22
  95.2 29.1 %collective-permute-start.24 = (bf16[256,2304]{1,0:T(8,128)(2,1)S(1)}, bf16[256,2304]{1,0:T(8,128)(2,1)S(1)}, u32[]{:S(2)}, u32[]{:S(2)}) collective-permute-start(bf16[256,2304]{1,0:T(8,128)(2,1)S(1)} %pad_maximum_fusion.3), channel_id=1, source_target_pairs={{0,24},{8,0},{16,8},{24,16},{32,56},{40,32},{48,40},{56,48},{64,88... | collective-permute-start | bytes 3538952 | tf_op jit(solution)/shard_map/ppermute | solution.py:22
  113.2 14.0 %collective-permute-start.27 = (bf16[128,2048]{1,0:T(8,128)(2,1)S(1)}, bf16[128,2048]{1,0:T(8,128)(2,1)S(1)}, u32[]{:S(2)}, u32[]{:S(2)}) collective-permute-start(bf16[128,2048]{1,0:T(8,128)(2,1)S(1)} %slice.30), channel_id=1, source_target_pairs={{0,32},{8,40},{16,48},{24,56},{32,64},{40,72},{48,80},{56,88},{64,... | collective-permute-start | bytes 1572872 | tf_op jit(solution)/shard_map/ppermute | solution.py:22
  115.9 11.3 %collective-permute-start.28 = (bf16[128,2048]{1,0:T(8,128)(2,1)S(1)}, bf16[128,2048]{1,0:T(8,128)(2,1)S(1)}, u32[]{:S(2)}, u32[]{:S(2)}) collective-permute-start(bf16[128,2048]{1,0:T(8,128)(2,1)S(1)} %slice.31), channel_id=1, source_target_pairs={{0,224},{8,232},{16,240},{24,248},{32,0},{40,8},{48,16},{56,24},{6... | collective-permute-start | bytes 1572872 | tf_op jit(solution)/shard_map/ppermute | solution.py:22
  (6 other events, 35.1 us)

commit v11 on v10

--- a/solution.py
+++ b/solution.py
@@ -170,11 +170,11 @@
     second = jnp.concatenate([halves(near_right)[1], halves(far_right)[1]])
 
     tall_halves = [hop(first, 0, 1), hop(second, 0, -1)]
+    tall_sum = contract(lefts[1], [far_left, far_right], tall_sum)
     below, above, wide_sum, tall_sum = together((below, above, wide_sum, tall_sum))
     wide_halves = [hop(halves(below)[0], 1, 0), hop(halves(above)[1], -1, 0)]
-    tall_sum = contract(lefts[1], [far_left, far_right], tall_sum)
     wide_sum = contract(lefts[4], [*wide_second, below, above], wide_sum)
-    tall_sum, wide_sum = together((tall_sum, wide_sum))
+    tall_halves, wide_sum = together((tall_halves, wide_sum))
     qkv = contract(lefts[2], tall_halves, tall_sum, dtype=jnp.bfloat16)
     out = contract(lefts[5], wide_halves, wide_sum, dtype=jnp.bfloat16)
     return qkv, out

time: 130 us -> 132 us (1.015)
  waiting for transfers between devices: 45.9 us -> 49.4 us
  starting transfers between devices: 44.3 us -> 42.8 us
    ppermute x4, waiting for transfers between devices: 6.48 us -> 9.36 us  [hop_y(): return lax.ppermute(value, 'col', pairs)]
  transfers between devices with their start and end apart: 29 -> 29, of which waited for: 13 -> 16; matrix products, arithmetic and copies ran while one was open for 25% -> 25% of each run, Pallas kernels for 3% -> 3%
where the time goes in v11:
time: 132 us; the launch traced here: 131 us
  waiting for transfers between devices  49.4 us (37%)
  starting transfers between devices  42.8 us (32%)
  matrix products  18.7 us (14%)
  local copies, waits for them, and re-layouts  13.2 us (10%)
  Pallas kernels  3.8 us (3%)
  other arithmetic  2.53 us (2%)
    ppermute x25, waiting for transfers between devices, hop(): return lax.ppermute(value, 'row', pairs)  40 us
    ppermute x25, starting transfers between devices, hop(): return lax.ppermute(value, 'row', pairs)  39.5 us
    dot_general x6, matrix products, contract(): jnp.dot(left, jnp.concatenate(grads), preferred_element_type=jnp.float32)  18.7 us
    ppermute x4, waiting for transfers between devices, hop_y(): return lax.ppermute(value, 'col', pairs)  9.36 us
    unnamed x23, local copies, waits for them, and re-layouts  7.36 us
    pallas_call x1, Pallas kernels, arrange(): pl.pallas_call(functools.partial(arrange_kernel, groups), out_shape=[jax....  3.8 us
    ppermute x4, starting transfers between devices, hop_y(): return lax.ppermute(value, 'col', pairs)  3.29 us
  transfers between devices with their start and end apart: 29, of which 16 were waited for; matrix products, arithmetic and copies ran while one was open for 25% of the time, Pallas kernels for 3%

profile of v11, /device:TPU:8, one launch (start us, length us, event | category | flops | bytes accessed | tf_op | source)
XLA Modules:
  0.0 131.3 jit_solution(17213425751546132670)
XLA Ops:
  0.6 2.8 %collective-permute-start.3 = (bf16[64,2048]{1,0:T(8,128)(2,1)}, bf16[64,2048]{1,0:T(8,128)(2,1)S(1)}, u32[]{:S(2)}, u32[]{:S(2)}) collective-permute-start(bf16[64,2048]{1,0:T(8,128)(2,1)} %param.7), channel_id=1, source_target_pairs={{0,24},{8,0},{16,8},{24,16},{32,56},{40,32},{48,40},{56,48},{64,88... | collective-permute-start | bytes 786440 | tf_op jit(solution)/shard_map/ppermute | solution.py:22
  3.5 1.9 %collective-permute-start = (bf16[64,2304]{1,0:T(8,128)(2,1)}, bf16[64,2304]{1,0:T(8,128)(2,1)S(1)}, u32[]{:S(2)}, u32[]{:S(2)}) collective-permute-start(bf16[64,2304]{1,0:T(8,128)(2,1)} %param.6), channel_id=1, source_target_pairs={{0,32},{8,40},{16,48},{24,56},{32,64},{40,72},{48,80},{56,88},{64,... | collective-permute-start | bytes 884744 | tf_op jit(solution)/shard_map/ppermute | solution.py:22
  5.4 3.9 %collective-permute-start.1 = (bf16[64,2304]{1,0:T(8,128)(2,1)}, bf16[64,2304]{1,0:T(8,128)(2,1)S(1)}, u32[]{:S(2)}, u32[]{:S(2)}) collective-permute-start(bf16[64,2304]{1,0:T(8,128)(2,1)} %param.6), channel_id=1, source_target_pairs={{0,224},{8,232},{16,240},{24,248},{32,0},{40,8},{48,16},{56,24},{6... | collective-permute-start | bytes 884744 | tf_op jit(solution)/shard_map/ppermute | solution.py:22
  14.6 2.3 %collective-permute-start.6 = (bf16[64,2048]{1,0:T(8,128)(2,1)}, bf16[64,2048]{1,0:T(8,128)(2,1)S(1)}, u32[]{:S(2)}, u32[]{:S(2)}) collective-permute-start(bf16[64,2048]{1,0:T(8,128)(2,1)} %param.7), channel_id=1, source_target_pairs={{0,16},{8,24},{16,0},{24,8},{32,48},{40,56},{48,32},{56,40},{64,80... | collective-permute-start | bytes 786440 | tf_op jit(solution)/shard_map/ppermute | solution.py:22
  17.0 3.2 %collective-permute-start.5 = (bf16[64,2304]{1,0:T(8,128)(2,1)S(1)}, bf16[64,2304]{1,0:T(8,128)(2,1)S(1)}, u32[]{:S(2)}, u32[]{:S(2)}) collective-permute-start(bf16[64,2304]{1,0:T(8,128)(2,1)S(1)} %collective-permute-done.1), channel_id=1, source_target_pairs={{0,224},{8,232},{16,240},{24,248},{32,0},{40,8},{48,16},{56,24},{6... | collective-permute-start | bytes 884744 | tf_op jit(solution)/shard_map/ppermute | solution.py:22
  21.3 2.3 %collective-permute-done.6 = bf16[64,2048]{1,0:T(8,128)(2,1)S(1)} collective-permute-done((bf16[64,2048]{1,0:T(8,128)(2,1)}, bf16[64,2048]{1,0:T(8,128)(2,1)S(1)}, u32[]{:S(2)}, u32[]{:S(2)}) %collective-permute-start.6) | collective-permute-done | bytes 262176 | tf_op jit(solution)/shard_map/ppermute | solution.py:22
  23.5 3.0 %collective-permute-start.14 = (bf16[192,2304]{1,0:T(8,128)(2,1)S(1)}, bf16[192,2304]{1,0:T(8,128)(2,1)S(1)}, u32[]{:S(2)}, u32[]{:S(2)}) collective-permute-start(bf16[192,2304]{1,0:T(8,128)(2,1)S(1)} %pad_maximum_fusion.4), channel_id=1, source_target_pairs={{0,24},{8,0},{16,8},{24,16},{32,56},{40,32},{48,40},{56,48},{64,88... | collective-permute-start | bytes 2654216 | tf_op jit(solution)/shard_map/ppermute | solution.py:22
  27.2 2.6 %collective-permute-start.9 = (bf16[64,2304]{1,0:T(8,128)(2,1)S(1)}, bf16[64,2304]{1,0:T(8,128)(2,1)S(1)}, u32[]{:S(2)}, u32[]{:S(2)}) collective-permute-start(bf16[64,2304]{1,0:T(8,128)(2,1)S(1)} %collective-permute-done.5), channel_id=1, source_target_pairs={{0,224},{8,232},{16,240},{24,248},{32,0},{40,8},{48,16},{56,24},{6... | collective-permute-start | bytes 884744 | tf_op jit(solution)/shard_map/ppermute | solution.py:22
  31.8 2.7 %collective-permute-done.8 = bf16[64,2304]{1,0:T(8,128)(2,1)S(1)} collective-permute-done((bf16[64,2304]{1,0:T(8,128)(2,1)S(1)}, bf16[64,2304]{1,0:T(8,128)(2,1)S(1)}, u32[]{:S(2)}, u32[]{:S(2)}) %collective-permute-start.8) | collective-permute-done | bytes 294944 | tf_op jit(solution)/shard_map/ppermute | solution.py:22
  34.7 3.3 %collective-permute-start.11 = (bf16[32,2304]{1,0:T(8,128)(2,1)S(1)}, bf16[32,2304]{1,0:T(8,128)(2,1)S(1)}, u32[]{:S(2)}, u32[]{:S(2)}) collective-permute-start(bf16[32,2304]{1,0:T(8,128)(2,1)S(1)} %slice.25), channel_id=1, source_target_pairs={{0,224},{8,232},{16,240},{24,248},{32,0},{40,8},{48,16},{56,24},{6... | collective-permute-start | bytes 442376 | tf_op jit(solution)/shard_map/ppermute | solution.py:22
  38.7 1.9 %collective-permute-done.12 = bf16[256,1024]{1,0:T(8,128)(2,1)S(1)} collective-permute-done((bf16[256,1024]{1,0:T(8,128)(2,1)S(1)}, bf16[256,1024]{1,0:T(8,128)(2,1)S(1)}, u32[]{:S(2)}, u32[]{:S(2)}) %collective-permute-start.12) | collective-permute-done | bytes 524320 | tf_op jit(solution)/shard_map/ppermute | solution.py:27
  43.4 3.4 %collective-permute-done.13 = bf16[192,2304]{1,0:T(8,128)(2,1)S(1)} collective-permute-done((bf16[192,2304]{1,0:T(8,128)(2,1)S(1)}, bf16[192,2304]{1,0:T(8,128)(2,1)S(1)}, u32[]{:S(2)}, u32[]{:S(2)}) %collective-permute-start.13) | collective-permute-done | bytes 884768 | tf_op jit(solution)/shard_map/ppermute | solution.py:22
  51.2 7.5 %collective-permute-done.15 = bf16[256,1024]{1,0:T(8,128)(2,1)S(1)} collective-permute-done((bf16[256,1024]{1,0:T(8,128)(2,1)S(1)}, bf16[256,1024]{1,0:T(8,128)(2,1)S(1)}, u32[]{:S(2)}, u32[]{:S(2)}) %collective-permute-start.15) | collective-permute-done | bytes 524320 | tf_op jit(solution)/shard_map/ppermute | solution.py:27
  58.8 4.9 %collective-permute-done.19 = bf16[256,2048]{1,0:T(8,128)(2,1)} collective-permute-done((bf16[256,2048]{1,0:T(8,128)(2,1)S(1)}, bf16[256,2048]{1,0:T(8,128)(2,1)}, u32[]{:S(2)}, u32[]{:S(2)}) %collective-permute-start.19) | collective-permute-done | bytes 1048608 | tf_op jit(solution)/shard_map/ppermute | solution.py:22
  63.7 2.0 %collective-permute-start.20 = (bf16[256,2048]{1,0:T(8,128)(2,1)}, bf16[256,2048]{1,0:T(8,128)(2,1)}, u32[]{:S(2)}, u32[]{:S(2)}) collective-permute-start(bf16[256,2048]{1,0:T(8,128)(2,1)} %collective-permute-done.19), channel_id=1, source_target_pairs={{0,224},{8,232},{16,240},{24,248},{32,0},{40,8},{48,16},{56,24},{6... | collective-permute-start | bytes 3145736 | tf_op jit(solution)/shard_map/ppermute | solution.py:22
  67.0 2.3 %constant_dynamic-update-slice_fusion.11 = bf16[768,2048]{1,0:T(8,128)(2,1)} fusion(bf16[768,2048]{1,0:T(8,128)(2,1)} %get-tuple-element.82, bf16[256,2048]{1,0:T(8,128)(2,1)} %collective-permute-done.17), kind=kLoop, calls=%fused_computation.46 | loop fusion | bytes 2097152
  69.3 2.4 %constant_dynamic-update-slice_fusion.10 = bf16[768,2048]{1,0:T(8,128)(2,1)} fusion(bf16[768,2048]{1,0:T(8,128)(2,1)} %constant_dynamic-update-slice_fusion.11, bf16[256,2048]{1,0:T(8,128)(2,1)} %collective-permute-done.19), kind=kLoop, calls=%fused_computation.45 | loop fusion | bytes 2097152 | tf_op jit(solution)/shard_map/concatenate | solution.py:88
  71.7 8.3 %collective-permute-done.22 = bf16[320,2304]{1,0:T(8,128)(2,1)} collective-permute-done((bf16[320,2304]{1,0:T(8,128)(2,1)}, bf16[320,2304]{1,0:T(8,128)(2,1)}, u32[]{:S(2)}, u32[]{:S(2)}) %collective-permute-start.22) | collective-permute-done | bytes 1474592 | tf_op jit(solution)/shard_map/ppermute | solution.py:22
  80.0 2.4 %collective-permute-done.21 = bf16[320,2304]{1,0:T(8,128)(2,1)} collective-permute-done((bf16[320,2304]{1,0:T(8,128)(2,1)}, bf16[320,2304]{1,0:T(8,128)(2,1)}, u32[]{:S(2)}, u32[]{:S(2)}) %collective-permute-start.21) | collective-permute-done | bytes 1474592 | tf_op jit(solution)/shard_map/ppermute | solution.py:22
  82.4 3.1 %collective-permute-done.20 = bf16[256,2048]{1,0:T(8,128)(2,1)} collective-permute-done((bf16[256,2048]{1,0:T(8,128)(2,1)}, bf16[256,2048]{1,0:T(8,128)(2,1)}, u32[]{:S(2)}, u32[]{:S(2)}) %collective-permute-start.20) | collective-permute-done | bytes 1048608 | tf_op jit(solution)/shard_map/ppermute | solution.py:22
  85.5 4.2 %collective-permute-done.18 = bf16[256,2048]{1,0:T(8,128)(2,1)} collective-permute-done((bf16[256,2048]{1,0:T(8,128)(2,1)}, bf16[256,2048]{1,0:T(8,128)(2,1)}, u32[]{:S(2)}, u32[]{:S(2)}) %collective-permute-start.18) | collective-permute-done | bytes 1048608 | tf_op jit(solution)/shard_map/ppermute | solution.py:22
  92.1 3.2 %collective-permute-start.26 = (bf16[256,2048]{1,0:T(8,128)(2,1)}, bf16[256,2048]{1,0:T(8,128)(2,1)S(1)}, u32[]{:S(2)}, u32[]{:S(2)}) collective-permute-start(bf16[256,2048]{1,0:T(8,128)(2,1)} %collective-permute-done.20), channel_id=1, source_target_pairs={{0,224},{8,232},{16,240},{24,248},{32,0},{40,8},{48,16},{56,24},{6... | collective-permute-start | bytes 3145736 | tf_op jit(solution)/shard_map/ppermute | solution.py:22
  95.5 3.2 %collective-permute-start.24 = (bf16[256,2304]{1,0:T(8,128)(2,1)S(1)}, bf16[256,2304]{1,0:T(8,128)(2,1)S(1)}, u32[]{:S(2)}, u32[]{:S(2)}) collective-permute-start(bf16[256,2304]{1,0:T(8,128)(2,1)S(1)} %pad_maximum_fusion.3), channel_id=1, source_target_pairs={{0,24},{8,0},{16,8},{24,16},{32,56},{40,32},{48,40},{56,48},{64,88... | collective-permute-start | bytes 3538952 | tf_op jit(solution)/shard_map/ppermute | solution.py:22
  98.9 3.8 %shard_map.59 = (bf16[512,896]{1,0:T(8,128)(2,1)S(1)}, bf16[512,640]{1,0:T(8,128)(2,1)S(1)}, bf16[512,512]{1,0:T(8,128)(2,1)S(1)}, bf16[512,768]{1,0:T(8,128)(2,...) custom-call(s32[4]{0:T(128)S(1)} %pad_add_fusion.place_ref, ...), custom_call_target="tpu_custom_call" | custom-call | bytes 12582912 | tf_op jit(solution)/shard_map/pallas_call | solution.py:71
  102.7 4.2 %fusion.9 = f32[512,2304]{1,0:T(8,128)S(1)} fusion(bf16[512,896]{1,0:T(8,128)(2,1)S(1)} %get-tuple-element.73, bf16[320,2304]{1,0:T(8,128)(2,1)} %pad_maximum_fusion, bf16[192,2304]{1,0:T(8,128)(2,1)S(1)} %copy-done.3, bf16[192,2304]{1,0:T(8,128)(2,1)S(1)} %copy-done.1, bf16[192,2304]{1,0:T(8,128)(2,1)S(1)} %copy-done.5), kind=kOutput, calls=%fused_computation.12 | convolution fusion | flops 2130444288 | bytes 9764864 | tf_op jit(solution)/shard_map/dot_general | solution.py:88
  106.9 4.1 %convolution_add_fusion.1 = f32[512,2304]{1,0:T(8,128)S(1)} fusion(f32[512,2304]{1,0:T(8,128)S(1)} %fusion.9, bf16[512,640]{1,0:T(8,128)(2,1)S(1)} %get-tuple-element.72, bf16[320,2304]{1,0:T(8,128)(2,1)} %collective-permute-done.22, bf16[320,2304]{1,0:T(8,128)(2,1)} %collective-permute-done.21), kind=kOutput, calls=%fused_computation.1 | convolution fusion | flops 1517027328 | bytes 13041664 | tf_op jit(solution)/shard_map/dot_general | solution.py:88
  111.0 1.8 %fusion.34 = f32[512,2048]{1,0:T(8,128)S(1)} fusion(bf16[512,768]{1,0:T(8,128)(2,1)S(1)} %get-tuple-element.71, bf16[768,2048]{1,0:T(8,128)(2,1)S(1)} %copy-done.6), kind=kOutput, calls=%fused_computation.57 | convolution fusion | flops 1610612736 | bytes 8126464 | tf_op jit(solution)/shard_map/dot_general | solution.py:88
  115.2 3.7 %collective-permute-start.28 = (bf16[128,2048]{1,0:T(8,128)(2,1)S(1)}, bf16[128,2048]{1,0:T(8,128)(2,1)S(1)}, u32[]{:S(2)}, u32[]{:S(2)}) collective-permute-start(bf16[128,2048]{1,0:T(8,128)(2,1)S(1)} %slice.31), channel_id=1, source_target_pairs={{0,224},{8,232},{16,240},{24,248},{32,0},{40,8},{48,16},{56,24},{6... | collective-permute-start | bytes 1572872 | tf_op jit(solution)/shard_map/ppermute | solution.py:22
  118.9 3.8 %fusion.17 = f32[512,2048]{1,0:T(8,128)S(1)} fusion(f32[512,2048]{1,0:T(8,128)S(1)} %fusion.34, bf16[512,1024]{1,0:T(8,128)(2,1)S(1)} %get-tuple-element.68, bf16[256,2048]{1,0:T(8,128)(2,1)S(1)} %collective-permute-done.26, bf16[256,2048]{1,0:T(8,128)(2,1)S(1)} %collective-permute-done.25, bf16[256,2048]{1,0:T(8,128)(2,1)} %collective-permute-done.20, ...), kind=kOutput, calls=%fused_computation.20 | convolution fusion | flops 2165309440 | bytes 13631488 | tf_op jit(solution)/shard_map/dot_general | solution.py:88
  122.7 2.8 %fusion = bf16[512,2304]{1,0:T(8,128)(2,1)} fusion(f32[512,2304]{1,0:T(8,128)S(1)} %convolution_add_fusion.1, bf16[512,512]{1,0:T(8,128)(2,1)S(1)} %get-tuple-element.59, bf16[256,2304]{1,0:T(8,128)(2,1)S(1)} %collective-permute-done.24, bf16[256,2304]{1,0:T(8,128)(2,1)S(1)} %collective-permute-done.23), kind=kOutput, calls=%fused_computation.2 | convolution fusion | flops 1215037440 | bytes 9961472 | tf_op jit(solution)/shard_map/dot_general | solution.py:88
  125.6 3.7 %collective-permute-done.27 = bf16[128,2048]{1,0:T(8,128)(2,1)S(1)} collective-permute-done((bf16[128,2048]{1,0:T(8,128)(2,1)S(1)}, bf16[128,2048]{1,0:T(8,128)(2,1)S(1)}, u32[]{:S(2)}, u32[]{:S(2)}) %collective-permute-start.27) | collective-permute-done | bytes 524320 | tf_op jit(solution)/shard_map/ppermute | solution.py:22
  129.3 2.0 %add_convert_fusion = bf16[512,2048]{1,0:T(8,128)(2,1)} fusion(f32[512,2048]{1,0:T(8,128)S(1)} %fusion.17, bf16[512,256]{1,0:T(8,128)(2,1)S(1)} %get-tuple-element.80, bf16[128,2048]{1,0:T(8,128)(2,1)S(1)} %collective-permute-done.28, bf16[128,2048]{1,0:T(8,128)(2,1)S(1)} %collective-permute-done.27), kind=kOutput, calls=%fused_computation.11 | convolution fusion | flops 541065216 | bytes 7602176 | tf_op jit(solution)/shard_map/dot_general | solution.py:88
  (75 shorter events, 23.6 us)
Async XLA Ops:
  0.6 14.0 %collective-permute-start.3 = (bf16[64,2048]{1,0:T(8,128)(2,1)}, bf16[64,2048]{1,0:T(8,128)(2,1)S(1)}, u32[]{:S(2)}, u32[]{:S(2)}) collective-permute-start(bf16[64,2048]{1,0:T(8,128)(2,1)} %param.7), channel_id=1, source_target_pairs={{0,24},{8,0},{16,8},{24,16},{32,56},{40,32},{48,40},{56,48},{64,88... | collective-permute-start | bytes 786440 | tf_op jit(solution)/shard_map/ppermute | solution.py:22
  3.5 13.4 %collective-permute-start.2 = (bf16[64,2048]{1,0:T(8,128)(2,1)}, bf16[64,2048]{1,0:T(8,128)(2,1)S(1)}, u32[]{:S(2)}, u32[]{:S(2)}) collective-permute-start(bf16[64,2048]{1,0:T(8,128)(2,1)} %param.7), channel_id=1, source_target_pairs={{0,8},{8,16},{16,24},{24,0},{32,40},{40,48},{48,56},{56,32},{64,72... | collective-permute-start | bytes 786440 | tf_op jit(solution)/shard_map/ppermute | solution.py:22
  3.5 13.4 %collective-permute-start = (bf16[64,2304]{1,0:T(8,128)(2,1)}, bf16[64,2304]{1,0:T(8,128)(2,1)S(1)}, u32[]{:S(2)}, u32[]{:S(2)}) collective-permute-start(bf16[64,2304]{1,0:T(8,128)(2,1)} %param.6), channel_id=1, source_target_pairs={{0,32},{8,40},{16,48},{24,56},{32,64},{40,72},{48,80},{56,88},{64,... | collective-permute-start | bytes 884744 | tf_op jit(solution)/shard_map/ppermute | solution.py:22
  5.4 11.5 %collective-permute-start.1 = (bf16[64,2304]{1,0:T(8,128)(2,1)}, bf16[64,2304]{1,0:T(8,128)(2,1)S(1)}, u32[]{:S(2)}, u32[]{:S(2)}) collective-permute-start(bf16[64,2304]{1,0:T(8,128)(2,1)} %param.6), channel_id=1, source_target_pairs={{0,224},{8,232},{16,240},{24,248},{32,0},{40,8},{48,16},{56,24},{6... | collective-permute-start | bytes 884744 | tf_op jit(solution)/shard_map/ppermute | solution.py:22
  11.3 15.2 %collective-permute-start.7 = (bf16[256,1024]{1,0:T(8,128)(2,1)S(1)}, bf16[256,1024]{1,0:T(8,128)(2,1)S(1)}, u32[]{:S(2)}, u32[]{:S(2)}) collective-permute-start(bf16[256,1024]{1,0:T(8,128)(2,1)S(1)} %constant_dynamic-update-slice_fusion), channel_id=1, source_target_pairs={{0,2},{1,3},{2,4},{3,5},{4,6},{5,7},{6,0},{7,1},{8,10},{9,11},{10,... | collective-permute-start | bytes 1572872 | tf_op jit(solution)/shard_map/ppermute | solution.py:27
  14.6 8.9 %collective-permute-start.6 = (bf16[64,2048]{1,0:T(8,128)(2,1)}, bf16[64,2048]{1,0:T(8,128)(2,1)S(1)}, u32[]{:S(2)}, u32[]{:S(2)}) collective-permute-start(bf16[64,2048]{1,0:T(8,128)(2,1)} %param.7), channel_id=1, source_target_pairs={{0,16},{8,24},{16,0},{24,8},{32,48},{40,56},{48,32},{56,40},{64,80... | collective-permute-start | bytes 786440 | tf_op jit(solution)/shard_map/ppermute | solution.py:22
  16.9 9.6 %collective-permute-start.4 = (bf16[64,2304]{1,0:T(8,128)(2,1)S(1)}, bf16[64,2304]{1,0:T(8,128)(2,1)S(1)}, u32[]{:S(2)}, u32[]{:S(2)}) collective-permute-start(bf16[64,2304]{1,0:T(8,128)(2,1)S(1)} %collective-permute-done), channel_id=1, source_target_pairs={{0,32},{8,40},{16,48},{24,56},{32,64},{40,72},{48,80},{56,88},{64,... | collective-permute-start | bytes 884744 | tf_op jit(solution)/shard_map/ppermute | solution.py:22
  17.0 9.5 %collective-permute-start.5 = (bf16[64,2304]{1,0:T(8,128)(2,1)S(1)}, bf16[64,2304]{1,0:T(8,128)(2,1)S(1)}, u32[]{:S(2)}, u32[]{:S(2)}) collective-permute-start(bf16[64,2304]{1,0:T(8,128)(2,1)S(1)} %collective-permute-done.1), channel_id=1, source_target_pairs={{0,224},{8,232},{16,240},{24,248},{32,0},{40,8},{48,16},{56,24},{6... | collective-permute-start | bytes 884744 | tf_op jit(solution)/shard_map/ppermute | solution.py:22
  21.3 26.6 %copy-start.4 = (bf16[192,2304]{1,0:T(8,128)(2,1)}, bf16[192,2304]{1,0:T(8,128)(2,1)S(1)}, u32[]{:S(2)}) copy-start(bf16[192,2304]{1,0:T(8,128)(2,1)S(1)} %pad_maximum_fusion.4) | copy-start | bytes 2654212
  23.5 19.8 %collective-permute-start.14 = (bf16[192,2304]{1,0:T(8,128)(2,1)S(1)}, bf16[192,2304]{1,0:T(8,128)(2,1)S(1)}, u32[]{:S(2)}, u32[]{:S(2)}) collective-permute-start(bf16[192,2304]{1,0:T(8,128)(2,1)S(1)} %pad_maximum_fusion.4), channel_id=1, source_target_pairs={{0,24},{8,0},{16,8},{24,16},{32,56},{40,32},{48,40},{56,48},{64,88... | collective-permute-start | bytes 2654216 | tf_op jit(solution)/shard_map/ppermute | solution.py:22
  26.5 20.3 %collective-permute-start.13 = (bf16[192,2304]{1,0:T(8,128)(2,1)S(1)}, bf16[192,2304]{1,0:T(8,128)(2,1)S(1)}, u32[]{:S(2)}, u32[]{:S(2)}) collective-permute-start(bf16[192,2304]{1,0:T(8,128)(2,1)S(1)} %pad_maximum_fusion.4), channel_id=1, source_target_pairs={{0,8},{8,16},{16,24},{24,0},{32,40},{40,48},{48,56},{56,32},{64,72... | collective-permute-start | bytes 2654216 | tf_op jit(solution)/shard_map/ppermute | solution.py:22
  26.5 8.0 %collective-permute-start.8 = (bf16[64,2304]{1,0:T(8,128)(2,1)S(1)}, bf16[64,2304]{1,0:T(8,128)(2,1)S(1)}, u32[]{:S(2)}, u32[]{:S(2)}) collective-permute-start(bf16[64,2304]{1,0:T(8,128)(2,1)S(1)} %collective-permute-done.4), channel_id=1, source_target_pairs={{0,32},{8,40},{16,48},{24,56},{32,64},{40,72},{48,80},{56,88},{64,... | collective-permute-start | bytes 884744 | tf_op jit(solution)/shard_map/ppermute | solution.py:22
  27.2 7.3 %collective-permute-start.9 = (bf16[64,2304]{1,0:T(8,128)(2,1)S(1)}, bf16[64,2304]{1,0:T(8,128)(2,1)S(1)}, u32[]{:S(2)}, u32[]{:S(2)}) collective-permute-start(bf16[64,2304]{1,0:T(8,128)(2,1)S(1)} %collective-permute-done.5), channel_id=1, source_target_pairs={{0,224},{8,232},{16,240},{24,248},{32,0},{40,8},{48,16},{56,24},{6... | collective-permute-start | bytes 884744 | tf_op jit(solution)/shard_map/ppermute | solution.py:22
  29.8 10.8 %collective-permute-start.12 = (bf16[256,1024]{1,0:T(8,128)(2,1)S(1)}, bf16[256,1024]{1,0:T(8,128)(2,1)S(1)}, u32[]{:S(2)}, u32[]{:S(2)}) collective-permute-start(bf16[256,1024]{1,0:T(8,128)(2,1)S(1)} %constant_dynamic-update-slice_fusion), channel_id=1, source_target_pairs={{0,6},{1,7},{2,0},{3,1},{4,2},{5,3},{6,4},{7,5},{8,14},{9,15},{10,... | collective-permute-start | bytes 1572872 | tf_op jit(solution)/shard_map/ppermute | solution.py:27
  34.7 13.2 %collective-permute-start.11 = (bf16[32,2304]{1,0:T(8,128)(2,1)S(1)}, bf16[32,2304]{1,0:T(8,128)(2,1)S(1)}, u32[]{:S(2)}, u32[]{:S(2)}) collective-permute-start(bf16[32,2304]{1,0:T(8,128)(2,1)S(1)} %slice.25), channel_id=1, source_target_pairs={{0,224},{8,232},{16,240},{24,248},{32,0},{40,8},{48,16},{56,24},{6... | collective-permute-start | bytes 442376 | tf_op jit(solution)/shard_map/ppermute | solution.py:22
  38.0 9.9 %collective-permute-start.10 = (bf16[32,2304]{1,0:T(8,128)(2,1)S(1)}, bf16[32,2304]{1,0:T(8,128)(2,1)S(1)}, u32[]{:S(2)}, u32[]{:S(2)}) collective-permute-start(bf16[32,2304]{1,0:T(8,128)(2,1)S(1)} %slice.24), channel_id=1, source_target_pairs={{0,32},{8,40},{16,48},{24,56},{32,64},{40,72},{48,80},{56,88},{64,... | collective-permute-start | bytes 442376 | tf_op jit(solution)/shard_map/ppermute | solution.py:22
  40.6 23.1 %collective-permute-start.19 = (bf16[256,2048]{1,0:T(8,128)(2,1)S(1)}, bf16[256,2048]{1,0:T(8,128)(2,1)}, u32[]{:S(2)}, u32[]{:S(2)}) collective-permute-start(bf16[256,2048]{1,0:T(8,128)(2,1)S(1)} %get-tuple-element.83), channel_id=1, source_target_pairs={{0,224},{8,232},{16,240},{24,248},{32,0},{40,8},{48,16},{56,24},{6... | collective-permute-start | bytes 3145736 | tf_op jit(solution)/shard_map/ppermute | solution.py:22
  43.4 23.5 %collective-permute-start.17 = (bf16[256,2048]{1,0:T(8,128)(2,1)S(1)}, bf16[256,2048]{1,0:T(8,128)(2,1)}, u32[]{:S(2)}, u32[]{:S(2)}) collective-permute-start(bf16[256,2048]{1,0:T(8,128)(2,1)S(1)} %get-tuple-element.83), channel_id=1, source_target_pairs={{0,32},{8,40},{16,48},{24,56},{32,64},{40,72},{48,80},{56,88},{64,... | collective-permute-start | bytes 3145736 | tf_op jit(solution)/shard_map/ppermute | solution.py:22
  46.8 11.9 %collective-permute-start.15 = (bf16[256,1024]{1,0:T(8,128)(2,1)S(1)}, bf16[256,1024]{1,0:T(8,128)(2,1)S(1)}, u32[]{:S(2)}, u32[]{:S(2)}) collective-permute-start(bf16[256,1024]{1,0:T(8,128)(2,1)S(1)} %constant_dynamic-update-slice_fusion), channel_id=1, source_target_pairs={{0,4},{1,5},{2,6},{3,7},{4,0},{5,1},{6,2},{7,3},{8,12},{9,13},{10,... | collective-permute-start | bytes 1572872 | tf_op jit(solution)/shard_map/ppermute | solution.py:27
  49.1 30.9 %collective-permute-start.22 = (bf16[320,2304]{1,0:T(8,128)(2,1)}, bf16[320,2304]{1,0:T(8,128)(2,1)}, u32[]{:S(2)}, u32[]{:S(2)}) collective-permute-start(bf16[320,2304]{1,0:T(8,128)(2,1)} %pad_maximum_fusion), channel_id=1, source_target_pairs={{0,24},{8,0},{16,8},{24,16},{32,56},{40,32},{48,40},{56,48},{64,88... | collective-permute-start | bytes 4423688 | tf_op jit(solution)/shard_map/ppermute | solution.py:22
  50.3 32.1 %collective-permute-start.21 = (bf16[320,2304]{1,0:T(8,128)(2,1)}, bf16[320,2304]{1,0:T(8,128)(2,1)}, u32[]{:S(2)}, u32[]{:S(2)}) collective-permute-start(bf16[320,2304]{1,0:T(8,128)(2,1)} %pad_maximum_fusion), channel_id=1, source_target_pairs={{0,8},{8,16},{16,24},{24,0},{32,40},{40,48},{48,56},{56,32},{64,72... | collective-permute-start | bytes 4423688 | tf_op jit(solution)/shard_map/ppermute | solution.py:22
  58.7 40.1 %collective-permute-start.16 = (bf16[1024,1024]{1,0:T(8,128)(2,1)S(1)}, bf16[1024,1024]{1,0:T(8,128)(2,1)}, u32[]{:S(2)}, u32[]{:S(2)}) collective-permute-start(bf16[1024,1024]{1,0:T(8,128)(2,1)S(1)} %constant_dynamic-update-slice_fusion.2.mine_ref), channel_id=1, source_target_pairs={{0,1},{1,0},{2,3},{3,2},{4,5},{5,4},{6,7},{7,6},{8,9},{9,8},{10,11... | collective-permute-start | bytes 6291464 | tf_op jit(solution)/shard_map/ppermute | solution.py:27
  63.7 21.8 %collective-permute-start.20 = (bf16[256,2048]{1,0:T(8,128)(2,1)}, bf16[256,2048]{1,0:T(8,128)(2,1)}, u32[]{:S(2)}, u32[]{:S(2)}) collective-permute-start(bf16[256,2048]{1,0:T(8,128)(2,1)} %collective-permute-done.19), channel_id=1, source_target_pairs={{0,224},{8,232},{16,240},{24,248},{32,0},{40,8},{48,16},{56,24},{6... | collective-permute-start | bytes 3145736 | tf_op jit(solution)/shard_map/ppermute | solution.py:22
  66.9 22.8 %collective-permute-start.18 = (bf16[256,2048]{1,0:T(8,128)(2,1)}, bf16[256,2048]{1,0:T(8,128)(2,1)}, u32[]{:S(2)}, u32[]{:S(2)}) collective-permute-start(bf16[256,2048]{1,0:T(8,128)(2,1)} %collective-permute-done.17), channel_id=1, source_target_pairs={{0,32},{8,40},{16,48},{24,56},{32,64},{40,72},{48,80},{56,88},{64,... | collective-permute-start | bytes 3145736 | tf_op jit(solution)/shard_map/ppermute | solution.py:22
  69.3 26.1 %slice-start.1 = ((bf16[192,2304]{1,0:T(8,128)(2,1)}), bf16[96,2304]{1,0:T(8,128)(2,1)S(1)}, s32[]{:S(2)}) async-start(bf16[192,2304]{1,0:T(8,128)(2,1)} %copy-done.2), calls=%async_computation.1 | async-start | bytes 884736 | tf_op jit(solution)/shard_map/slice | solution.py:32
  71.7 27.0 %slice-start = ((bf16[192,2304]{1,0:T(8,128)(2,1)}), bf16[96,2304]{1,0:T(8,128)(2,1)S(1)}, s32[]{:S(2)}) async-start(bf16[192,2304]{1,0:T(8,128)(2,1)} %copy-done), calls=%async_computation | async-start | bytes 884736 | tf_op jit(solution)/shard_map/slice | solution.py:32
  92.1 21.9 %collective-permute-start.25 = (bf16[256,2048]{1,0:T(8,128)(2,1)}, bf16[256,2048]{1,0:T(8,128)(2,1)S(1)}, u32[]{:S(2)}, u32[]{:S(2)}) collective-permute-start(bf16[256,2048]{1,0:T(8,128)(2,1)} %collective-permute-done.18), channel_id=1, source_target_pairs={{0,32},{8,40},{16,48},{24,56},{32,64},{40,72},{48,80},{56,88},{64,... | collective-permute-start | bytes 3145736 | tf_op jit(solution)/shard_map/ppermute | solution.py:22
  92.1 23.0 %collective-permute-start.26 = (bf16[256,2048]{1,0:T(8,128)(2,1)}, bf16[256,2048]{1,0:T(8,128)(2,1)S(1)}, u32[]{:S(2)}, u32[]{:S(2)}) collective-permute-start(bf16[256,2048]{1,0:T(8,128)(2,1)} %collective-permute-done.20), channel_id=1, source_target_pairs={{0,224},{8,232},{16,240},{24,248},{32,0},{40,8},{48,16},{56,24},{6... | collective-permute-start | bytes 3145736 | tf_op jit(solution)/shard_map/ppermute | solution.py:22
  95.5 27.2 %collective-permute-start.24 = (bf16[256,2304]{1,0:T(8,128)(2,1)S(1)}, bf16[256,2304]{1,0:T(8,128)(2,1)S(1)}, u32[]{:S(2)}, u32[]{:S(2)}) collective-permute-start(bf16[256,2304]{1,0:T(8,128)(2,1)S(1)} %pad_maximum_fusion.3), channel_id=1, source_target_pairs={{0,24},{8,0},{16,8},{24,16},{32,56},{40,32},{48,40},{56,48},{64,88... | collective-permute-start | bytes 3538952 | tf_op jit(solution)/shard_map/ppermute | solution.py:22
  98.8 24.0 %collective-permute-start.23 = (bf16[256,2304]{1,0:T(8,128)(2,1)S(1)}, bf16[256,2304]{1,0:T(8,128)(2,1)S(1)}, u32[]{:S(2)}, u32[]{:S(2)}) collective-permute-start(bf16[256,2304]{1,0:T(8,128)(2,1)S(1)} %pad_maximum_fusion.2), channel_id=1, source_target_pairs={{0,8},{8,16},{16,24},{24,0},{32,40},{40,48},{48,56},{56,32},{64,72... | collective-permute-start | bytes 3538952 | tf_op jit(solution)/shard_map/ppermute | solution.py:22
  115.2 10.4 %collective-permute-start.28 = (bf16[128,2048]{1,0:T(8,128)(2,1)S(1)}, bf16[128,2048]{1,0:T(8,128)(2,1)S(1)}, u32[]{:S(2)}, u32[]{:S(2)}) collective-permute-start(bf16[128,2048]{1,0:T(8,128)(2,1)S(1)} %slice.31), channel_id=1, source_target_pairs={{0,224},{8,232},{16,240},{24,248},{32,0},{40,8},{48,16},{56,24},{6... | collective-permute-start | bytes 1572872 | tf_op jit(solution)/shard_map/ppermute | solution.py:22
  118.9 10.4 %collective-permute-start.27 = (bf16[128,2048]{1,0:T(8,128)(2,1)S(1)}, bf16[128,2048]{1,0:T(8,128)(2,1)S(1)}, u32[]{:S(2)}, u32[]{:S(2)}) collective-permute-start(bf16[128,2048]{1,0:T(8,128)(2,1)S(1)} %slice.30), channel_id=1, source_target_pairs={{0,32},{8,40},{16,48},{24,56},{32,64},{40,72},{48,80},{56,88},{64,... | collective-permute-start | bytes 1572872 | tf_op jit(solution)/shard_map/ppermute | solution.py:22
  (6 other events, 49.4 us)

commit v12 on v11

--- a/solution.py
+++ b/solution.py
@@ -151,32 +151,30 @@
     wide_rows = {dz: [(dz, dx, 0, BLOCK) for dx in X_ORDER] for dz in range(-4, 5)}
     wide_split = parts(wide_rows[4])
     groups = [
-        (near_rows[0] + near_rows[-1] + near_rows[1] + far_rows[0], 0),
-        (far_rows[-1] + far_rows[1], 0),
+        (sum([near_rows[0], near_rows[-1], near_rows[1], *(far_rows[d] for d in (0, -1, 1))], []), 0),
         (near_split[0] + far_split[0] + near_split[1] + far_split[1], 0),
         (wide_rows[0] + wide_rows[-1] + wide_rows[1], 1),
         (sum([wide_rows[d] for d in (-2, 2, -3, 3)], []), 1),
         (wide_split[0] + wide_split[1], 1),
     ]
     lefts = arrange(place, (mine, hop_y(mine, 0, 1)), groups)
-    tall_sum = contract(lefts[0], tall_first)
 
     below, above = hop(below, 1, 0), hop(above, -1, 0)
     wide_second = [below, above]
-    wide_sum = contract(lefts[3], wide_first)
+    wide_sum = contract(lefts[2], wide_first)
+    tall_sum = contract(lefts[0], [*tall_first, far_left, far_right])
     below, above, far_left, far_right = together((below, above, far_left, far_right))
     below, above = hop(below, 1, 0), hop(above, -1, 0)
     first = jnp.concatenate([halves(near_left)[0], halves(far_left)[0]])
     second = jnp.concatenate([halves(near_right)[1], halves(far_right)[1]])
 
     tall_halves = [hop(first, 0, 1), hop(second, 0, -1)]
-    tall_sum = contract(lefts[1], [far_left, far_right], tall_sum)
     below, above, wide_sum, tall_sum = together((below, above, wide_sum, tall_sum))
     wide_halves = [hop(halves(below)[0], 1, 0), hop(halves(above)[1], -1, 0)]
-    wide_sum = contract(lefts[4], [*wide_second, below, above], wide_sum)
+    wide_sum = contract(lefts[3], [*wide_second, below, above], wide_sum)
     tall_halves, wide_sum = together((tall_halves, wide_sum))
-    qkv = contract(lefts[2], tall_halves, tall_sum, dtype=jnp.bfloat16)
-    out = contract(lefts[5], wide_halves, wide_sum, dtype=jnp.bfloat16)
+    qkv = contract(lefts[1], tall_halves, tall_sum, dtype=jnp.bfloat16)
+    out = contract(lefts[4], wide_halves, wide_sum, dtype=jnp.bfloat16)
     return qkv, out
 
 

time: 132 us -> 137 us (1.038)
  waiting for transfers between devices: 49.4 us -> 60.7 us
  local copies, waits for them, and re-layouts: 13.2 us -> 4.06 us
  starting transfers between devices: 42.8 us -> 51.1 us
  matrix products: 18.7 us -> 13.4 us
    ppermute x25, waiting for transfers between devices: 40 us -> 52.6 us  [hop(): return lax.ppermute(value, 'row', pairs)]
    ppermute x25, starting transfers between devices: 39.5 us -> 47.2 us  [hop(): return lax.ppermute(value, 'row', pairs)]
    dot_general x6 -> x5, matrix products: 18.7 us -> 13.4 us  [contract(): jnp.dot(left, jnp.concatenate(grads), preferred_element_type=jnp.float32)]
    unnamed x23 -> x18, local copies, waits for them, and re-layouts: 7.36 us -> 2.67 us
    slice x10, local copies, waits for them, and re-layouts: 2.44 us -> 0.22 us  [halves(): return (value[:half], value[half:])]
    concatenate x1 -> x2, local copies, waits for them, and re-layouts: 2.37 us -> 0.17 us  [contract(): jnp.concatenate(grads)]
  transfers between devices with their start and end apart: 29 -> 29, of which waited for: 16 -> 13; matrix products, arithmetic and copies ran while one was open for 25% -> 12% of each run, Pallas kernels for 3% -> 3%
where the time goes in v12:
time: 137 us; the launch traced here: 136 us
  waiting for transfers between devices  60.7 us (44%)
  starting transfers between devices  51.1 us (37%)
  matrix products  13.4 us (10%)
  Pallas kernels  4.17 us (3%)
  local copies, waits for them, and re-layouts  4.06 us (3%)
  other arithmetic  1.44 us (1%)
    ppermute x25, waiting for transfers between devices, hop(): return lax.ppermute(value, 'row', pairs)  52.6 us
    ppermute x25, starting transfers between devices, hop(): return lax.ppermute(value, 'row', pairs)  47.2 us
    dot_general x5, matrix products, contract(): jnp.dot(left, jnp.concatenate(grads), preferred_element_type=jnp.float32)  13.4 us
    ppermute x4, waiting for transfers between devices, hop_y(): return lax.ppermute(value, 'col', pairs)  8.14 us
    pallas_call x1, Pallas kernels, arrange(): pl.pallas_call(functools.partial(arrange_kernel, groups), out_shape=[jax....  4.17 us
    ppermute x4, starting transfers between devices, hop_y(): return lax.ppermute(value, 'col', pairs)  3.97 us
  transfers between devices with their start and end apart: 29, of which 13 were waited for; matrix products, arithmetic and copies ran while one was open for 12% of the time, Pallas kernels for 3%

profile of v12, /device:TPU:8, one launch (start us, length us, event | category | flops | bytes accessed | tf_op | source)
XLA Modules:
  0.0 136.0 jit_solution(10779911843878165182)
XLA Ops:
  0.6 2.0 %collective-permute-start = (bf16[64,2304]{1,0:T(8,128)(2,1)}, bf16[64,2304]{1,0:T(8,128)(2,1)S(1)}, u32[]{:S(2)}, u32[]{:S(2)}) collective-permute-start(bf16[64,2304]{1,0:T(8,128)(2,1)} %param.6), channel_id=1, source_target_pairs={{0,32},{8,40},{16,48},{24,56},{32,64},{40,72},{48,80},{56,88},{64,... | collective-permute-start | bytes 884744 | tf_op jit(solution)/shard_map/ppermute | solution.py:22
  2.6 4.0 %collective-permute-start.1 = (bf16[64,2304]{1,0:T(8,128)(2,1)}, bf16[64,2304]{1,0:T(8,128)(2,1)S(1)}, u32[]{:S(2)}, u32[]{:S(2)}) collective-permute-start(bf16[64,2304]{1,0:T(8,128)(2,1)} %param.6), channel_id=1, source_target_pairs={{0,224},{8,232},{16,240},{24,248},{32,0},{40,8},{48,16},{56,24},{6... | collective-permute-start | bytes 884744 | tf_op jit(solution)/shard_map/ppermute | solution.py:22
  6.7 1.5 %collective-permute-start.2 = (bf16[64,2048]{1,0:T(8,128)(2,1)}, bf16[64,2048]{1,0:T(8,128)(2,1)S(1)}, u32[]{:S(2)}, u32[]{:S(2)}) collective-permute-start(bf16[64,2048]{1,0:T(8,128)(2,1)} %param.7), channel_id=1, source_target_pairs={{0,8},{8,16},{16,24},{24,0},{32,40},{40,48},{48,56},{56,32},{64,72... | collective-permute-start | bytes 786440 | tf_op jit(solution)/shard_map/ppermute | solution.py:22
  8.1 1.7 %collective-permute-start.3 = (bf16[64,2048]{1,0:T(8,128)(2,1)}, bf16[64,2048]{1,0:T(8,128)(2,1)S(1)}, u32[]{:S(2)}, u32[]{:S(2)}) collective-permute-start(bf16[64,2048]{1,0:T(8,128)(2,1)} %param.7), channel_id=1, source_target_pairs={{0,24},{8,0},{16,8},{24,16},{32,56},{40,32},{48,40},{56,48},{64,88... | collective-permute-start | bytes 786440 | tf_op jit(solution)/shard_map/ppermute | solution.py:22
  9.9 1.8 %collective-permute-start.6 = (bf16[64,2048]{1,0:T(8,128)(2,1)}, bf16[64,2048]{1,0:T(8,128)(2,1)S(1)}, u32[]{:S(2)}, u32[]{:S(2)}) collective-permute-start(bf16[64,2048]{1,0:T(8,128)(2,1)} %param.7), channel_id=1, source_target_pairs={{0,16},{8,24},{16,0},{24,8},{32,48},{40,56},{48,32},{56,40},{64,80... | collective-permute-start | bytes 786440 | tf_op jit(solution)/shard_map/ppermute | solution.py:22
  14.8 1.5 %collective-permute-done.2 = bf16[64,2048]{1,0:T(8,128)(2,1)S(1)} collective-permute-done((bf16[64,2048]{1,0:T(8,128)(2,1)}, bf16[64,2048]{1,0:T(8,128)(2,1)S(1)}, u32[]{:S(2)}, u32[]{:S(2)}) %collective-permute-start.2) | collective-permute-done | bytes 262176 | tf_op jit(solution)/shard_map/ppermute | solution.py:22
  16.3 1.6 %collective-permute-start.7 = (bf16[256,1024]{1,0:T(8,128)(2,1)S(1)}, bf16[256,1024]{1,0:T(8,128)(2,1)S(1)}, u32[]{:S(2)}, u32[]{:S(2)}) collective-permute-start(bf16[256,1024]{1,0:T(8,128)(2,1)S(1)} %constant_dynamic-update-slice_fusion), channel_id=1, source_target_pairs={{0,2},{1,3},{2,4},{3,5},{4,6},{5,7},{6,0},{7,1},{8,10},{9,11},{10,... | collective-permute-start | bytes 1572872 | tf_op jit(solution)/shard_map/ppermute | solution.py:27
  17.9 3.0 %collective-permute-done.3 = bf16[64,2048]{1,0:T(8,128)(2,1)S(1)} collective-permute-done((bf16[64,2048]{1,0:T(8,128)(2,1)}, bf16[64,2048]{1,0:T(8,128)(2,1)S(1)}, u32[]{:S(2)}, u32[]{:S(2)}) %collective-permute-start.3) | collective-permute-done | bytes 262176 | tf_op jit(solution)/shard_map/ppermute | solution.py:22
  21.9 3.3 %collective-permute-start.5 = (bf16[64,2304]{1,0:T(8,128)(2,1)S(1)}, bf16[64,2304]{1,0:T(8,128)(2,1)S(1)}, u32[]{:S(2)}, u32[]{:S(2)}) collective-permute-start(bf16[64,2304]{1,0:T(8,128)(2,1)S(1)} %collective-permute-done.1), channel_id=1, source_target_pairs={{0,224},{8,232},{16,240},{24,248},{32,0},{40,8},{48,16},{56,24},{6... | collective-permute-start | bytes 884744 | tf_op jit(solution)/shard_map/ppermute | solution.py:22
  25.2 3.6 %collective-permute-start.14 = (bf16[192,2304]{1,0:T(8,128)(2,1)S(1)}, bf16[192,2304]{1,0:T(8,128)(2,1)S(1)}, u32[]{:S(2)}, u32[]{:S(2)}) collective-permute-start(bf16[192,2304]{1,0:T(8,128)(2,1)S(1)} %pad_maximum_fusion.4), channel_id=1, source_target_pairs={{0,24},{8,0},{16,8},{24,16},{32,56},{40,32},{48,40},{56,48},{64,88... | collective-permute-start | bytes 2654216 | tf_op jit(solution)/shard_map/ppermute | solution.py:22
  30.2 3.7 %collective-permute-start.9 = (bf16[64,2304]{1,0:T(8,128)(2,1)S(1)}, bf16[64,2304]{1,0:T(8,128)(2,1)S(1)}, u32[]{:S(2)}, u32[]{:S(2)}) collective-permute-start(bf16[64,2304]{1,0:T(8,128)(2,1)S(1)} %collective-permute-done.5), channel_id=1, source_target_pairs={{0,224},{8,232},{16,240},{24,248},{32,0},{40,8},{48,16},{56,24},{6... | collective-permute-start | bytes 884744 | tf_op jit(solution)/shard_map/ppermute | solution.py:22
  34.0 5.6 %collective-permute-done.8 = bf16[64,2304]{1,0:T(8,128)(2,1)S(1)} collective-permute-done((bf16[64,2304]{1,0:T(8,128)(2,1)S(1)}, bf16[64,2304]{1,0:T(8,128)(2,1)S(1)}, u32[]{:S(2)}, u32[]{:S(2)}) %collective-permute-start.8) | collective-permute-done | bytes 294944 | tf_op jit(solution)/shard_map/ppermute | solution.py:22
  40.0 3.8 %collective-permute-start.10 = (bf16[32,2304]{1,0:T(8,128)(2,1)S(1)}, bf16[32,2304]{1,0:T(8,128)(2,1)S(1)}, u32[]{:S(2)}, u32[]{:S(2)}) collective-permute-start(bf16[32,2304]{1,0:T(8,128)(2,1)S(1)} %slice.24), channel_id=1, source_target_pairs={{0,32},{8,40},{16,48},{24,56},{32,64},{40,72},{48,80},{56,88},{64,... | collective-permute-start | bytes 442376 | tf_op jit(solution)/shard_map/ppermute | solution.py:22
  44.0 4.1 %collective-permute-done.10 = bf16[32,2304]{1,0:T(8,128)(2,1)S(1)} collective-permute-done((bf16[32,2304]{1,0:T(8,128)(2,1)S(1)}, bf16[32,2304]{1,0:T(8,128)(2,1)S(1)}, u32[]{:S(2)}, u32[]{:S(2)}) %collective-permute-start.10) | collective-permute-done | bytes 147488 | tf_op jit(solution)/shard_map/ppermute | solution.py:22
  48.2 2.5 %collective-permute-start.17 = (bf16[256,2048]{1,0:T(8,128)(2,1)S(1)}, bf16[256,2048]{1,0:T(8,128)(2,1)S(1)}, u32[]{:S(2)}, u32[]{:S(2)}) collective-permute-start(bf16[256,2048]{1,0:T(8,128)(2,1)S(1)} %get-tuple-element.81), channel_id=1, source_target_pairs={{0,32},{8,40},{16,48},{24,56},{32,64},{40,72},{48,80},{56,88},{64,... | collective-permute-start | bytes 3145736 | tf_op jit(solution)/shard_map/ppermute | solution.py:22
  52.2 4.6 %collective-permute-start.22 = (bf16[320,2304]{1,0:T(8,128)(2,1)S(1)}, bf16[320,2304]{1,0:T(8,128)(2,1)S(1)}, u32[]{:S(2)}, u32[]{:S(2)}) collective-permute-start(bf16[320,2304]{1,0:T(8,128)(2,1)S(1)} %pad_maximum_fusion), channel_id=1, source_target_pairs={{0,24},{8,0},{16,8},{24,16},{32,56},{40,32},{48,40},{56,48},{64,88... | collective-permute-start | bytes 4423688 | tf_op jit(solution)/shard_map/ppermute | solution.py:22
  56.8 2.3 %collective-permute-start.15 = (bf16[256,1024]{1,0:T(8,128)(2,1)S(1)}, bf16[256,1024]{1,0:T(8,128)(2,1)S(1)}, u32[]{:S(2)}, u32[]{:S(2)}) collective-permute-start(bf16[256,1024]{1,0:T(8,128)(2,1)S(1)} %constant_dynamic-update-slice_fusion), channel_id=1, source_target_pairs={{0,4},{1,5},{2,6},{3,7},{4,0},{5,1},{6,2},{7,3},{8,12},{9,13},{10,... | collective-permute-start | bytes 1572872 | tf_op jit(solution)/shard_map/ppermute | solution.py:27
  59.4 8.1 %collective-permute-done.15 = bf16[256,1024]{1,0:T(8,128)(2,1)S(1)} collective-permute-done((bf16[256,1024]{1,0:T(8,128)(2,1)S(1)}, bf16[256,1024]{1,0:T(8,128)(2,1)S(1)}, u32[]{:S(2)}, u32[]{:S(2)}) %collective-permute-start.15) | collective-permute-done | bytes 524320 | tf_op jit(solution)/shard_map/ppermute | solution.py:27
  68.1 3.2 %collective-permute-start.20 = (bf16[256,2048]{1,0:T(8,128)(2,1)S(1)}, bf16[256,2048]{1,0:T(8,128)(2,1)S(1)}, u32[]{:S(2)}, u32[]{:S(2)}) collective-permute-start(bf16[256,2048]{1,0:T(8,128)(2,1)S(1)} %collective-permute-done.19), channel_id=1, source_target_pairs={{0,224},{8,232},{16,240},{24,248},{32,0},{40,8},{48,16},{56,24},{6... | collective-permute-start | bytes 3145736 | tf_op jit(solution)/shard_map/ppermute | solution.py:22
  71.5 7.3 %collective-permute-done.21 = bf16[320,2304]{1,0:T(8,128)(2,1)S(1)} collective-permute-done((bf16[320,2304]{1,0:T(8,128)(2,1)S(1)}, bf16[320,2304]{1,0:T(8,128)(2,1)S(1)}, u32[]{:S(2)}, u32[]{:S(2)}) %collective-permute-start.21) | collective-permute-done | bytes 1474592 | tf_op jit(solution)/shard_map/ppermute | solution.py:22
  79.1 15.5 %collective-permute-done.18 = bf16[256,2048]{1,0:T(8,128)(2,1)S(1)} collective-permute-done((bf16[256,2048]{1,0:T(8,128)(2,1)S(1)}, bf16[256,2048]{1,0:T(8,128)(2,1)S(1)}, u32[]{:S(2)}, u32[]{:S(2)}) %collective-permute-start.18) | collective-permute-done | bytes 1048608 | tf_op jit(solution)/shard_map/ppermute | solution.py:22
  94.6 3.2 %collective-permute-start.26 = (bf16[256,2048]{1,0:T(8,128)(2,1)S(1)}, bf16[256,2048]{1,0:T(8,128)(2,1)S(1)}, u32[]{:S(2)}, u32[]{:S(2)}) collective-permute-start(bf16[256,2048]{1,0:T(8,128)(2,1)S(1)} %collective-permute-done.20), channel_id=1, source_target_pairs={{0,224},{8,232},{16,240},{24,248},{32,0},{40,8},{48,16},{56,24},{6... | collective-permute-start | bytes 3145736 | tf_op jit(solution)/shard_map/ppermute | solution.py:22
  98.3 3.3 %collective-permute-start.24 = (bf16[256,2304]{1,0:T(8,128)(2,1)S(1)}, bf16[256,2304]{1,0:T(8,128)(2,1)S(1)}, u32[]{:S(2)}, u32[]{:S(2)}) collective-permute-start(bf16[256,2304]{1,0:T(8,128)(2,1)S(1)} %pad_maximum_fusion.3), channel_id=1, source_target_pairs={{0,24},{8,0},{16,8},{24,16},{32,56},{40,32},{48,40},{56,48},{64,88... | collective-permute-start | bytes 3538952 | tf_op jit(solution)/shard_map/ppermute | solution.py:22
  101.6 4.2 %shard_map.59 = (bf16[512,1536]{1,0:T(8,128)(2,1)S(1)}, bf16[512,512]{1,0:T(8,128)(2,1)S(1)}, bf16[512,768]{1,0:T(8,128)(2,1)S(1)}, bf16[512,1024]{1,0:T(8,128)(2,1)S(1)}, bf16[512,256]{1,0:T(8,128)(2,1)S(1)}) custom-call(s32[4]{0:T(128)S(1)} %pad_add_fusion.place_ref, bf16[1024,1024]{1,0:T(8,128)(2,1)S(1)} %constant_dynamic-update-slice_fusion.2.mine_ref, ...), custom_call_target="tpu_custom_call" | custom-call | bytes 12582912 | tf_op jit(solution)/shard_map/pallas_call | solution.py:71
  105.7 3.8 %fusion.22 = f32[512,2304]{1,0:T(8,128)S(1)} fusion(bf16[512,1536]{1,0:T(8,128)(2,1)S(1)} %get-tuple-element.71, bf16[1536,2304]{1,0:T(8,128)(2,1)S(1)} %constant_dynamic-update-slice_fusion.16), kind=kOutput, calls=%fused_computation.50 | convolution fusion | flops 3623878656 | bytes 13369344 | tf_op jit(solution)/shard_map/dot_general | solution.py:88
  109.6 1.8 %fusion.21 = f32[512,2048]{1,0:T(8,128)S(1)} fusion(bf16[512,768]{1,0:T(8,128)(2,1)S(1)} %get-tuple-element.70, bf16[768,2048]{1,0:T(8,128)(2,1)S(1)} %constant_dynamic-update-slice_fusion.10), kind=kOutput, calls=%fused_computation.49 | convolution fusion | flops 1610612736 | bytes 8126464 | tf_op jit(solution)/shard_map/dot_general | solution.py:88
  111.4 8.9 %collective-permute-done.25 = bf16[256,2048]{1,0:T(8,128)(2,1)S(1)} collective-permute-done((bf16[256,2048]{1,0:T(8,128)(2,1)S(1)}, bf16[256,2048]{1,0:T(8,128)(2,1)S(1)}, u32[]{:S(2)}, u32[]{:S(2)}) %collective-permute-start.25) | collective-permute-done | bytes 1048608 | tf_op jit(solution)/shard_map/ppermute | solution.py:22
  120.5 3.3 %collective-permute-start.28 = (bf16[128,2048]{1,0:T(8,128)(2,1)S(1)}, bf16[128,2048]{1,0:T(8,128)(2,1)S(1)}, u32[]{:S(2)}, u32[]{:S(2)}) collective-permute-start(bf16[128,2048]{1,0:T(8,128)(2,1)S(1)} %slice.31), channel_id=1, source_target_pairs={{0,224},{8,232},{16,240},{24,248},{32,0},{40,8},{48,16},{56,24},{6... | collective-permute-start | bytes 1572872 | tf_op jit(solution)/shard_map/ppermute | solution.py:22
  123.8 2.9 %fusion.9 = f32[512,2048]{1,0:T(8,128)S(1)} fusion(f32[512,2048]{1,0:T(8,128)S(1)} %fusion.21, bf16[512,1024]{1,0:T(8,128)(2,1)S(1)} %get-tuple-element.67, bf16[256,2048]{1,0:T(8,128)(2,1)S(1)} %collective-permute-done.26, bf16[256,2048]{1,0:T(8,128)(2,1)S(1)} %collective-permute-done.25, bf16[256,2048]{1,0:T(8,128)(2,1)S(1)} %collective-permute-done.20, ...), kind=kOutput, calls=%fused_computation.11 | convolution fusion | flops 2165309440 | bytes 13631488 | tf_op jit(solution)/shard_map/dot_general | solution.py:88
  126.7 2.8 %fusion = bf16[512,2304]{1,0:T(8,128)(2,1)} fusion(f32[512,2304]{1,0:T(8,128)S(1)} %fusion.22, bf16[512,512]{1,0:T(8,128)(2,1)S(1)} %get-tuple-element.58, bf16[256,2304]{1,0:T(8,128)(2,1)S(1)} %collective-permute-done.24, bf16[256,2304]{1,0:T(8,128)(2,1)S(1)} %collective-permute-done.23), kind=kOutput, calls=%fused_computation.1 | convolution fusion | flops 1215037440 | bytes 9961472 | tf_op jit(solution)/shard_map/dot_general | solution.py:88
  129.5 4.4 %collective-permute-done.27 = bf16[128,2048]{1,0:T(8,128)(2,1)S(1)} collective-permute-done((bf16[128,2048]{1,0:T(8,128)(2,1)S(1)}, bf16[128,2048]{1,0:T(8,128)(2,1)S(1)}, u32[]{:S(2)}, u32[]{:S(2)}) %collective-permute-start.27) | collective-permute-done | bytes 524320 | tf_op jit(solution)/shard_map/ppermute | solution.py:22
  134.0 2.0 %add_convert_fusion = bf16[512,2048]{1,0:T(8,128)(2,1)} fusion(f32[512,2048]{1,0:T(8,128)S(1)} %fusion.9, bf16[512,256]{1,0:T(8,128)(2,1)S(1)} %get-tuple-element.78, bf16[128,2048]{1,0:T(8,128)(2,1)S(1)} %collective-permute-done.28, bf16[128,2048]{1,0:T(8,128)(2,1)S(1)} %collective-permute-done.27), kind=kOutput, calls=%fused_computation.10 | convolution fusion | flops 541065216 | bytes 7602176 | tf_op jit(solution)/shard_map/dot_general | solution.py:88
  (70 shorter events, 9.3 us)
Async XLA Ops:
  0.6 20.2 %collective-permute-start = (bf16[64,2304]{1,0:T(8,128)(2,1)}, bf16[64,2304]{1,0:T(8,128)(2,1)S(1)}, u32[]{:S(2)}, u32[]{:S(2)}) collective-permute-start(bf16[64,2304]{1,0:T(8,128)(2,1)} %param.6), channel_id=1, source_target_pairs={{0,32},{8,40},{16,48},{24,56},{32,64},{40,72},{48,80},{56,88},{64,... | collective-permute-start | bytes 884744 | tf_op jit(solution)/shard_map/ppermute | solution.py:22
  2.6 18.2 %collective-permute-start.1 = (bf16[64,2304]{1,0:T(8,128)(2,1)}, bf16[64,2304]{1,0:T(8,128)(2,1)S(1)}, u32[]{:S(2)}, u32[]{:S(2)}) collective-permute-start(bf16[64,2304]{1,0:T(8,128)(2,1)} %param.6), channel_id=1, source_target_pairs={{0,224},{8,232},{16,240},{24,248},{32,0},{40,8},{48,16},{56,24},{6... | collective-permute-start | bytes 884744 | tf_op jit(solution)/shard_map/ppermute | solution.py:22
  6.7 9.7 %collective-permute-start.2 = (bf16[64,2048]{1,0:T(8,128)(2,1)}, bf16[64,2048]{1,0:T(8,128)(2,1)S(1)}, u32[]{:S(2)}, u32[]{:S(2)}) collective-permute-start(bf16[64,2048]{1,0:T(8,128)(2,1)} %param.7), channel_id=1, source_target_pairs={{0,8},{8,16},{16,24},{24,0},{32,40},{40,48},{48,56},{56,32},{64,72... | collective-permute-start | bytes 786440 | tf_op jit(solution)/shard_map/ppermute | solution.py:22
  8.1 12.7 %collective-permute-start.3 = (bf16[64,2048]{1,0:T(8,128)(2,1)}, bf16[64,2048]{1,0:T(8,128)(2,1)S(1)}, u32[]{:S(2)}, u32[]{:S(2)}) collective-permute-start(bf16[64,2048]{1,0:T(8,128)(2,1)} %param.7), channel_id=1, source_target_pairs={{0,24},{8,0},{16,8},{24,16},{32,56},{40,32},{48,40},{56,48},{64,88... | collective-permute-start | bytes 786440 | tf_op jit(solution)/shard_map/ppermute | solution.py:22
  9.9 15.3 %collective-permute-start.6 = (bf16[64,2048]{1,0:T(8,128)(2,1)}, bf16[64,2048]{1,0:T(8,128)(2,1)S(1)}, u32[]{:S(2)}, u32[]{:S(2)}) collective-permute-start(bf16[64,2048]{1,0:T(8,128)(2,1)} %param.7), channel_id=1, source_target_pairs={{0,16},{8,24},{16,0},{24,8},{32,48},{40,56},{48,32},{56,40},{64,80... | collective-permute-start | bytes 786440 | tf_op jit(solution)/shard_map/ppermute | solution.py:22
  16.3 12.5 %collective-permute-start.7 = (bf16[256,1024]{1,0:T(8,128)(2,1)S(1)}, bf16[256,1024]{1,0:T(8,128)(2,1)S(1)}, u32[]{:S(2)}, u32[]{:S(2)}) collective-permute-start(bf16[256,1024]{1,0:T(8,128)(2,1)S(1)} %constant_dynamic-update-slice_fusion), channel_id=1, source_target_pairs={{0,2},{1,3},{2,4},{3,5},{4,6},{5,7},{6,0},{7,1},{8,10},{9,11},{10,... | collective-permute-start | bytes 1572872 | tf_op jit(solution)/shard_map/ppermute | solution.py:27
  20.9 8.0 %collective-permute-start.4 = (bf16[64,2304]{1,0:T(8,128)(2,1)S(1)}, bf16[64,2304]{1,0:T(8,128)(2,1)S(1)}, u32[]{:S(2)}, u32[]{:S(2)}) collective-permute-start(bf16[64,2304]{1,0:T(8,128)(2,1)S(1)} %collective-permute-done), channel_id=1, source_target_pairs={{0,32},{8,40},{16,48},{24,56},{32,64},{40,72},{48,80},{56,88},{64,... | collective-permute-start | bytes 884744 | tf_op jit(solution)/shard_map/ppermute | solution.py:22
  21.9 8.3 %collective-permute-start.5 = (bf16[64,2304]{1,0:T(8,128)(2,1)S(1)}, bf16[64,2304]{1,0:T(8,128)(2,1)S(1)}, u32[]{:S(2)}, u32[]{:S(2)}) collective-permute-start(bf16[64,2304]{1,0:T(8,128)(2,1)S(1)} %collective-permute-done.1), channel_id=1, source_target_pairs={{0,224},{8,232},{16,240},{24,248},{32,0},{40,8},{48,16},{56,24},{6... | collective-permute-start | bytes 884744 | tf_op jit(solution)/shard_map/ppermute | solution.py:22
  25.2 26.9 %collective-permute-start.13 = (bf16[192,2304]{1,0:T(8,128)(2,1)S(1)}, bf16[192,2304]{1,0:T(8,128)(2,1)S(1)}, u32[]{:S(2)}, u32[]{:S(2)}) collective-permute-start(bf16[192,2304]{1,0:T(8,128)(2,1)S(1)} %pad_maximum_fusion.4), channel_id=1, source_target_pairs={{0,8},{8,16},{16,24},{24,0},{32,40},{40,48},{48,56},{56,32},{64,72... | collective-permute-start | bytes 2654216 | tf_op jit(solution)/shard_map/ppermute | solution.py:22
  25.2 26.9 %collective-permute-start.14 = (bf16[192,2304]{1,0:T(8,128)(2,1)S(1)}, bf16[192,2304]{1,0:T(8,128)(2,1)S(1)}, u32[]{:S(2)}, u32[]{:S(2)}) collective-permute-start(bf16[192,2304]{1,0:T(8,128)(2,1)S(1)} %pad_maximum_fusion.4), channel_id=1, source_target_pairs={{0,24},{8,0},{16,8},{24,16},{32,56},{40,32},{48,40},{56,48},{64,88... | collective-permute-start | bytes 2654216 | tf_op jit(solution)/shard_map/ppermute | solution.py:22
  30.2 9.5 %collective-permute-start.8 = (bf16[64,2304]{1,0:T(8,128)(2,1)S(1)}, bf16[64,2304]{1,0:T(8,128)(2,1)S(1)}, u32[]{:S(2)}, u32[]{:S(2)}) collective-permute-start(bf16[64,2304]{1,0:T(8,128)(2,1)S(1)} %collective-permute-done.4), channel_id=1, source_target_pairs={{0,32},{8,40},{16,48},{24,56},{32,64},{40,72},{48,80},{56,88},{64,... | collective-permute-start | bytes 884744 | tf_op jit(solution)/shard_map/ppermute | solution.py:22
  30.2 9.8 %collective-permute-start.9 = (bf16[64,2304]{1,0:T(8,128)(2,1)S(1)}, bf16[64,2304]{1,0:T(8,128)(2,1)S(1)}, u32[]{:S(2)}, u32[]{:S(2)}) collective-permute-start(bf16[64,2304]{1,0:T(8,128)(2,1)S(1)} %collective-permute-done.5), channel_id=1, source_target_pairs={{0,224},{8,232},{16,240},{24,248},{32,0},{40,8},{48,16},{56,24},{6... | collective-permute-start | bytes 884744 | tf_op jit(solution)/shard_map/ppermute | solution.py:22
  33.9 18.2 %collective-permute-start.12 = (bf16[256,1024]{1,0:T(8,128)(2,1)S(1)}, bf16[256,1024]{1,0:T(8,128)(2,1)S(1)}, u32[]{:S(2)}, u32[]{:S(2)}) collective-permute-start(bf16[256,1024]{1,0:T(8,128)(2,1)S(1)} %constant_dynamic-update-slice_fusion), channel_id=1, source_target_pairs={{0,6},{1,7},{2,0},{3,1},{4,2},{5,3},{6,4},{7,5},{8,14},{9,15},{10,... | collective-permute-start | bytes 1572872 | tf_op jit(solution)/shard_map/ppermute | solution.py:27
  40.0 8.1 %collective-permute-start.10 = (bf16[32,2304]{1,0:T(8,128)(2,1)S(1)}, bf16[32,2304]{1,0:T(8,128)(2,1)S(1)}, u32[]{:S(2)}, u32[]{:S(2)}) collective-permute-start(bf16[32,2304]{1,0:T(8,128)(2,1)S(1)} %slice.24), channel_id=1, source_target_pairs={{0,32},{8,40},{16,48},{24,56},{32,64},{40,72},{48,80},{56,88},{64,... | collective-permute-start | bytes 442376 | tf_op jit(solution)/shard_map/ppermute | solution.py:22
  43.9 6.9 %collective-permute-start.11 = (bf16[32,2304]{1,0:T(8,128)(2,1)S(1)}, bf16[32,2304]{1,0:T(8,128)(2,1)S(1)}, u32[]{:S(2)}, u32[]{:S(2)}) collective-permute-start(bf16[32,2304]{1,0:T(8,128)(2,1)S(1)} %slice.25), channel_id=1, source_target_pairs={{0,224},{8,232},{16,240},{24,248},{32,0},{40,8},{48,16},{56,24},{6... | collective-permute-start | bytes 442376 | tf_op jit(solution)/shard_map/ppermute | solution.py:22
  48.2 19.9 %collective-permute-start.17 = (bf16[256,2048]{1,0:T(8,128)(2,1)S(1)}, bf16[256,2048]{1,0:T(8,128)(2,1)S(1)}, u32[]{:S(2)}, u32[]{:S(2)}) collective-permute-start(bf16[256,2048]{1,0:T(8,128)(2,1)S(1)} %get-tuple-element.81), channel_id=1, source_target_pairs={{0,32},{8,40},{16,48},{24,56},{32,64},{40,72},{48,80},{56,88},{64,... | collective-permute-start | bytes 3145736 | tf_op jit(solution)/shard_map/ppermute | solution.py:22
  50.7 17.4 %collective-permute-start.19 = (bf16[256,2048]{1,0:T(8,128)(2,1)S(1)}, bf16[256,2048]{1,0:T(8,128)(2,1)S(1)}, u32[]{:S(2)}, u32[]{:S(2)}) collective-permute-start(bf16[256,2048]{1,0:T(8,128)(2,1)S(1)} %get-tuple-element.81), channel_id=1, source_target_pairs={{0,224},{8,232},{16,240},{24,248},{32,0},{40,8},{48,16},{56,24},{6... | collective-permute-start | bytes 3145736 | tf_op jit(solution)/shard_map/ppermute | solution.py:22
  52.1 15.7 %copy-start = (bf16[192,2304]{1,0:T(8,128)(2,1)}, bf16[192,2304]{1,0:T(8,128)(2,1)S(1)}, u32[]{:S(2)}) copy-start(bf16[192,2304]{1,0:T(8,128)(2,1)S(1)} %collective-permute-done.13) | copy-start | bytes 2654212
  52.1 26.7 %collective-permute-start.21 = (bf16[320,2304]{1,0:T(8,128)(2,1)S(1)}, bf16[320,2304]{1,0:T(8,128)(2,1)S(1)}, u32[]{:S(2)}, u32[]{:S(2)}) collective-permute-start(bf16[320,2304]{1,0:T(8,128)(2,1)S(1)} %pad_maximum_fusion), channel_id=1, source_target_pairs={{0,8},{8,16},{16,24},{24,0},{32,40},{40,48},{48,56},{56,32},{64,72... | collective-permute-start | bytes 4423688 | tf_op jit(solution)/shard_map/ppermute | solution.py:22
  52.2 26.8 %collective-permute-start.22 = (bf16[320,2304]{1,0:T(8,128)(2,1)S(1)}, bf16[320,2304]{1,0:T(8,128)(2,1)S(1)}, u32[]{:S(2)}, u32[]{:S(2)}) collective-permute-start(bf16[320,2304]{1,0:T(8,128)(2,1)S(1)} %pad_maximum_fusion), channel_id=1, source_target_pairs={{0,24},{8,0},{16,8},{24,16},{32,56},{40,32},{48,40},{56,48},{64,88... | collective-permute-start | bytes 4423688 | tf_op jit(solution)/shard_map/ppermute | solution.py:22
  56.8 10.7 %collective-permute-start.15 = (bf16[256,1024]{1,0:T(8,128)(2,1)S(1)}, bf16[256,1024]{1,0:T(8,128)(2,1)S(1)}, u32[]{:S(2)}, u32[]{:S(2)}) collective-permute-start(bf16[256,1024]{1,0:T(8,128)(2,1)S(1)} %constant_dynamic-update-slice_fusion), channel_id=1, source_target_pairs={{0,4},{1,5},{2,6},{3,7},{4,0},{5,1},{6,2},{7,3},{8,12},{9,13},{10,... | collective-permute-start | bytes 1572872 | tf_op jit(solution)/shard_map/ppermute | solution.py:27
  67.5 34.0 %collective-permute-start.16 = (bf16[1024,1024]{1,0:T(8,128)(2,1)S(1)}, bf16[1024,1024]{1,0:T(8,128)(2,1)S(1)}, u32[]{:S(2)}, u32[]{:S(2)}) collective-permute-start(bf16[1024,1024]{1,0:T(8,128)(2,1)S(1)} %constant_dynamic-update-slice_fusion.2.mine_ref), channel_id=1, source_target_pairs={{0,1},{1,0},{2,3},{3,2},{4,5},{5,4},{6,7},{7,6},{8,9},{9,8},{10,11... | collective-permute-start | bytes 6291464 | tf_op jit(solution)/shard_map/ppermute | solution.py:27
  68.1 26.5 %collective-permute-start.18 = (bf16[256,2048]{1,0:T(8,128)(2,1)S(1)}, bf16[256,2048]{1,0:T(8,128)(2,1)S(1)}, u32[]{:S(2)}, u32[]{:S(2)}) collective-permute-start(bf16[256,2048]{1,0:T(8,128)(2,1)S(1)} %collective-permute-done.17), channel_id=1, source_target_pairs={{0,32},{8,40},{16,48},{24,56},{32,64},{40,72},{48,80},{56,88},{64,... | collective-permute-start | bytes 3145736 | tf_op jit(solution)/shard_map/ppermute | solution.py:22
  68.1 26.5 %collective-permute-start.20 = (bf16[256,2048]{1,0:T(8,128)(2,1)S(1)}, bf16[256,2048]{1,0:T(8,128)(2,1)S(1)}, u32[]{:S(2)}, u32[]{:S(2)}) collective-permute-start(bf16[256,2048]{1,0:T(8,128)(2,1)S(1)} %collective-permute-done.19), channel_id=1, source_target_pairs={{0,224},{8,232},{16,240},{24,248},{32,0},{40,8},{48,16},{56,24},{6... | collective-permute-start | bytes 3145736 | tf_op jit(solution)/shard_map/ppermute | solution.py:22
  71.5 26.4 %slice-start = ((bf16[192,2304]{1,0:T(8,128)(2,1)}), bf16[96,2304]{1,0:T(8,128)(2,1)S(1)}, s32[]{:S(2)}) async-start(bf16[192,2304]{1,0:T(8,128)(2,1)} %copy-done), calls=%async_computation | async-start | bytes 884736 | tf_op jit(solution)/shard_map/slice | solution.py:32
  79.1 19.1 %slice-start.1 = ((bf16[192,2304]{1,0:T(8,128)(2,1)}), bf16[96,2304]{1,0:T(8,128)(2,1)S(1)}, s32[]{:S(2)}) async-start(bf16[192,2304]{1,0:T(8,128)(2,1)} %copy-done.1), calls=%async_computation.1 | async-start | bytes 884736 | tf_op jit(solution)/shard_map/slice | solution.py:32
  94.6 25.7 %collective-permute-start.25 = (bf16[256,2048]{1,0:T(8,128)(2,1)S(1)}, bf16[256,2048]{1,0:T(8,128)(2,1)S(1)}, u32[]{:S(2)}, u32[]{:S(2)}) collective-permute-start(bf16[256,2048]{1,0:T(8,128)(2,1)S(1)} %collective-permute-done.18), channel_id=1, source_target_pairs={{0,32},{8,40},{16,48},{24,56},{32,64},{40,72},{48,80},{56,88},{64,... | collective-permute-start | bytes 3145736 | tf_op jit(solution)/shard_map/ppermute | solution.py:22
  94.6 25.7 %collective-permute-start.26 = (bf16[256,2048]{1,0:T(8,128)(2,1)S(1)}, bf16[256,2048]{1,0:T(8,128)(2,1)S(1)}, u32[]{:S(2)}, u32[]{:S(2)}) collective-permute-start(bf16[256,2048]{1,0:T(8,128)(2,1)S(1)} %collective-permute-done.20), channel_id=1, source_target_pairs={{0,224},{8,232},{16,240},{24,248},{32,0},{40,8},{48,16},{56,24},{6... | collective-permute-start | bytes 3145736 | tf_op jit(solution)/shard_map/ppermute | solution.py:22
  98.0 28.7 %collective-permute-start.23 = (bf16[256,2304]{1,0:T(8,128)(2,1)S(1)}, bf16[256,2304]{1,0:T(8,128)(2,1)S(1)}, u32[]{:S(2)}, u32[]{:S(2)}) collective-permute-start(bf16[256,2304]{1,0:T(8,128)(2,1)S(1)} %pad_maximum_fusion.2), channel_id=1, source_target_pairs={{0,8},{8,16},{16,24},{24,0},{32,40},{40,48},{48,56},{56,32},{64,72... | collective-permute-start | bytes 3538952 | tf_op jit(solution)/shard_map/ppermute | solution.py:22
  98.3 28.5 %collective-permute-start.24 = (bf16[256,2304]{1,0:T(8,128)(2,1)S(1)}, bf16[256,2304]{1,0:T(8,128)(2,1)S(1)}, u32[]{:S(2)}, u32[]{:S(2)}) collective-permute-start(bf16[256,2304]{1,0:T(8,128)(2,1)S(1)} %pad_maximum_fusion.3), channel_id=1, source_target_pairs={{0,24},{8,0},{16,8},{24,16},{32,56},{40,32},{48,40},{56,48},{64,88... | collective-permute-start | bytes 3538952 | tf_op jit(solution)/shard_map/ppermute | solution.py:22
  120.4 13.6 %collective-permute-start.27 = (bf16[128,2048]{1,0:T(8,128)(2,1)S(1)}, bf16[128,2048]{1,0:T(8,128)(2,1)S(1)}, u32[]{:S(2)}, u32[]{:S(2)}) collective-permute-start(bf16[128,2048]{1,0:T(8,128)(2,1)S(1)} %slice.30), channel_id=1, source_target_pairs={{0,32},{8,40},{16,48},{24,56},{32,64},{40,72},{48,80},{56,88},{64,... | collective-permute-start | bytes 1572872 | tf_op jit(solution)/shard_map/ppermute | solution.py:22
  120.5 13.5 %collective-permute-start.28 = (bf16[128,2048]{1,0:T(8,128)(2,1)S(1)}, bf16[128,2048]{1,0:T(8,128)(2,1)S(1)}, u32[]{:S(2)}, u32[]{:S(2)}) collective-permute-start(bf16[128,2048]{1,0:T(8,128)(2,1)S(1)} %slice.31), channel_id=1, source_target_pairs={{0,224},{8,232},{16,240},{24,248},{32,0},{40,8},{48,16},{56,24},{6... | collective-permute-start | bytes 1572872 | tf_op jit(solution)/shard_map/ppermute | solution.py:22
  (1 other events, 15.6 us)
